TPU v7x, 256 devices: a whole 4x4x8 slice. The times are simulated.
256 devices in a mesh: tile: 128 (over y_lo, z, x, core), mode: 2 (over y_hi).
Axes of the slice: x: 4, y: 4 (y_hi: 2, y_lo: 2; y = y_hi * 2 + y_lo), z: 8, core: 2. Of those that a mesh axis runs over, the one named last changes fastest.
Arguments:
- object_tiles: float32 [128, 2, 2, 256, 256], P('tile'), may hold values from -1.5 to 1.5
- probe_modes: float32 [2, 12, 256, 256], P(None, 'mode'), may hold values from -0.9 to 0.9
- propagator: bfloat16 [2, 256, 256], replicated, may hold values from -1.5 to 1.5
- offsets: int32 [128, 2, 2], P('tile'), may hold values from -128 to 127
- counts: int32 [128], P('tile'), may hold values from 1 to 2, as said below
- measured: float32 [128, 2, 256, 256], P('tile'), may hold values from 0.3 to 3
Outputs:
- object_grad: float32 [128, 2, 2, 256, 256], P('tile')
- probe_grad: float32 [128, 2, 12, 256, 256], P('tile', None, 'mode')
Inputs may be any that keep to these rules, and one draw needn't show every extreme that they name: `counts`: each tile holds at least one position, and some tile holds 2 in every draw.
All inputs are finite; a program needn't handle non-finite values.
Results may differ from a plain program's by a relative error of at most 0.015.
Values sent between devices are 32-bit elements; how exact they have to be, the bound alone decides.
No kernel may reach another device: no remote copies, remote signals or barrier semaphores. Data moves between devices by JAX's collectives and lax.ppermute only.
A program may use at most 128 MiB of HBM per device.

v0:
```python
import math

import jax
import jax.numpy as jnp
from jax import lax
from jax.sharding import PartitionSpec as P

GY = 8


def from_behind(value, axis, steps):
    count = lax.axis_size(axis)
    first, last = (max(0, -steps), min(count, count - steps))
    return lax.ppermute(value, axis, [(source, source + steps) for source in range(first, last)])


def complex_product(einsum_form, left_pair, right_pair):

    def single_product(first_op, second_op):
        return jnp.einsum(einsum_form, first_op, second_op, preferred_element_type=jnp.float32)

    real_part = single_product(left_pair[0], right_pair[0]) - single_product(
        left_pair[1], right_pair[1]
    )
    imag_part = single_product(left_pair[0], right_pair[1]) + single_product(
        left_pair[1], right_pair[0]
    )
    return (real_part, imag_part)


def rounded(pair):
    return (pair[0].astype(jnp.bfloat16), pair[1].astype(jnp.bfloat16))


def sandwich(left_form, left_matrix, right_form, right_matrix, wavefield):
    first_pass = complex_product(left_form, left_matrix, rounded(wavefield))
    return complex_product(right_form, rounded(first_pass), right_matrix)


def dft_table(extent):
    counter = jnp.arange(extent, dtype=jnp.int32)
    phase_step = counter[:, None] * counter[None, :] % extent
    phase_angle = -2.0 * math.pi / extent * phase_step.astype(jnp.float32)
    norm_scale = 1.0 / math.sqrt(extent)
    return (
        (jnp.cos(phase_angle) * norm_scale).astype(jnp.bfloat16),
        (jnp.sin(phase_angle) * norm_scale).astype(jnp.bfloat16),
    )


def forward(probe_pair, patch_block, kernel_pair, dft_pair):
    wavefield = probe_pair
    fields = []
    layers = patch_block.shape[1]
    farfield = None
    for slice_index in range(layers):
        fields.append(wavefield)
        slab_re = patch_block[0, slice_index]
        slab_im = patch_block[1, slice_index]
        exit_re = wavefield[0] * slab_re - wavefield[1] * slab_im
        exit_im = wavefield[0] * slab_im + wavefield[1] * slab_re
        if slice_index + 1 < layers:
            wavefield = sandwich(
                "ij,mjk->mik", kernel_pair, "mij,kj->mik", kernel_pair, (exit_re, exit_im)
            )
        else:
            farfield = sandwich(
                "ij,mjk->mik", dft_pair, "mij,jk->mik", dft_pair, (exit_re, exit_im)
            )
    return (fields, farfield)


def backward(chi_field, fields, patch_block, kernel_pair, dft_pair):
    conj_table = (dft_pair[0], -dft_pair[1])
    conj_kernel = (kernel_pair[0], -kernel_pair[1])
    back_wave = sandwich("ij,mjk->mik", conj_table, "mij,jk->mik", conj_table, chi_field)
    layers = patch_block.shape[1]
    slice_grads = [None] * layers
    bar_re, bar_im = back_wave
    for slice_index in reversed(range(layers)):
        wavefield = fields[slice_index]
        slab_re = patch_block[0, slice_index]
        slab_im = patch_block[1, slice_index]
        grad_re = jnp.sum(wavefield[0] * back_wave[0] + wavefield[1] * back_wave[1], axis=0)
        grad_im = jnp.sum(wavefield[0] * back_wave[1] - wavefield[1] * back_wave[0], axis=0)
        slice_grads[slice_index] = (grad_re, grad_im)
        bar_re = slab_re * back_wave[0] + slab_im * back_wave[1]
        bar_im = slab_re * back_wave[1] - slab_im * back_wave[0]
        if slice_index > 0:
            back_wave = sandwich(
                "ji,mjk->mik", conj_kernel, "mij,jk->mik", conj_kernel, (bar_re, bar_im)
            )
    patch_grad = jnp.stack(
        [jnp.stack([pair[0] for pair in slice_grads]), jnp.stack([pair[1] for pair in slice_grads])]
    )
    return (patch_grad, (bar_re, bar_im))


def rim_block(block, vertical, lateral, margin):
    extent = block.shape[-1]
    if vertical < 0:
        block = block[:, :, extent - margin :, :]
    elif vertical > 0:
        block = block[:, :, :margin, :]
    if lateral < 0:
        block = block[:, :, :, extent - margin :]
    elif lateral > 0:
        block = block[:, :, :, :margin]
    return block


def body(object_tiles, probe_modes, propagator, offsets, counts, measured):
    extent = probe_modes.shape[-1]
    margin = extent // 2
    own_tile = object_tiles[0]
    layers = own_tile.shape[1]
    span = own_tile.shape[-1]
    column = lax.axis_index("tile") % GY
    directions = [
        (vertical, lateral)
        for vertical in (-1, 0, 1)
        for lateral in (-1, 0, 1)
        if vertical != 0 or lateral != 0
    ]
    gathered = {}
    for vertical, lateral in directions:
        offset_by = -(vertical * GY + lateral)
        incoming = rim_block(from_behind(own_tile, "tile", offset_by), vertical, lateral, margin)
        inside = ((column + lateral >= 0) & (column + lateral < GY)).astype(jnp.float32)
        gathered[vertical, lateral] = incoming * inside
    gathered[0, 0] = own_tile
    row_bands = []
    for vertical in (-1, 0, 1):
        row_bands.append(
            jnp.concatenate([gathered[vertical, lateral] for lateral in (-1, 0, 1)], axis=3)
        )
    canvas = jnp.concatenate(row_bands, axis=2)
    dft_pair = dft_table(extent)
    kernel_pair = (propagator[0], propagator[1])
    probe_pair = (probe_modes[0], probe_modes[1])
    anchor = jnp.zeros((), jnp.int32)

    def visit_slot(slot_index, loop_state):
        grad_canvas, probe_sum = loop_state
        row_start = offsets[0, slot_index, 0] + margin
        col_start = offsets[0, slot_index, 1] + margin
        corner = (anchor, anchor, row_start, col_start)
        patch_block = lax.dynamic_slice(canvas, corner, (2, layers, extent, extent))
        fields, farfield = forward(probe_pair, patch_block, kernel_pair, dft_pair)
        partial_sum = jnp.sum(farfield[0] * farfield[0] + farfield[1] * farfield[1], axis=0)
        intensity = lax.psum(partial_sum, "mode")
        is_valid = (slot_index < counts[0]).astype(jnp.float32)
        residual = (intensity - measured[0, slot_index]) * is_valid
        chi_field = (2.0 * residual * farfield[0], 2.0 * residual * farfield[1])
        patch_grad, probe_part = backward(chi_field, fields, patch_block, kernel_pair, dft_pair)
        previous = lax.dynamic_slice(grad_canvas, corner, (2, layers, extent, extent))
        grad_canvas = lax.dynamic_update_slice(grad_canvas, previous + patch_grad, corner)
        return (grad_canvas, probe_sum + jnp.stack(probe_part))

    upper = measured.shape[1]
    start_state = (jnp.zeros(canvas.shape, jnp.float32), jnp.zeros(probe_modes.shape, jnp.float32))
    grad_canvas, probe_sum = lax.fori_loop(0, upper, visit_slot, start_state)

    def canvas_range(direction):
        if direction < 0:
            return (0, margin)
        if direction > 0:
            return (margin + span, margin)
        return (margin, span)

    def tile_start(direction):
        return span - margin if direction < 0 else 0

    own_grad = grad_canvas[:, :, margin : margin + span, margin : margin + span]
    for vertical, lateral in directions:
        row_from, row_len = canvas_range(vertical)
        col_from, col_len = canvas_range(lateral)
        outgoing = grad_canvas[:, :, row_from : row_from + row_len, col_from : col_from + col_len]
        incoming = from_behind(outgoing, "tile", vertical * GY + lateral)
        inside = ((column - lateral >= 0) & (column - lateral < GY)).astype(jnp.float32)
        row_to = tile_start(vertical)
        col_to = tile_start(lateral)
        own_grad = own_grad.at[:, :, row_to : row_to + row_len, col_to : col_to + col_len].add(
            incoming * inside
        )
    object_grad = lax.psum(own_grad, "mode")
    return (object_grad.reshape(object_tiles.shape), probe_sum[None])


def solution(mesh):
    placed = (
        P("tile", None, None, None, None),
        P(None, "mode", None, None),
        P(),
        P("tile", None, None),
        P("tile"),
        P("tile", None, None, None),
    )
    return jax.shard_map(
        body,
        mesh=mesh,
        in_specs=placed,
        out_specs=(P("tile", None, None, None, None), P("tile", None, "mode", None, None)),
        check_vma=False,
    )
```

profile of v0, /device:TPU:1, one launch (start us, length us, event | category | flops | bytes accessed | tf_op | source)
XLA Modules:
  0.0 479.3 jit_solution(11236431859196244065)
XLA Ops:
  8.0 5.2 %collective-permute-start.4 = (f32[2,2,256,256]{3,2,1,0:T(8,128)}, f32[2,2,256,256]{3,2,1,0:T(8,128)}, u32[]{:S(2)}, u32[]{:S(2)}) collective-permute-start(f32[2,2,256,256]{3,2,1,0:T(8,128)} %bitcast.335), channel_id=1, source_target_pairs={{2,0},{4,2},{6,4},{8,6},{10,8},{12,10},{14,12},{16,14},{18,16},{20... | collective-permute-start | bytes 3145736 | tf_op jit(solution)/shard_map/ppermute | solution.py:14
  17.7 5.3 %collective-permute-start.2 = (f32[2,2,256,256]{3,2,1,0:T(8,128)}, f32[2,2,256,256]{3,2,1,0:T(8,128)}, u32[]{:S(2)}, u32[]{:S(2)}) collective-permute-start(f32[2,2,256,256]{3,2,1,0:T(8,128)} %bitcast.339), channel_id=1, source_target_pairs={{0,14},{2,16},{4,18},{6,20},{8,22},{10,24},{12,26},{14,28},{16,30}... | collective-permute-start | bytes 3145736 | tf_op jit(solution)/shard_map/ppermute | solution.py:14
  24.5 2.4 slice_bitcast_fusion
  28.8 15.1 %collective-permute-done.7 = f32[2,2,256,256]{3,2,1,0:T(8,128)} collective-permute-done((f32[2,2,256,256]{3,2,1,0:T(8,128)}, f32[2,2,256,256]{3,2,1,0:T(8,128)}, u32[]{:S(2)}, u32[]{:S(2)}) %collective-permute-start.7) | collective-permute-done | bytes 1048608 | tf_op jit(solution)/shard_map/ppermute | solution.py:14
  46.2 5.1 %collective-permute-start.1 = (f32[2,2,256,256]{3,2,1,0:T(8,128)S(1)}, f32[2,2,256,256]{3,2,1,0:T(8,128)S(1)}, u32[]{:S(2)}, u32[]{:S(2)}) collective-permute-start(f32[2,2,256,256]{3,2,1,0:T(8,128)S(1)} %bitcast.341), channel_id=1, source_target_pairs={{0,16},{2,18},{4,20},{6,22},{8,24},{10,26},{12,28},{14,30},{16,32}... | collective-permute-start | bytes 3145736 | tf_op jit(solution)/shard_map/ppermute | solution.py:14
  52.3 13.7 %collective-permute-done.5 = f32[2,2,256,256]{3,2,1,0:T(8,128)} collective-permute-done((f32[2,2,256,256]{3,2,1,0:T(8,128)}, f32[2,2,256,256]{3,2,1,0:T(8,128)}, u32[]{:S(2)}, u32[]{:S(2)}) %collective-permute-start.5) | collective-permute-done | bytes 1048608 | tf_op jit(solution)/shard_map/ppermute | solution.py:14
  66.1 14.9 %collective-permute-start = (f32[2,2,256,256]{3,2,1,0:T(8,128)S(1)}, f32[2,2,256,256]{3,2,1,0:T(8,128)S(1)}, u32[]{:S(2)}, u32[]{:S(2)}) collective-permute-start(f32[2,2,256,256]{3,2,1,0:T(8,128)S(1)} %bitcast.342), channel_id=1, source_target_pairs={{0,18},{2,20},{4,22},{6,24},{8,26},{10,28},{12,30},{14,32},{16,34}... | collective-permute-start | bytes 3145736 | tf_op jit(solution)/shard_map/ppermute | solution.py:14
  84.1 10.7 %collective-permute-done.6 = f32[2,2,256,256]{3,2,1,0:T(8,128)S(1)} collective-permute-done((f32[2,2,256,256]{3,2,1,0:T(8,128)S(1)}, f32[2,2,256,256]{3,2,1,0:T(8,128)S(1)}, u32[]{:S(2)}, u32[]{:S(2)}) %collective-permute-start.6) | collective-permute-done | bytes 1048608 | tf_op jit(solution)/shard_map/ppermute | solution.py:14
  94.9 2.2 maximum_maximum_fusion
  97.1 2.6 broadcast_in_dim.15
  99.7 260.6 %while.28 = (s32[]{:T(128)}, f32[2,2,512,512]{3,2,1,0:T(8,128)}, f32[2,6,256,256]{3,2,1,0:T(8,128)}, s32[1,2,2]{2,1,0:T(2,128)S(1)}, f32[2,2,512,512]{3,2,1,0:T(...) while((s32[]{:T(128)}, f32[2,2,512,512]{3,2,1,0:T(8,128)}, ...), condition=%wide.region_7.8_spmd.clone.clone, body=%wide.region_0.7_spmd.clone.clone.sunk | while | flops 6495338496 | bytes 190841648 | solution.py:162
  140.3 3.3 add_reduce_fusion.4
  144.4 75.2 %all-reduce.5.cloned.1.call-done = f32[256,256]{1,0:T(8,128)} async-done(((f32[256,256]{1,0:T(8,128)}), f32[256,256]{1,0:T(8,128)}) %all-reduce.5.cloned.1.call-update) | async-done | bytes 262160 | tf_op jit(solution)/shard_map/while/body/eval_jaxpr/psum | solution.py:151
  230.4 2.7 subtract_convert_fusion.8
  238.0 2.9 add_bitcast_fusion.2
  241.0 2.8 maximum_add_fusion.4
  243.8 11.8 %dynamic_update_slice.14 = f32[2,2,512,512]{3,2,1,0:T(8,128)} dynamic-update-slice(f32[2,2,512,512]{3,2,1,0:T(8,128)} %get-tuple-element.797, f32[2,2,256,256]{3,2,1,0:T(8,128)} %maximum_add_fusion.4, s32[]{:T(128)} %constant.334.clone.1..sunk, s32[]{:T(128)} %constant.334.clone.1..sunk, s32[]{:T(128)S(6)} %select_n.179, s32[]{:T(128)S(6)} %select_n.180) | dynamic-update-slice | bytes 2097156 | tf_op jit(solution)/shard_map/while/body/eval_jaxpr/dynamic_update_slice | solution.py:157
  255.6 4.0 maximum_add_fusion.5
  280.0 3.3 add_reduce_fusion.4
  284.0 35.1 %all-reduce.5.cloned.1.call-done = f32[256,256]{1,0:T(8,128)} async-done(((f32[256,256]{1,0:T(8,128)}), f32[256,256]{1,0:T(8,128)}) %all-reduce.5.cloned.1.call-update) | async-done | bytes 262160 | tf_op jit(solution)/shard_map/while/body/eval_jaxpr/psum | solution.py:151
  329.9 2.7 subtract_convert_fusion.8
  337.6 2.9 add_bitcast_fusion.2
  340.6 2.8 maximum_add_fusion.4
  343.4 12.0 %dynamic_update_slice.14 = f32[2,2,512,512]{3,2,1,0:T(8,128)} dynamic-update-slice(f32[2,2,512,512]{3,2,1,0:T(8,128)} %get-tuple-element.797, f32[2,2,256,256]{3,2,1,0:T(8,128)} %maximum_add_fusion.4, s32[]{:T(128)} %constant.334.clone.1..sunk, s32[]{:T(128)} %constant.334.clone.1..sunk, s32[]{:T(128)S(6)} %select_n.179, s32[]{:T(128)S(6)} %select_n.180) | dynamic-update-slice | bytes 2097156 | tf_op jit(solution)/shard_map/while/body/eval_jaxpr/dynamic_update_slice | solution.py:157
  355.4 4.9 %maximum_add_fusion.5 = f32[2,6,256,256]{3,2,1,0:T(8,128)} fusion(f32[1,6,256,256]{3,2,1,0:T(8,128)} %get-tuple-element.777, f32[1,6,256,256]{3,2,1,0:T(8,128)} %get-tuple-element.778, f32[2,6,256,256]{3,2,1,0:T(8,128)} %get-tuple-element.798, pred[]{:T(512)S(6)} %compare.55), kind=kLoop, calls=%fused_computation.3.clone.1 | loop fusion | flops 2359296 | bytes 9437185 | tf_op jit(solution)/shard_map/while/body/eval_jaxpr/add | solution.py:158
  368.0 3.3 collective-permute-start.11
  373.6 11.4 %collective-permute-done.8 = f32[2,2,128,128]{3,2,1,0:T(8,128)S(1)} collective-permute-done((f32[2,2,128,128]{3,2,1,0:T(8,128)S(1)}, f32[2,2,128,128]{3,2,1,0:T(8,128)S(1)}, u32[]{:S(2)}, u32[]{:S(2)}) %collective-permute-start.8) | collective-permute-done | bytes 262176 | tf_op jit(solution)/shard_map/ppermute | solution.py:14
  387.0 4.7 collective-permute-start.14
  391.9 6.1 %collective-permute-start.15 = (f32[2,2,128,128]{3,2,1,0:T(8,128)}, f32[2,2,128,128]{3,2,1,0:T(8,128)S(1)}, u32[]{:S(2)}, u32[]{:S(2)}) collective-permute-start(f32[2,2,128,128]{3,2,1,0:T(8,128)} %get-tuple-element.646), channel_id=1, source_target_pairs={{0,18},{2,20},{4,22},{6,24},{8,26},{10,28},{12,30},{14,32},{16,34}... | collective-permute-start | bytes 786440 | tf_op jit(solution)/shard_map/ppermute | solution.py:14
  400.6 2.6 scatter-add.35
  405.6 63.6 %all-reduce.3.cloned.1.call-done = f32[1,2,2,256,256]{4,3,2,1,0:T(8,128)} async-done(((f32[1,2,2,256,256]{4,3,2,1,0:T(8,128)}), f32[1,2,2,256,256]{4,3,2,1,0:T(8,128)}) %all-reduce.3.cloned.1.call-update) | async-done | bytes 1048592 | tf_op jit(solution)/shard_map/psum | solution.py:186
  469.1 2.3 copy.92
  (188 shorter events, 98.3 us)
Async XLA Ops:
  8.0 73.9 %collective-permute-start.4 = (f32[2,2,256,256]{3,2,1,0:T(8,128)}, f32[2,2,256,256]{3,2,1,0:T(8,128)}, u32[]{:S(2)}, u32[]{:S(2)}) collective-permute-start(f32[2,2,256,256]{3,2,1,0:T(8,128)} %bitcast.335), channel_id=1, source_target_pairs={{2,0},{4,2},{6,4},{8,6},{10,8},{12,10},{14,12},{16,14},{18,16},{20... | collective-permute-start | bytes 3145736 | tf_op jit(solution)/shard_map/ppermute | solution.py:14
  13.2 69.9 %collective-permute-start.3 = (f32[2,2,256,256]{3,2,1,0:T(8,128)}, f32[2,2,256,256]{3,2,1,0:T(8,128)}, u32[]{:S(2)}, u32[]{:S(2)}) collective-permute-start(f32[2,2,256,256]{3,2,1,0:T(8,128)} %bitcast.336), channel_id=1, source_target_pairs={{0,2},{2,4},{4,6},{6,8},{8,10},{10,12},{12,14},{14,16},{16,18},{18... | collective-permute-start | bytes 3145736 | tf_op jit(solution)/shard_map/ppermute | solution.py:14
  15.1 28.9 %collective-permute-start.7 = (f32[2,2,256,256]{3,2,1,0:T(8,128)}, f32[2,2,256,256]{3,2,1,0:T(8,128)}, u32[]{:S(2)}, u32[]{:S(2)}) collective-permute-start(f32[2,2,256,256]{3,2,1,0:T(8,128)} %bitcast.337), channel_id=1, source_target_pairs={{18,0},{20,2},{22,4},{24,6},{26,8},{28,10},{30,12},{32,14},{34,16}... | collective-permute-start | bytes 3145736 | tf_op jit(solution)/shard_map/ppermute | solution.py:14
  16.4 49.7 %collective-permute-start.5 = (f32[2,2,256,256]{3,2,1,0:T(8,128)}, f32[2,2,256,256]{3,2,1,0:T(8,128)}, u32[]{:S(2)}, u32[]{:S(2)}) collective-permute-start(f32[2,2,256,256]{3,2,1,0:T(8,128)} %bitcast.338), channel_id=1, source_target_pairs={{14,0},{16,2},{18,4},{20,6},{22,8},{24,10},{26,12},{28,14},{30,16}... | collective-permute-start | bytes 3145736 | tf_op jit(solution)/shard_map/ppermute | solution.py:14
  17.7 28.5 %collective-permute-start.2 = (f32[2,2,256,256]{3,2,1,0:T(8,128)}, f32[2,2,256,256]{3,2,1,0:T(8,128)}, u32[]{:S(2)}, u32[]{:S(2)}) collective-permute-start(f32[2,2,256,256]{3,2,1,0:T(8,128)} %bitcast.339), channel_id=1, source_target_pairs={{0,14},{2,16},{4,18},{6,20},{8,22},{10,24},{12,26},{14,28},{16,30}... | collective-permute-start | bytes 3145736 | tf_op jit(solution)/shard_map/ppermute | solution.py:14
  24.5 2.4 copy-start.17
  24.5 19.5 %copy-start.16 = (f32[1,2,2,256,256]{4,3,2,1,0:T(8,128)S(1)}, f32[1,2,2,256,256]{4,3,2,1,0:T(8,128)}, u32[]{:S(2)}) copy-start(f32[1,2,2,256,256]{4,3,2,1,0:T(8,128)} %param.24) | copy-start | bytes 3145732
  44.0 50.8 %collective-permute-start.6 = (f32[2,2,256,256]{3,2,1,0:T(8,128)S(1)}, f32[2,2,256,256]{3,2,1,0:T(8,128)S(1)}, u32[]{:S(2)}, u32[]{:S(2)}) collective-permute-start(f32[2,2,256,256]{3,2,1,0:T(8,128)S(1)} %bitcast.340), channel_id=1, source_target_pairs={{16,0},{18,2},{20,4},{22,6},{24,8},{26,10},{28,12},{30,14},{32,16}... | collective-permute-start | bytes 3145736 | tf_op jit(solution)/shard_map/ppermute | solution.py:14
  46.2 48.6 %collective-permute-start.1 = (f32[2,2,256,256]{3,2,1,0:T(8,128)S(1)}, f32[2,2,256,256]{3,2,1,0:T(8,128)S(1)}, u32[]{:S(2)}, u32[]{:S(2)}) collective-permute-start(f32[2,2,256,256]{3,2,1,0:T(8,128)S(1)} %bitcast.341), channel_id=1, source_target_pairs={{0,16},{2,18},{4,20},{6,22},{8,24},{10,26},{12,28},{14,30},{16,32}... | collective-permute-start | bytes 3145736 | tf_op jit(solution)/shard_map/ppermute | solution.py:14
  66.1 28.8 %collective-permute-start = (f32[2,2,256,256]{3,2,1,0:T(8,128)S(1)}, f32[2,2,256,256]{3,2,1,0:T(8,128)S(1)}, u32[]{:S(2)}, u32[]{:S(2)}) collective-permute-start(f32[2,2,256,256]{3,2,1,0:T(8,128)S(1)} %bitcast.342), channel_id=1, source_target_pairs={{0,18},{2,20},{4,22},{6,24},{8,26},{10,28},{12,30},{14,32},{16,34}... | collective-permute-start | bytes 3145736 | tf_op jit(solution)/shard_map/ppermute | solution.py:14
  97.1 2.6 copy-start.18
  119.8 5.5 %copy-start.1 = (f32[6,256,256]{2,1,0:T(8,128)}, f32[6,256,256]{2,1,0:T(8,128)S(1)}, u32[]{:S(2)}) copy-start(f32[6,256,256]{2,1,0:T(8,128)S(1)} %get-tuple-element.819) | copy-start | bytes 4718596 | tf_op jit(solution)/shard_map/while
  119.8 5.5 %copy-start.3 = (f32[6,256,256]{2,1,0:T(8,128)}, f32[6,256,256]{2,1,0:T(8,128)S(1)}, u32[]{:S(2)}) copy-start(f32[6,256,256]{2,1,0:T(8,128)S(1)} %get-tuple-element.818) | copy-start | bytes 4718596 | tf_op jit(solution)/shard_map/while
  119.8 99.8 %all-reduce.5.cloned.1.call-start = ((), (), s32[]{:S(2)}) async-start(), calls=%async_computation.1 | async-start | bytes 524288 | tf_op jit(solution)/shard_map/while/body/eval_jaxpr/psum | solution.py:151
  124.8 4.1 copy-start.8
  124.9 4.1 copy-start.10
  236.1 1.9 copy-start.7
  259.6 5.4 %copy-start.1 = (f32[6,256,256]{2,1,0:T(8,128)}, f32[6,256,256]{2,1,0:T(8,128)S(1)}, u32[]{:S(2)}) copy-start(f32[6,256,256]{2,1,0:T(8,128)S(1)} %get-tuple-element.819) | copy-start | bytes 4718596 | tf_op jit(solution)/shard_map/while
  259.6 5.4 %copy-start.3 = (f32[6,256,256]{2,1,0:T(8,128)}, f32[6,256,256]{2,1,0:T(8,128)S(1)}, u32[]{:S(2)}) copy-start(f32[6,256,256]{2,1,0:T(8,128)S(1)} %get-tuple-element.818) | copy-start | bytes 4718596 | tf_op jit(solution)/shard_map/while
  259.6 59.6 %all-reduce.5.cloned.1.call-start = ((), (), s32[]{:S(2)}) async-start(), calls=%async_computation.1 | async-start | bytes 524288 | tf_op jit(solution)/shard_map/while/body/eval_jaxpr/psum | solution.py:151
  264.5 4.1 copy-start.8
  264.6 4.1 copy-start.10
  360.3 108.9 %all-reduce.3.cloned.1.call-start = ((), (), s32[]{:S(2)}) async-start(), calls=%async_computation | async-start | bytes 2097152 | tf_op jit(solution)/shard_map/psum | solution.py:186
  360.3 4.9 %copy-start.14 = (f32[2,2,512,512]{3,2,1,0:T(8,128)S(1)}, f32[2,2,512,512]{3,2,1,0:T(8,128)}, u32[]{:S(2)}) copy-start(f32[2,2,512,512]{3,2,1,0:T(8,128)} %get-tuple-element.494) | copy-start | bytes 12582916
  361.8 25.2 %collective-permute-start.9 = (f32[2,2,128,256]{3,2,1,0:T(8,128)S(1)}, f32[2,2,128,256]{3,2,1,0:T(8,128)S(1)}, u32[]{:S(2)}, u32[]{:S(2)}) collective-permute-start(f32[2,2,128,256]{3,2,1,0:T(8,128)S(1)} %get-tuple-element.651), channel_id=1, source_target_pairs={{16,0},{18,2},{20,4},{22,6},{24,8},{26,10},{28,12},{30,14},{32,16}... | collective-permute-start | bytes 1572872 | tf_op jit(solution)/shard_map/ppermute | solution.py:14
  365.3 19.7 %collective-permute-start.8 = (f32[2,2,128,128]{3,2,1,0:T(8,128)S(1)}, f32[2,2,128,128]{3,2,1,0:T(8,128)S(1)}, u32[]{:S(2)}, u32[]{:S(2)}) collective-permute-start(f32[2,2,128,128]{3,2,1,0:T(8,128)S(1)} %get-tuple-element.648), channel_id=1, source_target_pairs={{18,0},{20,2},{22,4},{24,6},{26,8},{28,10},{30,12},{32,14},{34,16}... | collective-permute-start | bytes 786440 | tf_op jit(solution)/shard_map/ppermute | solution.py:14
  366.6 25.3 %collective-permute-start.10 = (f32[2,2,128,128]{3,2,1,0:T(8,128)S(1)}, f32[2,2,128,128]{3,2,1,0:T(8,128)S(1)}, u32[]{:S(2)}, u32[]{:S(2)}) collective-permute-start(f32[2,2,128,128]{3,2,1,0:T(8,128)S(1)} %get-tuple-element.647), channel_id=1, source_target_pairs={{14,0},{16,2},{18,4},{20,6},{22,8},{24,10},{26,12},{28,14},{30,16}... | collective-permute-start | bytes 786440 | tf_op jit(solution)/shard_map/ppermute | solution.py:14
  368.0 30.1 %collective-permute-start.11 = (f32[2,2,256,128]{3,2,1,0:T(8,128)S(1)}, f32[2,2,256,128]{3,2,1,0:T(8,128)S(1)}, u32[]{:S(2)}, u32[]{:S(2)}) collective-permute-start(f32[2,2,256,128]{3,2,1,0:T(8,128)S(1)} %get-tuple-element.653), channel_id=1, source_target_pairs={{2,0},{4,2},{6,4},{8,6},{10,8},{12,10},{14,12},{16,14},{18,16},{20... | collective-permute-start | bytes 1572872 | tf_op jit(solution)/shard_map/ppermute | solution.py:14
  371.4 26.9 %collective-permute-start.12 = (f32[2,2,256,128]{3,2,1,0:T(8,128)S(1)}, f32[2,2,256,128]{3,2,1,0:T(8,128)S(1)}, u32[]{:S(2)}, u32[]{:S(2)}) collective-permute-start(f32[2,2,256,128]{3,2,1,0:T(8,128)S(1)} %get-tuple-element.652), channel_id=1, source_target_pairs={{0,2},{2,4},{4,6},{6,8},{8,10},{10,12},{12,14},{14,16},{16,18},{18... | collective-permute-start | bytes 1572872 | tf_op jit(solution)/shard_map/ppermute | solution.py:14
  385.0 13.4 %collective-permute-start.13 = (f32[2,2,128,128]{3,2,1,0:T(8,128)S(1)}, f32[2,2,128,128]{3,2,1,0:T(8,128)S(1)}, u32[]{:S(2)}, u32[]{:S(2)}) collective-permute-start(f32[2,2,128,128]{3,2,1,0:T(8,128)S(1)} %get-tuple-element.649), channel_id=1, source_target_pairs={{0,14},{2,16},{4,18},{6,20},{8,22},{10,24},{12,26},{14,28},{16,30}... | collective-permute-start | bytes 786440 | tf_op jit(solution)/shard_map/ppermute | solution.py:14
  387.0 16.3 %collective-permute-start.14 = (f32[2,2,128,256]{3,2,1,0:T(8,128)S(1)}, f32[2,2,128,256]{3,2,1,0:T(8,128)S(1)}, u32[]{:S(2)}, u32[]{:S(2)}) collective-permute-start(f32[2,2,128,256]{3,2,1,0:T(8,128)S(1)} %get-tuple-element.650), channel_id=1, source_target_pairs={{0,16},{2,18},{4,20},{6,22},{8,24},{10,26},{12,28},{14,30},{16,32}... | collective-permute-start | bytes 1572872 | tf_op jit(solution)/shard_map/ppermute | solution.py:14
  391.9 12.6 %collective-permute-start.15 = (f32[2,2,128,128]{3,2,1,0:T(8,128)}, f32[2,2,128,128]{3,2,1,0:T(8,128)S(1)}, u32[]{:S(2)}, u32[]{:S(2)}) collective-permute-start(f32[2,2,128,128]{3,2,1,0:T(8,128)} %get-tuple-element.646), channel_id=1, source_target_pairs={{0,18},{2,20},{4,22},{6,24},{8,26},{10,28},{12,30},{14,32},{16,34}... | collective-permute-start | bytes 786440 | tf_op jit(solution)/shard_map/ppermute | solution.py:14
  (20 other events, 25.9 us)
Sparse Core Ops, SparseCore 0:
  143.8 75.7 all-reduce.4
  283.5 35.6 all-reduce.4
Sparse Core Ops, SparseCore 1:
  405.6 63.5 all-reduce.2
where the time goes:
time: 484 us; the launch traced here: 479 us
  waiting for transfers between devices  226 us (47%)
  matrix products  71.2 us (15%)
  starting transfers between devices  58.5 us (12%)
  local copies, waits for them, and re-layouts  50.2 us (10%)
  other arithmetic  29.9 us (6%)
  loops' own time  27.1 us (6%)
  between operations  16.2 us (3%)
    psum x2, waiting for transfers between devices, visit_slot(): intensity = lax.psum(partial_sum, 'mode')  110 us
    dot_general x64, matrix products, single_product(): jnp.einsum(einsum_form, first_op, second_op, preferred_element_type=jnp.f...  71.2 us
    psum x1, waiting for transfers between devices, body(): object_grad = lax.psum(own_grad, 'mode')  63.6 us
    ppermute x16, starting transfers between devices, from_behind(): lax.ppermute(value, axis, [(source, source + steps) for source in range(f...  58.5 us
    ppermute x16, waiting for transfers between devices, from_behind(): lax.ppermute(value, axis, [(source, source + steps) for source in range(f...  52.2 us
    another operation x1, loops' own time, body(): grad_canvas, probe_sum = lax.fori_loop(0, upper, visit_slot, start_state)  27.1 us
    dynamic_update_slice x2, local copies, waits for them, and re-layouts, visit_slot(): lax.dynamic_update_slice(grad_canvas, previous + patch_grad, corner)  23.9 us
  transfers between devices with their start and end apart: 19, of which 8 were waited for; matrix products, arithmetic and copies ran while one was open for 4% of the time, Pallas kernels for 0%

commit v1 on v0

v1 whole, which is shorter than its diff:
```python
import math

import jax
import jax.numpy as jnp
import ml_dtypes
import numpy as np
from jax import lax
from jax.experimental import pallas as pl
from jax.experimental.pallas import tpu as pltpu
from jax.sharding import PartitionSpec as P

GY = 8
F32 = jnp.float32
BF16 = jnp.bfloat16
VMEM_LIMIT = 40 * 1024 * 1024


def dft_pair(extent):
    counter = np.arange(extent)
    angle = -2.0 * math.pi / extent * (counter[:, None] * counter[None, :] % extent)
    scale = 1.0 / math.sqrt(extent)
    return (
        (np.cos(angle) * scale).astype(ml_dtypes.bfloat16),
        (np.sin(angle) * scale).astype(ml_dtypes.bfloat16),
    )


def left_form(re, im, xp):
    return xp.concatenate(
        [xp.concatenate([re, -im], axis=1), xp.concatenate([im, re], axis=1)], axis=0
    )


def right_form(re, im, xp):
    return xp.concatenate(
        [xp.concatenate([re, im], axis=1), xp.concatenate([-im, re], axis=1)], axis=0
    )


def sandwich(left, stacked, right):
    n = stacked.shape[1]
    half = jnp.dot(left, stacked, preferred_element_type=F32)
    beside = jnp.concatenate([half[:n].astype(BF16), half[n:].astype(BF16)], axis=1)
    both = jnp.dot(beside, right, preferred_element_type=F32)
    return both[:, :n], both[:, n:]


def stack_rounded(re, im):
    return jnp.concatenate([re.astype(BF16), im.astype(BF16)], axis=0)


def extract_kernel(off_ref, own, up, down, left, right, corner_l, corner_r, out, canvas):
    n = own.shape[-1]
    h = n // 2
    canvas[:, :, h : h + n, h : h + n] = own[...]
    canvas[:, :, 0:h, h : h + n] = up[...]
    canvas[:, :, h + n :, h : h + n] = down[...]
    canvas[:, :, h : h + n, 0:h] = left[...]
    canvas[:, :, h : h + n, h + n :] = right[...]
    canvas[:, :, 0:h, 0:h] = corner_l[0]
    canvas[:, :, h + n :, 0:h] = corner_l[1]
    canvas[:, :, 0:h, h + n :] = corner_r[0]
    canvas[:, :, h + n :, h + n :] = corner_r[1]
    for slot in range(out.shape[0]):
        row = off_ref[slot, 0] + h
        col = off_ref[slot, 1] + h
        top = pl.multiple_of((row >> 3) * 8, 8)
        block = pl.multiple_of((col >> 7) * 128, 128)
        row_rest, col_rest = row & 7, col & 127
        row_shift = jnp.where(row_rest == 0, 0, n + 8 - row_rest)
        col_shift = jnp.where(col_rest == 0, 0, n + h - col_rest)
        for part in range(2):
            for layer in range(2):
                window = canvas[part, layer, pl.ds(top, n + 8), pl.ds(block, n + h)]
                window = pltpu.roll(window, col_shift, 1)[:, :n]
                out[slot, part, layer] = pltpu.roll(window, row_shift, 0)[:n]


def forward_kernel(probe, patch, prop_l, prop_r, dft_l, dft_r, wave, far, inten):
    first = pl.program_id(0) == 0
    p_re, p_im = probe[0, 0], probe[1, 0]
    o_re, o_im = patch[0, 0, 0], patch[0, 1, 0]
    e = stack_rounded(p_re * o_re - p_im * o_im, p_re * o_im + p_im * o_re)
    w_re, w_im = sandwich(prop_l[...], e, prop_r[...])
    wave[0, 0] = w_re
    wave[0, 1] = w_im
    o_re, o_im = patch[0, 0, 1], patch[0, 1, 1]
    e = stack_rounded(w_re * o_re - w_im * o_im, w_re * o_im + w_im * o_re)
    f_re, f_im = sandwich(dft_l[...], e, dft_r[...])
    far[0, 0] = f_re
    far[0, 1] = f_im
    part = f_re * f_re + f_im * f_im

    @pl.when(first)
    def _():
        inten[...] = part

    @pl.when(jnp.logical_not(first))
    def _():
        inten[...] += part


def back_last_kernel(
    slot, counts, mine, other, measured, far, wave, patch, cdft_l, cdft_r, grad, bar, resid
):
    first = pl.program_id(0) == 0

    @pl.when(first)
    def _():
        live = jnp.where(slot < counts[0], 2.0, 0.0).astype(F32)
        resid[...] = (mine[...] + other[...] - measured[0]) * live

    r = resid[...]
    c = stack_rounded(r * far[0, 0], r * far[0, 1])
    b_re, b_im = sandwich(cdft_l[...], c, cdft_r[...])
    w_re, w_im = wave[0, 0], wave[0, 1]
    g_re = w_re * b_re + w_im * b_im
    g_im = w_re * b_im - w_im * b_re

    @pl.when(first)
    def _():
        grad[0] = g_re
        grad[1] = g_im

    @pl.when(jnp.logical_not(first))
    def _():
        grad[0] += g_re
        grad[1] += g_im

    o_re, o_im = patch[0, 0, 1], patch[0, 1, 1]
    bar[0] = stack_rounded(o_re * b_re + o_im * b_im, o_re * b_im - o_im * b_re)


def back_first_kernel(bar0, bar1, probe, patches, prop_l, prop_r, grad, probe_grad):
    first = pl.program_id(0) == 0
    p_re, p_im = probe[0, 0], probe[1, 0]
    sum_re = sum_im = None
    for slot, bar in enumerate((bar0, bar1)):
        b_re, b_im = sandwich(prop_l[...], bar[0], prop_r[...])
        g_re = p_re * b_re + p_im * b_im
        g_im = p_re * b_im - p_im * b_re

        @pl.when(first)
        def _():
            grad[slot, 0] = g_re
            grad[slot, 1] = g_im

        @pl.when(jnp.logical_not(first))
        def _():
            grad[slot, 0] += g_re
            grad[slot, 1] += g_im

        o_re, o_im = patches[slot, 0, 0], patches[slot, 1, 0]
        q_re = o_re * b_re + o_im * b_im
        q_im = o_re * b_im - o_im * b_re
        sum_re = q_re if sum_re is None else sum_re + q_re
        sum_im = q_im if sum_im is None else sum_im + q_im
    probe_grad[0, 0, 0] = sum_re
    probe_grad[0, 1, 0] = sum_im


def place_kernel(off_ref, grad0, grad1, out_l, out_c, out_r, canvas):
    n = grad0.shape[-1]
    h = n // 2
    canvas[...] = jnp.zeros_like(canvas)
    for slot, grad in enumerate((grad0, grad1)):
        row = off_ref[slot, 0] + h
        col = off_ref[slot, 1] + h
        top = pl.multiple_of((row >> 3) * 8, 8)
        block = pl.multiple_of((col >> 7) * 128, 128)
        for part in range(2):
            tall = jnp.concatenate([grad[part], jnp.zeros((8, n), F32)], axis=0)
            tall = pltpu.roll(tall, row & 7, 0)
            wide = jnp.concatenate([tall, jnp.zeros((n + 8, h), F32)], axis=1)
            wide = pltpu.roll(wide, col & 127, 1)
            canvas[part, pl.ds(top, n + 8), pl.ds(block, n + h)] += wide
    out_l[...] = canvas[:, :, 0:h]
    out_c[...] = canvas[:, :, h : h + n]
    out_r[...] = canvas[:, :, h + n :]


def rows_by(value, step):
    count = lax.axis_size("tile")
    pairs = [(i, i + GY * step) for i in range(count) if 0 <= i + GY * step < count]
    return lax.ppermute(value, "tile", pairs)


def cols_by(value, step):
    count = lax.axis_size("tile")
    pairs = [(i, i + step) for i in range(count) if 0 <= i % GY + step < GY]
    return lax.ppermute(value, "tile", pairs)


def swap_mode(value):
    return lax.ppermute(value, "mode", [(0, 1), (1, 0)])


def params(grid):
    return pltpu.CompilerParams(
        dimension_semantics=("arbitrary",) * grid, vmem_limit_bytes=VMEM_LIMIT
    )


def whole(shape):
    return pl.BlockSpec(shape, lambda m: (0,) * len(shape))


SMEM = pl.BlockSpec(memory_space=pltpu.SMEM)


def body(object_tiles, probe_modes, propagator, offsets, counts, measured):
    n = probe_modes.shape[-1]
    h = n // 2
    modes = probe_modes.shape[1]
    slots = measured.shape[1]
    own = object_tiles[0]
    off = offsets[0]

    down_strip = rows_by(own[:, :, :h, :], -1)
    up_strip = rows_by(own[:, :, h:, :], 1)
    left_strip = cols_by(own[:, :, :, h:], 1)
    right_strip = cols_by(own[:, :, :, :h], -1)
    corner_l = cols_by(jnp.stack([up_strip[..., h:], down_strip[..., h:]]), 1)
    corner_r = cols_by(jnp.stack([up_strip[..., :h], down_strip[..., :h]]), -1)

    k_re, k_im = propagator[0], propagator[1]
    prop_l = left_form(k_re, k_im, jnp)
    prop_r = right_form(k_re.T, k_im.T, jnp)
    back_prop_l = left_form(k_re.T, -k_im.T, jnp)
    back_prop_r = right_form(k_re, -k_im, jnp)
    f_re, f_im = dft_pair(n)
    dft_l = jnp.asarray(left_form(f_re, f_im, np))
    dft_r = jnp.asarray(right_form(f_re, f_im, np))
    cdft_l = jnp.asarray(left_form(f_re, -f_im, np))
    cdft_r = jnp.asarray(right_form(f_re, -f_im, np))

    vmem = pl.BlockSpec(memory_space=pltpu.VMEM)
    patches = pl.pallas_call(
        extract_kernel,
        out_shape=jax.ShapeDtypeStruct((slots, 2, 2, n, n), F32),
        in_specs=[SMEM] + [vmem] * 7,
        out_specs=vmem,
        scratch_shapes=[pltpu.VMEM((2, 2, 2 * n, 2 * n), F32)],
        compiler_params=pltpu.CompilerParams(vmem_limit_bytes=VMEM_LIMIT),
        name="extract",
    )(off, own, up_strip, down_strip, left_strip, right_strip, corner_l, corner_r)

    mat = whole((2 * n, 2 * n))
    probe_spec = pl.BlockSpec((2, 1, n, n), lambda m: (0, m, 0, 0))
    field_spec = pl.BlockSpec((1, 2, n, n), lambda m: (m, 0, 0, 0))
    field_shape = jax.ShapeDtypeStruct((modes, 2, n, n), F32)
    plane = jax.ShapeDtypeStruct((n, n), F32)

    def patch_spec(slot):
        return pl.BlockSpec((1, 2, 2, n, n), lambda m: (slot, 0, 0, 0, 0))

    waves, fars, intens = [], [], []
    for slot in range(slots):
        wave, far, inten = pl.pallas_call(
            forward_kernel,
            grid=(modes,),
            out_shape=(field_shape, field_shape, plane),
            in_specs=[probe_spec, patch_spec(slot), mat, mat, mat, mat],
            out_specs=(field_spec, field_spec, whole((n, n))),
            compiler_params=params(1),
            name=f"forward_{slot}",
        )(probe_modes, patches, prop_l, prop_r, dft_l, dft_r)
        waves.append(wave)
        fars.append(far)
        intens.append(inten)
    others = [swap_mode(inten) for inten in intens]

    bar_spec = pl.BlockSpec((1, 2 * n, n), lambda m: (m, 0, 0))
    grads_last, bars = [], []
    for slot in range(slots):
        grad, bar = pl.pallas_call(
            lambda *refs, slot=slot: back_last_kernel(slot, *refs),
            grid=(modes,),
            out_shape=(
                jax.ShapeDtypeStruct((2, n, n), F32),
                jax.ShapeDtypeStruct((modes, 2 * n, n), BF16),
            ),
            in_specs=[
                SMEM,
                whole((n, n)),
                whole((n, n)),
                pl.BlockSpec((1, n, n), lambda m, slot=slot: (slot, 0, 0)),
                field_spec,
                field_spec,
                patch_spec(slot),
                mat,
                mat,
            ],
            out_specs=(whole((2, n, n)), bar_spec),
            scratch_shapes=[pltpu.VMEM((n, n), F32)],
            compiler_params=params(1),
            name=f"back_last_{slot}",
        )(counts, intens[slot], others[slot], measured[0], fars[slot], waves[slot], patches,
          cdft_l, cdft_r)
        grads_last.append(grad)
        bars.append(bar)

    def place(grad0, grad1, name):
        return pl.pallas_call(
            place_kernel,
            out_shape=(
                jax.ShapeDtypeStruct((2, 2 * n, h), F32),
                jax.ShapeDtypeStruct((2, 2 * n, n), F32),
                jax.ShapeDtypeStruct((2, 2 * n, h), F32),
            ),
            in_specs=[SMEM, vmem, vmem],
            out_specs=(vmem, vmem, vmem),
            scratch_shapes=[pltpu.VMEM((2, 2 * n, 2 * n), F32)],
            compiler_params=pltpu.CompilerParams(vmem_limit_bytes=VMEM_LIMIT),
            name=name,
        )(off, grad0, grad1)

    def collect(grad0, grad1, name):
        out_l, out_c, out_r = place(grad0, grad1, name)
        from_left = cols_by(out_r, 1)
        from_right = cols_by(out_l, -1)
        tall = out_c + jnp.concatenate([from_left, from_right], axis=2)
        from_up = rows_by(tall[:, n + h :, :], 1)
        from_down = rows_by(tall[:, :h, :], -1)
        mine = tall[:, h : h + n, :] + jnp.concatenate([from_up, from_down], axis=1)
        return mine + swap_mode(mine)

    last = collect(grads_last[0], grads_last[1], "place_last")

    grads_first, probe_grad = pl.pallas_call(
        back_first_kernel,
        grid=(modes,),
        out_shape=(
            jax.ShapeDtypeStruct((slots, 2, n, n), F32),
            jax.ShapeDtypeStruct((1, 2, modes, n, n), F32),
        ),
        in_specs=[bar_spec, bar_spec, probe_spec, whole((slots, 2, 2, n, n)), mat, mat],
        out_specs=(
            whole((slots, 2, n, n)),
            pl.BlockSpec((1, 2, 1, n, n), lambda m: (0, 0, m, 0, 0)),
        ),
        compiler_params=params(1),
        name="back_first",
    )(bars[0], bars[1], probe_modes, patches, back_prop_l, back_prop_r)
    first = collect(grads_first[0], grads_first[1], "place_first")
    object_grad = jnp.stack([first, last], axis=1)
    return (object_grad.reshape(object_tiles.shape), probe_grad)


def solution(mesh):
    placed = (
        P("tile", None, None, None, None),
        P(None, "mode", None, None),
        P(),
        P("tile", None, None),
        P("tile"),
        P("tile", None, None, None),
    )
    return jax.shard_map(
        body,
        mesh=mesh,
        in_specs=placed,
        out_specs=(P("tile", None, None, None, None), P("tile", None, "mode", None, None)),
        check_vma=False,
    )
```

time: 484 us -> 162 us (0.33)
  waiting for transfers between devices: 226 us -> 38.3 us
  matrix products: 71.2 us -> 0 us
  Pallas kernels: 0 us -> 44.5 us
  local copies, waits for them, and re-layouts: 50.2 us -> 21 us
  loops' own time: 27.1 us -> 0 us
  other arithmetic: 29.9 us -> 4.14 us
  between operations: 16.2 us -> 1.74 us
  starting transfers between devices: 58.5 us -> 49.5 us
    psum x3 -> x0, waiting for transfers between devices: 174 us -> none  [the longest x2 110 us: visit_slot(): intensity = lax.psum(partial_sum, 'mode')]
    dot_general x64 -> x0, matrix products: 71.2 us -> none  [single_product(): jnp.einsum(einsum_form, first_op, second_op, preferred_element_type=jnp.f...]
    pallas_call x0 -> x8, Pallas kernels: none -> 44.5 us  [the longest x2 17 us: body(): pl.pallas_call(forward_kernel, grid=(modes,), out_shape=(field_shape, fie...]
    another operation x1 -> x0, loops' own time: 27.1 us -> none  [body(): grad_canvas, probe_sum = lax.fori_loop(0, upper, visit_slot, start_state)]
    dynamic_update_slice x2 -> x0, local copies, waits for them, and re-layouts: 23.9 us -> none  [visit_slot(): lax.dynamic_update_slice(grad_canvas, previous + patch_grad, corner)]
    add x4, other arithmetic: 14.5 us -> 0.34 us  [the longest x2 0.21 us: collect(): tall = out_c + jnp.concatenate([from_left, from_right], axis=2)]
    ppermute x16 -> x18, waiting for transfers between devices: 52.2 us -> 38.3 us  [the longest x4 25.9 us: swap_mode(): return lax.ppermute(value, 'mode', [(0, 1), (1, 0)])]
    unnamed x12 -> x31, local copies, waits for them, and re-layouts: 3.35 us -> 15.3 us
  transfers between devices with their start and end apart: 19 -> 18, of which waited for: 8 -> 7; matrix products, arithmetic and copies ran while one was open for 4% -> 5% of each run, Pallas kernels for 0% -> 9%
where the time goes in v1:
time: 162 us; the launch traced here: 159 us
  starting transfers between devices  49.5 us (31%)
  Pallas kernels  44.5 us (27%)
  waiting for transfers between devices  38.3 us (24%)
  local copies, waits for them, and re-layouts  21 us (13%)
  other arithmetic  4.14 us (3%)
  between operations  1.74 us (1%)
    ppermute x4, waiting for transfers between devices, swap_mode(): return lax.ppermute(value, 'mode', [(0, 1), (1, 0)])  25.9 us
    ppermute x8, starting transfers between devices, cols_by(): return lax.ppermute(value, 'tile', pairs)  24.2 us
    ppermute x6, starting transfers between devices, rows_by(): return lax.ppermute(value, 'tile', pairs)  17 us
    pallas_call x2, Pallas kernels, body(): pl.pallas_call(forward_kernel, grid=(modes,), out_shape=(field_shape, fie...  17 us
    unnamed x31, local copies, waits for them, and re-layouts  15.3 us
    pallas_call x1, Pallas kernels, body(): pl.pallas_call(back_first_kernel, grid=(modes,), out_shape=(jax.ShapeDtyp...  11.2 us
    pallas_call x2, Pallas kernels, body(): pl.pallas_call(lambda *refs, slot=slot: back_last_kernel(slot, *refs), gr...  10.2 us
    ppermute x8, waiting for transfers between devices, cols_by(): return lax.ppermute(value, 'tile', pairs)  9.07 us
  transfers between devices with their start and end apart: 18, of which 7 were waited for; matrix products, arithmetic and copies ran while one was open for 5% of the time, Pallas kernels for 9%

profile of v1, /device:TPU:1, one launch (start us, length us, event | category | flops | bytes accessed | tf_op | source)
XLA Modules:
  0.0 159.1 jit_solution(11691725933072148771)
XLA Ops:
  3.3 5.0 %collective-permute-start = (f32[2,2,128,256]{3,2,1,0:T(8,128)S(1)}, f32[2,2,128,256]{3,2,1,0:T(8,128)S(1)}, u32[]{:S(2)}, u32[]{:S(2)}) collective-permute-start(f32[2,2,128,256]{3,2,1,0:T(8,128)S(1)} %get-tuple-element.49), channel_id=1, source_target_pairs={{0,16},{2,18},{4,20},{6,22},{8,24},{10,26},{12,28},{14,30},{16,32}... | collective-permute-start | bytes 1572872 | tf_op jit(solution)/shard_map/ppermute | solution.py:185
  8.3 2.2 %fusion.4 = (f32[2,2,256,128]{3,2,1,0:T(8,128)}, f32[2,2,256,128]{3,2,1,0:T(8,128)}) fusion(f32[2,2,256,256]{3,2,1,0:T(8,128)} %bitcast.36), kind=kLoop, calls=%fused_computation.25 | loop fusion | bytes 2097152 | tf_op jit(solution)/shard_map/slice | solution.py:222
  10.5 4.7 %collective-permute-start.3 = (f32[2,2,256,128]{3,2,1,0:T(8,128)}, f32[2,2,256,128]{3,2,1,0:T(8,128)S(1)}, u32[]{:S(2)}, u32[]{:S(2)}) collective-permute-start(f32[2,2,256,128]{3,2,1,0:T(8,128)} %get-tuple-element.46), channel_id=1, source_target_pairs={{2,0},{4,2},{6,4},{8,6},{10,8},{12,10},{14,12},{18,16},{20,18},{22... | collective-permute-start | bytes 1572872 | tf_op jit(solution)/shard_map/ppermute | solution.py:191
  15.2 1.9 %collective-permute-start.2 = (f32[2,2,256,128]{3,2,1,0:T(8,128)}, f32[2,2,256,128]{3,2,1,0:T(8,128)}, u32[]{:S(2)}, u32[]{:S(2)}) collective-permute-start(f32[2,2,256,128]{3,2,1,0:T(8,128)} %get-tuple-element.47), channel_id=1, source_target_pairs={{0,2},{2,4},{4,6},{6,8},{8,10},{10,12},{12,14},{16,18},{18,20},{20... | collective-permute-start | bytes 1572872 | tf_op jit(solution)/shard_map/ppermute | solution.py:191
  18.8 5.5 %collective-permute-start.4 = (f32[2,2,2,128,128]{4,3,2,1,0:T(8,128)}, f32[2,2,2,128,128]{4,3,2,1,0:T(8,128)}, u32[]{:S(2)}, u32[]{:S(2)}) collective-permute-start(f32[2,2,2,128,128]{4,3,2,1,0:T(8,128)} %pad_maximum_fusion), channel_id=1, source_target_pairs={{0,2},{2,4},{4,6},{6,8},{8,10},{10,12},{12,14},{16,18},{18,20},{20... | collective-permute-start | bytes 1572872 | tf_op jit(solution)/shard_map/ppermute | solution.py:191
  25.1 1.9 %collective-permute-start.5 = (f32[2,2,2,128,128]{4,3,2,1,0:T(8,128)}, f32[2,2,2,128,128]{4,3,2,1,0:T(8,128)}, u32[]{:S(2)}, u32[]{:S(2)}) collective-permute-start(f32[2,2,2,128,128]{4,3,2,1,0:T(8,128)} %pad_maximum_fusion.1), channel_id=1, source_target_pairs={{2,0},{4,2},{6,4},{8,6},{10,8},{12,10},{14,12},{18,16},{20,18},{22... | collective-permute-start | bytes 1572872 | tf_op jit(solution)/shard_map/ppermute | solution.py:191
  30.7 5.2 %collective-permute-done.5.corner_r = f32[2,2,2,128,128]{4,3,2,1,0:T(8,128)} collective-permute-done((f32[2,2,2,128,128]{4,3,2,1,0:T(8,128)}, f32[2,2,2,128,128]{4,3,2,1,0:T(8,128)}, u32[]{:S(2)}, u32[]{:S(2)}) %collective-permute-start.5) | collective-permute-done | bytes 524320 | tf_op jit(solution)/shard_map/ppermute | solution.py:191
  36.0 3.2 %extract.1.patch.refs_6_.patches = f32[2,2,2,256,256]{4,3,2,1,0:T(8,128)S(1)} custom-call(s32[2,2]{1,0:T(2,128)S(1)} %bitcast.40, f32[2,2,256,256]{3,2,1,0:T(8,128)S(1)} %bitcast.37, f32[2,2,128,256]{3,2,1,0:T(8,128)S(1)} %collective-permute-done.up, f32[2,2,128,256]{3,2,1,0:T(8,128)S(1)} %collective-permute-done.1.down, ...), custom_call_target="tpu_custom_call" | custom-call | tf_op jit(solution)/shard_map/extract/pallas_call | solution.py:238
  39.2 8.5 %forward_1.1 = (f32[6,2,256,256]{3,2,1,0:T(8,128)S(1)}, f32[6,2,256,256]{3,2,1,0:T(8,128)S(1)}, f32[256,256]{1,0:T(8,128)S(1)}) custom-call(f32[2,6,256,256]{3,2,1,0:T(8,128)S(1)} %copy-done, f32[2,2,2,256,256]{4,3,2,1,0:T(8,128)S(1)} %extract.1.patch.refs_6_.patches, bf16[512,512]{1,0:T(8,128)(2,1)S(1)} %maximum_maximum_fusion.prop_l.prop_r, ...), custom_call_target="tpu_custom_call" | custom-call | tf_op jit(solution)/shard_map/forward_1/pallas_call | solution.py:259
  47.7 1.7 %copy-done.8 = f32[6,2,256,256]{3,2,1,0:T(8,128)} copy-done((f32[6,2,256,256]{3,2,1,0:T(8,128)}, f32[6,2,256,256]{3,2,1,0:T(8,128)S(1)}, u32[]{:S(2)}) %copy-start.8) | copy-done | bytes 3145752
  49.4 1.7 %copy-done.10 = f32[6,2,256,256]{3,2,1,0:T(8,128)} copy-done((f32[6,2,256,256]{3,2,1,0:T(8,128)}, f32[6,2,256,256]{3,2,1,0:T(8,128)S(1)}, u32[]{:S(2)}) %copy-start.10) | copy-done | bytes 3145752
  51.1 2.9 %collective-permute-start.7 = (f32[256,256]{1,0:T(8,128)S(1)}, f32[256,256]{1,0:T(8,128)S(1)}, u32[]{:S(2)}, u32[]{:S(2)}) collective-permute-start(f32[256,256]{1,0:T(8,128)S(1)} %get-tuple-element.24.refs_1_), channel_id=1, source_target_pairs={{0,1},{1,0},{2,3},{3,2},{4,5},{5,4},{6,7},{7,6},{8,9},{9,8},{10,11... | collective-permute-start | bytes 786440 | tf_op jit(solution)/shard_map/ppermute | solution.py:195
  54.0 8.5 %forward_0.1 = (f32[6,2,256,256]{3,2,1,0:T(8,128)S(1)}, f32[6,2,256,256]{3,2,1,0:T(8,128)S(1)}, f32[256,256]{1,0:T(8,128)S(1)}) custom-call(f32[2,6,256,256]{3,2,1,0:T(8,128)S(1)} %copy-done, f32[2,2,2,256,256]{4,3,2,1,0:T(8,128)S(1)} %extract.1.patch.refs_6_.patches, bf16[512,512]{1,0:T(8,128)(2,1)S(1)} %maximum_maximum_fusion.prop_l.prop_r, ...), custom_call_target="tpu_custom_call" | custom-call | tf_op jit(solution)/shard_map/forward_0/pallas_call | solution.py:259
  66.5 1.9 %copy-done.9 = f32[6,2,256,256]{3,2,1,0:T(8,128)S(1)} copy-done((f32[6,2,256,256]{3,2,1,0:T(8,128)S(1)}, f32[6,2,256,256]{3,2,1,0:T(8,128)}, u32[]{:S(2)}) %copy-start.9) | copy-done | bytes 3145752
  68.4 1.9 %copy-done.11 = f32[6,2,256,256]{3,2,1,0:T(8,128)S(1)} copy-done((f32[6,2,256,256]{3,2,1,0:T(8,128)S(1)}, f32[6,2,256,256]{3,2,1,0:T(8,128)}, u32[]{:S(2)}) %copy-start.11) | copy-done | bytes 3145752
  70.3 5.1 %back_last_1.1 = (f32[2,256,256]{2,1,0:T(8,128)S(1)}, bf16[6,512,256]{2,1,0:T(8,128)(2,1)S(1)}) custom-call(s32[1]{0:T(128)S(6)} %copy.16.refs_0_, f32[256,256]{1,0:T(8,128)S(1)} %get-tuple-element.24.refs_1_, f32[256,256]{1,0:T(8,128)S(1)} %collective-permute-done.7.refs_2_, f32[2,256,256]{2,1,0:T(8,128)S(1)} %bitcast.38, ...), custom_call_target="tpu_custom_call" | custom-call | tf_op jit(solution)/shard_map/back_last_1/pallas_call | solution.py:276
  75.4 1.9 %copy-done.5 = f32[6,2,256,256]{3,2,1,0:T(8,128)S(1)} copy-done((f32[6,2,256,256]{3,2,1,0:T(8,128)S(1)}, f32[6,2,256,256]{3,2,1,0:T(8,128)}, u32[]{:S(2)}) %copy-start.5) | copy-done | bytes 3145752
  77.3 1.9 %copy-done.7 = f32[6,2,256,256]{3,2,1,0:T(8,128)S(1)} copy-done((f32[6,2,256,256]{3,2,1,0:T(8,128)S(1)}, f32[6,2,256,256]{3,2,1,0:T(8,128)}, u32[]{:S(2)}) %copy-start.7) | copy-done | bytes 3145752
  79.1 5.1 %back_last_0.1 = (f32[2,256,256]{2,1,0:T(8,128)S(1)}, bf16[6,512,256]{2,1,0:T(8,128)(2,1)S(1)}) custom-call(s32[1]{0:T(128)S(6)} %copy.16.refs_0_, f32[256,256]{1,0:T(8,128)S(1)} %get-tuple-element.20.refs_1_, f32[256,256]{1,0:T(8,128)S(1)} %collective-permute-done.6.refs_2_, f32[2,256,256]{2,1,0:T(8,128)S(1)} %bitcast.39, f32[6,2,256,256]{3,2,1,0:T(8,128)S(1)} %copy-done.7, ...), custom_call_target="tpu_custom_call" | custom-call | tf_op jit(solution)/shard_map/back_last_0/pallas_call | solution.py:276
  84.2 11.2 %back_first.1 = (f32[2,2,256,256]{3,2,1,0:T(8,128)S(1)}, f32[1,2,6,256,256]{4,3,2,1,0:T(8,128)}) custom-call(bf16[6,512,256]{2,1,0:T(8,128)(2,1)S(1)} %get-tuple-element.23.bar0, bf16[6,512,256]{2,1,0:T(8,128)(2,1)S(1)} %get-tuple-element.27.bar1, f32[2,6,256,256]{3,2,1,0:T(8,128)S(1)} %copy-done, f32[2,2,2,256,256]{4,3,2,1,0:T(8,128)S(1)} %extract.1.patch.refs_6_.patches, ...), custom_call_target="tpu_custom_call" | custom-call | tf_op jit(solution)/shard_map/back_first/pallas_call | solution.py:330
  97.0 2.7 %collective-permute-start.8 = (f32[2,512,128]{2,1,0:T(8,128)S(1)}, f32[2,512,128]{2,1,0:T(8,128)S(1)}, u32[]{:S(2)}, u32[]{:S(2)}) collective-permute-start(f32[2,512,128]{2,1,0:T(8,128)S(1)} %get-tuple-element.30), channel_id=1, source_target_pairs={{0,2},{2,4},{4,6},{6,8},{8,10},{10,12},{12,14},{16,18},{18,20},{20... | collective-permute-start | bytes 1572872 | tf_op jit(solution)/shard_map/ppermute | solution.py:191
  99.7 1.9 %collective-permute-start.9 = (f32[2,512,128]{2,1,0:T(8,128)S(1)}, f32[2,512,128]{2,1,0:T(8,128)S(1)}, u32[]{:S(2)}, u32[]{:S(2)}) collective-permute-start(f32[2,512,128]{2,1,0:T(8,128)S(1)} %get-tuple-element.31), channel_id=1, source_target_pairs={{2,0},{4,2},{6,4},{8,6},{10,8},{12,10},{14,12},{18,16},{20,18},{22... | collective-permute-start | bytes 1572872 | tf_op jit(solution)/shard_map/ppermute | solution.py:191
  103.1 3.7 %collective-permute-start.13 = (f32[2,512,128]{2,1,0:T(8,128)S(1)}, f32[2,512,128]{2,1,0:T(8,128)S(1)}, u32[]{:S(2)}, u32[]{:S(2)}) collective-permute-start(f32[2,512,128]{2,1,0:T(8,128)S(1)} %get-tuple-element.35), channel_id=1, source_target_pairs={{0,2},{2,4},{4,6},{6,8},{8,10},{10,12},{12,14},{16,18},{18,20},{20... | collective-permute-start | bytes 1572872 | tf_op jit(solution)/shard_map/ppermute | solution.py:191
  106.8 1.9 %collective-permute-start.14 = (f32[2,512,128]{2,1,0:T(8,128)S(1)}, f32[2,512,128]{2,1,0:T(8,128)S(1)}, u32[]{:S(2)}, u32[]{:S(2)}) collective-permute-start(f32[2,512,128]{2,1,0:T(8,128)S(1)} %get-tuple-element.36), channel_id=1, source_target_pairs={{2,0},{4,2},{6,4},{8,6},{10,8},{12,10},{14,12},{18,16},{20,18},{22... | collective-permute-start | bytes 1572872 | tf_op jit(solution)/shard_map/ppermute | solution.py:191
  110.3 4.0 %collective-permute-start.10 = (f32[2,128,256]{2,1,0:T(8,128)S(1)}, f32[2,128,256]{2,1,0:T(8,128)S(1)}, u32[]{:S(2)}, u32[]{:S(2)}) collective-permute-start(f32[2,128,256]{2,1,0:T(8,128)S(1)} %get-tuple-element.40), channel_id=1, source_target_pairs={{0,16},{2,18},{4,20},{6,22},{8,24},{10,26},{12,28},{14,30},{16,32}... | collective-permute-start | bytes 786440 | tf_op jit(solution)/shard_map/ppermute | solution.py:185
  115.7 1.9 %collective-permute-done.14 = f32[2,512,128]{2,1,0:T(8,128)S(1)} collective-permute-done((f32[2,512,128]{2,1,0:T(8,128)S(1)}, f32[2,512,128]{2,1,0:T(8,128)S(1)}, u32[]{:S(2)}, u32[]{:S(2)}) %collective-permute-start.14) | collective-permute-done | bytes 524320 | tf_op jit(solution)/shard_map/ppermute | solution.py:191
  117.7 4.0 %collective-permute-start.15 = (f32[2,128,256]{2,1,0:T(8,128)S(1)}, f32[2,128,256]{2,1,0:T(8,128)S(1)}, u32[]{:S(2)}, u32[]{:S(2)}) collective-permute-start(f32[2,128,256]{2,1,0:T(8,128)S(1)} %get-tuple-element.44), channel_id=1, source_target_pairs={{0,16},{2,18},{4,20},{6,22},{8,24},{10,26},{12,28},{14,30},{16,32}... | collective-permute-start | bytes 786440 | tf_op jit(solution)/shard_map/ppermute | solution.py:185
  123.2 2.7 %collective-permute-start.12 = (f32[2,256,256]{2,1,0:T(8,128)S(1)}, f32[2,256,256]{2,1,0:T(8,128)S(1)}, u32[]{:S(2)}, u32[]{:S(2)}) collective-permute-start(f32[2,256,256]{2,1,0:T(8,128)S(1)} %slice_add_fusion.1), channel_id=1, source_target_pairs={{0,1},{1,0},{2,3},{3,2},{4,5},{5,4},{6,7},{7,6},{8,9},{9,8},{10,11... | collective-permute-start | bytes 1572872 | tf_op jit(solution)/shard_map/ppermute | solution.py:195
  125.9 3.3 %collective-permute-done.16 = f32[2,128,256]{2,1,0:T(8,128)S(1)} collective-permute-done((f32[2,128,256]{2,1,0:T(8,128)S(1)}, f32[2,128,256]{2,1,0:T(8,128)S(1)}, u32[]{:S(2)}, u32[]{:S(2)}) %collective-permute-start.16) | collective-permute-done | bytes 262176 | tf_op jit(solution)/shard_map/ppermute | solution.py:185
  129.3 2.7 %collective-permute-start.17 = (f32[2,256,256]{2,1,0:T(8,128)S(1)}, f32[2,256,256]{2,1,0:T(8,128)S(1)}, u32[]{:S(2)}, u32[]{:S(2)}) collective-permute-start(f32[2,256,256]{2,1,0:T(8,128)S(1)} %slice_add_fusion), channel_id=1, source_target_pairs={{0,1},{1,0},{2,3},{3,2},{4,5},{5,4},{6,7},{7,6},{8,9},{9,8},{10,11... | collective-permute-start | bytes 1572872 | tf_op jit(solution)/shard_map/ppermute | solution.py:195
  132.0 15.6 %collective-permute-done.12 = f32[2,256,256]{2,1,0:T(8,128)S(1)} collective-permute-done((f32[2,256,256]{2,1,0:T(8,128)S(1)}, f32[2,256,256]{2,1,0:T(8,128)S(1)}, u32[]{:S(2)}, u32[]{:S(2)}) %collective-permute-start.12) | collective-permute-done | bytes 524320 | tf_op jit(solution)/shard_map/ppermute | solution.py:195
  147.6 10.3 %collective-permute-done.17 = f32[2,256,256]{2,1,0:T(8,128)S(1)} collective-permute-done((f32[2,256,256]{2,1,0:T(8,128)S(1)}, f32[2,256,256]{2,1,0:T(8,128)S(1)}, u32[]{:S(2)}, u32[]{:S(2)}) %collective-permute-start.17) | collective-permute-done | bytes 524320 | tf_op jit(solution)/shard_map/ppermute | solution.py:195
  (65 shorter events, 20.9 us)
Async XLA Ops:
  0.6 16.5 %copy-start.14 = (bf16[2,256,256]{2,1,0:T(8,128)(2,1)S(1)}, bf16[2,256,256]{2,1,0:T(8,128)(2,1)}, u32[]{:S(2)}) copy-start(bf16[2,256,256]{2,1,0:T(8,128)(2,1)} %param.12) | copy-start | bytes 786436
  2.0 15.9 %collective-permute-start.1 = (f32[2,2,128,256]{3,2,1,0:T(8,128)S(1)}, f32[2,2,128,256]{3,2,1,0:T(8,128)S(1)}, u32[]{:S(2)}, u32[]{:S(2)}) collective-permute-start(f32[2,2,128,256]{3,2,1,0:T(8,128)S(1)} %get-tuple-element.48), channel_id=1, source_target_pairs={{16,0},{18,2},{20,4},{22,6},{24,8},{26,10},{28,12},{30,14},{32,16}... | collective-permute-start | bytes 1572872 | tf_op jit(solution)/shard_map/ppermute | solution.py:185
  3.3 14.7 %collective-permute-start = (f32[2,2,128,256]{3,2,1,0:T(8,128)S(1)}, f32[2,2,128,256]{3,2,1,0:T(8,128)S(1)}, u32[]{:S(2)}, u32[]{:S(2)}) collective-permute-start(f32[2,2,128,256]{3,2,1,0:T(8,128)S(1)} %get-tuple-element.49), channel_id=1, source_target_pairs={{0,16},{2,18},{4,20},{6,22},{8,24},{10,26},{12,28},{14,30},{16,32}... | collective-permute-start | bytes 1572872 | tf_op jit(solution)/shard_map/ppermute | solution.py:185
  10.5 19.7 %collective-permute-start.3 = (f32[2,2,256,128]{3,2,1,0:T(8,128)}, f32[2,2,256,128]{3,2,1,0:T(8,128)S(1)}, u32[]{:S(2)}, u32[]{:S(2)}) collective-permute-start(f32[2,2,256,128]{3,2,1,0:T(8,128)} %get-tuple-element.46), channel_id=1, source_target_pairs={{2,0},{4,2},{6,4},{8,6},{10,8},{12,10},{14,12},{18,16},{20,18},{22... | collective-permute-start | bytes 1572872 | tf_op jit(solution)/shard_map/ppermute | solution.py:191
  15.2 15.0 %collective-permute-start.2 = (f32[2,2,256,128]{3,2,1,0:T(8,128)}, f32[2,2,256,128]{3,2,1,0:T(8,128)}, u32[]{:S(2)}, u32[]{:S(2)}) collective-permute-start(f32[2,2,256,128]{3,2,1,0:T(8,128)} %get-tuple-element.47), channel_id=1, source_target_pairs={{0,2},{2,4},{4,6},{6,8},{8,10},{10,12},{12,14},{16,18},{18,20},{20... | collective-permute-start | bytes 1572872 | tf_op jit(solution)/shard_map/ppermute | solution.py:191
  17.9 18.0 %copy-start.1 = (f32[1,2,2,256,256]{4,3,2,1,0:T(8,128)S(1)}, f32[1,2,2,256,256]{4,3,2,1,0:T(8,128)}, u32[]{:S(2)}) copy-start(f32[1,2,2,256,256]{4,3,2,1,0:T(8,128)} %param.10) | copy-start | bytes 3145732
  17.9 18.0 %copy-start.13 = (s32[1,2,2]{2,1,0:T(2,128)S(1)}, s32[1,2,2]{2,1,0:T(2,128)}, u32[]{:S(2)}) copy-start(s32[1,2,2]{2,1,0:T(2,128)} %param.13) | copy-start | bytes 52
  18.8 11.9 %collective-permute-start.4 = (f32[2,2,2,128,128]{4,3,2,1,0:T(8,128)}, f32[2,2,2,128,128]{4,3,2,1,0:T(8,128)}, u32[]{:S(2)}, u32[]{:S(2)}) collective-permute-start(f32[2,2,2,128,128]{4,3,2,1,0:T(8,128)} %pad_maximum_fusion), channel_id=1, source_target_pairs={{0,2},{2,4},{4,6},{6,8},{8,10},{10,12},{12,14},{16,18},{18,20},{20... | collective-permute-start | bytes 1572872 | tf_op jit(solution)/shard_map/ppermute | solution.py:191
  25.1 10.8 %collective-permute-start.5 = (f32[2,2,2,128,128]{4,3,2,1,0:T(8,128)}, f32[2,2,2,128,128]{4,3,2,1,0:T(8,128)}, u32[]{:S(2)}, u32[]{:S(2)}) collective-permute-start(f32[2,2,2,128,128]{4,3,2,1,0:T(8,128)} %pad_maximum_fusion.1), channel_id=1, source_target_pairs={{2,0},{4,2},{6,4},{8,6},{10,8},{12,10},{14,12},{18,16},{20,18},{22... | collective-permute-start | bytes 1572872 | tf_op jit(solution)/shard_map/ppermute | solution.py:191
  35.9 3.2 %copy-start = (f32[2,6,256,256]{3,2,1,0:T(8,128)S(1)}, f32[2,6,256,256]{3,2,1,0:T(8,128)}, u32[]{:S(2)}) copy-start(f32[2,6,256,256]{3,2,1,0:T(8,128)} %probe.5) | copy-start | bytes 9437188
  35.9 3.2 %copy-start.2 = (bf16[512,512]{1,0:T(8,128)(2,1)S(1)}, bf16[512,512]{1,0:T(8,128)(2,1)}, u32[]{:S(2)}) copy-start(bf16[512,512]{1,0:T(8,128)(2,1)} %constant.5.clone.dft_r.refs_7_) | copy-start | bytes 1572868
  35.9 3.2 %copy-start.3 = (bf16[512,512]{1,0:T(8,128)(2,1)S(1)}, bf16[512,512]{1,0:T(8,128)(2,1)}, u32[]{:S(2)}) copy-start(bf16[512,512]{1,0:T(8,128)(2,1)} %constant.4.clone.dft_l.refs_8_) | copy-start | bytes 1572868
  47.7 1.7 %copy-start.8 = (f32[6,2,256,256]{3,2,1,0:T(8,128)}, f32[6,2,256,256]{3,2,1,0:T(8,128)S(1)}, u32[]{:S(2)}) copy-start(f32[6,2,256,256]{3,2,1,0:T(8,128)S(1)} %get-tuple-element.26.refs_5_) | copy-start | bytes 9437188
  49.4 1.7 %copy-start.10 = (f32[6,2,256,256]{3,2,1,0:T(8,128)}, f32[6,2,256,256]{3,2,1,0:T(8,128)S(1)}, u32[]{:S(2)}) copy-start(f32[6,2,256,256]{3,2,1,0:T(8,128)S(1)} %get-tuple-element.25.refs_4_) | copy-start | bytes 9437188
  51.1 15.4 %copy-start.12 = (f32[1,2,256,256]{3,2,1,0:T(8,128)S(1)}, f32[1,2,256,256]{3,2,1,0:T(8,128)}, u32[]{:S(2)}) copy-start(f32[1,2,256,256]{3,2,1,0:T(8,128)} %param.15) | copy-start | bytes 1572868
  51.1 15.4 %collective-permute-start.7 = (f32[256,256]{1,0:T(8,128)S(1)}, f32[256,256]{1,0:T(8,128)S(1)}, u32[]{:S(2)}, u32[]{:S(2)}) collective-permute-start(f32[256,256]{1,0:T(8,128)S(1)} %get-tuple-element.24.refs_1_), channel_id=1, source_target_pairs={{0,1},{1,0},{2,3},{3,2},{4,5},{5,4},{6,7},{7,6},{8,9},{9,8},{10,11... | collective-permute-start | bytes 786440 | tf_op jit(solution)/shard_map/ppermute | solution.py:195
  64.1 1.7 %copy-start.6 = (f32[6,2,256,256]{3,2,1,0:T(8,128)}, f32[6,2,256,256]{3,2,1,0:T(8,128)S(1)}, u32[]{:S(2)}) copy-start(f32[6,2,256,256]{3,2,1,0:T(8,128)S(1)} %get-tuple-element.21.refs_4_) | copy-start | bytes 9437188
  65.8 9.6 %collective-permute-start.6 = (f32[256,256]{1,0:T(8,128)S(1)}, f32[256,256]{1,0:T(8,128)S(1)}, u32[]{:S(2)}, u32[]{:S(2)}) collective-permute-start(f32[256,256]{1,0:T(8,128)S(1)} %get-tuple-element.20.refs_1_), channel_id=1, source_target_pairs={{0,1},{1,0},{2,3},{3,2},{4,5},{5,4},{6,7},{7,6},{8,9},{9,8},{10,11... | collective-permute-start | bytes 786440 | tf_op jit(solution)/shard_map/ppermute | solution.py:195
  66.5 1.9 %copy-start.9 = (f32[6,2,256,256]{3,2,1,0:T(8,128)S(1)}, f32[6,2,256,256]{3,2,1,0:T(8,128)}, u32[]{:S(2)}) copy-start(f32[6,2,256,256]{3,2,1,0:T(8,128)} %copy-done.8) | copy-start | bytes 9437188
  68.4 1.9 %copy-start.11 = (f32[6,2,256,256]{3,2,1,0:T(8,128)S(1)}, f32[6,2,256,256]{3,2,1,0:T(8,128)}, u32[]{:S(2)}) copy-start(f32[6,2,256,256]{3,2,1,0:T(8,128)} %copy-done.10) | copy-start | bytes 9437188
  75.4 1.9 %copy-start.5 = (f32[6,2,256,256]{3,2,1,0:T(8,128)S(1)}, f32[6,2,256,256]{3,2,1,0:T(8,128)}, u32[]{:S(2)}) copy-start(f32[6,2,256,256]{3,2,1,0:T(8,128)} %copy-done.4) | copy-start | bytes 9437188
  77.3 1.9 %copy-start.7 = (f32[6,2,256,256]{3,2,1,0:T(8,128)S(1)}, f32[6,2,256,256]{3,2,1,0:T(8,128)}, u32[]{:S(2)}) copy-start(f32[6,2,256,256]{3,2,1,0:T(8,128)} %copy-done.6) | copy-start | bytes 9437188
  97.0 11.7 %collective-permute-start.8 = (f32[2,512,128]{2,1,0:T(8,128)S(1)}, f32[2,512,128]{2,1,0:T(8,128)S(1)}, u32[]{:S(2)}, u32[]{:S(2)}) collective-permute-start(f32[2,512,128]{2,1,0:T(8,128)S(1)} %get-tuple-element.30), channel_id=1, source_target_pairs={{0,2},{2,4},{4,6},{6,8},{8,10},{10,12},{12,14},{16,18},{18,20},{20... | collective-permute-start | bytes 1572872 | tf_op jit(solution)/shard_map/ppermute | solution.py:191
  99.7 10.5 %collective-permute-start.9 = (f32[2,512,128]{2,1,0:T(8,128)S(1)}, f32[2,512,128]{2,1,0:T(8,128)S(1)}, u32[]{:S(2)}, u32[]{:S(2)}) collective-permute-start(f32[2,512,128]{2,1,0:T(8,128)S(1)} %get-tuple-element.31), channel_id=1, source_target_pairs={{2,0},{4,2},{6,4},{8,6},{10,8},{12,10},{14,12},{18,16},{20,18},{22... | collective-permute-start | bytes 1572872 | tf_op jit(solution)/shard_map/ppermute | solution.py:191
  103.1 12.6 %collective-permute-start.13 = (f32[2,512,128]{2,1,0:T(8,128)S(1)}, f32[2,512,128]{2,1,0:T(8,128)S(1)}, u32[]{:S(2)}, u32[]{:S(2)}) collective-permute-start(f32[2,512,128]{2,1,0:T(8,128)S(1)} %get-tuple-element.35), channel_id=1, source_target_pairs={{0,2},{2,4},{4,6},{6,8},{8,10},{10,12},{12,14},{16,18},{18,20},{20... | collective-permute-start | bytes 1572872 | tf_op jit(solution)/shard_map/ppermute | solution.py:191
  106.8 10.8 %collective-permute-start.14 = (f32[2,512,128]{2,1,0:T(8,128)S(1)}, f32[2,512,128]{2,1,0:T(8,128)S(1)}, u32[]{:S(2)}, u32[]{:S(2)}) collective-permute-start(f32[2,512,128]{2,1,0:T(8,128)S(1)} %get-tuple-element.36), channel_id=1, source_target_pairs={{2,0},{4,2},{6,4},{8,6},{10,8},{12,10},{14,12},{18,16},{20,18},{22... | collective-permute-start | bytes 1572872 | tf_op jit(solution)/shard_map/ppermute | solution.py:191
  110.3 12.7 %collective-permute-start.10 = (f32[2,128,256]{2,1,0:T(8,128)S(1)}, f32[2,128,256]{2,1,0:T(8,128)S(1)}, u32[]{:S(2)}, u32[]{:S(2)}) collective-permute-start(f32[2,128,256]{2,1,0:T(8,128)S(1)} %get-tuple-element.40), channel_id=1, source_target_pairs={{0,16},{2,18},{4,20},{6,22},{8,24},{10,26},{12,28},{14,30},{16,32}... | collective-permute-start | bytes 786440 | tf_op jit(solution)/shard_map/ppermute | solution.py:185
  114.4 8.7 %collective-permute-start.11 = (f32[2,128,256]{2,1,0:T(8,128)S(1)}, f32[2,128,256]{2,1,0:T(8,128)S(1)}, u32[]{:S(2)}, u32[]{:S(2)}) collective-permute-start(f32[2,128,256]{2,1,0:T(8,128)S(1)} %get-tuple-element.41), channel_id=1, source_target_pairs={{16,0},{18,2},{20,4},{22,6},{24,8},{26,10},{28,12},{30,14},{32,16}... | collective-permute-start | bytes 786440 | tf_op jit(solution)/shard_map/ppermute | solution.py:185
  117.7 8.1 %collective-permute-start.15 = (f32[2,128,256]{2,1,0:T(8,128)S(1)}, f32[2,128,256]{2,1,0:T(8,128)S(1)}, u32[]{:S(2)}, u32[]{:S(2)}) collective-permute-start(f32[2,128,256]{2,1,0:T(8,128)S(1)} %get-tuple-element.44), channel_id=1, source_target_pairs={{0,16},{2,18},{4,20},{6,22},{8,24},{10,26},{12,28},{14,30},{16,32}... | collective-permute-start | bytes 786440 | tf_op jit(solution)/shard_map/ppermute | solution.py:185
  121.8 7.4 %collective-permute-start.16 = (f32[2,128,256]{2,1,0:T(8,128)S(1)}, f32[2,128,256]{2,1,0:T(8,128)S(1)}, u32[]{:S(2)}, u32[]{:S(2)}) collective-permute-start(f32[2,128,256]{2,1,0:T(8,128)S(1)} %get-tuple-element.45), channel_id=1, source_target_pairs={{16,0},{18,2},{20,4},{22,6},{24,8},{26,10},{28,12},{30,14},{32,16}... | collective-permute-start | bytes 786440 | tf_op jit(solution)/shard_map/ppermute | solution.py:185
  123.2 24.4 %collective-permute-start.12 = (f32[2,256,256]{2,1,0:T(8,128)S(1)}, f32[2,256,256]{2,1,0:T(8,128)S(1)}, u32[]{:S(2)}, u32[]{:S(2)}) collective-permute-start(f32[2,256,256]{2,1,0:T(8,128)S(1)} %slice_add_fusion.1), channel_id=1, source_target_pairs={{0,1},{1,0},{2,3},{3,2},{4,5},{5,4},{6,7},{7,6},{8,9},{9,8},{10,11... | collective-permute-start | bytes 1572872 | tf_op jit(solution)/shard_map/ppermute | solution.py:195
  129.3 28.6 %collective-permute-start.17 = (f32[2,256,256]{2,1,0:T(8,128)S(1)}, f32[2,256,256]{2,1,0:T(8,128)S(1)}, u32[]{:S(2)}, u32[]{:S(2)}) collective-permute-start(f32[2,256,256]{2,1,0:T(8,128)S(1)} %slice_add_fusion), channel_id=1, source_target_pairs={{0,1},{1,0},{2,3},{3,2},{4,5},{5,4},{6,7},{7,6},{8,9},{9,8},{10,11... | collective-permute-start | bytes 1572872 | tf_op jit(solution)/shard_map/ppermute | solution.py:195
  (1 other events, 1.6 us)

commit v2 on v0

v2 whole, which is shorter than its diff:
```python
import functools
import math

import jax
import jax.numpy as jnp
import ml_dtypes
import numpy as np
from jax import lax
from jax.experimental import pallas as pl
from jax.experimental.pallas import tpu as pltpu
from jax.sharding import PartitionSpec as P

GY = 8
F32 = jnp.float32
BF16 = jnp.bfloat16
VMEM_LIMIT = 24 * 1024 * 1024


def dft_pair(extent):
    counter = np.arange(extent)
    angle = -2.0 * math.pi / extent * (counter[:, None] * counter[None, :] % extent)
    scale = 1.0 / math.sqrt(extent)
    return (
        (np.cos(angle) * scale).astype(ml_dtypes.bfloat16),
        (np.sin(angle) * scale).astype(ml_dtypes.bfloat16),
    )


def left_form(re, im, xp):
    return xp.concatenate(
        [xp.concatenate([re, -im], axis=1), xp.concatenate([im, re], axis=1)], axis=0
    )


def right_form(re, im, xp):
    return xp.concatenate(
        [xp.concatenate([re, im], axis=1), xp.concatenate([-im, re], axis=1)], axis=0
    )


def dft_tables(extent):
    re, im = dft_pair(extent)
    h = extent // 2

    def tables(re, im, evens_first):
        by_row = [(re[b::2, :h], im[b::2, :h]) for b in range(2)]
        by_col = [(re[:h, b::2], im[:h, b::2]) for b in range(2)]
        lefts, rights = (by_row, by_col) if evens_first else (by_col, by_row)
        return np.stack(
            [left_form(*pair, np) for pair in lefts] + [right_form(*pair, np) for pair in rights]
        )

    return tables(re, im, True), tables(re, -im, False)


def mm(a, b):
    return jnp.dot(a, b, preferred_element_type=F32)


def beside(a, b):
    return jnp.concatenate([a, b], axis=1)


def above(a, b):
    return jnp.concatenate([a, b], axis=0)


def sandwich(left, re, im, right):
    n = re.shape[0]
    half = mm(left, above(re.astype(BF16), im.astype(BF16)))
    both = mm(beside(half[:n].astype(BF16), half[n:].astype(BF16)), right)
    return both[:, :n], both[:, n:]


def dft_sandwich(tabs, re, im):
    h = re.shape[0] // 2
    even = mm(tabs[0], above(re[:h] + re[h:], im[:h] + im[h:]).astype(BF16))
    odd = mm(tabs[1], above(re[:h] - re[h:], im[:h] - im[h:]).astype(BF16))
    re, im = above(even[:h], odd[:h]), above(even[h:], odd[h:])
    e = mm(beside(re[:, :h] + re[:, h:], im[:, :h] + im[:, h:]).astype(BF16), tabs[2])
    o = mm(beside(re[:, :h] - re[:, h:], im[:, :h] - im[:, h:]).astype(BF16), tabs[3])
    return e, o


def conj_dft_sandwich(tabs, e, o):
    h = e.shape[0] // 2
    e, o = e.astype(BF16), o.astype(BF16)
    even = mm(tabs[0], above(beside(e[:h, :h], o[:h, :h]), beside(e[:h, h:], o[:h, h:])))
    odd = mm(tabs[1], above(beside(e[h:, :h], o[h:, :h]), beside(e[h:, h:], o[h:, h:])))
    re = above(even[:h] + odd[:h], even[:h] - odd[:h]).astype(BF16)
    im = above(even[h:] + odd[h:], even[h:] - odd[h:]).astype(BF16)
    e = mm(beside(re[:, :h], im[:, :h]), tabs[2])
    o = mm(beside(re[:, h:], im[:, h:]), tabs[3])
    return (
        beside(e[:, :h] + o[:, :h], e[:, :h] - o[:, :h]),
        beside(e[:, h:] + o[:, h:], e[:, h:] - o[:, h:]),
    )


def place_of(off_ref, slot, h):
    row = off_ref[slot, 0] + h
    col = off_ref[slot, 1] + h
    top = pl.multiple_of((row >> 3) * 8, 8)
    block = pl.multiple_of((col >> 7) * 128, 128)
    return top, block, row & 7, col & 127


def build_canvas(own, up, down, left, right, corner_l, corner_r, canvas):
    n = own.shape[-1]
    h = n // 2
    canvas[:, :, h : h + n, h : h + n] = own[...]
    canvas[:, :, 0:h, h : h + n] = up[...]
    canvas[:, :, h + n :, h : h + n] = down[...]
    canvas[:, :, h : h + n, 0:h] = left[...]
    canvas[:, :, h : h + n, h + n :] = right[...]
    canvas[:, :, 0:h, 0:h] = corner_l[0]
    canvas[:, :, h + n :, 0:h] = corner_l[1]
    canvas[:, :, 0:h, h + n :] = corner_r[0]
    canvas[:, :, h + n :, h + n :] = corner_r[1]


def extract(off_ref, slot, canvas, patch):
    n = patch.shape[-1]
    h = n // 2
    top, block, row_rest, col_rest = place_of(off_ref, slot, h)
    row_shift = jnp.where(row_rest == 0, 0, n + 8 - row_rest)
    col_shift = jnp.where(col_rest == 0, 0, n + h - col_rest)
    for part in range(2):
        for layer in range(2):
            window = canvas[part, layer, pl.ds(top, n + 8), pl.ds(block, n + h)]
            window = pltpu.roll(window, col_shift, 1)[:, :n]
            patch[part, layer] = pltpu.roll(window, row_shift, 0)[:n]


def place(off_ref, grads, out_l, out_c, out_r, canvas):
    n = grads[0].shape[-1]
    h = n // 2
    canvas[...] = jnp.zeros_like(canvas)
    for slot, grad in enumerate(grads):
        top, block, row_rest, col_rest = place_of(off_ref, slot, h)
        for part in range(2):
            tall = above(grad[part], jnp.zeros((8, n), F32))
            tall = pltpu.roll(tall, row_rest, 0)
            wide = beside(tall, jnp.zeros((n + 8, h), F32))
            canvas[part, pl.ds(top, n + 8), pl.ds(block, n + h)] += pltpu.roll(wide, col_rest, 1)
    out_l[...] = canvas[:, :, 0:h]
    out_c[...] = canvas[:, :, h : h + n]
    out_r[...] = canvas[:, :, h + n :]


def each_mode(modes, step):
    def pair(i, carry):
        for j in range(2):
            step(i * 2 + j)
        return carry

    lax.fori_loop(0, modes // 2, pair, 0)


def forward(probe, patch, prop_l, prop_r, tabs, wave, far, inten):
    n = inten.shape[0]
    h = n // 2
    inten[...] = jnp.zeros_like(inten)

    def step(m):
        p_re, p_im = probe[0, m], probe[1, m]
        o_re, o_im = patch[0, 0], patch[1, 0]
        w_re, w_im = sandwich(
            prop_l[...], p_re * o_re - p_im * o_im, p_re * o_im + p_im * o_re, prop_r[...]
        )
        wave[m, 0] = w_re
        wave[m, 1] = w_im
        o_re, o_im = patch[0, 1], patch[1, 1]
        e, o = dft_sandwich(tabs, w_re * o_re - w_im * o_im, w_re * o_im + w_im * o_re)
        far[m, 0] = e
        far[m, 1] = o
        e, o = e * e, o * o
        inten[...] += beside(e[:, :h] + e[:, h:], o[:, :h] + o[:, h:])

    each_mode(probe.shape[1], step)


def forward_first_kernel(off, own, up, down, left, right, corner_l, corner_r, probe, prop_l,
                         prop_r, tabs, canvas, patch, wave, far, inten):
    build_canvas(own, up, down, left, right, corner_l, corner_r, canvas)
    extract(off, 0, canvas, patch)
    forward(probe, patch, prop_l, prop_r, tabs, wave, far, inten)


def forward_next_kernel(slot, off, canvas, probe, prop_l, prop_r, tabs, patch, wave, far, inten):
    extract(off, slot, canvas, patch)
    forward(probe, patch, prop_l, prop_r, tabs, wave, far, inten)


def back_last(slot, counts, mine, other, measured, far, wave, patch, tabs, grad, bar, resid):
    n = mine.shape[0]
    h = n // 2
    live = jnp.where(slot < counts[0], 2.0, 0.0).astype(F32)
    r = (mine[...] + other[...] - measured[slot]) * live
    resid[0] = beside(r[:, :h], r[:, :h])
    resid[1] = beside(r[:, h:], r[:, h:])
    grad[...] = jnp.zeros_like(grad)

    def step(m):
        b_re, b_im = conj_dft_sandwich(tabs, resid[0] * far[m, 0], resid[1] * far[m, 1])
        w_re, w_im = wave[m, 0], wave[m, 1]
        grad[0] += w_re * b_re + w_im * b_im
        grad[1] += w_re * b_im - w_im * b_re
        o_re, o_im = patch[0, 1], patch[1, 1]
        bar[m, 0] = (o_re * b_re + o_im * b_im).astype(BF16)
        bar[m, 1] = (o_re * b_im - o_im * b_re).astype(BF16)

    each_mode(far.shape[0], step)


def back_last_place_kernel(slot, counts, off, before, mine, other, measured, far, wave, patch,
                           tabs, bar, out_l, out_c, out_r, resid, grad, canvas):
    back_last(slot, counts, mine, other, measured, far, wave, patch, tabs, grad, bar, resid)
    place(off, (before, grad), out_l, out_c, out_r, canvas)


def back_first(bar, probe, patch, prop_l, prop_r, grad, emit):
    grad[...] = jnp.zeros_like(grad)

    def step(m):
        b_re, b_im = sandwich(prop_l[...], bar[m, 0], bar[m, 1], prop_r[...])
        p_re, p_im = probe[0, m], probe[1, m]
        grad[0] += p_re * b_re + p_im * b_im
        grad[1] += p_re * b_im - p_im * b_re
        o_re, o_im = patch[0, 0], patch[1, 0]
        emit(m, o_re * b_re + o_im * b_im, o_re * b_im - o_im * b_re)

    each_mode(probe.shape[1], step)


def back_first_kernel(bar, probe, patch, prop_l, prop_r, grad, part):
    def emit(m, re, im):
        part[0, m] = re
        part[1, m] = im

    back_first(bar, probe, patch, prop_l, prop_r, grad, emit)


def back_first_add_kernel(bar, probe, patch, prop_l, prop_r, part, grad, total):
    def emit(m, re, im):
        total[0, 0, m] = part[0, m] + re
        total[0, 1, m] = part[1, m] + im

    back_first(bar, probe, patch, prop_l, prop_r, grad, emit)


def place_kernel(off, grad0, grad1, out_l, out_c, out_r, canvas):
    place(off, (grad0, grad1), out_l, out_c, out_r, canvas)


def prepare_kernel(prop, probe, measured, order, order_t, dft_in, conj_in, prop_l, prop_r,
                   back_l, back_r, probe_out, meas_out, dft_out, conj_out):
    re, im = prop[0].astype(F32), prop[1].astype(F32)
    re_t, im_t = re.T, im.T
    prop_l[...] = left_form(re, im, jnp).astype(BF16)
    prop_r[...] = right_form(re_t, im_t, jnp).astype(BF16)
    back_l[...] = left_form(re_t, -im_t, jnp).astype(BF16)
    back_r[...] = right_form(re, -im, jnp).astype(BF16)
    probe_out[...] = probe[...]
    dft_out[...] = dft_in[...]
    conj_out[...] = conj_in[...]
    exact = functools.partial(
        jnp.dot, precision=lax.Precision.HIGHEST, preferred_element_type=F32
    )
    for slot in range(measured.shape[0]):
        meas_out[slot] = exact(exact(order[...], measured[slot]), order_t[...])


def rows_by(value, step):
    count = lax.axis_size("tile")
    pairs = [(i, i + GY * step) for i in range(count) if 0 <= i + GY * step < count]
    return lax.ppermute(value, "tile", pairs)


def cols_by(value, step):
    count = lax.axis_size("tile")
    pairs = [(i, i + step) for i in range(count) if 0 <= i % GY + step < GY]
    return lax.ppermute(value, "tile", pairs)


def swap_mode(value):
    return lax.ppermute(value, "mode", [(0, 1), (1, 0)])


def call(kernel, name, outs, args, scratch=(), smem=1, after=()):
    vmem = pl.BlockSpec(memory_space=pltpu.VMEM)
    scalars = pl.BlockSpec(memory_space=pltpu.SMEM)
    n_args, n_after = len(args), len(after)

    def run(*refs):
        kernel(*refs[:n_args], *refs[n_args + n_after :])

    return pl.pallas_call(
        run,
        out_shape=tuple(jax.ShapeDtypeStruct(shape, dtype) for shape, dtype in outs),
        in_specs=[scalars] * smem
        + [vmem] * (n_args - smem)
        + [pl.BlockSpec(memory_space=pl.ANY)] * n_after,
        out_specs=tuple(vmem for _ in outs),
        scratch_shapes=[pltpu.VMEM(shape, F32) for shape in scratch],
        compiler_params=pltpu.CompilerParams(vmem_limit_bytes=VMEM_LIMIT),
        name=name,
    )(*args, *after)


def body(object_tiles, probe_modes, propagator, offsets, counts, measured):
    n = probe_modes.shape[-1]
    h = n // 2
    modes = probe_modes.shape[1]
    slots = measured.shape[1]
    own = object_tiles[0]
    off = offsets[0]

    down_strip = rows_by(own[:, :, :h, :], -1)
    up_strip = rows_by(own[:, :, h:, :], 1)
    left_strip = cols_by(own[:, :, :, h:], 1)
    right_strip = cols_by(own[:, :, :, :h], -1)
    corner_l = cols_by(jnp.stack([up_strip[..., h:], down_strip[..., h:]]), 1)
    corner_r = cols_by(jnp.stack([up_strip[..., :h], down_strip[..., :h]]), -1)

    dft, conj_dft = dft_tables(n)
    order = np.eye(n, dtype=np.float32)[np.r_[0:n:2, 1:n:2]]
    plane, pair, mat = ((n, n), F32), ((2, n, n), F32), ((2 * n, 2 * n), BF16)
    patch_out, field = ((2, 2, n, n), F32), ((modes, 2, n, n), F32)
    probes, tables = ((2, modes, n, n), F32), (dft.shape, BF16)
    prop_l, prop_r, back_prop_l, back_prop_r, probe, measured, dft, conj_dft = call(
        prepare_kernel,
        "prepare",
        (mat, mat, mat, mat, probes, ((slots, n, n), F32), tables, tables),
        (propagator, probe_modes, measured[0], jnp.asarray(order), jnp.asarray(order.T.copy()),
         jnp.asarray(dft), jnp.asarray(conj_dft)),
        smem=0,
    )

    canvas, patch0, wave0, far0, inten0 = call(
        forward_first_kernel,
        "forward_0",
        (((2, 2, 2 * n, 2 * n), F32), patch_out, field, field, plane),
        (off, own, up_strip, down_strip, left_strip, right_strip, corner_l, corner_r,
         probe, prop_l, prop_r, dft),
    )
    other0 = swap_mode(inten0)
    patch1, wave1, far1, inten1 = call(
        functools.partial(forward_next_kernel, 1),
        "forward_1",
        (patch_out, field, field, plane),
        (off, canvas, probe, prop_l, prop_r, dft),
    )
    other1 = swap_mode(inten1)

    bar_out = ((modes, 2, n, n), BF16)
    strips = (((2, 2 * n, h), F32), ((2, 2 * n, n), F32), ((2, 2 * n, h), F32))
    wide = (2, 2 * n, 2 * n)
    grad_last0, bar0 = call(
        functools.partial(back_last, 0),
        "back_last_0",
        (pair, bar_out),
        (counts, inten0, other0, measured, far0, wave0, patch0, conj_dft),
        scratch=((2, n, n),),
    )
    grad_first0, part = call(
        back_first_kernel,
        "back_first_0",
        (pair, probes),
        (bar0, probe, patch0, back_prop_l, back_prop_r),
        smem=0,
    )
    bar1, out_l, out_c, out_r = call(
        functools.partial(back_last_place_kernel, 1),
        "back_last_1",
        (bar_out,) + strips,
        (counts, off, grad_last0, inten1, other1, measured, far1, wave1, patch1, conj_dft),
        scratch=((2, n, n), (2, n, n), wide),
        smem=2,
        after=(grad_first0,),
    )

    def add_cols(out_l, out_c, out_r):
        from_left = cols_by(out_r, 1)
        from_right = cols_by(out_l, -1)
        return out_c + jnp.concatenate([from_left, from_right], axis=2)

    def add_rows(tall):
        from_up = rows_by(tall[:, n + h :, :], 1)
        from_down = rows_by(tall[:, :h, :], -1)
        return tall[:, h : h + n, :] + jnp.concatenate([from_up, from_down], axis=1)

    tall_last = add_cols(out_l, out_c, out_r)
    grad_first1, probe_grad = call(
        back_first_add_kernel,
        "back_first_1",
        (pair, ((1, 2, modes, n, n), F32)),
        (bar1, probe, patch1, back_prop_l, back_prop_r, part),
        smem=0,
    )
    mine_last = add_rows(tall_last)
    other_last = swap_mode(mine_last)
    out_l, out_c, out_r = call(
        place_kernel,
        "place_first",
        strips,
        (off, grad_first0, grad_first1),
        scratch=(wide,),
        after=(tall_last,),
    )
    mine_first = add_rows(add_cols(out_l, out_c, out_r))
    other_first = swap_mode(mine_first)
    object_grad = jnp.stack([mine_first + other_first, mine_last + other_last], axis=1)
    return (object_grad.reshape(object_tiles.shape), probe_grad)


def solution(mesh):
    placed = (
        P("tile", None, None, None, None),
        P(None, "mode", None, None),
        P(),
        P("tile", None, None),
        P("tile"),
        P("tile", None, None, None),
    )
    return jax.shard_map(
        body,
        mesh=mesh,
        in_specs=placed,
        out_specs=(P("tile", None, None, None, None), P("tile", None, "mode", None, None)),
        check_vma=False,
    )
```

time: 484 us -> 137 us (0.28)
  waiting for transfers between devices: 226 us -> 41.8 us
  matrix products: 71.2 us -> 0 us
  local copies, waits for them, and re-layouts: 50.2 us -> 3.8 us
  Pallas kernels: 0 us -> 34.7 us
  other arithmetic: 29.9 us -> 0.73 us
  loops' own time: 27.1 us -> 0 us
  between operations: 16.2 us -> 1.72 us
  starting transfers between devices: 58.5 us -> 52.8 us
    psum x3 -> x0, waiting for transfers between devices: 174 us -> none  [the longest x2 110 us: visit_slot(): intensity = lax.psum(partial_sum, 'mode')]
    dot_general x64 -> x0, matrix products: 71.2 us -> none  [single_product(): jnp.einsum(einsum_form, first_op, second_op, preferred_element_type=jnp.f...]
    pallas_call x0 -> x8, Pallas kernels: none -> 34.7 us  [call(): pl.pallas_call(run, out_shape=tuple((jax.ShapeDtypeStruct(shape, dtype) f...]
    another operation x1 -> x0, loops' own time: 27.1 us -> none  [body(): grad_canvas, probe_sum = lax.fori_loop(0, upper, visit_slot, start_state)]
    dynamic_update_slice x2 -> x0, local copies, waits for them, and re-layouts: 23.9 us -> none  [visit_slot(): lax.dynamic_update_slice(grad_canvas, previous + patch_grad, corner)]
    add x4, other arithmetic: 14.5 us -> 0.44 us  [the longest x2 0.3 us: add_cols(): return out_c + jnp.concatenate([from_left, from_right], axis=2)]
    ppermute x16 -> x18, waiting for transfers between devices: 52.2 us -> 41.8 us  [the longest x4 30.4 us: swap_mode(): return lax.ppermute(value, 'mode', [(0, 1), (1, 0)])]
    mul x10 -> x0, other arithmetic: 7.34 us -> none  [the longest x8 5.22 us: body(): gathered[vertical, lateral] = incoming * inside]
  transfers between devices with their start and end apart: 19 -> 18, of which waited for: 8 -> 9; matrix products, arithmetic and copies ran while one was open for 4% -> 1% of each run, Pallas kernels for 0% -> 15%
where the time goes in v2:
time: 137 us; the launch traced here: 136 us
  starting transfers between devices  52.8 us (39%)
  waiting for transfers between devices  41.8 us (31%)
  Pallas kernels  34.7 us (25%)
  local copies, waits for them, and re-layouts  3.8 us (3%)
  between operations  1.72 us (1%)
    pallas_call x8, Pallas kernels, call(): pl.pallas_call(run, out_shape=tuple((jax.ShapeDtypeStruct(shape, dtype) f...  34.7 us
    ppermute x4, waiting for transfers between devices, swap_mode(): return lax.ppermute(value, 'mode', [(0, 1), (1, 0)])  30.4 us
    ppermute x8, starting transfers between devices, cols_by(): return lax.ppermute(value, 'tile', pairs)  28.1 us
    ppermute x6, starting transfers between devices, rows_by(): return lax.ppermute(value, 'tile', pairs)  18.6 us
    ppermute x8, waiting for transfers between devices, cols_by(): return lax.ppermute(value, 'tile', pairs)  7.24 us
    ppermute x4, starting transfers between devices, swap_mode(): return lax.ppermute(value, 'mode', [(0, 1), (1, 0)])  6.08 us
    ppermute x6, waiting for transfers between devices, rows_by(): return lax.ppermute(value, 'tile', pairs)  4.2 us
  transfers between devices with their start and end apart: 18, of which 9 were waited for; matrix products, arithmetic and copies ran while one was open for 1% of the time, Pallas kernels for 15%

profile of v2, /device:TPU:1, one launch (start us, length us, event | category | flops | bytes accessed | tf_op | source)
XLA Modules:
  0.0 135.6 jit_solution(12166698492916486607)
XLA Ops:
  0.6 1.3 fusion.3
  1.9 1.3 collective-permute-start.1
  3.3 5.3 %collective-permute-start = (f32[2,2,128,256]{3,2,1,0:T(8,128)S(1)}, f32[2,2,128,256]{3,2,1,0:T(8,128)S(1)}, u32[]{:S(2)}, u32[]{:S(2)}) collective-permute-start(f32[2,2,128,256]{3,2,1,0:T(8,128)S(1)} %get-tuple-element.71), channel_id=1, source_target_pairs={{0,16},{2,18},{4,20},{6,22},{8,24},{10,26},{12,28},{14,30},{16,32}... | collective-permute-start | bytes 1572872 | tf_op jit(solution)/shard_map/ppermute | solution.py:277
  8.6 1.3 fusion.2
  9.9 4.1 %collective-permute-start.2 = (f32[2,2,256,128]{3,2,1,0:T(8,128)S(1)}, f32[2,2,256,128]{3,2,1,0:T(8,128)S(1)}, u32[]{:S(2)}, u32[]{:S(2)}) collective-permute-start(f32[2,2,256,128]{3,2,1,0:T(8,128)S(1)} %get-tuple-element.69), channel_id=1, source_target_pairs={{0,2},{2,4},{4,6},{6,8},{8,10},{10,12},{12,14},{16,18},{18,20},{20... | collective-permute-start | bytes 1572872 | tf_op jit(solution)/shard_map/ppermute | solution.py:283
  14.0 2.0 %collective-permute-start.3 = (f32[2,2,256,128]{3,2,1,0:T(8,128)S(1)}, f32[2,2,256,128]{3,2,1,0:T(8,128)S(1)}, u32[]{:S(2)}, u32[]{:S(2)}) collective-permute-start(f32[2,2,256,128]{3,2,1,0:T(8,128)S(1)} %get-tuple-element.68), channel_id=1, source_target_pairs={{2,0},{4,2},{6,4},{8,6},{10,8},{12,10},{14,12},{18,16},{20,18},{22... | collective-permute-start | bytes 1572872 | tf_op jit(solution)/shard_map/ppermute | solution.py:283
  17.3 6.4 %collective-permute-start.4 = (f32[2,2,2,128,128]{4,3,2,1,0:T(8,128)S(1)}, f32[2,2,2,128,128]{4,3,2,1,0:T(8,128)S(1)}, u32[]{:S(2)}, u32[]{:S(2)}) collective-permute-start(f32[2,2,2,128,128]{4,3,2,1,0:T(8,128)S(1)} %pad_maximum_fusion), channel_id=1, source_target_pairs={{0,2},{2,4},{4,6},{6,8},{8,10},{10,12},{12,14},{16,18},{18,20},{20... | collective-permute-start | bytes 1572872 | tf_op jit(solution)/shard_map/ppermute | solution.py:283
  23.9 2.1 %collective-permute-start.5 = (f32[2,2,2,128,128]{4,3,2,1,0:T(8,128)S(1)}, f32[2,2,2,128,128]{4,3,2,1,0:T(8,128)S(1)}, u32[]{:S(2)}, u32[]{:S(2)}) collective-permute-start(f32[2,2,2,128,128]{4,3,2,1,0:T(8,128)S(1)} %pad_maximum_fusion.1), channel_id=1, source_target_pairs={{2,0},{4,2},{6,4},{8,6},{10,8},{12,10},{14,12},{18,16},{20,18},{22... | collective-permute-start | bytes 1572872 | tf_op jit(solution)/shard_map/ppermute | solution.py:283
  26.0 1.7 %prepare.1 = (bf16[512,512]{1,0:T(8,128)(2,1)S(1)}, bf16[512,512]{1,0:T(8,128)(2,1)S(1)}, bf16[512,512]{1,0:T(8,128)(2,1)S(1)}, bf16[512,512]{1,0:T(8,128)(2,1)S...) custom-call(bf16[2,256,256]{2,1,0:T(8,128)(2,1)S(1)} %copy-done.5, ...), custom_call_target="tpu_custom_call" | custom-call | tf_op jit(solution)/shard_map/prepare/pallas_call | solution.py:298
  27.7 2.2 %collective-permute-done.4.refs_6_ = f32[2,2,2,128,128]{4,3,2,1,0:T(8,128)S(1)} collective-permute-done((f32[2,2,2,128,128]{4,3,2,1,0:T(8,128)S(1)}, f32[2,2,2,128,128]{4,3,2,1,0:T(8,128)S(1)}, u32[]{:S(2)}, u32[]{:S(2)}) %collective-permute-start.4) | collective-permute-done | bytes 524320 | tf_op jit(solution)/shard_map/ppermute | solution.py:283
  29.9 4.6 %collective-permute-done.5.refs_7_ = f32[2,2,2,128,128]{4,3,2,1,0:T(8,128)S(1)} collective-permute-done((f32[2,2,2,128,128]{4,3,2,1,0:T(8,128)S(1)}, f32[2,2,2,128,128]{4,3,2,1,0:T(8,128)S(1)}, u32[]{:S(2)}, u32[]{:S(2)}) %collective-permute-start.5) | collective-permute-done | bytes 524320 | tf_op jit(solution)/shard_map/ppermute | solution.py:283
  34.5 8.0 %forward_0.1 = (f32[2,2,512,512]{3,2,1,0:T(8,128)S(1)}, f32[2,2,256,256]{3,2,1,0:T(8,128)S(1)}, f32[6,2,256,256]{3,2,1,0:T(8,128)S(1)}, f32[6,2,256,256]{3,2,1,0:T(8,128)S(1)}, f32[256,256]{1,0:T(8,128)S(1)}) custom-call(s32[2,2]{1,0:T(2,128)S(1)} %bitcast.21, f32[2,2,256,256]{3,2,1,0:T(8,128)S(1)} %bitcast.19, ...), custom_call_target="tpu_custom_call" | custom-call | tf_op jit(solution)/shard_map/forward_0/pallas_call | solution.py:298
  42.5 3.0 %collective-permute-start.6 = (f32[256,256]{1,0:T(8,128)S(1)}, f32[256,256]{1,0:T(8,128)S(1)}, u32[]{:S(2)}, u32[]{:S(2)}) collective-permute-start(f32[256,256]{1,0:T(8,128)S(1)} %get-tuple-element.36.refs_1_), channel_id=1, source_target_pairs={{0,1},{1,0},{2,3},{3,2},{4,5},{5,4},{6,7},{7,6},{8,9},{9,8},{10,11... | collective-permute-start | bytes 786440 | tf_op jit(solution)/shard_map/ppermute | solution.py:287
  45.5 7.5 %forward_1.1 = (f32[2,2,256,256]{3,2,1,0:T(8,128)S(1)}, f32[6,2,256,256]{3,2,1,0:T(8,128)S(1)}, f32[6,2,256,256]{3,2,1,0:T(8,128)S(1)}, f32[256,256]{1,0:T(8,128)S(1)}) custom-call(s32[2,2]{1,0:T(2,128)S(1)} %bitcast.22, f32[2,2,512,512]{3,2,1,0:T(8,128)S(1)} %get-tuple-element.47.refs_1_, f32[2,6,256,256]{3,2,1,0:T(8,128)S(1)} %get-tuple-element.32.refs_8_.refs_1_.refs_2_, ...), custom_call_target="tpu_custom_call" | custom-call | tf_op jit(solution)/shard_map/forward_1/pallas_call | solution.py:298
  53.9 2.7 %back_last_0.1 = (f32[2,256,256]{2,1,0:T(8,128)S(1)}, bf16[6,2,256,256]{3,2,1,0:T(8,128)(2,1)S(1)}) custom-call(s32[1]{0:T(128)S(6)} %copy.13.refs_0_, f32[256,256]{1,0:T(8,128)S(1)} %get-tuple-element.36.refs_1_, f32[256,256]{1,0:T(8,128)S(1)} %collective-permute-done.6.refs_2_, f32[2,256,256]{2,1,0:T(8,128)S(1)} %get-tuple-element.37.refs_3_.refs_5_, ...), custom_call_target="tpu_custom_call" | custom-call | tf_op jit(solution)/shard_map/back_last_0/pallas_call | solution.py:298
  56.6 3.6 %back_first_0.1 = (f32[2,256,256]{2,1,0:T(8,128)S(1)}, f32[2,6,256,256]{3,2,1,0:T(8,128)S(1)}) custom-call(bf16[6,2,256,256]{3,2,1,0:T(8,128)(2,1)S(1)} %get-tuple-element.42.refs_0_, f32[2,6,256,256]{3,2,1,0:T(8,128)S(1)} %get-tuple-element.32.refs_8_.refs_1_.refs_2_, f32[2,2,256,256]{3,2,1,0:T(8,128)S(1)} %get-tuple-element.40.refs_6_.refs_2_, ...), custom_call_target="tpu_custom_call" | custom-call | tf_op jit(solution)/shard_map/back_first_0/pallas_call | solution.py:298
  60.2 4.2 %back_last_1.1 = (bf16[6,2,256,256]{3,2,1,0:T(8,128)(2,1)S(1)}, f32[2,512,128]{2,1,0:T(8,128)S(1)}, f32[2,512,256]{2,1,0:T(8,128)S(1)}, f32[2,512,128]{2,1,0:T(8,128)S(1)}) custom-call(s32[1]{0:T(128)S(6)} %copy.13.refs_0_, s32[2,2]{1,0:T(2,128)S(1)} %bitcast.23, f32[2,256,256]{2,1,0:T(8,128)S(1)} %get-tuple-element.46.refs_2_, ...), custom_call_target="tpu_custom_call" | custom-call | tf_op jit(solution)/shard_map/back_last_1/pallas_call | solution.py:298
  64.4 1.9 %collective-permute-start.9 = (f32[2,512,128]{2,1,0:T(8,128)S(1)}, f32[2,512,128]{2,1,0:T(8,128)S(1)}, u32[]{:S(2)}, u32[]{:S(2)}) collective-permute-start(f32[2,512,128]{2,1,0:T(8,128)S(1)} %get-tuple-element.57), channel_id=1, source_target_pairs={{2,0},{4,2},{6,4},{8,6},{10,8},{12,10},{14,12},{18,16},{20,18},{22... | collective-permute-start | bytes 1572872 | tf_op jit(solution)/shard_map/ppermute | solution.py:283
  66.3 5.4 %collective-permute-start.8 = (f32[2,512,128]{2,1,0:T(8,128)S(1)}, f32[2,512,128]{2,1,0:T(8,128)S(1)}, u32[]{:S(2)}, u32[]{:S(2)}) collective-permute-start(f32[2,512,128]{2,1,0:T(8,128)S(1)} %get-tuple-element.56), channel_id=1, source_target_pairs={{0,2},{2,4},{4,6},{6,8},{8,10},{10,12},{12,14},{16,18},{18,20},{20... | collective-permute-start | bytes 1572872 | tf_op jit(solution)/shard_map/ppermute | solution.py:283
  71.7 5.5 %back_first_1.1 = (f32[2,256,256]{2,1,0:T(8,128)S(1)}, f32[1,2,6,256,256]{4,3,2,1,0:T(8,128)}) custom-call(bf16[6,2,256,256]{3,2,1,0:T(8,128)(2,1)S(1)} %get-tuple-element.52.refs_0_, f32[2,6,256,256]{3,2,1,0:T(8,128)S(1)} %get-tuple-element.32.refs_8_.refs_1_.refs_2_, f32[2,2,256,256]{3,2,1,0:T(8,128)S(1)} %get-tuple-element.51.refs_8_.refs_2_, ...), custom_call_target="tpu_custom_call" | custom-call | tf_op jit(solution)/shard_map/back_first_1/pallas_call | solution.py:298
  77.8 1.5 %place_first.1 = (f32[2,512,128]{2,1,0:T(8,128)S(1)}, f32[2,512,256]{2,1,0:T(8,128)S(1)}, f32[2,512,128]{2,1,0:T(8,128)S(1)}) custom-call(s32[2,2]{1,0:T(2,128)S(1)} %bitcast.24, f32[2,256,256]{2,1,0:T(8,128)S(1)} %get-tuple-element.45.refs_10_.refs_1_, f32[2,256,256]{2,1,0:T(8,128)S(1)} %get-tuple-element.54.refs_2_, f32[2,512,256]{2,1,0:T(8,128)S(1)} %maximum_add_fusion.refs_3_), custom_call_target="tpu_custom_call" | custom-call | tf_op jit(solution)/shard_map/place_first/pallas_call | solution.py:298
  79.3 1.9 %collective-permute-start.11 = (f32[2,512,128]{2,1,0:T(8,128)S(1)}, f32[2,512,128]{2,1,0:T(8,128)S(1)}, u32[]{:S(2)}, u32[]{:S(2)}) collective-permute-start(f32[2,512,128]{2,1,0:T(8,128)S(1)} %get-tuple-element.60), channel_id=1, source_target_pairs={{2,0},{4,2},{6,4},{8,6},{10,8},{12,10},{14,12},{18,16},{20,18},{22... | collective-permute-start | bytes 1572872 | tf_op jit(solution)/shard_map/ppermute | solution.py:283
  81.2 4.4 %collective-permute-start.10 = (f32[2,512,128]{2,1,0:T(8,128)S(1)}, f32[2,512,128]{2,1,0:T(8,128)S(1)}, u32[]{:S(2)}, u32[]{:S(2)}) collective-permute-start(f32[2,512,128]{2,1,0:T(8,128)S(1)} %get-tuple-element.59), channel_id=1, source_target_pairs={{0,2},{2,4},{4,6},{6,8},{8,10},{10,12},{12,14},{16,18},{18,20},{20... | collective-permute-start | bytes 1572872 | tf_op jit(solution)/shard_map/ppermute | solution.py:283
  85.7 1.3 collective-permute-start.16
  87.0 4.7 %collective-permute-start.15 = (f32[2,128,256]{2,1,0:T(8,128)S(1)}, f32[2,128,256]{2,1,0:T(8,128)S(1)}, u32[]{:S(2)}, u32[]{:S(2)}) collective-permute-start(f32[2,128,256]{2,1,0:T(8,128)S(1)} %get-tuple-element.66), channel_id=1, source_target_pairs={{0,16},{2,18},{4,20},{6,22},{8,24},{10,26},{12,28},{14,30},{16,32}... | collective-permute-start | bytes 786440 | tf_op jit(solution)/shard_map/ppermute | solution.py:277
  91.9 1.3 collective-permute-start.13
  93.2 4.7 %collective-permute-start.12 = (f32[2,128,256]{2,1,0:T(8,128)S(1)}, f32[2,128,256]{2,1,0:T(8,128)S(1)}, u32[]{:S(2)}, u32[]{:S(2)}) collective-permute-start(f32[2,128,256]{2,1,0:T(8,128)S(1)} %get-tuple-element.64), channel_id=1, source_target_pairs={{0,16},{2,18},{4,20},{6,22},{8,24},{10,26},{12,28},{14,30},{16,32}... | collective-permute-start | bytes 786440 | tf_op jit(solution)/shard_map/ppermute | solution.py:277
  98.0 1.5 %collective-permute-start.17 = (f32[2,256,256]{2,1,0:T(8,128)S(1)}, f32[2,256,256]{2,1,0:T(8,128)S(1)}, u32[]{:S(2)}, u32[]{:S(2)}) collective-permute-start(f32[2,256,256]{2,1,0:T(8,128)S(1)} %slice_add_fusion), channel_id=1, source_target_pairs={{0,1},{1,0},{2,3},{3,2},{4,5},{5,4},{6,7},{7,6},{8,9},{9,8},{10,11... | collective-permute-start | bytes 1572872 | tf_op jit(solution)/shard_map/ppermute | solution.py:287
  100.7 1.8 %collective-permute-done.12 = f32[2,128,256]{2,1,0:T(8,128)S(1)} collective-permute-done((f32[2,128,256]{2,1,0:T(8,128)S(1)}, f32[2,128,256]{2,1,0:T(8,128)S(1)}, u32[]{:S(2)}, u32[]{:S(2)}) %collective-permute-start.12) | collective-permute-done | bytes 262176 | tf_op jit(solution)/shard_map/ppermute | solution.py:277
  102.5 1.5 %collective-permute-start.14 = (f32[2,256,256]{2,1,0:T(8,128)S(1)}, f32[2,256,256]{2,1,0:T(8,128)S(1)}, u32[]{:S(2)}, u32[]{:S(2)}) collective-permute-start(f32[2,256,256]{2,1,0:T(8,128)S(1)} %slice_add_fusion.1), channel_id=1, source_target_pairs={{0,1},{1,0},{2,3},{3,2},{4,5},{5,4},{6,7},{7,6},{8,9},{9,8},{10,11... | collective-permute-start | bytes 1572872 | tf_op jit(solution)/shard_map/ppermute | solution.py:287
  103.9 20.8 %collective-permute-done.17 = f32[2,256,256]{2,1,0:T(8,128)S(1)} collective-permute-done((f32[2,256,256]{2,1,0:T(8,128)S(1)}, f32[2,256,256]{2,1,0:T(8,128)S(1)}, u32[]{:S(2)}, u32[]{:S(2)}) %collective-permute-start.17) | collective-permute-done | bytes 524320 | tf_op jit(solution)/shard_map/ppermute | solution.py:287
  124.8 9.6 %collective-permute-done.14 = f32[2,256,256]{2,1,0:T(8,128)S(1)} collective-permute-done((f32[2,256,256]{2,1,0:T(8,128)S(1)}, f32[2,256,256]{2,1,0:T(8,128)S(1)}, u32[]{:S(2)}, u32[]{:S(2)}) %collective-permute-start.14) | collective-permute-done | bytes 524320 | tf_op jit(solution)/shard_map/ppermute | solution.py:287
  (46 shorter events, 5.0 us)
Async XLA Ops:
  1.9 14.1 %collective-permute-start.1 = (f32[2,2,128,256]{3,2,1,0:T(8,128)S(1)}, f32[2,2,128,256]{3,2,1,0:T(8,128)S(1)}, u32[]{:S(2)}, u32[]{:S(2)}) collective-permute-start(f32[2,2,128,256]{3,2,1,0:T(8,128)S(1)} %get-tuple-element.70), channel_id=1, source_target_pairs={{16,0},{18,2},{20,4},{22,6},{24,8},{26,10},{28,12},{30,14},{32,16}... | collective-permute-start | bytes 1572872 | tf_op jit(solution)/shard_map/ppermute | solution.py:277
  3.2 22.7 %copy-start.1 = (f32[2,6,256,256]{3,2,1,0:T(8,128)S(1)}, f32[2,6,256,256]{3,2,1,0:T(8,128)}, u32[]{:S(2)}) copy-start(f32[2,6,256,256]{3,2,1,0:T(8,128)} %refs_1_.1) | copy-start | bytes 9437188
  3.2 22.7 %copy-start.2 = (f32[1,2,256,256]{3,2,1,0:T(8,128)S(1)}, f32[1,2,256,256]{3,2,1,0:T(8,128)}, u32[]{:S(2)}) copy-start(f32[1,2,256,256]{3,2,1,0:T(8,128)} %param.15) | copy-start | bytes 1572868
  3.2 22.7 %copy-start.3 = (bf16[4,256,256]{2,1,0:T(8,128)(2,1)S(1)}, bf16[4,256,256]{2,1,0:T(8,128)(2,1)}, u32[]{:S(2)}) copy-start(bf16[4,256,256]{2,1,0:T(8,128)(2,1)} %constant.10.clone.refs_5_) | copy-start | bytes 1572868
  3.2 22.7 %copy-start.4 = (bf16[4,256,256]{2,1,0:T(8,128)(2,1)S(1)}, bf16[4,256,256]{2,1,0:T(8,128)(2,1)}, u32[]{:S(2)}) copy-start(bf16[4,256,256]{2,1,0:T(8,128)(2,1)} %constant.11.clone.refs_6_) | copy-start | bytes 1572868
  3.3 22.7 %copy-start.5 = (bf16[2,256,256]{2,1,0:T(8,128)(2,1)S(1)}, bf16[2,256,256]{2,1,0:T(8,128)(2,1)}, u32[]{:S(2)}) copy-start(bf16[2,256,256]{2,1,0:T(8,128)(2,1)} %refs_0_.3) | copy-start | bytes 786436
  3.3 22.7 %copy-start.6 = (f32[256,256]{1,0:T(8,128)S(1)}, f32[256,256]{1,0:T(8,128)}, u32[]{:S(2)}) copy-start(f32[256,256]{1,0:T(8,128)} %constant.8.clone.refs_3_) | copy-start | bytes 786436
  3.3 22.7 %copy-start.7 = (f32[256,256]{1,0:T(8,128)S(1)}, f32[256,256]{1,0:T(8,128)}, u32[]{:S(2)}) copy-start(f32[256,256]{1,0:T(8,128)} %constant.9.clone.refs_4_) | copy-start | bytes 786436
  3.3 14.0 %collective-permute-start = (f32[2,2,128,256]{3,2,1,0:T(8,128)S(1)}, f32[2,2,128,256]{3,2,1,0:T(8,128)S(1)}, u32[]{:S(2)}, u32[]{:S(2)}) collective-permute-start(f32[2,2,128,256]{3,2,1,0:T(8,128)S(1)} %get-tuple-element.71), channel_id=1, source_target_pairs={{0,16},{2,18},{4,20},{6,22},{8,24},{10,26},{12,28},{14,30},{16,32}... | collective-permute-start | bytes 1572872 | tf_op jit(solution)/shard_map/ppermute | solution.py:277
  9.9 17.8 %collective-permute-start.2 = (f32[2,2,256,128]{3,2,1,0:T(8,128)S(1)}, f32[2,2,256,128]{3,2,1,0:T(8,128)S(1)}, u32[]{:S(2)}, u32[]{:S(2)}) collective-permute-start(f32[2,2,256,128]{3,2,1,0:T(8,128)S(1)} %get-tuple-element.69), channel_id=1, source_target_pairs={{0,2},{2,4},{4,6},{6,8},{8,10},{10,12},{12,14},{16,18},{18,20},{20... | collective-permute-start | bytes 1572872 | tf_op jit(solution)/shard_map/ppermute | solution.py:283
  14.0 13.8 %collective-permute-start.3 = (f32[2,2,256,128]{3,2,1,0:T(8,128)S(1)}, f32[2,2,256,128]{3,2,1,0:T(8,128)S(1)}, u32[]{:S(2)}, u32[]{:S(2)}) collective-permute-start(f32[2,2,256,128]{3,2,1,0:T(8,128)S(1)} %get-tuple-element.68), channel_id=1, source_target_pairs={{2,0},{4,2},{6,4},{8,6},{10,8},{12,10},{14,12},{18,16},{20,18},{22... | collective-permute-start | bytes 1572872 | tf_op jit(solution)/shard_map/ppermute | solution.py:283
  17.3 12.5 %collective-permute-start.4 = (f32[2,2,2,128,128]{4,3,2,1,0:T(8,128)S(1)}, f32[2,2,2,128,128]{4,3,2,1,0:T(8,128)S(1)}, u32[]{:S(2)}, u32[]{:S(2)}) collective-permute-start(f32[2,2,2,128,128]{4,3,2,1,0:T(8,128)S(1)} %pad_maximum_fusion), channel_id=1, source_target_pairs={{0,2},{2,4},{4,6},{6,8},{8,10},{10,12},{12,14},{16,18},{18,20},{20... | collective-permute-start | bytes 1572872 | tf_op jit(solution)/shard_map/ppermute | solution.py:283
  23.8 10.7 %copy-start = (f32[1,2,2,256,256]{4,3,2,1,0:T(8,128)S(1)}, f32[1,2,2,256,256]{4,3,2,1,0:T(8,128)}, u32[]{:S(2)}) copy-start(f32[1,2,2,256,256]{4,3,2,1,0:T(8,128)} %param.10) | copy-start | bytes 3145732
  23.8 10.7 %copy-start.8 = (s32[1,2,2]{2,1,0:T(2,128)S(1)}, s32[1,2,2]{2,1,0:T(2,128)}, u32[]{:S(2)}) copy-start(s32[1,2,2]{2,1,0:T(2,128)} %param.13) | copy-start | bytes 52
  23.9 10.6 %collective-permute-start.5 = (f32[2,2,2,128,128]{4,3,2,1,0:T(8,128)S(1)}, f32[2,2,2,128,128]{4,3,2,1,0:T(8,128)S(1)}, u32[]{:S(2)}, u32[]{:S(2)}) collective-permute-start(f32[2,2,2,128,128]{4,3,2,1,0:T(8,128)S(1)} %pad_maximum_fusion.1), channel_id=1, source_target_pairs={{2,0},{4,2},{6,4},{8,6},{10,8},{12,10},{14,12},{18,16},{20,18},{22... | collective-permute-start | bytes 1572872 | tf_op jit(solution)/shard_map/ppermute | solution.py:283
  42.5 11.3 %collective-permute-start.6 = (f32[256,256]{1,0:T(8,128)S(1)}, f32[256,256]{1,0:T(8,128)S(1)}, u32[]{:S(2)}, u32[]{:S(2)}) collective-permute-start(f32[256,256]{1,0:T(8,128)S(1)} %get-tuple-element.36.refs_1_), channel_id=1, source_target_pairs={{0,1},{1,0},{2,3},{3,2},{4,5},{5,4},{6,7},{7,6},{8,9},{9,8},{10,11... | collective-permute-start | bytes 786440 | tf_op jit(solution)/shard_map/ppermute | solution.py:287
  53.0 7.2 %collective-permute-start.7 = (f32[256,256]{1,0:T(8,128)S(1)}, f32[256,256]{1,0:T(8,128)S(1)}, u32[]{:S(2)}, u32[]{:S(2)}) collective-permute-start(f32[256,256]{1,0:T(8,128)S(1)} %get-tuple-element.48.refs_3_), channel_id=1, source_target_pairs={{0,1},{1,0},{2,3},{3,2},{4,5},{5,4},{6,7},{7,6},{8,9},{9,8},{10,11... | collective-permute-start | bytes 786440 | tf_op jit(solution)/shard_map/ppermute | solution.py:287
  64.4 12.8 %collective-permute-start.9 = (f32[2,512,128]{2,1,0:T(8,128)S(1)}, f32[2,512,128]{2,1,0:T(8,128)S(1)}, u32[]{:S(2)}, u32[]{:S(2)}) collective-permute-start(f32[2,512,128]{2,1,0:T(8,128)S(1)} %get-tuple-element.57), channel_id=1, source_target_pairs={{2,0},{4,2},{6,4},{8,6},{10,8},{12,10},{14,12},{18,16},{20,18},{22... | collective-permute-start | bytes 1572872 | tf_op jit(solution)/shard_map/ppermute | solution.py:283
  66.3 11.3 %collective-permute-start.8 = (f32[2,512,128]{2,1,0:T(8,128)S(1)}, f32[2,512,128]{2,1,0:T(8,128)S(1)}, u32[]{:S(2)}, u32[]{:S(2)}) collective-permute-start(f32[2,512,128]{2,1,0:T(8,128)S(1)} %get-tuple-element.56), channel_id=1, source_target_pairs={{0,2},{2,4},{4,6},{6,8},{8,10},{10,12},{12,14},{16,18},{18,20},{20... | collective-permute-start | bytes 1572872 | tf_op jit(solution)/shard_map/ppermute | solution.py:283
  79.3 12.4 %collective-permute-start.11 = (f32[2,512,128]{2,1,0:T(8,128)S(1)}, f32[2,512,128]{2,1,0:T(8,128)S(1)}, u32[]{:S(2)}, u32[]{:S(2)}) collective-permute-start(f32[2,512,128]{2,1,0:T(8,128)S(1)} %get-tuple-element.60), channel_id=1, source_target_pairs={{2,0},{4,2},{6,4},{8,6},{10,8},{12,10},{14,12},{18,16},{20,18},{22... | collective-permute-start | bytes 1572872 | tf_op jit(solution)/shard_map/ppermute | solution.py:283
  81.2 10.5 %collective-permute-start.10 = (f32[2,512,128]{2,1,0:T(8,128)S(1)}, f32[2,512,128]{2,1,0:T(8,128)S(1)}, u32[]{:S(2)}, u32[]{:S(2)}) collective-permute-start(f32[2,512,128]{2,1,0:T(8,128)S(1)} %get-tuple-element.59), channel_id=1, source_target_pairs={{0,2},{2,4},{4,6},{6,8},{8,10},{10,12},{12,14},{16,18},{18,20},{20... | collective-permute-start | bytes 1572872 | tf_op jit(solution)/shard_map/ppermute | solution.py:283
  85.7 12.3 %collective-permute-start.16 = (f32[2,128,256]{2,1,0:T(8,128)S(1)}, f32[2,128,256]{2,1,0:T(8,128)S(1)}, u32[]{:S(2)}, u32[]{:S(2)}) collective-permute-start(f32[2,128,256]{2,1,0:T(8,128)S(1)} %get-tuple-element.67), channel_id=1, source_target_pairs={{16,0},{18,2},{20,4},{22,6},{24,8},{26,10},{28,12},{30,14},{32,16}... | collective-permute-start | bytes 786440 | tf_op jit(solution)/shard_map/ppermute | solution.py:277
  87.0 11.0 %collective-permute-start.15 = (f32[2,128,256]{2,1,0:T(8,128)S(1)}, f32[2,128,256]{2,1,0:T(8,128)S(1)}, u32[]{:S(2)}, u32[]{:S(2)}) collective-permute-start(f32[2,128,256]{2,1,0:T(8,128)S(1)} %get-tuple-element.66), channel_id=1, source_target_pairs={{0,16},{2,18},{4,20},{6,22},{8,24},{10,26},{12,28},{14,30},{16,32}... | collective-permute-start | bytes 786440 | tf_op jit(solution)/shard_map/ppermute | solution.py:277
  91.9 8.7 %collective-permute-start.13 = (f32[2,128,256]{2,1,0:T(8,128)S(1)}, f32[2,128,256]{2,1,0:T(8,128)S(1)}, u32[]{:S(2)}, u32[]{:S(2)}) collective-permute-start(f32[2,128,256]{2,1,0:T(8,128)S(1)} %get-tuple-element.65), channel_id=1, source_target_pairs={{16,0},{18,2},{20,4},{22,6},{24,8},{26,10},{28,12},{30,14},{32,16}... | collective-permute-start | bytes 786440 | tf_op jit(solution)/shard_map/ppermute | solution.py:277
  93.2 9.2 %collective-permute-start.12 = (f32[2,128,256]{2,1,0:T(8,128)S(1)}, f32[2,128,256]{2,1,0:T(8,128)S(1)}, u32[]{:S(2)}, u32[]{:S(2)}) collective-permute-start(f32[2,128,256]{2,1,0:T(8,128)S(1)} %get-tuple-element.64), channel_id=1, source_target_pairs={{0,16},{2,18},{4,20},{6,22},{8,24},{10,26},{12,28},{14,30},{16,32}... | collective-permute-start | bytes 786440 | tf_op jit(solution)/shard_map/ppermute | solution.py:277
  98.0 26.7 %collective-permute-start.17 = (f32[2,256,256]{2,1,0:T(8,128)S(1)}, f32[2,256,256]{2,1,0:T(8,128)S(1)}, u32[]{:S(2)}, u32[]{:S(2)}) collective-permute-start(f32[2,256,256]{2,1,0:T(8,128)S(1)} %slice_add_fusion), channel_id=1, source_target_pairs={{0,1},{1,0},{2,3},{3,2},{4,5},{5,4},{6,7},{7,6},{8,9},{9,8},{10,11... | collective-permute-start | bytes 1572872 | tf_op jit(solution)/shard_map/ppermute | solution.py:287
  102.5 31.9 %collective-permute-start.14 = (f32[2,256,256]{2,1,0:T(8,128)S(1)}, f32[2,256,256]{2,1,0:T(8,128)S(1)}, u32[]{:S(2)}, u32[]{:S(2)}) collective-permute-start(f32[2,256,256]{2,1,0:T(8,128)S(1)} %slice_add_fusion.1), channel_id=1, source_target_pairs={{0,1},{1,0},{2,3},{3,2},{4,5},{5,4},{6,7},{7,6},{8,9},{9,8},{10,11... | collective-permute-start | bytes 1572872 | tf_op jit(solution)/shard_map/ppermute | solution.py:287

commit v3 on v2

--- a/solution.py
+++ b/solution.py
@@ -11,6 +11,7 @@
 from jax.sharding import PartitionSpec as P
 
 GY = 8
+BAND = 16
 F32 = jnp.float32
 BF16 = jnp.bfloat16
 VMEM_LIMIT = 24 * 1024 * 1024
@@ -65,10 +66,28 @@
     return jnp.concatenate([a, b], axis=0)
 
 
-def sandwich(left, re, im, right):
+def band_left(re, im):
     n = re.shape[0]
-    half = mm(left, above(re.astype(BF16), im.astype(BF16)))
-    both = mm(beside(half[:n].astype(BF16), half[n:].astype(BF16)), right)
+    h, a, b = n // 2, n // 2 - BAND, n // 2 + BAND
+    diag = [left_form(re[r, r], im[r, r], jnp) for r in (slice(0, h), slice(h, n))]
+    row = lax.broadcasted_iota(jnp.int32, (2 * BAND, 2 * BAND), 0) < BAND
+    col = lax.broadcasted_iota(jnp.int32, (2 * BAND, 2 * BAND), 1) < BAND
+    corners = [jnp.where(row == col, 0.0, part[a:b, a:b]) for part in (re, im)]
+    return diag, left_form(*corners, jnp)
+
+
+def sandwich(diag, corner, re, im, right):
+    n = re.shape[0]
+    h, a, b = n // 2, n // 2 - BAND, n // 2 + BAND
+    re, im = re.astype(BF16), im.astype(BF16)
+    top = mm(diag[0], above(re[:h], im[:h]))
+    low = mm(diag[1], above(re[h:], im[h:]))
+    mid = mm(corner[...], above(re[a:b], im[a:b]))
+    re = [top[:a], top[a:h] + mid[:BAND], low[:BAND] + mid[BAND : 2 * BAND], low[BAND:h]]
+    mid, top, low = mid[2 * BAND :], top[h:], low[h:]
+    im = [top[:a], top[a:h] + mid[:BAND], low[:BAND] + mid[BAND:], low[BAND:]]
+    re, im = jnp.concatenate(re, axis=0), jnp.concatenate(im, axis=0)
+    both = mm(beside(re.astype(BF16), im.astype(BF16)), right[...])
     return both[:, :n], both[:, n:]
 
 
@@ -132,32 +151,25 @@
             patch[part, layer] = pltpu.roll(window, row_shift, 0)[:n]
 
 
-def place(off_ref, grads, out_l, out_c, out_r, canvas):
+def lay(off_ref, grads, canvas):
     n = grads[0].shape[-1]
     h = n // 2
     canvas[...] = jnp.zeros_like(canvas)
     for slot, grad in enumerate(grads):
         top, block, row_rest, col_rest = place_of(off_ref, slot, h)
-        for part in range(2):
+        for part in range(canvas.shape[0]):
             tall = above(grad[part], jnp.zeros((8, n), F32))
             tall = pltpu.roll(tall, row_rest, 0)
             wide = beside(tall, jnp.zeros((n + 8, h), F32))
             canvas[part, pl.ds(top, n + 8), pl.ds(block, n + h)] += pltpu.roll(wide, col_rest, 1)
-    out_l[...] = canvas[:, :, 0:h]
-    out_c[...] = canvas[:, :, h : h + n]
-    out_r[...] = canvas[:, :, h + n :]
 
 
 def each_mode(modes, step):
-    def pair(i, carry):
-        for j in range(2):
-            step(i * 2 + j)
-        return carry
-
-    lax.fori_loop(0, modes // 2, pair, 0)
-
-
-def forward(probe, patch, prop_l, prop_r, tabs, wave, far, inten):
+    for m in range(modes):
+        step(m)
+
+
+def forward(probe, patch, diag, corner, right, tabs, wave, far, inten):
     n = inten.shape[0]
     h = n // 2
     inten[...] = jnp.zeros_like(inten)
@@ -166,7 +178,7 @@
         p_re, p_im = probe[0, m], probe[1, m]
         o_re, o_im = patch[0, 0], patch[1, 0]
         w_re, w_im = sandwich(
-            prop_l[...], p_re * o_re - p_im * o_im, p_re * o_im + p_im * o_re, prop_r[...]
+            diag, corner, p_re * o_re - p_im * o_im, p_re * o_im + p_im * o_re, right
         )
         wave[m, 0] = w_re
         wave[m, 1] = w_im
@@ -180,16 +192,17 @@
     each_mode(probe.shape[1], step)
 
 
-def forward_first_kernel(off, own, up, down, left, right, corner_l, corner_r, probe, prop_l,
-                         prop_r, tabs, canvas, patch, wave, far, inten):
+def forward_first_kernel(off, own, up, down, left, right, corner_l, corner_r, probe, diag,
+                         corner, mat, tabs, canvas, patch, wave, far, inten):
     build_canvas(own, up, down, left, right, corner_l, corner_r, canvas)
     extract(off, 0, canvas, patch)
-    forward(probe, patch, prop_l, prop_r, tabs, wave, far, inten)
-
-
-def forward_next_kernel(slot, off, canvas, probe, prop_l, prop_r, tabs, patch, wave, far, inten):
+    forward(probe, patch, diag, corner, mat, tabs, wave, far, inten)
+
+
+def forward_next_kernel(slot, off, canvas, probe, diag, corner, mat, tabs, patch, wave, far,
+                        inten):
     extract(off, slot, canvas, patch)
-    forward(probe, patch, prop_l, prop_r, tabs, wave, far, inten)
+    forward(probe, patch, diag, corner, mat, tabs, wave, far, inten)
 
 
 def back_last(slot, counts, mine, other, measured, far, wave, patch, tabs, grad, bar, resid):
@@ -216,14 +229,19 @@
 def back_last_place_kernel(slot, counts, off, before, mine, other, measured, far, wave, patch,
                            tabs, bar, out_l, out_c, out_r, resid, grad, canvas):
     back_last(slot, counts, mine, other, measured, far, wave, patch, tabs, grad, bar, resid)
-    place(off, (before, grad), out_l, out_c, out_r, canvas)
-
-
-def back_first(bar, probe, patch, prop_l, prop_r, grad, emit):
+    lay(off, (before, grad), canvas)
+    n = grad.shape[-1]
+    h = n // 2
+    out_l[...] = canvas[:, :, 0:h]
+    out_c[...] = canvas[:, :, h : h + n]
+    out_r[...] = canvas[:, :, h + n :]
+
+
+def back_first(bar, probe, patch, diag, corner, mat, grad, emit):
     grad[...] = jnp.zeros_like(grad)
 
     def step(m):
-        b_re, b_im = sandwich(prop_l[...], bar[m, 0], bar[m, 1], prop_r[...])
+        b_re, b_im = sandwich(diag, corner, bar[m, 0], bar[m, 1], mat)
         p_re, p_im = probe[0, m], probe[1, m]
         grad[0] += p_re * b_re + p_im * b_im
         grad[1] += p_re * b_im - p_im * b_re
@@ -233,34 +251,65 @@
     each_mode(probe.shape[1], step)
 
 
-def back_first_kernel(bar, probe, patch, prop_l, prop_r, grad, part):
+def back_first_kernel(bar, probe, patch, diag, corner, mat, grad, part):
     def emit(m, re, im):
         part[0, m] = re
         part[1, m] = im
 
-    back_first(bar, probe, patch, prop_l, prop_r, grad, emit)
-
-
-def back_first_add_kernel(bar, probe, patch, prop_l, prop_r, part, grad, total):
+    back_first(bar, probe, patch, diag, corner, mat, grad, emit)
+
+
+def back_first_add_kernel(bar, probe, patch, diag, corner, mat, part, grad, total):
     def emit(m, re, im):
         total[0, 0, m] = part[0, m] + re
         total[0, 1, m] = part[1, m] + im
 
-    back_first(bar, probe, patch, prop_l, prop_r, grad, emit)
-
-
-def place_kernel(off, grad0, grad1, out_l, out_c, out_r, canvas):
-    place(off, (grad0, grad1), out_l, out_c, out_r, canvas)
-
-
-def prepare_kernel(prop, probe, measured, order, order_t, dft_in, conj_in, prop_l, prop_r,
-                   back_l, back_r, probe_out, meas_out, dft_out, conj_out):
+    back_first(bar, probe, patch, diag, corner, mat, grad, emit)
+
+
+def place_sides_kernel(off, grad0, grad1, out_l, out_r, canvas):
+    lay(off, (grad0, grad1), canvas)
+    h = grad0.shape[-1] // 2
+    out_l[...] = canvas[:, :, 0:h]
+    out_r[...] = canvas[:, :, 3 * h :]
+
+
+def place_center_kernel(off, grad0, grad1, out_c, canvas):
+    lay(off, (grad0, grad1), canvas)
+    h = grad0.shape[-1] // 2
+    out_c[...] = canvas[:, :, h : 3 * h]
+
+
+def fold_cols_kernel(center, from_left, from_right, top, mid, low):
+    n = center.shape[-1]
+    h = n // 2
+    for out, rows in ((top, slice(0, h)), (mid, slice(h, h + n)), (low, slice(h + n, 2 * n))):
+        out[:, :, :h] = center[:, rows, :h] + from_left[:, rows]
+        out[:, :, h:] = center[:, rows, h:] + from_right[:, rows]
+
+
+def fold_rows_kernel(mid, from_up, from_down, out):
+    h = from_up.shape[1]
+    out[:, :h] = mid[:, :h] + from_up[...]
+    out[:, h:] = mid[:, h:] + from_down[...]
+
+
+def finish_kernel(mine_first, other_first, mine_last, other_last, out):
+    out[0, :, 0] = mine_first[...] + other_first[...]
+    out[0, :, 1] = mine_last[...] + other_last[...]
+
+
+def prepare_kernel(prop, probe, measured, order, order_t, dft_in, conj_in, diag, corner, right,
+                   back_diag, back_corner, back_right, probe_out, meas_out, dft_out, conj_out):
     re, im = prop[0].astype(F32), prop[1].astype(F32)
     re_t, im_t = re.T, im.T
-    prop_l[...] = left_form(re, im, jnp).astype(BF16)
-    prop_r[...] = right_form(re_t, im_t, jnp).astype(BF16)
-    back_l[...] = left_form(re_t, -im_t, jnp).astype(BF16)
-    back_r[...] = right_form(re, -im, jnp).astype(BF16)
+    for out, edge, pair in ((diag, corner, (re, im)), (back_diag, back_corner, (re_t, -im_t))):
+        blocks, corners = band_left(*pair)
+        out[0] = blocks[0].astype(BF16)
+        out[1] = blocks[1].astype(BF16)
+        edge[...] = corners.astype(BF16)
+    right[...] = right_form(re_t, im_t, jnp).astype(BF16)
+    back_right[...] = right_form(re, -im, jnp).astype(BF16)
     probe_out[...] = probe[...]
     dft_out[...] = dft_in[...]
     conj_out[...] = conj_in[...]
@@ -328,28 +377,30 @@
     plane, pair, mat = ((n, n), F32), ((2, n, n), F32), ((2 * n, 2 * n), BF16)
     patch_out, field = ((2, 2, n, n), F32), ((modes, 2, n, n), F32)
     probes, tables = ((2, modes, n, n), F32), (dft.shape, BF16)
-    prop_l, prop_r, back_prop_l, back_prop_r, probe, measured, dft, conj_dft = call(
+    band = (((2, n, n), BF16), ((4 * BAND, 4 * BAND), BF16), mat)
+    *made, probe, measured, dft, conj_dft = call(
         prepare_kernel,
         "prepare",
-        (mat, mat, mat, mat, probes, ((slots, n, n), F32), tables, tables),
+        band + band + (probes, ((slots, n, n), F32), tables, tables),
         (propagator, probe_modes, measured[0], jnp.asarray(order), jnp.asarray(order.T.copy()),
          jnp.asarray(dft), jnp.asarray(conj_dft)),
         smem=0,
     )
+    prop, back_prop = made[:3], made[3:]
 
     canvas, patch0, wave0, far0, inten0 = call(
         forward_first_kernel,
         "forward_0",
         (((2, 2, 2 * n, 2 * n), F32), patch_out, field, field, plane),
         (off, own, up_strip, down_strip, left_strip, right_strip, corner_l, corner_r,
-         probe, prop_l, prop_r, dft),
+         probe, *prop, dft),
     )
     other0 = swap_mode(inten0)
     patch1, wave1, far1, inten1 = call(
         functools.partial(forward_next_kernel, 1),
         "forward_1",
         (patch_out, field, field, plane),
-        (off, canvas, probe, prop_l, prop_r, dft),
+        (off, canvas, probe, *prop, dft),
     )
     other1 = swap_mode(inten1)
 
@@ -367,7 +418,7 @@
         back_first_kernel,
         "back_first_0",
         (pair, probes),
-        (bar0, probe, patch0, back_prop_l, back_prop_r),
+        (bar0, probe, patch0, *back_prop),
         smem=0,
     )
     bar1, out_l, out_c, out_r = call(
@@ -380,38 +431,57 @@
         after=(grad_first0,),
     )
 
-    def add_cols(out_l, out_c, out_r):
+    half = ((2, h, n), F32)
+
+    def fold_cols(name, out_l, out_c, out_r, after):
         from_left = cols_by(out_r, 1)
         from_right = cols_by(out_l, -1)
-        return out_c + jnp.concatenate([from_left, from_right], axis=2)
-
-    def add_rows(tall):
-        from_up = rows_by(tall[:, n + h :, :], 1)
-        from_down = rows_by(tall[:, :h, :], -1)
-        return tall[:, h : h + n, :] + jnp.concatenate([from_up, from_down], axis=1)
-
-    tall_last = add_cols(out_l, out_c, out_r)
+        return call(fold_cols_kernel, name, (half, pair, half), (out_c, from_left, from_right),
+                    smem=0, after=after)
+
+    def fold_rows(name, top, mid, low, after):
+        from_up = rows_by(low, 1)
+        from_down = rows_by(top, -1)
+        return call(fold_rows_kernel, name, (pair,), (mid, from_up, from_down), smem=0,
+                    after=after)[0]
+
     grad_first1, probe_grad = call(
         back_first_add_kernel,
         "back_first_1",
         (pair, ((1, 2, modes, n, n), F32)),
-        (bar1, probe, patch1, back_prop_l, back_prop_r, part),
+        (bar1, probe, patch1, *back_prop, part),
         smem=0,
     )
-    mine_last = add_rows(tall_last)
+    strips_last = fold_cols("cols_last", out_l, out_c, out_r, (grad_first1,))
+    mine_last = fold_rows("rows_last", *strips_last, ())
     other_last = swap_mode(mine_last)
-    out_l, out_c, out_r = call(
-        place_kernel,
-        "place_first",
-        strips,
+    out_l, out_r = call(
+        place_sides_kernel,
+        "place_sides",
+        (strips[0], strips[2]),
         (off, grad_first0, grad_first1),
         scratch=(wide,),
-        after=(tall_last,),
-    )
-    mine_first = add_rows(add_cols(out_l, out_c, out_r))
+        after=(strips_last[0],),
+    )
+    (out_c,) = call(
+        place_center_kernel,
+        "place_center",
+        (strips[1],),
+        (off, grad_first0, grad_first1),
+        scratch=(wide,),
+        after=(out_l,),
+    )
+    strips_first = fold_cols("cols_first", out_l, out_c, out_r, ())
+    mine_first = fold_rows("rows_first", *strips_first, (other_last,))
     other_first = swap_mode(mine_first)
-    object_grad = jnp.stack([mine_first + other_first, mine_last + other_last], axis=1)
-    return (object_grad.reshape(object_tiles.shape), probe_grad)
+    (object_grad,) = call(
+        finish_kernel,
+        "finish",
+        ((object_tiles.shape, F32),),
+        (mine_first, other_first, mine_last, other_last),
+        smem=0,
+    )
+    return (object_grad, probe_grad)
 
 
 def solution(mesh):

time: 137 us -> 133 us (0.971)
  the two profiles are of different devices: /device:TPU:1 before, /device:TPU:11 now
where the time goes in v3:
time: 133 us; the launch traced here: 132 us
  starting transfers between devices  50.1 us (38%)
  waiting for transfers between devices  46.5 us (35%)
  Pallas kernels  31.3 us (24%)
  local copies, waits for them, and re-layouts  2.68 us (2%)
  between operations  1.66 us (1%)
    pallas_call x14, Pallas kernels, call(): pl.pallas_call(run, out_shape=tuple((jax.ShapeDtypeStruct(shape, dtype) f...  31.3 us
    ppermute x8, starting transfers between devices, cols_by(): return lax.ppermute(value, 'tile', pairs)  22.6 us
    ppermute x6, starting transfers between devices, rows_by(): return lax.ppermute(value, 'tile', pairs)  22.4 us
    ppermute x4, waiting for transfers between devices, swap_mode(): return lax.ppermute(value, 'mode', [(0, 1), (1, 0)])  19.1 us
    ppermute x8, waiting for transfers between devices, cols_by(): return lax.ppermute(value, 'tile', pairs)  14.3 us
    ppermute x6, waiting for transfers between devices, rows_by(): return lax.ppermute(value, 'tile', pairs)  13.2 us
    ppermute x4, starting transfers between devices, swap_mode(): return lax.ppermute(value, 'mode', [(0, 1), (1, 0)])  5.17 us
  transfers between devices with their start and end apart: 18, of which 12 were waited for; matrix products, arithmetic and copies ran while one was open for 1% of the time, Pallas kernels for 15%

profile of v3, /device:TPU:11, one launch (start us, length us, event | category | flops | bytes accessed | tf_op | source)
XLA Modules:
  0.0 132.3 jit_solution(8481869400304383179)
XLA Ops:
  1.9 7.4 %collective-permute-start.1 = (f32[2,2,128,256]{3,2,1,0:T(8,128)S(1)}, f32[2,2,128,256]{3,2,1,0:T(8,128)S(1)}, u32[]{:S(2)}, u32[]{:S(2)}) collective-permute-start(f32[2,2,128,256]{3,2,1,0:T(8,128)S(1)} %get-tuple-element.78), channel_id=1, source_target_pairs={{16,0},{18,2},{20,4},{22,6},{24,8},{26,10},{28,12},{30,14},{32,16}... | collective-permute-start | bytes 1572872 | tf_op jit(solution)/shard_map/ppermute | solution.py:326
  9.4 2.3 %collective-permute-start = (f32[2,2,128,256]{3,2,1,0:T(8,128)S(1)}, f32[2,2,128,256]{3,2,1,0:T(8,128)S(1)}, u32[]{:S(2)}, u32[]{:S(2)}) collective-permute-start(f32[2,2,128,256]{3,2,1,0:T(8,128)S(1)} %get-tuple-element.79), channel_id=1, source_target_pairs={{0,16},{2,18},{4,20},{6,22},{8,24},{10,26},{12,28},{14,30},{16,32}... | collective-permute-start | bytes 1572872 | tf_op jit(solution)/shard_map/ppermute | solution.py:326
  13.0 2.9 %collective-permute-start.3 = (f32[2,2,256,128]{3,2,1,0:T(8,128)S(1)}, f32[2,2,256,128]{3,2,1,0:T(8,128)S(1)}, u32[]{:S(2)}, u32[]{:S(2)}) collective-permute-start(f32[2,2,256,128]{3,2,1,0:T(8,128)S(1)} %get-tuple-element.76), channel_id=1, source_target_pairs={{2,0},{4,2},{6,4},{8,6},{10,8},{12,10},{14,12},{18,16},{20,18},{22... | collective-permute-start | bytes 1572872 | tf_op jit(solution)/shard_map/ppermute | solution.py:332
  15.9 3.0 %collective-permute-start.2 = (f32[2,2,256,128]{3,2,1,0:T(8,128)S(1)}, f32[2,2,256,128]{3,2,1,0:T(8,128)S(1)}, u32[]{:S(2)}, u32[]{:S(2)}) collective-permute-start(f32[2,2,256,128]{3,2,1,0:T(8,128)S(1)} %get-tuple-element.77), channel_id=1, source_target_pairs={{0,2},{2,4},{4,6},{6,8},{8,10},{10,12},{12,14},{16,18},{18,20},{20... | collective-permute-start | bytes 1572872 | tf_op jit(solution)/shard_map/ppermute | solution.py:332
  19.9 6.2 %collective-permute-done.refs_2_ = f32[2,2,128,256]{3,2,1,0:T(8,128)S(1)} collective-permute-done((f32[2,2,128,256]{3,2,1,0:T(8,128)S(1)}, f32[2,2,128,256]{3,2,1,0:T(8,128)S(1)}, u32[]{:S(2)}, u32[]{:S(2)}) %collective-permute-start) | collective-permute-done | bytes 524320 | tf_op jit(solution)/shard_map/ppermute | solution.py:326
  26.2 4.9 %collective-permute-start.4 = (f32[2,2,2,128,128]{4,3,2,1,0:T(8,128)S(1)}, f32[2,2,2,128,128]{4,3,2,1,0:T(8,128)S(1)}, u32[]{:S(2)}, u32[]{:S(2)}) collective-permute-start(f32[2,2,2,128,128]{4,3,2,1,0:T(8,128)S(1)} %pad_maximum_fusion), channel_id=1, source_target_pairs={{0,2},{2,4},{4,6},{6,8},{8,10},{10,12},{12,14},{16,18},{18,20},{20... | collective-permute-start | bytes 1572872 | tf_op jit(solution)/shard_map/ppermute | solution.py:332
  31.2 2.1 %collective-permute-start.5 = (f32[2,2,2,128,128]{4,3,2,1,0:T(8,128)S(1)}, f32[2,2,2,128,128]{4,3,2,1,0:T(8,128)S(1)}, u32[]{:S(2)}, u32[]{:S(2)}) collective-permute-start(f32[2,2,2,128,128]{4,3,2,1,0:T(8,128)S(1)} %pad_maximum_fusion.1), channel_id=1, source_target_pairs={{2,0},{4,2},{6,4},{8,6},{10,8},{12,10},{14,12},{18,16},{20,18},{22... | collective-permute-start | bytes 1572872 | tf_op jit(solution)/shard_map/ppermute | solution.py:332
  33.3 1.7 %prepare.1 = (bf16[2,256,256]{2,1,0:T(8,128)(2,1)S(1)}, bf16[64,64]{1,0:T(8,128)(2,1)S(1)}, bf16[512,512]{1,0:T(8,128)(2,1)S(1)}, bf16[2,256,256]{2,1,0:T(8,128)...) custom-call(bf16[2,256,256]{2,1,0:T(8,128)(2,1)S(1)} %copy-done.5, ...), custom_call_target="tpu_custom_call" | custom-call | tf_op jit(solution)/shard_map/prepare/pallas_call | solution.py:347
  35.0 2.2 %collective-permute-done.4.refs_6_ = f32[2,2,2,128,128]{4,3,2,1,0:T(8,128)S(1)} collective-permute-done((f32[2,2,2,128,128]{4,3,2,1,0:T(8,128)S(1)}, f32[2,2,2,128,128]{4,3,2,1,0:T(8,128)S(1)}, u32[]{:S(2)}, u32[]{:S(2)}) %collective-permute-start.4) | collective-permute-done | bytes 524320 | tf_op jit(solution)/shard_map/ppermute | solution.py:332
  37.2 4.6 %collective-permute-done.5.refs_7_ = f32[2,2,2,128,128]{4,3,2,1,0:T(8,128)S(1)} collective-permute-done((f32[2,2,2,128,128]{4,3,2,1,0:T(8,128)S(1)}, f32[2,2,2,128,128]{4,3,2,1,0:T(8,128)S(1)}, u32[]{:S(2)}, u32[]{:S(2)}) %collective-permute-start.5) | collective-permute-done | bytes 524320 | tf_op jit(solution)/shard_map/ppermute | solution.py:332
  41.8 6.4 %forward_0.1 = (f32[2,2,512,512]{3,2,1,0:T(8,128)S(1)}, f32[2,2,256,256]{3,2,1,0:T(8,128)S(1)}, f32[6,2,256,256]{3,2,1,0:T(8,128)S(1)}, f32[6,2,256,256]{3,2,1,0:T(8,128)S(1)}, f32[256,256]{1,0:T(8,128)S(1)}) custom-call(s32[2,2]{1,0:T(2,128)S(1)} %bitcast.15, f32[2,2,256,256]{3,2,1,0:T(8,128)S(1)} %bitcast.13, ...), custom_call_target="tpu_custom_call" | custom-call | tf_op jit(solution)/shard_map/forward_0/pallas_call | solution.py:347
  48.2 2.4 %collective-permute-start.6 = (f32[256,256]{1,0:T(8,128)S(1)}, f32[256,256]{1,0:T(8,128)S(1)}, u32[]{:S(2)}, u32[]{:S(2)}) collective-permute-start(f32[256,256]{1,0:T(8,128)S(1)} %get-tuple-element.44.refs_1_), channel_id=1, source_target_pairs={{0,1},{1,0},{2,3},{3,2},{4,5},{5,4},{6,7},{7,6},{8,9},{9,8},{10,11... | collective-permute-start | bytes 786440 | tf_op jit(solution)/shard_map/ppermute | solution.py:336
  50.6 6.0 %forward_1.1 = (f32[2,2,256,256]{3,2,1,0:T(8,128)S(1)}, f32[6,2,256,256]{3,2,1,0:T(8,128)S(1)}, f32[6,2,256,256]{3,2,1,0:T(8,128)S(1)}, f32[256,256]{1,0:T(8,128)S(1)}) custom-call(s32[2,2]{1,0:T(2,128)S(1)} %bitcast.16, f32[2,2,512,512]{3,2,1,0:T(8,128)S(1)} %get-tuple-element.56.refs_1_, f32[2,6,256,256]{3,2,1,0:T(8,128)S(1)} %get-tuple-element.39.refs_8_.refs_1_.refs_2_, ...), custom_call_target="tpu_custom_call" | custom-call | tf_op jit(solution)/shard_map/forward_1/pallas_call | solution.py:347
  58.2 2.3 %back_last_0.1 = (f32[2,256,256]{2,1,0:T(8,128)S(1)}, bf16[6,2,256,256]{3,2,1,0:T(8,128)(2,1)S(1)}) custom-call(s32[1]{0:T(128)S(6)} %copy.12.refs_0_, f32[256,256]{1,0:T(8,128)S(1)} %get-tuple-element.44.refs_1_, f32[256,256]{1,0:T(8,128)S(1)} %collective-permute-done.6.refs_2_, f32[2,256,256]{2,1,0:T(8,128)S(1)} %get-tuple-element.45.refs_3_.refs_5_, ...), custom_call_target="tpu_custom_call" | custom-call | tf_op jit(solution)/shard_map/back_last_0/pallas_call | solution.py:347
  60.5 2.6 %back_first_0.1 = (f32[2,256,256]{2,1,0:T(8,128)S(1)}, f32[2,6,256,256]{3,2,1,0:T(8,128)S(1)}) custom-call(bf16[6,2,256,256]{3,2,1,0:T(8,128)(2,1)S(1)} %get-tuple-element.50.refs_0_, f32[2,6,256,256]{3,2,1,0:T(8,128)S(1)} %get-tuple-element.39.refs_8_.refs_1_.refs_2_, f32[2,2,256,256]{3,2,1,0:T(8,128)S(1)} %get-tuple-element.48.refs_6_.refs_2_, ...), custom_call_target="tpu_custom_call" | custom-call | tf_op jit(solution)/shard_map/back_first_0/pallas_call | solution.py:347
  63.1 2.7 %collective-permute-done.7.refs_4_ = f32[256,256]{1,0:T(8,128)S(1)} collective-permute-done((f32[256,256]{1,0:T(8,128)S(1)}, f32[256,256]{1,0:T(8,128)S(1)}, u32[]{:S(2)}, u32[]{:S(2)}) %collective-permute-start.7) | collective-permute-done | bytes 262176 | tf_op jit(solution)/shard_map/ppermute | solution.py:336
  65.9 3.8 %back_last_1.1 = (bf16[6,2,256,256]{3,2,1,0:T(8,128)(2,1)S(1)}, f32[2,512,128]{2,1,0:T(8,128)S(1)}, f32[2,512,256]{2,1,0:T(8,128)S(1)}, f32[2,512,128]{2,1,0:T(8,128)S(1)}) custom-call(s32[1]{0:T(128)S(6)} %copy.12.refs_0_, s32[2,2]{1,0:T(2,128)S(1)} %bitcast.17, f32[2,256,256]{2,1,0:T(8,128)S(1)} %get-tuple-element.55.refs_2_, ...), custom_call_target="tpu_custom_call" | custom-call | tf_op jit(solution)/shard_map/back_last_1/pallas_call | solution.py:347
  69.6 3.5 %collective-permute-start.8 = (f32[2,512,128]{2,1,0:T(8,128)S(1)}, f32[2,512,128]{2,1,0:T(8,128)S(1)}, u32[]{:S(2)}, u32[]{:S(2)}) collective-permute-start(f32[2,512,128]{2,1,0:T(8,128)S(1)} %get-tuple-element.65), channel_id=1, source_target_pairs={{0,2},{2,4},{4,6},{6,8},{8,10},{10,12},{12,14},{16,18},{18,20},{20... | collective-permute-start | bytes 1572872 | tf_op jit(solution)/shard_map/ppermute | solution.py:332
  73.2 1.9 %collective-permute-start.9 = (f32[2,512,128]{2,1,0:T(8,128)S(1)}, f32[2,512,128]{2,1,0:T(8,128)S(1)}, u32[]{:S(2)}, u32[]{:S(2)}) collective-permute-start(f32[2,512,128]{2,1,0:T(8,128)S(1)} %get-tuple-element.66), channel_id=1, source_target_pairs={{2,0},{4,2},{6,4},{8,6},{10,8},{12,10},{14,12},{18,16},{20,18},{22... | collective-permute-start | bytes 1572872 | tf_op jit(solution)/shard_map/ppermute | solution.py:332
  75.1 4.3 %back_first_1.1 = (f32[2,256,256]{2,1,0:T(8,128)S(1)}, f32[1,2,6,256,256]{4,3,2,1,0:T(8,128)}) custom-call(bf16[6,2,256,256]{3,2,1,0:T(8,128)(2,1)S(1)} %get-tuple-element.61.refs_0_, f32[2,6,256,256]{3,2,1,0:T(8,128)S(1)} %get-tuple-element.39.refs_8_.refs_1_.refs_2_, f32[2,2,256,256]{3,2,1,0:T(8,128)S(1)} %get-tuple-element.60.refs_8_.refs_2_, ...), custom_call_target="tpu_custom_call" | custom-call | tf_op jit(solution)/shard_map/back_first_1/pallas_call | solution.py:347
  79.4 4.3 %collective-permute-done.9.refs_2_ = f32[2,512,128]{2,1,0:T(8,128)S(1)} collective-permute-done((f32[2,512,128]{2,1,0:T(8,128)S(1)}, f32[2,512,128]{2,1,0:T(8,128)S(1)}, u32[]{:S(2)}, u32[]{:S(2)}) %collective-permute-start.9) | collective-permute-done | bytes 524320 | tf_op jit(solution)/shard_map/ppermute | solution.py:332
  83.8 1.9 %collective-permute-start.15 = (f32[2,128,256]{2,1,0:T(8,128)S(1)}, f32[2,128,256]{2,1,0:T(8,128)S(1)}, u32[]{:S(2)}, u32[]{:S(2)}) collective-permute-start(f32[2,128,256]{2,1,0:T(8,128)S(1)} %get-tuple-element.67.refs_3_), channel_id=1, source_target_pairs={{16,0},{18,2},{20,4},{22,6},{24,8},{26,10},{28,12},{30,14},{32,16}... | collective-permute-start | bytes 786440 | tf_op jit(solution)/shard_map/ppermute | solution.py:326
  87.1 3.4 %collective-permute-start.14 = (f32[2,128,256]{2,1,0:T(8,128)S(1)}, f32[2,128,256]{2,1,0:T(8,128)S(1)}, u32[]{:S(2)}, u32[]{:S(2)}) collective-permute-start(f32[2,128,256]{2,1,0:T(8,128)S(1)} %get-tuple-element.74), channel_id=1, source_target_pairs={{0,16},{2,18},{4,20},{6,22},{8,24},{10,26},{12,28},{14,30},{16,32}... | collective-permute-start | bytes 786440 | tf_op jit(solution)/shard_map/ppermute | solution.py:326
  90.5 2.3 %collective-permute-start.10 = (f32[2,512,128]{2,1,0:T(8,128)S(1)}, f32[2,512,128]{2,1,0:T(8,128)S(1)}, u32[]{:S(2)}, u32[]{:S(2)}) collective-permute-start(f32[2,512,128]{2,1,0:T(8,128)S(1)} %get-tuple-element.69), channel_id=1, source_target_pairs={{0,2},{2,4},{4,6},{6,8},{8,10},{10,12},{12,14},{16,18},{18,20},{20... | collective-permute-start | bytes 1572872 | tf_op jit(solution)/shard_map/ppermute | solution.py:332
  92.8 2.0 %collective-permute-start.11 = (f32[2,512,128]{2,1,0:T(8,128)S(1)}, f32[2,512,128]{2,1,0:T(8,128)S(1)}, u32[]{:S(2)}, u32[]{:S(2)}) collective-permute-start(f32[2,512,128]{2,1,0:T(8,128)S(1)} %get-tuple-element.68.refs_3_), channel_id=1, source_target_pairs={{2,0},{4,2},{6,4},{8,6},{10,8},{12,10},{14,12},{18,16},{20,18},{22... | collective-permute-start | bytes 1572872 | tf_op jit(solution)/shard_map/ppermute | solution.py:332
  94.8 3.5 %collective-permute-done.14.refs_1_ = f32[2,128,256]{2,1,0:T(8,128)S(1)} collective-permute-done((f32[2,128,256]{2,1,0:T(8,128)S(1)}, f32[2,128,256]{2,1,0:T(8,128)S(1)}, u32[]{:S(2)}, u32[]{:S(2)}) %collective-permute-start.14) | collective-permute-done | bytes 262176 | tf_op jit(solution)/shard_map/ppermute | solution.py:326
  100.4 3.2 %collective-permute-done.11.refs_2_ = f32[2,512,128]{2,1,0:T(8,128)S(1)} collective-permute-done((f32[2,512,128]{2,1,0:T(8,128)S(1)}, f32[2,512,128]{2,1,0:T(8,128)S(1)}, u32[]{:S(2)}, u32[]{:S(2)}) %collective-permute-start.11) | collective-permute-done | bytes 524320 | tf_op jit(solution)/shard_map/ppermute | solution.py:332
  103.7 1.9 %collective-permute-start.12 = (f32[2,128,256]{2,1,0:T(8,128)S(1)}, f32[2,128,256]{2,1,0:T(8,128)S(1)}, u32[]{:S(2)}, u32[]{:S(2)}) collective-permute-start(f32[2,128,256]{2,1,0:T(8,128)S(1)} %get-tuple-element.71), channel_id=1, source_target_pairs={{0,16},{2,18},{4,20},{6,22},{8,24},{10,26},{12,28},{14,30},{16,32}... | collective-permute-start | bytes 786440 | tf_op jit(solution)/shard_map/ppermute | solution.py:326
  105.6 5.5 %collective-permute-start.13 = (f32[2,128,256]{2,1,0:T(8,128)S(1)}, f32[2,128,256]{2,1,0:T(8,128)S(1)}, u32[]{:S(2)}, u32[]{:S(2)}) collective-permute-start(f32[2,128,256]{2,1,0:T(8,128)S(1)} %get-tuple-element.72), channel_id=1, source_target_pairs={{16,0},{18,2},{20,4},{22,6},{24,8},{26,10},{28,12},{30,14},{32,16}... | collective-permute-start | bytes 786440 | tf_op jit(solution)/shard_map/ppermute | solution.py:326
  111.1 2.6 %collective-permute-done.16.refs_3_ = f32[2,256,256]{2,1,0:T(8,128)S(1)} collective-permute-done((f32[2,256,256]{2,1,0:T(8,128)S(1)}, f32[2,256,256]{2,1,0:T(8,128)S(1)}, u32[]{:S(2)}, u32[]{:S(2)}) %collective-permute-start.16) | collective-permute-done | bytes 524320 | tf_op jit(solution)/shard_map/ppermute | solution.py:336
  114.5 1.7 %collective-permute-done.13.refs_2_ = f32[2,128,256]{2,1,0:T(8,128)S(1)} collective-permute-done((f32[2,128,256]{2,1,0:T(8,128)S(1)}, f32[2,128,256]{2,1,0:T(8,128)S(1)}, u32[]{:S(2)}, u32[]{:S(2)}) %collective-permute-start.13) | collective-permute-done | bytes 262176 | tf_op jit(solution)/shard_map/ppermute | solution.py:326
  117.4 13.8 %collective-permute-done.17.refs_1_ = f32[2,256,256]{2,1,0:T(8,128)S(1)} collective-permute-done((f32[2,256,256]{2,1,0:T(8,128)S(1)}, f32[2,256,256]{2,1,0:T(8,128)S(1)}, u32[]{:S(2)}, u32[]{:S(2)}) %collective-permute-start.17) | collective-permute-done | bytes 524320 | tf_op jit(solution)/shard_map/ppermute | solution.py:336
  (42 shorter events, 11.4 us)
Async XLA Ops:
  1.9 17.9 %collective-permute-start.1 = (f32[2,2,128,256]{3,2,1,0:T(8,128)S(1)}, f32[2,2,128,256]{3,2,1,0:T(8,128)S(1)}, u32[]{:S(2)}, u32[]{:S(2)}) collective-permute-start(f32[2,2,128,256]{3,2,1,0:T(8,128)S(1)} %get-tuple-element.78), channel_id=1, source_target_pairs={{16,0},{18,2},{20,4},{22,6},{24,8},{26,10},{28,12},{30,14},{32,16}... | collective-permute-start | bytes 1572872 | tf_op jit(solution)/shard_map/ppermute | solution.py:326
  9.3 23.9 %copy-start.1 = (f32[2,6,256,256]{3,2,1,0:T(8,128)S(1)}, f32[2,6,256,256]{3,2,1,0:T(8,128)}, u32[]{:S(2)}) copy-start(f32[2,6,256,256]{3,2,1,0:T(8,128)} %refs_1_.1) | copy-start | bytes 9437188
  9.3 23.9 %copy-start.2 = (f32[1,2,256,256]{3,2,1,0:T(8,128)S(1)}, f32[1,2,256,256]{3,2,1,0:T(8,128)}, u32[]{:S(2)}) copy-start(f32[1,2,256,256]{3,2,1,0:T(8,128)} %param.15) | copy-start | bytes 1572868
  9.3 23.9 %copy-start.3 = (bf16[4,256,256]{2,1,0:T(8,128)(2,1)S(1)}, bf16[4,256,256]{2,1,0:T(8,128)(2,1)}, u32[]{:S(2)}) copy-start(bf16[4,256,256]{2,1,0:T(8,128)(2,1)} %constant.11.clone.refs_6_) | copy-start | bytes 1572868
  9.3 23.9 %copy-start.4 = (bf16[4,256,256]{2,1,0:T(8,128)(2,1)S(1)}, bf16[4,256,256]{2,1,0:T(8,128)(2,1)}, u32[]{:S(2)}) copy-start(bf16[4,256,256]{2,1,0:T(8,128)(2,1)} %constant.10.clone.refs_5_) | copy-start | bytes 1572868
  9.3 23.9 %copy-start.5 = (bf16[2,256,256]{2,1,0:T(8,128)(2,1)S(1)}, bf16[2,256,256]{2,1,0:T(8,128)(2,1)}, u32[]{:S(2)}) copy-start(bf16[2,256,256]{2,1,0:T(8,128)(2,1)} %refs_0_.3) | copy-start | bytes 786436
  9.4 23.9 %copy-start.6 = (f32[256,256]{1,0:T(8,128)S(1)}, f32[256,256]{1,0:T(8,128)}, u32[]{:S(2)}) copy-start(f32[256,256]{1,0:T(8,128)} %constant.9.clone.refs_4_) | copy-start | bytes 786436
  9.4 23.9 %copy-start.7 = (f32[256,256]{1,0:T(8,128)S(1)}, f32[256,256]{1,0:T(8,128)}, u32[]{:S(2)}) copy-start(f32[256,256]{1,0:T(8,128)} %constant.8.clone.refs_3_) | copy-start | bytes 786436
  9.4 16.7 %collective-permute-start = (f32[2,2,128,256]{3,2,1,0:T(8,128)S(1)}, f32[2,2,128,256]{3,2,1,0:T(8,128)S(1)}, u32[]{:S(2)}, u32[]{:S(2)}) collective-permute-start(f32[2,2,128,256]{3,2,1,0:T(8,128)S(1)} %get-tuple-element.79), channel_id=1, source_target_pairs={{0,16},{2,18},{4,20},{6,22},{8,24},{10,26},{12,28},{14,30},{16,32}... | collective-permute-start | bytes 1572872 | tf_op jit(solution)/shard_map/ppermute | solution.py:326
  13.0 22.0 %collective-permute-start.3 = (f32[2,2,256,128]{3,2,1,0:T(8,128)S(1)}, f32[2,2,256,128]{3,2,1,0:T(8,128)S(1)}, u32[]{:S(2)}, u32[]{:S(2)}) collective-permute-start(f32[2,2,256,128]{3,2,1,0:T(8,128)S(1)} %get-tuple-element.76), channel_id=1, source_target_pairs={{2,0},{4,2},{6,4},{8,6},{10,8},{12,10},{14,12},{18,16},{20,18},{22... | collective-permute-start | bytes 1572872 | tf_op jit(solution)/shard_map/ppermute | solution.py:332
  15.9 19.2 %collective-permute-start.2 = (f32[2,2,256,128]{3,2,1,0:T(8,128)S(1)}, f32[2,2,256,128]{3,2,1,0:T(8,128)S(1)}, u32[]{:S(2)}, u32[]{:S(2)}) collective-permute-start(f32[2,2,256,128]{3,2,1,0:T(8,128)S(1)} %get-tuple-element.77), channel_id=1, source_target_pairs={{0,2},{2,4},{4,6},{6,8},{8,10},{10,12},{12,14},{16,18},{18,20},{20... | collective-permute-start | bytes 1572872 | tf_op jit(solution)/shard_map/ppermute | solution.py:332
  26.2 11.0 %collective-permute-start.4 = (f32[2,2,2,128,128]{4,3,2,1,0:T(8,128)S(1)}, f32[2,2,2,128,128]{4,3,2,1,0:T(8,128)S(1)}, u32[]{:S(2)}, u32[]{:S(2)}) collective-permute-start(f32[2,2,2,128,128]{4,3,2,1,0:T(8,128)S(1)} %pad_maximum_fusion), channel_id=1, source_target_pairs={{0,2},{2,4},{4,6},{6,8},{8,10},{10,12},{12,14},{16,18},{18,20},{20... | collective-permute-start | bytes 1572872 | tf_op jit(solution)/shard_map/ppermute | solution.py:332
  31.1 10.7 %copy-start = (f32[1,2,2,256,256]{4,3,2,1,0:T(8,128)S(1)}, f32[1,2,2,256,256]{4,3,2,1,0:T(8,128)}, u32[]{:S(2)}) copy-start(f32[1,2,2,256,256]{4,3,2,1,0:T(8,128)} %param.10) | copy-start | bytes 3145732
  31.1 10.7 %copy-start.8 = (s32[1,2,2]{2,1,0:T(2,128)S(1)}, s32[1,2,2]{2,1,0:T(2,128)}, u32[]{:S(2)}) copy-start(s32[1,2,2]{2,1,0:T(2,128)} %param.13) | copy-start | bytes 52
  31.2 10.6 %collective-permute-start.5 = (f32[2,2,2,128,128]{4,3,2,1,0:T(8,128)S(1)}, f32[2,2,2,128,128]{4,3,2,1,0:T(8,128)S(1)}, u32[]{:S(2)}, u32[]{:S(2)}) collective-permute-start(f32[2,2,2,128,128]{4,3,2,1,0:T(8,128)S(1)} %pad_maximum_fusion.1), channel_id=1, source_target_pairs={{2,0},{4,2},{6,4},{8,6},{10,8},{12,10},{14,12},{18,16},{20,18},{22... | collective-permute-start | bytes 1572872 | tf_op jit(solution)/shard_map/ppermute | solution.py:332
  48.2 10.0 %collective-permute-start.6 = (f32[256,256]{1,0:T(8,128)S(1)}, f32[256,256]{1,0:T(8,128)S(1)}, u32[]{:S(2)}, u32[]{:S(2)}) collective-permute-start(f32[256,256]{1,0:T(8,128)S(1)} %get-tuple-element.44.refs_1_), channel_id=1, source_target_pairs={{0,1},{1,0},{2,3},{3,2},{4,5},{5,4},{6,7},{7,6},{8,9},{9,8},{10,11... | collective-permute-start | bytes 786440 | tf_op jit(solution)/shard_map/ppermute | solution.py:336
  56.6 9.3 %collective-permute-start.7 = (f32[256,256]{1,0:T(8,128)S(1)}, f32[256,256]{1,0:T(8,128)S(1)}, u32[]{:S(2)}, u32[]{:S(2)}) collective-permute-start(f32[256,256]{1,0:T(8,128)S(1)} %get-tuple-element.57.refs_3_), channel_id=1, source_target_pairs={{0,1},{1,0},{2,3},{3,2},{4,5},{5,4},{6,7},{7,6},{8,9},{9,8},{10,11... | collective-permute-start | bytes 786440 | tf_op jit(solution)/shard_map/ppermute | solution.py:336
  69.6 9.8 %collective-permute-start.8 = (f32[2,512,128]{2,1,0:T(8,128)S(1)}, f32[2,512,128]{2,1,0:T(8,128)S(1)}, u32[]{:S(2)}, u32[]{:S(2)}) collective-permute-start(f32[2,512,128]{2,1,0:T(8,128)S(1)} %get-tuple-element.65), channel_id=1, source_target_pairs={{0,2},{2,4},{4,6},{6,8},{8,10},{10,12},{12,14},{16,18},{18,20},{20... | collective-permute-start | bytes 1572872 | tf_op jit(solution)/shard_map/ppermute | solution.py:332
  73.2 10.5 %collective-permute-start.9 = (f32[2,512,128]{2,1,0:T(8,128)S(1)}, f32[2,512,128]{2,1,0:T(8,128)S(1)}, u32[]{:S(2)}, u32[]{:S(2)}) collective-permute-start(f32[2,512,128]{2,1,0:T(8,128)S(1)} %get-tuple-element.66), channel_id=1, source_target_pairs={{2,0},{4,2},{6,4},{8,6},{10,8},{12,10},{14,12},{18,16},{20,18},{22... | collective-permute-start | bytes 1572872 | tf_op jit(solution)/shard_map/ppermute | solution.py:332
  83.8 14.5 %collective-permute-start.15 = (f32[2,128,256]{2,1,0:T(8,128)S(1)}, f32[2,128,256]{2,1,0:T(8,128)S(1)}, u32[]{:S(2)}, u32[]{:S(2)}) collective-permute-start(f32[2,128,256]{2,1,0:T(8,128)S(1)} %get-tuple-element.67.refs_3_), channel_id=1, source_target_pairs={{16,0},{18,2},{20,4},{22,6},{24,8},{26,10},{28,12},{30,14},{32,16}... | collective-permute-start | bytes 786440 | tf_op jit(solution)/shard_map/ppermute | solution.py:326
  87.1 11.2 %collective-permute-start.14 = (f32[2,128,256]{2,1,0:T(8,128)S(1)}, f32[2,128,256]{2,1,0:T(8,128)S(1)}, u32[]{:S(2)}, u32[]{:S(2)}) collective-permute-start(f32[2,128,256]{2,1,0:T(8,128)S(1)} %get-tuple-element.74), channel_id=1, source_target_pairs={{0,16},{2,18},{4,20},{6,22},{8,24},{10,26},{12,28},{14,30},{16,32}... | collective-permute-start | bytes 786440 | tf_op jit(solution)/shard_map/ppermute | solution.py:326
  90.5 9.9 %collective-permute-start.10 = (f32[2,512,128]{2,1,0:T(8,128)S(1)}, f32[2,512,128]{2,1,0:T(8,128)S(1)}, u32[]{:S(2)}, u32[]{:S(2)}) collective-permute-start(f32[2,512,128]{2,1,0:T(8,128)S(1)} %get-tuple-element.69), channel_id=1, source_target_pairs={{0,2},{2,4},{4,6},{6,8},{8,10},{10,12},{12,14},{16,18},{18,20},{20... | collective-permute-start | bytes 1572872 | tf_op jit(solution)/shard_map/ppermute | solution.py:332
  92.8 10.8 %collective-permute-start.11 = (f32[2,512,128]{2,1,0:T(8,128)S(1)}, f32[2,512,128]{2,1,0:T(8,128)S(1)}, u32[]{:S(2)}, u32[]{:S(2)}) collective-permute-start(f32[2,512,128]{2,1,0:T(8,128)S(1)} %get-tuple-element.68.refs_3_), channel_id=1, source_target_pairs={{2,0},{4,2},{6,4},{8,6},{10,8},{12,10},{14,12},{18,16},{20,18},{22... | collective-permute-start | bytes 1572872 | tf_op jit(solution)/shard_map/ppermute | solution.py:332
  98.4 15.3 %collective-permute-start.16 = (f32[2,256,256]{2,1,0:T(8,128)S(1)}, f32[2,256,256]{2,1,0:T(8,128)S(1)}, u32[]{:S(2)}, u32[]{:S(2)}) collective-permute-start(f32[2,256,256]{2,1,0:T(8,128)S(1)} %rows_last.1.refs_2_), channel_id=1, source_target_pairs={{0,1},{1,0},{2,3},{3,2},{4,5},{5,4},{6,7},{7,6},{8,9},{9,8},{10,11... | collective-permute-start | bytes 1572872 | tf_op jit(solution)/shard_map/ppermute | solution.py:336
  103.7 10.7 %collective-permute-start.12 = (f32[2,128,256]{2,1,0:T(8,128)S(1)}, f32[2,128,256]{2,1,0:T(8,128)S(1)}, u32[]{:S(2)}, u32[]{:S(2)}) collective-permute-start(f32[2,128,256]{2,1,0:T(8,128)S(1)} %get-tuple-element.71), channel_id=1, source_target_pairs={{0,16},{2,18},{4,20},{6,22},{8,24},{10,26},{12,28},{14,30},{16,32}... | collective-permute-start | bytes 786440 | tf_op jit(solution)/shard_map/ppermute | solution.py:326
  105.6 10.5 %collective-permute-start.13 = (f32[2,128,256]{2,1,0:T(8,128)S(1)}, f32[2,128,256]{2,1,0:T(8,128)S(1)}, u32[]{:S(2)}, u32[]{:S(2)}) collective-permute-start(f32[2,128,256]{2,1,0:T(8,128)S(1)} %get-tuple-element.72), channel_id=1, source_target_pairs={{16,0},{18,2},{20,4},{22,6},{24,8},{26,10},{28,12},{30,14},{32,16}... | collective-permute-start | bytes 786440 | tf_op jit(solution)/shard_map/ppermute | solution.py:326
  116.2 15.0 %collective-permute-start.17 = (f32[2,256,256]{2,1,0:T(8,128)S(1)}, f32[2,256,256]{2,1,0:T(8,128)S(1)}, u32[]{:S(2)}, u32[]{:S(2)}) collective-permute-start(f32[2,256,256]{2,1,0:T(8,128)S(1)} %rows_first.1.refs_0_), channel_id=1, source_target_pairs={{0,1},{1,0},{2,3},{3,2},{4,5},{5,4},{6,7},{7,6},{8,9},{9,8},{10,11... | collective-permute-start | bytes 1572872 | tf_op jit(solution)/shard_map/ppermute | solution.py:336

commit v4 on v3

--- a/solution.py
+++ b/solution.py
@@ -124,18 +124,31 @@
     return top, block, row & 7, col & 127
 
 
-def build_canvas(own, up, down, left, right, corner_l, corner_r, canvas):
+def ends(info, axis, before, after):
+    odd = info[axis]
+    first = jnp.where(odd == 1, before, after)
+    second = jnp.where(odd == 1, after, before)
+    return pl.multiple_of(first, 128), pl.multiple_of(second, 128), info[2 + axis] == 1
+
+
+def kept(good, value):
+    return jnp.where(good, value, 0.0)
+
+
+def build_canvas(info, own, rows_a, rows_b, cols_a, cols_b, corners_a, corners_b, canvas):
     n = own.shape[-1]
     h = n // 2
+    ra, rb, row_ok = ends(info, 0, 0, h + n)
+    ca, cb, col_ok = ends(info, 1, 0, h + n)
     canvas[:, :, h : h + n, h : h + n] = own[...]
-    canvas[:, :, 0:h, h : h + n] = up[...]
-    canvas[:, :, h + n :, h : h + n] = down[...]
-    canvas[:, :, h : h + n, 0:h] = left[...]
-    canvas[:, :, h : h + n, h + n :] = right[...]
-    canvas[:, :, 0:h, 0:h] = corner_l[0]
-    canvas[:, :, h + n :, 0:h] = corner_l[1]
-    canvas[:, :, 0:h, h + n :] = corner_r[0]
-    canvas[:, :, h + n :, h + n :] = corner_r[1]
+    canvas[:, :, pl.ds(ra, h), h : h + n] = rows_a[...]
+    canvas[:, :, pl.ds(rb, h), h : h + n] = kept(row_ok, rows_b[...])
+    canvas[:, :, h : h + n, pl.ds(ca, h)] = cols_a[...]
+    canvas[:, :, h : h + n, pl.ds(cb, h)] = kept(col_ok, cols_b[...])
+    canvas[:, :, pl.ds(ra, h), pl.ds(ca, h)] = corners_a[0]
+    canvas[:, :, pl.ds(rb, h), pl.ds(ca, h)] = kept(row_ok, corners_a[1])
+    canvas[:, :, pl.ds(ra, h), pl.ds(cb, h)] = kept(col_ok, corners_b[0])
+    canvas[:, :, pl.ds(rb, h), pl.ds(cb, h)] = kept(row_ok & col_ok, corners_b[1])
 
 
 def extract(off_ref, slot, canvas, patch):
@@ -192,9 +205,9 @@
     each_mode(probe.shape[1], step)
 
 
-def forward_first_kernel(off, own, up, down, left, right, corner_l, corner_r, probe, diag,
-                         corner, mat, tabs, canvas, patch, wave, far, inten):
-    build_canvas(own, up, down, left, right, corner_l, corner_r, canvas)
+def forward_first_kernel(off, info, own, rows_a, rows_b, cols_a, cols_b, corners_a, corners_b,
+                         probe, diag, corner, mat, tabs, canvas, patch, wave, far, inten):
+    build_canvas(info, own, rows_a, rows_b, cols_a, cols_b, corners_a, corners_b, canvas)
     extract(off, 0, canvas, patch)
     forward(probe, patch, diag, corner, mat, tabs, wave, far, inten)
 
@@ -226,15 +239,14 @@
     each_mode(far.shape[0], step)
 
 
-def back_last_place_kernel(slot, counts, off, before, mine, other, measured, far, wave, patch,
-                           tabs, bar, out_l, out_c, out_r, resid, grad, canvas):
+def back_last_place_kernel(slot, counts, off, info, before, mine, other, measured, far, wave, patch,
+                           tabs, bar, out_a, out_c, out_b, resid, grad, canvas):
     back_last(slot, counts, mine, other, measured, far, wave, patch, tabs, grad, bar, resid)
     lay(off, (before, grad), canvas)
     n = grad.shape[-1]
     h = n // 2
-    out_l[...] = canvas[:, :, 0:h]
+    sides(info, canvas, out_a, out_b)
     out_c[...] = canvas[:, :, h : h + n]
-    out_r[...] = canvas[:, :, h + n :]
 
 
 def back_first(bar, probe, patch, diag, corner, mat, grad, emit):
@@ -267,11 +279,16 @@
     back_first(bar, probe, patch, diag, corner, mat, grad, emit)
 
 
-def place_sides_kernel(off, grad0, grad1, out_l, out_r, canvas):
+def sides(info, canvas, out_a, out_b):
+    h = out_a.shape[-1]
+    a, b, _ = ends(info, 1, 0, 3 * h)
+    out_a[...] = canvas[:, :, pl.ds(a, h)]
+    out_b[...] = canvas[:, :, pl.ds(b, h)]
+
+
+def place_sides_kernel(off, info, grad0, grad1, out_a, out_b, canvas):
     lay(off, (grad0, grad1), canvas)
-    h = grad0.shape[-1] // 2
-    out_l[...] = canvas[:, :, 0:h]
-    out_r[...] = canvas[:, :, 3 * h :]
+    sides(info, canvas, out_a, out_b)
 
 
 def place_center_kernel(off, grad0, grad1, out_c, canvas):
@@ -280,18 +297,27 @@
     out_c[...] = canvas[:, :, h : 3 * h]
 
 
-def fold_cols_kernel(center, from_left, from_right, top, mid, low):
+def fold_cols_kernel(info, center, got_a, got_b, out_a, mid, out_b):
     n = center.shape[-1]
     h = n // 2
-    for out, rows in ((top, slice(0, h)), (mid, slice(h, h + n)), (low, slice(h + n, 2 * n))):
-        out[:, :, :h] = center[:, rows, :h] + from_left[:, rows]
-        out[:, :, h:] = center[:, rows, h:] + from_right[:, rows]
-
-
-def fold_rows_kernel(mid, from_up, from_down, out):
-    h = from_up.shape[1]
-    out[:, :h] = mid[:, :h] + from_up[...]
-    out[:, h:] = mid[:, h:] + from_down[...]
+    ca, cb, col_ok = ends(info, 1, 0, h)
+    ra, rb, _ = ends(info, 0, 0, h + n)
+    for a, out in ((ra, out_a), (rb, out_b)):
+        out[:, :, pl.ds(ca, h)] = center[:, pl.ds(a, h), pl.ds(ca, h)] + got_a[:, pl.ds(a, h)]
+        out[:, :, pl.ds(cb, h)] = center[:, pl.ds(a, h), pl.ds(cb, h)] + kept(
+            col_ok, got_b[:, pl.ds(a, h)]
+        )
+    mid[:, :, pl.ds(ca, h)] = center[:, h : h + n, pl.ds(ca, h)] + got_a[:, h : h + n]
+    mid[:, :, pl.ds(cb, h)] = center[:, h : h + n, pl.ds(cb, h)] + kept(
+        col_ok, got_b[:, h : h + n]
+    )
+
+
+def fold_rows_kernel(info, mid, got_a, got_b, out):
+    h = got_a.shape[1]
+    ra, rb, row_ok = ends(info, 0, 0, h)
+    out[:, pl.ds(ra, h)] = mid[:, pl.ds(ra, h)] + got_a[...]
+    out[:, pl.ds(rb, h)] = mid[:, pl.ds(rb, h)] + kept(row_ok, got_b[...])
 
 
 def finish_kernel(mine_first, other_first, mine_last, other_last, out):
@@ -320,15 +346,14 @@
         meas_out[slot] = exact(exact(order[...], measured[slot]), order_t[...])
 
 
-def rows_by(value, step):
+def swap(value, axis, second):
     count = lax.axis_size("tile")
-    pairs = [(i, i + GY * step) for i in range(count) if 0 <= i + GY * step < count]
-    return lax.ppermute(value, "tile", pairs)
-
-
-def cols_by(value, step):
-    count = lax.axis_size("tile")
-    pairs = [(i, i + step) for i in range(count) if 0 <= i % GY + step < GY]
+    step, length = (GY, count // GY) if axis == 0 else (1, GY)
+    pairs = []
+    for i in range(count):
+        at = i // step % length
+        to = (at + (1 if (at % 2 == 1) == second else -1)) % length
+        pairs.append((i, i + (to - at) * step))
     return lax.ppermute(value, "tile", pairs)
 
 
@@ -365,12 +390,24 @@
     own = object_tiles[0]
     off = offsets[0]
 
-    down_strip = rows_by(own[:, :, :h, :], -1)
-    up_strip = rows_by(own[:, :, h:, :], 1)
-    left_strip = cols_by(own[:, :, :, h:], 1)
-    right_strip = cols_by(own[:, :, :, :h], -1)
-    corner_l = cols_by(jnp.stack([up_strip[..., h:], down_strip[..., h:]]), 1)
-    corner_r = cols_by(jnp.stack([up_strip[..., :h], down_strip[..., :h]]), -1)
+    tile = lax.axis_index("tile")
+    row, col = tile // GY, tile % GY
+    n_rows = lax.axis_size("tile") // GY
+    odd_row, odd_col = row % 2 == 1, col % 2 == 1
+    info = jnp.stack(
+        [odd_row, odd_col, (row > 0) & (row < n_rows - 1), (col > 0) & (col < GY - 1)]
+    ).astype(jnp.int32)
+
+    top, low = own[:, :, :h, :], own[:, :, h:, :]
+    rows_a = swap(jnp.where(odd_row, top, low), 0, False)
+    rows_b = swap(jnp.where(odd_row, low, top), 0, True)
+    left, right = own[:, :, :, :h], own[:, :, :, h:]
+    cols_a = swap(jnp.where(odd_col, left, right), 1, False)
+    cols_b = swap(jnp.where(odd_col, right, left), 1, True)
+    strips = jnp.stack([rows_a, rows_b])
+    left, right = strips[..., :h], strips[..., h:]
+    corners_a = swap(jnp.where(odd_col, left, right), 1, False)
+    corners_b = swap(jnp.where(odd_col, right, left), 1, True)
 
     dft, conj_dft = dft_tables(n)
     order = np.eye(n, dtype=np.float32)[np.r_[0:n:2, 1:n:2]]
@@ -392,8 +429,8 @@
         forward_first_kernel,
         "forward_0",
         (((2, 2, 2 * n, 2 * n), F32), patch_out, field, field, plane),
-        (off, own, up_strip, down_strip, left_strip, right_strip, corner_l, corner_r,
-         probe, *prop, dft),
+        (off, info, own, rows_a, rows_b, cols_a, cols_b, corners_a, corners_b, probe, *prop, dft),
+        smem=2,
     )
     other0 = swap_mode(inten0)
     patch1, wave1, far1, inten1 = call(
@@ -421,29 +458,26 @@
         (bar0, probe, patch0, *back_prop),
         smem=0,
     )
-    bar1, out_l, out_c, out_r = call(
+    bar1, out_a, out_c, out_b = call(
         functools.partial(back_last_place_kernel, 1),
         "back_last_1",
         (bar_out,) + strips,
-        (counts, off, grad_last0, inten1, other1, measured, far1, wave1, patch1, conj_dft),
+        (counts, off, info, grad_last0, inten1, other1, measured, far1, wave1, patch1, conj_dft),
         scratch=((2, n, n), (2, n, n), wide),
-        smem=2,
+        smem=3,
         after=(grad_first0,),
     )
 
     half = ((2, h, n), F32)
 
-    def fold_cols(name, out_l, out_c, out_r, after):
-        from_left = cols_by(out_r, 1)
-        from_right = cols_by(out_l, -1)
-        return call(fold_cols_kernel, name, (half, pair, half), (out_c, from_left, from_right),
-                    smem=0, after=after)
-
-    def fold_rows(name, top, mid, low, after):
-        from_up = rows_by(low, 1)
-        from_down = rows_by(top, -1)
-        return call(fold_rows_kernel, name, (pair,), (mid, from_up, from_down), smem=0,
-                    after=after)[0]
+    def fold_cols(name, out_a, out_c, out_b, after):
+        got_a, got_b = swap(out_a, 1, False), swap(out_b, 1, True)
+        return call(fold_cols_kernel, name, (half, pair, half), (info, out_c, got_a, got_b),
+                    after=after)
+
+    def fold_rows(name, out_a, mid, out_b, after):
+        got_a, got_b = swap(out_a, 0, False), swap(out_b, 0, True)
+        return call(fold_rows_kernel, name, (pair,), (info, mid, got_a, got_b), after=after)[0]
 
     grad_first1, probe_grad = call(
         back_first_add_kernel,
@@ -452,15 +486,16 @@
         (bar1, probe, patch1, *back_prop, part),
         smem=0,
     )
-    strips_last = fold_cols("cols_last", out_l, out_c, out_r, (grad_first1,))
+    strips_last = fold_cols("cols_last", out_a, out_c, out_b, (grad_first1,))
     mine_last = fold_rows("rows_last", *strips_last, ())
     other_last = swap_mode(mine_last)
-    out_l, out_r = call(
+    out_a, out_b = call(
         place_sides_kernel,
         "place_sides",
         (strips[0], strips[2]),
-        (off, grad_first0, grad_first1),
+        (off, info, grad_first0, grad_first1),
         scratch=(wide,),
+        smem=2,
         after=(strips_last[0],),
     )
     (out_c,) = call(
@@ -469,9 +504,9 @@
         (strips[1],),
         (off, grad_first0, grad_first1),
         scratch=(wide,),
-        after=(out_l,),
-    )
-    strips_first = fold_cols("cols_first", out_l, out_c, out_r, ())
+        after=(out_a,),
+    )
+    strips_first = fold_cols("cols_first", out_a, out_c, out_b, ())
     mine_first = fold_rows("rows_first", *strips_first, (other_last,))
     other_first = swap_mode(mine_first)
     (object_grad,) = call(

time: 133 us -> 124 us (0.932)
  the two profiles are of different devices: /device:TPU:11 before, /device:TPU:6 now
where the time goes in v4:
time: 124 us; the launch traced here: 123 us
  waiting for transfers between devices  53.2 us (43%)
  Pallas kernels  34.6 us (28%)
  starting transfers between devices  22.3 us (18%)
  local copies, waits for them, and re-layouts  6.92 us (6%)
  other arithmetic  4.77 us (4%)
  between operations  1.5 us (1%)
    pallas_call x14, Pallas kernels, call(): pl.pallas_call(run, out_shape=tuple((jax.ShapeDtypeStruct(shape, dtype) f...  34.6 us
    ppermute x4, waiting for transfers between devices, swap_mode(): return lax.ppermute(value, 'mode', [(0, 1), (1, 0)])  33.4 us
    ppermute x14, waiting for transfers between devices, swap(): return lax.ppermute(value, 'tile', pairs)  19.8 us
    ppermute x14, starting transfers between devices, swap(): return lax.ppermute(value, 'tile', pairs)  17 us
    unnamed x18, local copies, waits for them, and re-layouts  6.92 us
    ppermute x4, starting transfers between devices, swap_mode(): return lax.ppermute(value, 'mode', [(0, 1), (1, 0)])  5.35 us
  transfers between devices with their start and end apart: 18, of which 7 were waited for; matrix products, arithmetic and copies ran while one was open for 3% of the time, Pallas kernels for 17%

profile of v4, /device:TPU:6, one launch (start us, length us, event | category | flops | bytes accessed | tf_op | source)
XLA Modules:
  0.0 123.4 jit_solution(10596773351910707347)
XLA Ops:
  0.7 1.3 %slice_select_fusion.2 = (f32[2,2,128,256]{3,2,1,0:T(8,128)S(1)}, f32[2,2,128,256]{3,2,1,0:T(8,128)S(1)}) fusion(f32[2,2,256,256]{3,2,1,0:T(8,128)} %bitcast.9, pred[]{:T(512)} %eq.10), kind=kLoop, calls=%fused_computation.6 | loop fusion | flops 262144 | bytes 2097153 | tf_op jit(solution)/shard_map/jit(_where)/select_n | solution.py:403
  2.0 7.0 %collective-permute-start.1 = (f32[2,2,128,256]{3,2,1,0:T(8,128)S(1)}, f32[2,2,128,256]{3,2,1,0:T(8,128)S(1)}, u32[]{:S(2)}, u32[]{:S(2)}) collective-permute-start(f32[2,2,128,256]{3,2,1,0:T(8,128)S(1)} %get-tuple-element.80), channel_id=1, source_target_pairs={{0,240},{2,242},{4,244},{6,246},{8,248},{10,250},{12,252},{14,254}... | collective-permute-start | bytes 1572872 | tf_op jit(solution)/shard_map/ppermute | solution.py:357
  9.0 2.3 %slice_select_fusion = (f32[2,2,256,128]{3,2,1,0:T(8,128)}, f32[2,2,256,128]{3,2,1,0:T(8,128)}) fusion(f32[2,2,256,256]{3,2,1,0:T(8,128)} %bitcast.10, pred[]{:T(512)} %eq.11), kind=kLoop, calls=%fused_computation.4 | loop fusion | flops 262144 | bytes 2097153 | tf_op jit(solution)/shard_map/jit(_where)/select_n | solution.py:406
  11.8 9.1 %collective-permute-done.1.refs_4_ = f32[2,2,128,256]{3,2,1,0:T(8,128)S(1)} collective-permute-done((f32[2,2,128,256]{3,2,1,0:T(8,128)S(1)}, f32[2,2,128,256]{3,2,1,0:T(8,128)S(1)}, u32[]{:S(2)}, u32[]{:S(2)}) %collective-permute-start.1) | collective-permute-done | bytes 524320 | tf_op jit(solution)/shard_map/ppermute | solution.py:357
  20.9 1.5 %collective-permute-done.refs_3_ = f32[2,2,128,256]{3,2,1,0:T(8,128)S(1)} collective-permute-done((f32[2,2,128,256]{3,2,1,0:T(8,128)S(1)}, f32[2,2,128,256]{3,2,1,0:T(8,128)S(1)}, u32[]{:S(2)}, u32[]{:S(2)}) %collective-permute-start) | collective-permute-done | bytes 524320 | tf_op jit(solution)/shard_map/ppermute | solution.py:357
  22.4 1.1 broadcast_select_fusion
  24.1 1.9 %copy-done.1 = f32[2,6,256,256]{3,2,1,0:T(8,128)S(1)} copy-done((f32[2,6,256,256]{3,2,1,0:T(8,128)S(1)}, f32[2,6,256,256]{3,2,1,0:T(8,128)}, u32[]{:S(2)}) %copy-start.1) | copy-done | bytes 3145752
  26.0 1.0 copy-done.2
  27.0 1.0 copy-done.3
  28.0 1.0 copy-done.4
  29.1 0.9 copy-done.6
  31.0 1.7 %prepare.1 = (bf16[2,256,256]{2,1,0:T(8,128)(2,1)S(1)}, bf16[64,64]{1,0:T(8,128)(2,1)S(1)}, bf16[512,512]{1,0:T(8,128)(2,1)S(1)}, bf16[2,256,256]{2,1,0:T(8,128)...) custom-call(bf16[2,256,256]{2,1,0:T(8,128)(2,1)S(1)} %copy-done.5, ...), custom_call_target="tpu_custom_call" | custom-call | tf_op jit(solution)/shard_map/prepare/pallas_call | solution.py:372
  32.8 7.2 %forward_0.1 = (f32[2,2,512,512]{3,2,1,0:T(8,128)S(1)}, f32[2,2,256,256]{3,2,1,0:T(8,128)S(1)}, f32[6,2,256,256]{3,2,1,0:T(8,128)S(1)}, f32[6,2,256,256]{3,2,1,0:T(8,128)S(1)}, f32[256,256]{1,0:T(8,128)S(1)}) custom-call(s32[2,2]{1,0:T(2,128)S(1)} %bitcast.15, s32[4]{0:T(128)S(1)} %add_convert_fusion.refs_1_.refs_2_.refs_0_, ...), custom_call_target="tpu_custom_call" | custom-call | tf_op jit(solution)/shard_map/forward_0/pallas_call | solution.py:372
  40.0 3.2 %collective-permute-start.6 = (f32[256,256]{1,0:T(8,128)S(1)}, f32[256,256]{1,0:T(8,128)S(1)}, u32[]{:S(2)}, u32[]{:S(2)}) collective-permute-start(f32[256,256]{1,0:T(8,128)S(1)} %get-tuple-element.44.refs_1_), channel_id=1, source_target_pairs={{0,1},{1,0},{2,3},{3,2},{4,5},{5,4},{6,7},{7,6},{8,9},{9,8},{10,11... | collective-permute-start | bytes 786440 | tf_op jit(solution)/shard_map/ppermute | solution.py:361
  43.2 6.0 %forward_1.1 = (f32[2,2,256,256]{3,2,1,0:T(8,128)S(1)}, f32[6,2,256,256]{3,2,1,0:T(8,128)S(1)}, f32[6,2,256,256]{3,2,1,0:T(8,128)S(1)}, f32[256,256]{1,0:T(8,128)S(1)}) custom-call(s32[2,2]{1,0:T(2,128)S(1)} %bitcast.16, f32[2,2,512,512]{3,2,1,0:T(8,128)S(1)} %get-tuple-element.56.refs_1_, f32[2,6,256,256]{3,2,1,0:T(8,128)S(1)} %get-tuple-element.39.refs_9_.refs_1_.refs_2_, ...), custom_call_target="tpu_custom_call" | custom-call | tf_op jit(solution)/shard_map/forward_1/pallas_call | solution.py:372
  50.5 2.3 %back_last_0.1 = (f32[2,256,256]{2,1,0:T(8,128)S(1)}, bf16[6,2,256,256]{3,2,1,0:T(8,128)(2,1)S(1)}) custom-call(s32[1]{0:T(128)S(6)} %copy.12.refs_0_, f32[256,256]{1,0:T(8,128)S(1)} %get-tuple-element.44.refs_1_, f32[256,256]{1,0:T(8,128)S(1)} %collective-permute-done.6.refs_2_, f32[2,256,256]{2,1,0:T(8,128)S(1)} %get-tuple-element.45.refs_3_.refs_6_, ...), custom_call_target="tpu_custom_call" | custom-call | tf_op jit(solution)/shard_map/back_last_0/pallas_call | solution.py:372
  52.9 2.5 %back_first_0.1 = (f32[2,256,256]{2,1,0:T(8,128)S(1)}, f32[2,6,256,256]{3,2,1,0:T(8,128)S(1)}) custom-call(bf16[6,2,256,256]{3,2,1,0:T(8,128)(2,1)S(1)} %get-tuple-element.50.refs_0_, f32[2,6,256,256]{3,2,1,0:T(8,128)S(1)} %get-tuple-element.39.refs_9_.refs_1_.refs_2_, f32[2,2,256,256]{3,2,1,0:T(8,128)S(1)} %get-tuple-element.48.refs_6_.refs_2_, ...), custom_call_target="tpu_custom_call" | custom-call | tf_op jit(solution)/shard_map/back_first_0/pallas_call | solution.py:372
  55.4 3.3 %collective-permute-done.7.refs_5_ = f32[256,256]{1,0:T(8,128)S(1)} collective-permute-done((f32[256,256]{1,0:T(8,128)S(1)}, f32[256,256]{1,0:T(8,128)S(1)}, u32[]{:S(2)}, u32[]{:S(2)}) %collective-permute-start.7) | collective-permute-done | bytes 262176 | tf_op jit(solution)/shard_map/ppermute | solution.py:361
  58.7 3.8 %back_last_1.1 = (bf16[6,2,256,256]{3,2,1,0:T(8,128)(2,1)S(1)}, f32[2,512,128]{2,1,0:T(8,128)S(1)}, f32[2,512,256]{2,1,0:T(8,128)S(1)}, f32[2,512,128]{2,1,0:T(8,128)S(1)}) custom-call(s32[1]{0:T(128)S(6)} %copy.12.refs_0_, s32[2,2]{1,0:T(2,128)S(1)} %bitcast.17, s32[4]{0:T(128)S(1)} %add_convert_fusion.refs_1_.refs_2_.refs_0_, ...), custom_call_target="tpu_custom_call" | custom-call | tf_op jit(solution)/shard_map/back_last_1/pallas_call | solution.py:372
  62.6 1.6 %collective-permute-start.9 = (f32[2,512,128]{2,1,0:T(8,128)S(1)}, f32[2,512,128]{2,1,0:T(8,128)S(1)}, u32[]{:S(2)}, u32[]{:S(2)}) collective-permute-start(f32[2,512,128]{2,1,0:T(8,128)S(1)} %get-tuple-element.66), channel_id=1, source_target_pairs={{0,14},{2,4},{4,2},{6,8},{8,6},{10,12},{12,10},{14,0},{16,30},{18,... | collective-permute-start | bytes 1572872 | tf_op jit(solution)/shard_map/ppermute | solution.py:357
  64.2 4.6 %back_first_1.1 = (f32[2,256,256]{2,1,0:T(8,128)S(1)}, f32[1,2,6,256,256]{4,3,2,1,0:T(8,128)}) custom-call(bf16[6,2,256,256]{3,2,1,0:T(8,128)(2,1)S(1)} %get-tuple-element.61.refs_0_, f32[2,6,256,256]{3,2,1,0:T(8,128)S(1)} %get-tuple-element.39.refs_9_.refs_1_.refs_2_, f32[2,2,256,256]{3,2,1,0:T(8,128)S(1)} %get-tuple-element.60.refs_9_.refs_2_, ...), custom_call_target="tpu_custom_call" | custom-call | tf_op jit(solution)/shard_map/back_first_1/pallas_call | solution.py:372
  68.8 2.7 %collective-permute-done.9.refs_3_ = f32[2,512,128]{2,1,0:T(8,128)S(1)} collective-permute-done((f32[2,512,128]{2,1,0:T(8,128)S(1)}, f32[2,512,128]{2,1,0:T(8,128)S(1)}, u32[]{:S(2)}, u32[]{:S(2)}) %collective-permute-start.9) | collective-permute-done | bytes 524320 | tf_op jit(solution)/shard_map/ppermute | solution.py:357
  72.6 1.4 %place_sides.1 = (f32[2,512,128]{2,1,0:T(8,128)S(1)}, f32[2,512,128]{2,1,0:T(8,128)S(1)}) custom-call(s32[2,2]{1,0:T(2,128)S(1)} %bitcast.18, s32[4]{0:T(128)S(1)} %add_convert_fusion.refs_1_.refs_2_.refs_0_, f32[2,256,256]{2,1,0:T(8,128)S(1)} %get-tuple-element.54.refs_11_.refs_2_.refs_1_, f32[2,256,256]{2,1,0:T(8,128)S(1)} %get-tuple-element.63.refs_4_.refs_3_.refs_2_, ...), custom_call_target="tpu_custom_call" | custom-call | tf_op jit(solution)/shard_map/place_sides/pallas_call | solution.py:372
  74.0 1.6 %collective-permute-start.15 = (f32[2,128,256]{2,1,0:T(8,128)S(1)}, f32[2,128,256]{2,1,0:T(8,128)S(1)}, u32[]{:S(2)}, u32[]{:S(2)}) collective-permute-start(f32[2,128,256]{2,1,0:T(8,128)S(1)} %get-tuple-element.74), channel_id=1, source_target_pairs={{0,240},{2,242},{4,244},{6,246},{8,248},{10,250},{12,252},{14,254}... | collective-permute-start | bytes 786440 | tf_op jit(solution)/shard_map/ppermute | solution.py:357
  75.6 1.1 collective-permute-start.11
  76.7 2.0 %collective-permute-start.10 = (f32[2,512,128]{2,1,0:T(8,128)S(1)}, f32[2,512,128]{2,1,0:T(8,128)S(1)}, u32[]{:S(2)}, u32[]{:S(2)}) collective-permute-start(f32[2,512,128]{2,1,0:T(8,128)S(1)} %get-tuple-element.68.refs_3_), channel_id=1, source_target_pairs={{0,2},{2,0},{4,6},{6,4},{8,10},{10,8},{12,14},{14,12},{16,18},{18,... | collective-permute-start | bytes 1572872 | tf_op jit(solution)/shard_map/ppermute | solution.py:357
  78.6 6.6 %collective-permute-done.15.refs_3_ = f32[2,128,256]{2,1,0:T(8,128)S(1)} collective-permute-done((f32[2,128,256]{2,1,0:T(8,128)S(1)}, f32[2,128,256]{2,1,0:T(8,128)S(1)}, u32[]{:S(2)}, u32[]{:S(2)}) %collective-permute-start.15) | collective-permute-done | bytes 262176 | tf_op jit(solution)/shard_map/ppermute | solution.py:357
  86.5 1.4 %place_center.1.refs_1_ = f32[2,512,256]{2,1,0:T(8,128)S(1)} custom-call(s32[2,2]{1,0:T(2,128)S(1)} %bitcast.19, f32[2,256,256]{2,1,0:T(8,128)S(1)} %get-tuple-element.54.refs_11_.refs_2_.refs_1_, f32[2,256,256]{2,1,0:T(8,128)S(1)} %get-tuple-element.63.refs_4_.refs_3_.refs_2_, f32[2,512,128]{2,1,0:T(8,128)S(1)} %get-tuple-element.68.refs_3_), custom_call_target="tpu_custom_call" | custom-call | tf_op jit(solution)/shard_map/place_center/pallas_call | solution.py:372
  88.8 2.0 %collective-permute-start.13 = (f32[2,128,256]{2,1,0:T(8,128)S(1)}, f32[2,128,256]{2,1,0:T(8,128)S(1)}, u32[]{:S(2)}, u32[]{:S(2)}) collective-permute-start(f32[2,128,256]{2,1,0:T(8,128)S(1)} %get-tuple-element.72), channel_id=1, source_target_pairs={{0,240},{2,242},{4,244},{6,246},{8,248},{10,250},{12,252},{14,254}... | collective-permute-start | bytes 786440 | tf_op jit(solution)/shard_map/ppermute | solution.py:357
  90.8 16.2 %collective-permute-done.16.refs_4_.refs_3_ = f32[2,256,256]{2,1,0:T(8,128)S(1)} collective-permute-done((f32[2,256,256]{2,1,0:T(8,128)S(1)}, f32[2,256,256]{2,1,0:T(8,128)S(1)}, u32[]{:S(2)}, u32[]{:S(2)}) %collective-permute-start.16) | collective-permute-done | bytes 524320 | tf_op jit(solution)/shard_map/ppermute | solution.py:361
  108.3 14.0 %collective-permute-done.17.refs_1_ = f32[2,256,256]{2,1,0:T(8,128)S(1)} collective-permute-done((f32[2,256,256]{2,1,0:T(8,128)S(1)}, f32[2,256,256]{2,1,0:T(8,128)S(1)}, u32[]{:S(2)}, u32[]{:S(2)}) %collective-permute-start.17) | collective-permute-done | bytes 524320 | tf_op jit(solution)/shard_map/ppermute | solution.py:361
  122.3 1.1 finish.1
  (40 shorter events, 7.6 us)
Async XLA Ops:
  0.7 23.4 %copy-start.5 = (bf16[2,256,256]{2,1,0:T(8,128)(2,1)S(1)}, bf16[2,256,256]{2,1,0:T(8,128)(2,1)}, u32[]{:S(2)}) copy-start(bf16[2,256,256]{2,1,0:T(8,128)(2,1)} %refs_0_.3) | copy-start | bytes 786436
  2.0 18.9 %collective-permute-start.1 = (f32[2,2,128,256]{3,2,1,0:T(8,128)S(1)}, f32[2,2,128,256]{3,2,1,0:T(8,128)S(1)}, u32[]{:S(2)}, u32[]{:S(2)}) collective-permute-start(f32[2,2,128,256]{3,2,1,0:T(8,128)S(1)} %get-tuple-element.80), channel_id=1, source_target_pairs={{0,240},{2,242},{4,244},{6,246},{8,248},{10,250},{12,252},{14,254}... | collective-permute-start | bytes 1572872 | tf_op jit(solution)/shard_map/ppermute | solution.py:357
  9.0 13.4 %collective-permute-start = (f32[2,2,128,256]{3,2,1,0:T(8,128)S(1)}, f32[2,2,128,256]{3,2,1,0:T(8,128)S(1)}, u32[]{:S(2)}, u32[]{:S(2)}) collective-permute-start(f32[2,2,128,256]{3,2,1,0:T(8,128)S(1)} %get-tuple-element.81), channel_id=1, source_target_pairs={{0,16},{2,18},{4,20},{6,22},{8,24},{10,26},{12,28},{14,30},{16,0},... | collective-permute-start | bytes 1572872 | tf_op jit(solution)/shard_map/ppermute | solution.py:357
  11.2 21.5 %collective-permute-start.3 = (f32[2,2,256,128]{3,2,1,0:T(8,128)}, f32[2,2,256,128]{3,2,1,0:T(8,128)S(1)}, u32[]{:S(2)}, u32[]{:S(2)}) collective-permute-start(f32[2,2,256,128]{3,2,1,0:T(8,128)} %get-tuple-element.78), channel_id=1, source_target_pairs={{0,14},{2,4},{4,2},{6,8},{8,6},{10,12},{12,10},{14,0},{16,30},{18,... | collective-permute-start | bytes 1572872 | tf_op jit(solution)/shard_map/ppermute | solution.py:357
  11.2 21.5 %collective-permute-start.2 = (f32[2,2,256,128]{3,2,1,0:T(8,128)}, f32[2,2,256,128]{3,2,1,0:T(8,128)S(1)}, u32[]{:S(2)}, u32[]{:S(2)}) collective-permute-start(f32[2,2,256,128]{3,2,1,0:T(8,128)} %get-tuple-element.79), channel_id=1, source_target_pairs={{0,2},{2,0},{4,6},{6,4},{8,10},{10,8},{12,14},{14,12},{16,18},{18,... | collective-permute-start | bytes 1572872 | tf_op jit(solution)/shard_map/ppermute | solution.py:357
  22.4 10.4 %copy-start.8 = (s32[1,2,2]{2,1,0:T(2,128)S(1)}, s32[1,2,2]{2,1,0:T(2,128)}, u32[]{:S(2)}) copy-start(s32[1,2,2]{2,1,0:T(2,128)} %param.13) | copy-start | bytes 52
  23.5 9.3 %copy-start = (f32[1,2,2,256,256]{4,3,2,1,0:T(8,128)S(1)}, f32[1,2,2,256,256]{4,3,2,1,0:T(8,128)}, u32[]{:S(2)}) copy-start(f32[1,2,2,256,256]{4,3,2,1,0:T(8,128)} %param.10) | copy-start | bytes 3145732
  23.5 9.3 %collective-permute-start.5 = (f32[2,2,2,128,128]{4,3,2,1,0:T(8,128)}, f32[2,2,2,128,128]{4,3,2,1,0:T(8,128)}, u32[]{:S(2)}, u32[]{:S(2)}) collective-permute-start(f32[2,2,2,128,128]{4,3,2,1,0:T(8,128)} %get-tuple-element.76), channel_id=1, source_target_pairs={{0,14},{2,4},{4,2},{6,8},{8,6},{10,12},{12,10},{14,0},{16,30},{18,... | collective-permute-start | bytes 1572872 | tf_op jit(solution)/shard_map/ppermute | solution.py:357
  23.5 9.3 %collective-permute-start.4 = (f32[2,2,2,128,128]{4,3,2,1,0:T(8,128)}, f32[2,2,2,128,128]{4,3,2,1,0:T(8,128)}, u32[]{:S(2)}, u32[]{:S(2)}) collective-permute-start(f32[2,2,2,128,128]{4,3,2,1,0:T(8,128)} %get-tuple-element.77), channel_id=1, source_target_pairs={{0,2},{2,0},{4,6},{6,4},{8,10},{10,8},{12,14},{14,12},{16,18},{18,... | collective-permute-start | bytes 1572872 | tf_op jit(solution)/shard_map/ppermute | solution.py:357
  24.1 1.9 %copy-start.1 = (f32[2,6,256,256]{3,2,1,0:T(8,128)S(1)}, f32[2,6,256,256]{3,2,1,0:T(8,128)}, u32[]{:S(2)}) copy-start(f32[2,6,256,256]{3,2,1,0:T(8,128)} %refs_1_.1) | copy-start | bytes 9437188
  25.9 1.0 copy-start.2
  27.0 1.0 copy-start.3
  28.0 1.0 copy-start.4
  29.1 0.9 copy-start.6
  30.0 0.9 copy-start.7
  40.0 10.6 %collective-permute-start.6 = (f32[256,256]{1,0:T(8,128)S(1)}, f32[256,256]{1,0:T(8,128)S(1)}, u32[]{:S(2)}, u32[]{:S(2)}) collective-permute-start(f32[256,256]{1,0:T(8,128)S(1)} %get-tuple-element.44.refs_1_), channel_id=1, source_target_pairs={{0,1},{1,0},{2,3},{3,2},{4,5},{5,4},{6,7},{7,6},{8,9},{9,8},{10,11... | collective-permute-start | bytes 786440 | tf_op jit(solution)/shard_map/ppermute | solution.py:361
  49.2 9.5 %collective-permute-start.7 = (f32[256,256]{1,0:T(8,128)S(1)}, f32[256,256]{1,0:T(8,128)S(1)}, u32[]{:S(2)}, u32[]{:S(2)}) collective-permute-start(f32[256,256]{1,0:T(8,128)S(1)} %get-tuple-element.57.refs_4_), channel_id=1, source_target_pairs={{0,1},{1,0},{2,3},{3,2},{4,5},{5,4},{6,7},{7,6},{8,9},{9,8},{10,11... | collective-permute-start | bytes 786440 | tf_op jit(solution)/shard_map/ppermute | solution.py:361
  62.5 6.3 %collective-permute-start.8 = (f32[2,512,128]{2,1,0:T(8,128)S(1)}, f32[2,512,128]{2,1,0:T(8,128)S(1)}, u32[]{:S(2)}, u32[]{:S(2)}) collective-permute-start(f32[2,512,128]{2,1,0:T(8,128)S(1)} %get-tuple-element.65), channel_id=1, source_target_pairs={{0,2},{2,0},{4,6},{6,4},{8,10},{10,8},{12,14},{14,12},{16,18},{18,... | collective-permute-start | bytes 1572872 | tf_op jit(solution)/shard_map/ppermute | solution.py:357
  62.6 8.9 %collective-permute-start.9 = (f32[2,512,128]{2,1,0:T(8,128)S(1)}, f32[2,512,128]{2,1,0:T(8,128)S(1)}, u32[]{:S(2)}, u32[]{:S(2)}) collective-permute-start(f32[2,512,128]{2,1,0:T(8,128)S(1)} %get-tuple-element.66), channel_id=1, source_target_pairs={{0,14},{2,4},{4,2},{6,8},{8,6},{10,12},{12,10},{14,0},{16,30},{18,... | collective-permute-start | bytes 1572872 | tf_op jit(solution)/shard_map/ppermute | solution.py:357
  72.2 13.0 %collective-permute-start.14 = (f32[2,128,256]{2,1,0:T(8,128)S(1)}, f32[2,128,256]{2,1,0:T(8,128)S(1)}, u32[]{:S(2)}, u32[]{:S(2)}) collective-permute-start(f32[2,128,256]{2,1,0:T(8,128)S(1)} %get-tuple-element.67.refs_4_), channel_id=1, source_target_pairs={{0,16},{2,18},{4,20},{6,22},{8,24},{10,26},{12,28},{14,30},{16,0},... | collective-permute-start | bytes 786440 | tf_op jit(solution)/shard_map/ppermute | solution.py:357
  74.0 11.2 %collective-permute-start.15 = (f32[2,128,256]{2,1,0:T(8,128)S(1)}, f32[2,128,256]{2,1,0:T(8,128)S(1)}, u32[]{:S(2)}, u32[]{:S(2)}) collective-permute-start(f32[2,128,256]{2,1,0:T(8,128)S(1)} %get-tuple-element.74), channel_id=1, source_target_pairs={{0,240},{2,242},{4,244},{6,246},{8,248},{10,250},{12,252},{14,254}... | collective-permute-start | bytes 786440 | tf_op jit(solution)/shard_map/ppermute | solution.py:357
  75.6 12.3 %collective-permute-start.11 = (f32[2,512,128]{2,1,0:T(8,128)S(1)}, f32[2,512,128]{2,1,0:T(8,128)S(1)}, u32[]{:S(2)}, u32[]{:S(2)}) collective-permute-start(f32[2,512,128]{2,1,0:T(8,128)S(1)} %get-tuple-element.69), channel_id=1, source_target_pairs={{0,14},{2,4},{4,2},{6,8},{8,6},{10,12},{12,10},{14,0},{16,30},{18,... | collective-permute-start | bytes 1572872 | tf_op jit(solution)/shard_map/ppermute | solution.py:357
  76.7 11.3 %collective-permute-start.10 = (f32[2,512,128]{2,1,0:T(8,128)S(1)}, f32[2,512,128]{2,1,0:T(8,128)S(1)}, u32[]{:S(2)}, u32[]{:S(2)}) collective-permute-start(f32[2,512,128]{2,1,0:T(8,128)S(1)} %get-tuple-element.68.refs_3_), channel_id=1, source_target_pairs={{0,2},{2,0},{4,6},{6,4},{8,10},{10,8},{12,14},{14,12},{16,18},{18,... | collective-permute-start | bytes 1572872 | tf_op jit(solution)/shard_map/ppermute | solution.py:357
  85.8 21.2 %collective-permute-start.16 = (f32[2,256,256]{2,1,0:T(8,128)S(1)}, f32[2,256,256]{2,1,0:T(8,128)S(1)}, u32[]{:S(2)}, u32[]{:S(2)}) collective-permute-start(f32[2,256,256]{2,1,0:T(8,128)S(1)} %rows_last.1.refs_2_), channel_id=1, source_target_pairs={{0,1},{1,0},{2,3},{3,2},{4,5},{5,4},{6,7},{7,6},{8,9},{9,8},{10,11... | collective-permute-start | bytes 1572872 | tf_op jit(solution)/shard_map/ppermute | solution.py:361
  88.7 18.3 %collective-permute-start.12 = (f32[2,128,256]{2,1,0:T(8,128)S(1)}, f32[2,128,256]{2,1,0:T(8,128)S(1)}, u32[]{:S(2)}, u32[]{:S(2)}) collective-permute-start(f32[2,128,256]{2,1,0:T(8,128)S(1)} %get-tuple-element.71), channel_id=1, source_target_pairs={{0,16},{2,18},{4,20},{6,22},{8,24},{10,26},{12,28},{14,30},{16,0},... | collective-permute-start | bytes 786440 | tf_op jit(solution)/shard_map/ppermute | solution.py:357
  88.8 18.2 %collective-permute-start.13 = (f32[2,128,256]{2,1,0:T(8,128)S(1)}, f32[2,128,256]{2,1,0:T(8,128)S(1)}, u32[]{:S(2)}, u32[]{:S(2)}) collective-permute-start(f32[2,128,256]{2,1,0:T(8,128)S(1)} %get-tuple-element.72), channel_id=1, source_target_pairs={{0,240},{2,242},{4,244},{6,246},{8,248},{10,250},{12,252},{14,254}... | collective-permute-start | bytes 786440 | tf_op jit(solution)/shard_map/ppermute | solution.py:357
  107.6 14.7 %collective-permute-start.17 = (f32[2,256,256]{2,1,0:T(8,128)S(1)}, f32[2,256,256]{2,1,0:T(8,128)S(1)}, u32[]{:S(2)}, u32[]{:S(2)}) collective-permute-start(f32[2,256,256]{2,1,0:T(8,128)S(1)} %rows_first.1.refs_0_), channel_id=1, source_target_pairs={{0,1},{1,0},{2,3},{3,2},{4,5},{5,4},{6,7},{7,6},{8,9},{9,8},{10,11... | collective-permute-start | bytes 1572872 | tf_op jit(solution)/shard_map/ppermute | solution.py:361

commit v5 on v4

--- a/solution.py
+++ b/solution.py
@@ -249,7 +249,7 @@
     out_c[...] = canvas[:, :, h : h + n]
 
 
-def back_first(bar, probe, patch, diag, corner, mat, grad, emit):
+def back_first(info, bar, probe, patch, diag, corner, mat, keep, send, grad, emit):
     grad[...] = jnp.zeros_like(grad)
 
     def step(m):
@@ -261,22 +261,26 @@
         emit(m, o_re * b_re + o_im * b_im, o_re * b_im - o_im * b_re)
 
     each_mode(probe.shape[1], step)
-
-
-def back_first_kernel(bar, probe, patch, diag, corner, mat, grad, part):
+    part = info[4]
+    keep[0] = grad[part]
+    send[0] = grad[1 - part]
+
+
+def back_first_kernel(info, bar, probe, patch, diag, corner, mat, keep, send, part, grad):
     def emit(m, re, im):
         part[0, m] = re
         part[1, m] = im
 
-    back_first(bar, probe, patch, diag, corner, mat, grad, emit)
-
-
-def back_first_add_kernel(bar, probe, patch, diag, corner, mat, part, grad, total):
+    back_first(info, bar, probe, patch, diag, corner, mat, keep, send, grad, emit)
+
+
+def back_first_add_kernel(info, bar, probe, patch, diag, corner, mat, part, keep, send, total,
+                          grad):
     def emit(m, re, im):
         total[0, 0, m] = part[0, m] + re
         total[0, 1, m] = part[1, m] + im
 
-    back_first(bar, probe, patch, diag, corner, mat, grad, emit)
+    back_first(info, bar, probe, patch, diag, corner, mat, keep, send, grad, emit)
 
 
 def sides(info, canvas, out_a, out_b):
@@ -286,14 +290,20 @@
     out_b[...] = canvas[:, :, pl.ds(b, h)]
 
 
-def place_sides_kernel(off, info, grad0, grad1, out_a, out_b, canvas):
-    lay(off, (grad0, grad1), canvas)
+def lay_sums(off, parts, canvas, sums):
+    for slot in range(2):
+        sums[slot] = parts[2 * slot][...] + parts[2 * slot + 1][...]
+    lay(off, (sums.at[0], sums.at[1]), canvas)
+
+
+def place_sides_kernel(off, info, keep0, got0, keep1, got1, out_a, out_b, canvas, sums):
+    lay_sums(off, (keep0, got0, keep1, got1), canvas, sums)
     sides(info, canvas, out_a, out_b)
 
 
-def place_center_kernel(off, grad0, grad1, out_c, canvas):
-    lay(off, (grad0, grad1), canvas)
-    h = grad0.shape[-1] // 2
+def place_center_kernel(off, keep0, got0, keep1, got1, out_c, canvas, sums):
+    lay_sums(off, (keep0, got0, keep1, got1), canvas, sums)
+    h = keep0.shape[-1] // 2
     out_c[...] = canvas[:, :, h : 3 * h]
 
 
@@ -313,20 +323,41 @@
     )
 
 
-def fold_rows_kernel(info, mid, got_a, got_b, out):
+def fold_rows_kernel(info, mid, got_a, got_b, *outs):
     h = got_a.shape[1]
     ra, rb, row_ok = ends(info, 0, 0, h)
-    out[:, pl.ds(ra, h)] = mid[:, pl.ds(ra, h)] + got_a[...]
-    out[:, pl.ds(rb, h)] = mid[:, pl.ds(rb, h)] + kept(row_ok, got_b[...])
-
-
-def finish_kernel(mine_first, other_first, mine_last, other_last, out):
-    out[0, :, 0] = mine_first[...] + other_first[...]
-    out[0, :, 1] = mine_last[...] + other_last[...]
-
-
-def prepare_kernel(prop, probe, measured, order, order_t, dft_in, conj_in, diag, corner, right,
-                   back_diag, back_corner, back_right, probe_out, meas_out, dft_out, conj_out):
+    for plane, out in enumerate(outs):
+        out[0, pl.ds(ra, h)] = mid[plane, pl.ds(ra, h)] + got_a[plane]
+        out[0, pl.ds(rb, h)] = mid[plane, pl.ds(rb, h)] + kept(row_ok, got_b[plane])
+
+
+def finish_kernel(info, mine_first, other_first, mine_re, other_re, mine_im, other_im, out):
+    part = info[4]
+    out[0, part, 0] = mine_first[0]
+    out[0, 1 - part, 0] = other_first[0]
+    out[0, 0, 1] = mine_re[0] + other_re[0]
+    out[0, 1, 1] = mine_im[0] + other_im[0]
+
+
+def pick_corners_kernel(info, rows_a, rows_b, out_a, out_b):
+    h = out_a.shape[-1]
+    a, b, _ = ends(info, 1, 0, h)
+    for i, rows in enumerate((rows_a, rows_b)):
+        out_a[i] = rows[:, :, :, pl.ds(a, h)]
+        out_b[i] = rows[:, :, :, pl.ds(b, h)]
+
+
+def prepare_kernel(prop_in, probe_in, meas_in, order_in, order_t_in, dft_in, conj_in, diag, corner,
+                   right, back_diag, back_corner, back_right, probe_out, meas_out, dft_out,
+                   conj_out, prop, meas, order, order_t, sems):
+    moves = (
+        (prop_in, prop), (meas_in, meas), (order_in, order), (order_t_in, order_t),
+        (probe_in, probe_out), (dft_in, dft_out), (conj_in, conj_out),
+    )
+    copies = [pltpu.make_async_copy(a, b, sems.at[i]) for i, (a, b) in enumerate(moves)]
+    for copy in copies:
+        copy.start()
+    copies[0].wait()
     re, im = prop[0].astype(F32), prop[1].astype(F32)
     re_t, im_t = re.T, im.T
     for out, edge, pair in ((diag, corner, (re, im)), (back_diag, back_corner, (re_t, -im_t))):
@@ -336,14 +367,13 @@
         edge[...] = corners.astype(BF16)
     right[...] = right_form(re_t, im_t, jnp).astype(BF16)
     back_right[...] = right_form(re, -im, jnp).astype(BF16)
-    probe_out[...] = probe[...]
-    dft_out[...] = dft_in[...]
-    conj_out[...] = conj_in[...]
+    for copy in copies[1:]:
+        copy.wait()
     exact = functools.partial(
         jnp.dot, precision=lax.Precision.HIGHEST, preferred_element_type=F32
     )
-    for slot in range(measured.shape[0]):
-        meas_out[slot] = exact(exact(order[...], measured[slot]), order_t[...])
+    for slot in range(meas.shape[0]):
+        meas_out[slot] = exact(exact(order[...], meas[slot]), order_t[...])
 
 
 def swap(value, axis, second):
@@ -361,8 +391,9 @@
     return lax.ppermute(value, "mode", [(0, 1), (1, 0)])
 
 
-def call(kernel, name, outs, args, scratch=(), smem=1, after=()):
+def call(kernel, name, outs, args, scratch=(), smem=1, after=(), copies=0):
     vmem = pl.BlockSpec(memory_space=pltpu.VMEM)
+    held = pl.BlockSpec(memory_space=pltpu.HBM) if copies else vmem
     scalars = pl.BlockSpec(memory_space=pltpu.SMEM)
     n_args, n_after = len(args), len(after)
 
@@ -373,10 +404,11 @@
         run,
         out_shape=tuple(jax.ShapeDtypeStruct(shape, dtype) for shape, dtype in outs),
         in_specs=[scalars] * smem
-        + [vmem] * (n_args - smem)
+        + [held] * (n_args - smem)
         + [pl.BlockSpec(memory_space=pl.ANY)] * n_after,
         out_specs=tuple(vmem for _ in outs),
-        scratch_shapes=[pltpu.VMEM(shape, F32) for shape in scratch],
+        scratch_shapes=[pltpu.VMEM(shape, dtype) for shape, dtype in scratch]
+        + [pltpu.SemaphoreType.DMA((copies,))] * (copies > 0),
         compiler_params=pltpu.CompilerParams(vmem_limit_bytes=VMEM_LIMIT),
         name=name,
     )(*args, *after)
@@ -394,9 +426,8 @@
     row, col = tile // GY, tile % GY
     n_rows = lax.axis_size("tile") // GY
     odd_row, odd_col = row % 2 == 1, col % 2 == 1
-    info = jnp.stack(
-        [odd_row, odd_col, (row > 0) & (row < n_rows - 1), (col > 0) & (col < GY - 1)]
-    ).astype(jnp.int32)
+    paired = [(row > 0) & (row < n_rows - 1), (col > 0) & (col < GY - 1)]
+    info = jnp.stack([odd_row, odd_col, *paired, lax.axis_index("mode") == 1]).astype(jnp.int32)
 
     top, low = own[:, :, :h, :], own[:, :, h:, :]
     rows_a = swap(jnp.where(odd_row, top, low), 0, False)
@@ -404,11 +435,6 @@
     left, right = own[:, :, :, :h], own[:, :, :, h:]
     cols_a = swap(jnp.where(odd_col, left, right), 1, False)
     cols_b = swap(jnp.where(odd_col, right, left), 1, True)
-    strips = jnp.stack([rows_a, rows_b])
-    left, right = strips[..., :h], strips[..., h:]
-    corners_a = swap(jnp.where(odd_col, left, right), 1, False)
-    corners_b = swap(jnp.where(odd_col, right, left), 1, True)
-
     dft, conj_dft = dft_tables(n)
     order = np.eye(n, dtype=np.float32)[np.r_[0:n:2, 1:n:2]]
     plane, pair, mat = ((n, n), F32), ((2, n, n), F32), ((2 * n, 2 * n), BF16)
@@ -421,9 +447,20 @@
         band + band + (probes, ((slots, n, n), F32), tables, tables),
         (propagator, probe_modes, measured[0], jnp.asarray(order), jnp.asarray(order.T.copy()),
          jnp.asarray(dft), jnp.asarray(conj_dft)),
+        scratch=(((2, n, n), BF16), ((slots, n, n), F32), plane, plane),
         smem=0,
+        copies=7,
     )
     prop, back_prop = made[:3], made[3:]
+    quarter = ((2, 2, 2, h, h), F32)
+    corners_a, corners_b = call(
+        pick_corners_kernel,
+        "pick_corners",
+        (quarter, quarter),
+        (info, rows_a, rows_b),
+        after=(probe,),
+    )
+    corners_a, corners_b = swap(corners_a, 1, False), swap(corners_b, 1, True)
 
     canvas, patch0, wave0, far0, inten0 = call(
         forward_first_kernel,
@@ -443,58 +480,66 @@
 
     bar_out = ((modes, 2, n, n), BF16)
     strips = (((2, 2 * n, h), F32), ((2, 2 * n, n), F32), ((2, 2 * n, h), F32))
-    wide = (2, 2 * n, 2 * n)
+    wide = ((2, 2 * n, 2 * n), F32)
     grad_last0, bar0 = call(
         functools.partial(back_last, 0),
         "back_last_0",
         (pair, bar_out),
         (counts, inten0, other0, measured, far0, wave0, patch0, conj_dft),
-        scratch=((2, n, n),),
-    )
-    grad_first0, part = call(
+        scratch=(pair,),
+    )
+    one = ((1, n, n), F32)
+    keep0, send0, part = call(
         back_first_kernel,
         "back_first_0",
-        (pair, probes),
-        (bar0, probe, patch0, *back_prop),
-        smem=0,
-    )
+        (one, one, probes),
+        (info, bar0, probe, patch0, *back_prop),
+        scratch=(pair,),
+    )
+    got0 = swap_mode(send0)
     bar1, out_a, out_c, out_b = call(
         functools.partial(back_last_place_kernel, 1),
         "back_last_1",
         (bar_out,) + strips,
         (counts, off, info, grad_last0, inten1, other1, measured, far1, wave1, patch1, conj_dft),
-        scratch=((2, n, n), (2, n, n), wide),
+        scratch=(pair, pair, wide),
         smem=3,
-        after=(grad_first0,),
-    )
-
-    half = ((2, h, n), F32)
+        after=(keep0,),
+    )
 
     def fold_cols(name, out_a, out_c, out_b, after):
         got_a, got_b = swap(out_a, 1, False), swap(out_b, 1, True)
-        return call(fold_cols_kernel, name, (half, pair, half), (info, out_c, got_a, got_b),
+        planes = out_c.shape[0]
+        half, mid = ((planes, h, n), F32), ((planes, n, n), F32)
+        return call(fold_cols_kernel, name, (half, mid, half), (info, out_c, got_a, got_b),
                     after=after)
 
     def fold_rows(name, out_a, mid, out_b, after):
         got_a, got_b = swap(out_a, 0, False), swap(out_b, 0, True)
-        return call(fold_rows_kernel, name, (pair,), (info, mid, got_a, got_b), after=after)[0]
-
-    grad_first1, probe_grad = call(
+        return call(fold_rows_kernel, name, (one,) * mid.shape[0], (info, mid, got_a, got_b),
+                    after=after)
+
+    keep1, send1, probe_grad = call(
         back_first_add_kernel,
         "back_first_1",
-        (pair, ((1, 2, modes, n, n), F32)),
-        (bar1, probe, patch1, *back_prop, part),
-        smem=0,
-    )
-    strips_last = fold_cols("cols_last", out_a, out_c, out_b, (grad_first1,))
-    mine_last = fold_rows("rows_last", *strips_last, ())
-    other_last = swap_mode(mine_last)
+        (one, one, ((1, 2, modes, n, n), F32)),
+        (info, bar1, probe, patch1, *back_prop, part),
+        scratch=(pair,),
+        after=(),
+    )
+    got1 = swap_mode(send1)
+    strips_last = fold_cols("cols_last", out_a, out_c, out_b, (keep1,))
+    mine_re, mine_im = fold_rows("rows_last", *strips_last, ())
+    other_re, other_im = swap_mode(mine_re), swap_mode(mine_im)
+    strips = [((1,) + shape[1:], dtype) for shape, dtype in strips]
+    wide = ((1, 2 * n, 2 * n), F32)
+    parts = (keep0, got0, keep1, got1)
     out_a, out_b = call(
         place_sides_kernel,
         "place_sides",
         (strips[0], strips[2]),
-        (off, info, grad_first0, grad_first1),
-        scratch=(wide,),
+        (off, info, *parts),
+        scratch=(wide, ((2, 1, n, n), F32)),
         smem=2,
         after=(strips_last[0],),
     )
@@ -502,19 +547,18 @@
         place_center_kernel,
         "place_center",
         (strips[1],),
-        (off, grad_first0, grad_first1),
-        scratch=(wide,),
+        (off, *parts),
+        scratch=(wide, ((2, 1, n, n), F32)),
         after=(out_a,),
     )
     strips_first = fold_cols("cols_first", out_a, out_c, out_b, ())
-    mine_first = fold_rows("rows_first", *strips_first, (other_last,))
+    (mine_first,) = fold_rows("rows_first", *strips_first, (other_re,))
     other_first = swap_mode(mine_first)
     (object_grad,) = call(
         finish_kernel,
         "finish",
         ((object_tiles.shape, F32),),
-        (mine_first, other_first, mine_last, other_last),
-        smem=0,
+        (info, mine_first, other_first, mine_re, other_re, mine_im, other_im),
     )
     return (object_grad, probe_grad)
 

time: 124 us -> 117 us (0.944)
  the two profiles are of different devices: /device:TPU:6 before, /device:TPU:1 now
where the time goes in v5:
time: 117 us
  starting transfers between devices  43.9 us (38%)
  Pallas kernels  37.3 us (32%)
  waiting for transfers between devices  24 us (21%)
  local copies, waits for them, and re-layouts  5.14 us (4%)
  other arithmetic  4.72 us (4%)
  between operations  1.5 us (1%)
    pallas_call x15, Pallas kernels, call(): pl.pallas_call(run, out_shape=tuple((jax.ShapeDtypeStruct(shape, dtype) f...  37.3 us
    ppermute x14, starting transfers between devices, swap(): return lax.ppermute(value, 'tile', pairs)  30.2 us
    ppermute x7, waiting for transfers between devices, swap_mode(): return lax.ppermute(value, 'mode', [(0, 1), (1, 0)])  14.1 us
    ppermute x7, starting transfers between devices, swap_mode(): return lax.ppermute(value, 'mode', [(0, 1), (1, 0)])  13.8 us
    ppermute x14, waiting for transfers between devices, swap(): return lax.ppermute(value, 'tile', pairs)  9.89 us
    unnamed x18, local copies, waits for them, and re-layouts  5.04 us
    select_n x1, other arithmetic, body(): rows_b = swap(jnp.where(odd_row, low, top), 0, True)  2.43 us
  transfers between devices with their start and end apart: 21, of which 10 were waited for; matrix products, arithmetic and copies ran while one was open for 2% of the time, Pallas kernels for 21%

profile of v5, /device:TPU:1, one launch (start us, length us, event | category | flops | bytes accessed | tf_op | source)
XLA Modules:
  0.0 116.5 jit_solution(11174150721028958336)
XLA Ops:
  0.7 2.4 %slice_select_fusion.2 = (f32[2,2,128,256]{3,2,1,0:T(8,128)}, f32[2,2,128,256]{3,2,1,0:T(8,128)}) fusion(f32[2,2,256,256]{3,2,1,0:T(8,128)} %bitcast.8, pred[]{:T(512)} %eq.13), kind=kLoop, calls=%fused_computation.2 | loop fusion | flops 262144 | bytes 2097153 | tf_op jit(solution)/shard_map/jit(_where)/select_n | solution.py:434
  3.1 7.4 %collective-permute-start.1 = (f32[2,2,128,256]{3,2,1,0:T(8,128)}, f32[2,2,128,256]{3,2,1,0:T(8,128)}, u32[]{:S(2)}, u32[]{:S(2)}) collective-permute-start(f32[2,2,128,256]{3,2,1,0:T(8,128)} %get-tuple-element.90), channel_id=1, source_target_pairs={{0,240},{2,242},{4,244},{6,246},{8,248},{10,250},{12,252},{14,254}... | collective-permute-start | bytes 1572872 | tf_op jit(solution)/shard_map/ppermute | solution.py:387
  10.5 2.3 %slice_select_fusion = (f32[2,2,256,128]{3,2,1,0:T(8,128)}, f32[2,2,256,128]{3,2,1,0:T(8,128)}) fusion(f32[2,2,256,256]{3,2,1,0:T(8,128)} %bitcast.9, pred[]{:T(512)} %eq.14), kind=kLoop, calls=%fused_computation | loop fusion | flops 262144 | bytes 2097153 | tf_op jit(solution)/shard_map/jit(_where)/select_n | solution.py:437
  12.8 2.1 %collective-permute-start.3 = (f32[2,2,256,128]{3,2,1,0:T(8,128)}, f32[2,2,256,128]{3,2,1,0:T(8,128)}, u32[]{:S(2)}, u32[]{:S(2)}) collective-permute-start(f32[2,2,256,128]{3,2,1,0:T(8,128)} %get-tuple-element.88), channel_id=1, source_target_pairs={{0,14},{2,4},{4,2},{6,8},{8,6},{10,12},{12,10},{14,0},{16,30},{18,... | collective-permute-start | bytes 1572872 | tf_op jit(solution)/shard_map/ppermute | solution.py:387
  16.9 1.0 copy-done.3
  17.9 1.0 copy-done.4
  20.8 2.2 %prepare.1 = (bf16[2,256,256]{2,1,0:T(8,128)(2,1)S(1)}, bf16[64,64]{1,0:T(8,128)(2,1)S(1)}, bf16[512,512]{1,0:T(8,128)(2,1)S(1)}, bf16[2,256,256]{2,1,0:T(8,128)...) custom-call(bf16[2,256,256]{2,1,0:T(8,128)(2,1)S(1)} %copy-done.5, ...), custom_call_target="tpu_custom_call" | custom-call | tf_op jit(solution)/shard_map/prepare/pallas_call | solution.py:403
  23.3 1.3 %pick_corners.1 = (f32[2,2,2,128,128]{4,3,2,1,0:T(8,128)S(1)}, f32[2,2,2,128,128]{4,3,2,1,0:T(8,128)S(1)}) custom-call(s32[5]{0:T(128)S(1)} %convert_element_type.3.refs_0_.refs_1_.refs_2_, f32[2,2,128,256]{3,2,1,0:T(8,128)} %collective-permute-done.refs_1_.refs_3_, f32[2,2,128,256]{3,2,1,0:T(8,128)} %collective-permute-done.1.refs_2_.refs_4_, ...), custom_call_target="tpu_custom_call" | custom-call | tf_op jit(solution)/shard_map/pick_corners/pallas_call | solution.py:403
  24.6 1.9 %collective-permute-start.4 = (f32[2,2,2,128,128]{4,3,2,1,0:T(8,128)S(1)}, f32[2,2,2,128,128]{4,3,2,1,0:T(8,128)S(1)}, u32[]{:S(2)}, u32[]{:S(2)}) collective-permute-start(f32[2,2,2,128,128]{4,3,2,1,0:T(8,128)S(1)} %get-tuple-element.46), channel_id=1, source_target_pairs={{0,2},{2,0},{4,6},{6,4},{8,10},{10,8},{12,14},{14,12},{16,18},{18,... | collective-permute-start | bytes 1572872 | tf_op jit(solution)/shard_map/ppermute | solution.py:387
  26.6 1.2 %collective-permute-start.5 = (f32[2,2,2,128,128]{4,3,2,1,0:T(8,128)S(1)}, f32[2,2,2,128,128]{4,3,2,1,0:T(8,128)S(1)}, u32[]{:S(2)}, u32[]{:S(2)}) collective-permute-start(f32[2,2,2,128,128]{4,3,2,1,0:T(8,128)S(1)} %get-tuple-element.47), channel_id=1, source_target_pairs={{0,14},{2,4},{4,2},{6,8},{8,6},{10,12},{12,10},{14,0},{16,30},{18,... | collective-permute-start | bytes 1572872 | tf_op jit(solution)/shard_map/ppermute | solution.py:387
  28.1 7.4 %collective-permute-done.5.refs_8_ = f32[2,2,2,128,128]{4,3,2,1,0:T(8,128)S(1)} collective-permute-done((f32[2,2,2,128,128]{4,3,2,1,0:T(8,128)S(1)}, f32[2,2,2,128,128]{4,3,2,1,0:T(8,128)S(1)}, u32[]{:S(2)}, u32[]{:S(2)}) %collective-permute-start.5) | collective-permute-done | bytes 524320 | tf_op jit(solution)/shard_map/ppermute | solution.py:387
  35.5 7.5 %forward_0.1 = (f32[2,2,512,512]{3,2,1,0:T(8,128)S(1)}, f32[2,2,256,256]{3,2,1,0:T(8,128)S(1)}, f32[6,2,256,256]{3,2,1,0:T(8,128)S(1)}, f32[6,2,256,256]{3,2,1,0:T(8,128)S(1)}, f32[256,256]{1,0:T(8,128)S(1)}) custom-call(s32[2,2]{1,0:T(2,128)S(1)} %bitcast.12, s32[5]{0:T(128)S(1)} %convert_element_type.3.refs_0_.refs_1_.refs_2_, ...), custom_call_target="tpu_custom_call" | custom-call | tf_op jit(solution)/shard_map/forward_0/pallas_call | solution.py:403
  43.0 2.9 %collective-permute-start.6 = (f32[256,256]{1,0:T(8,128)S(1)}, f32[256,256]{1,0:T(8,128)S(1)}, u32[]{:S(2)}, u32[]{:S(2)}) collective-permute-start(f32[256,256]{1,0:T(8,128)S(1)} %get-tuple-element.52.refs_1_), channel_id=1, source_target_pairs={{0,1},{1,0},{2,3},{3,2},{4,5},{5,4},{6,7},{7,6},{8,9},{9,8},{10,11... | collective-permute-start | bytes 786440 | tf_op jit(solution)/shard_map/ppermute | solution.py:391
  45.9 6.0 %forward_1.1 = (f32[2,2,256,256]{3,2,1,0:T(8,128)S(1)}, f32[6,2,256,256]{3,2,1,0:T(8,128)S(1)}, f32[6,2,256,256]{3,2,1,0:T(8,128)S(1)}, f32[256,256]{1,0:T(8,128)S(1)}) custom-call(s32[2,2]{1,0:T(2,128)S(1)} %bitcast.13, f32[2,2,512,512]{3,2,1,0:T(8,128)S(1)} %get-tuple-element.65.refs_1_, f32[2,6,256,256]{3,2,1,0:T(8,128)S(1)} %get-tuple-element.45.refs_3_.refs_9_.refs_2_, ...), custom_call_target="tpu_custom_call" | custom-call | tf_op jit(solution)/shard_map/forward_1/pallas_call | solution.py:403
  53.0 2.3 %back_last_0.1 = (f32[2,256,256]{2,1,0:T(8,128)S(1)}, bf16[6,2,256,256]{3,2,1,0:T(8,128)(2,1)S(1)}) custom-call(s32[1]{0:T(128)S(6)} %copy.12.refs_0_, f32[256,256]{1,0:T(8,128)S(1)} %get-tuple-element.52.refs_1_, f32[256,256]{1,0:T(8,128)S(1)} %collective-permute-done.6.refs_2_, f32[2,256,256]{2,1,0:T(8,128)S(1)} %get-tuple-element.53.refs_3_.refs_6_, ...), custom_call_target="tpu_custom_call" | custom-call | tf_op jit(solution)/shard_map/back_last_0/pallas_call | solution.py:403
  55.3 3.1 %back_first_0.1 = (f32[1,256,256]{2,1,0:T(8,128)S(1)}, f32[1,256,256]{2,1,0:T(8,128)S(1)}, f32[2,6,256,256]{3,2,1,0:T(8,128)S(1)}) custom-call(s32[5]{0:T(128)S(1)} %convert_element_type.3.refs_0_.refs_1_.refs_2_, bf16[6,2,256,256]{3,2,1,0:T(8,128)(2,1)S(1)} %get-tuple-element.58.refs_1_, f32[2,6,256,256]{3,2,1,0:T(8,128)S(1)} %get-tuple-element.45.refs_3_.refs_9_.refs_2_, ...), custom_call_target="tpu_custom_call" | custom-call | tf_op jit(solution)/shard_map/back_first_0/pallas_call | solution.py:403
  58.5 1.5 %collective-permute-done.8.refs_5_ = f32[256,256]{1,0:T(8,128)S(1)} collective-permute-done((f32[256,256]{1,0:T(8,128)S(1)}, f32[256,256]{1,0:T(8,128)S(1)}, u32[]{:S(2)}, u32[]{:S(2)}) %collective-permute-start.8) | collective-permute-done | bytes 262176 | tf_op jit(solution)/shard_map/ppermute | solution.py:391
  60.0 3.8 %back_last_1.1 = (bf16[6,2,256,256]{3,2,1,0:T(8,128)(2,1)S(1)}, f32[2,512,128]{2,1,0:T(8,128)S(1)}, f32[2,512,256]{2,1,0:T(8,128)S(1)}, f32[2,512,128]{2,1,0:T(8,128)S(1)}) custom-call(s32[1]{0:T(128)S(6)} %copy.12.refs_0_, s32[2,2]{1,0:T(2,128)S(1)} %bitcast.14, s32[5]{0:T(128)S(1)} %convert_element_type.3.refs_0_.refs_1_.refs_2_, ...), custom_call_target="tpu_custom_call" | custom-call | tf_op jit(solution)/shard_map/back_last_1/pallas_call | solution.py:403
  63.8 2.3 %collective-permute-start.10 = (f32[2,512,128]{2,1,0:T(8,128)S(1)}, f32[2,512,128]{2,1,0:T(8,128)S(1)}, u32[]{:S(2)}, u32[]{:S(2)}) collective-permute-start(f32[2,512,128]{2,1,0:T(8,128)S(1)} %get-tuple-element.75), channel_id=1, source_target_pairs={{0,2},{2,0},{4,6},{6,4},{8,10},{10,8},{12,14},{14,12},{16,18},{18,... | collective-permute-start | bytes 1572872 | tf_op jit(solution)/shard_map/ppermute | solution.py:387
  67.3 5.0 %back_first_1.1 = (f32[1,256,256]{2,1,0:T(8,128)S(1)}, f32[1,256,256]{2,1,0:T(8,128)S(1)}, f32[1,2,6,256,256]{4,3,2,1,0:T(8,128)}) custom-call(s32[5]{0:T(128)S(1)} %convert_element_type.3.refs_0_.refs_1_.refs_2_, bf16[6,2,256,256]{3,2,1,0:T(8,128)(2,1)S(1)} %get-tuple-element.70.refs_1_, f32[2,6,256,256]{3,2,1,0:T(8,128)S(1)} %get-tuple-element.45.refs_3_.refs_9_.refs_2_, ...), custom_call_target="tpu_custom_call" | custom-call | tf_op jit(solution)/shard_map/back_first_1/pallas_call | solution.py:403
  72.3 2.6 %collective-permute-start.9 = (f32[1,256,256]{2,1,0:T(8,128)S(1)}, f32[1,256,256]{2,1,0:T(8,128)S(1)}, u32[]{:S(2)}, u32[]{:S(2)}) collective-permute-start(f32[1,256,256]{2,1,0:T(8,128)S(1)} %get-tuple-element.73), channel_id=1, source_target_pairs={{0,1},{1,0},{2,3},{3,2},{4,5},{5,4},{6,7},{7,6},{8,9},{9,8},{10,11... | collective-permute-start | bytes 786440 | tf_op jit(solution)/shard_map/ppermute | solution.py:391
  75.7 1.6 %collective-permute-start.17 = (f32[2,128,256]{2,1,0:T(8,128)S(1)}, f32[2,128,256]{2,1,0:T(8,128)S(1)}, u32[]{:S(2)}, u32[]{:S(2)}) collective-permute-start(f32[2,128,256]{2,1,0:T(8,128)S(1)} %get-tuple-element.84), channel_id=1, source_target_pairs={{0,240},{2,242},{4,244},{6,246},{8,248},{10,250},{12,252},{14,254}... | collective-permute-start | bytes 786440 | tf_op jit(solution)/shard_map/ppermute | solution.py:387
  77.3 2.5 %collective-permute-done.9.refs_5_.refs_4_ = f32[1,256,256]{2,1,0:T(8,128)S(1)} collective-permute-done((f32[1,256,256]{2,1,0:T(8,128)S(1)}, f32[1,256,256]{2,1,0:T(8,128)S(1)}, u32[]{:S(2)}, u32[]{:S(2)}) %collective-permute-start.9) | collective-permute-done | bytes 262176 | tf_op jit(solution)/shard_map/ppermute | solution.py:391
  80.8 9.9 %collective-permute-start.13 = (f32[1,512,128]{2,1,0:T(8,128)S(1)}, f32[1,512,128]{2,1,0:T(8,128)S(1)}, u32[]{:S(2)}, u32[]{:S(2)}) collective-permute-start(f32[1,512,128]{2,1,0:T(8,128)S(1)} %get-tuple-element.79), channel_id=1, source_target_pairs={{0,14},{2,4},{4,2},{6,8},{8,6},{10,12},{12,10},{14,0},{16,30},{18,... | collective-permute-start | bytes 786440 | tf_op jit(solution)/shard_map/ppermute | solution.py:387
  91.3 2.4 %collective-permute-start.18 = (f32[1,256,256]{2,1,0:T(8,128)S(1)}, f32[1,256,256]{2,1,0:T(8,128)S(1)}, u32[]{:S(2)}, u32[]{:S(2)}) collective-permute-start(f32[1,256,256]{2,1,0:T(8,128)S(1)} %get-tuple-element.85.refs_3_), channel_id=1, source_target_pairs={{0,1},{1,0},{2,3},{3,2},{4,5},{5,4},{6,7},{7,6},{8,9},{9,8},{10,11... | collective-permute-start | bytes 786440 | tf_op jit(solution)/shard_map/ppermute | solution.py:391
  95.8 1.9 %collective-permute-start.15 = (f32[1,128,256]{2,1,0:T(8,128)S(1)}, f32[1,128,256]{2,1,0:T(8,128)S(1)}, u32[]{:S(2)}, u32[]{:S(2)}) collective-permute-start(f32[1,128,256]{2,1,0:T(8,128)S(1)} %get-tuple-element.82), channel_id=1, source_target_pairs={{0,240},{2,242},{4,244},{6,246},{8,248},{10,250},{12,252},{14,254}... | collective-permute-start | bytes 393224 | tf_op jit(solution)/shard_map/ppermute | solution.py:387
  97.7 2.6 %collective-permute-start.20 = (f32[1,256,256]{2,1,0:T(8,128)S(1)}, f32[1,256,256]{2,1,0:T(8,128)S(1)}, u32[]{:S(2)}, u32[]{:S(2)}) collective-permute-start(f32[1,256,256]{2,1,0:T(8,128)S(1)} %get-tuple-element.86.refs_5_), channel_id=1, source_target_pairs={{0,1},{1,0},{2,3},{3,2},{4,5},{5,4},{6,7},{7,6},{8,9},{9,8},{10,11... | collective-permute-start | bytes 786440 | tf_op jit(solution)/shard_map/ppermute | solution.py:391
  100.3 1.5 %collective-permute-done.15.refs_3_ = f32[1,128,256]{2,1,0:T(8,128)S(1)} collective-permute-done((f32[1,128,256]{2,1,0:T(8,128)S(1)}, f32[1,128,256]{2,1,0:T(8,128)S(1)}, u32[]{:S(2)}, u32[]{:S(2)}) %collective-permute-start.15) | collective-permute-done | bytes 131104 | tf_op jit(solution)/shard_map/ppermute | solution.py:387
  102.4 2.4 %collective-permute-start.19 = (f32[1,256,256]{2,1,0:T(8,128)S(1)}, f32[1,256,256]{2,1,0:T(8,128)S(1)}, u32[]{:S(2)}, u32[]{:S(2)}) collective-permute-start(f32[1,256,256]{2,1,0:T(8,128)S(1)} %rows_first.1.refs_1_), channel_id=1, source_target_pairs={{0,1},{1,0},{2,3},{3,2},{4,5},{5,4},{6,7},{7,6},{8,9},{9,8},{10,11... | collective-permute-start | bytes 786440 | tf_op jit(solution)/shard_map/ppermute | solution.py:391
  104.9 4.5 %collective-permute-done.20.refs_6_ = f32[1,256,256]{2,1,0:T(8,128)S(1)} collective-permute-done((f32[1,256,256]{2,1,0:T(8,128)S(1)}, f32[1,256,256]{2,1,0:T(8,128)S(1)}, u32[]{:S(2)}, u32[]{:S(2)}) %collective-permute-start.20) | collective-permute-done | bytes 262176 | tf_op jit(solution)/shard_map/ppermute | solution.py:391
  109.3 5.6 %collective-permute-done.19.refs_2_ = f32[1,256,256]{2,1,0:T(8,128)S(1)} collective-permute-done((f32[1,256,256]{2,1,0:T(8,128)S(1)}, f32[1,256,256]{2,1,0:T(8,128)S(1)}, u32[]{:S(2)}, u32[]{:S(2)}) %collective-permute-start.19) | collective-permute-done | bytes 262176 | tf_op jit(solution)/shard_map/ppermute | solution.py:391
  114.9 1.6 %finish.1 = f32[1,2,2,256,256]{4,3,2,1,0:T(8,128)} custom-call(s32[5]{0:T(128)S(1)} %convert_element_type.3.refs_0_.refs_1_.refs_2_, f32[1,256,256]{2,1,0:T(8,128)S(1)} %rows_first.1.refs_1_, f32[1,256,256]{2,1,0:T(8,128)S(1)} %collective-permute-done.19.refs_2_, f32[1,256,256]{2,1,0:T(8,128)S(1)} %get-tuple-element.85.refs_3_, ...), custom_call_target="tpu_custom_call" | custom-call | tf_op jit(solution)/shard_map/finish/pallas_call | solution.py:403
  (47 shorter events, 11.2 us)
Async XLA Ops:
  0.6 15.2 %copy-start.5 = (bf16[2,256,256]{2,1,0:T(8,128)(2,1)S(1)}, bf16[2,256,256]{2,1,0:T(8,128)(2,1)}, u32[]{:S(2)}) copy-start(bf16[2,256,256]{2,1,0:T(8,128)(2,1)} %refs_0_.3) | copy-start | bytes 786436
  0.6 15.2 %copy-start.1 = (f32[2,6,256,256]{3,2,1,0:T(8,128)S(1)}, f32[2,6,256,256]{3,2,1,0:T(8,128)}, u32[]{:S(2)}) copy-start(f32[2,6,256,256]{3,2,1,0:T(8,128)} %refs_1_.1) | copy-start | bytes 9437188
  3.1 19.9 %collective-permute-start.1 = (f32[2,2,128,256]{3,2,1,0:T(8,128)}, f32[2,2,128,256]{3,2,1,0:T(8,128)}, u32[]{:S(2)}, u32[]{:S(2)}) collective-permute-start(f32[2,2,128,256]{3,2,1,0:T(8,128)} %get-tuple-element.90), channel_id=1, source_target_pairs={{0,240},{2,242},{4,244},{6,246},{8,248},{10,250},{12,252},{14,254}... | collective-permute-start | bytes 1572872 | tf_op jit(solution)/shard_map/ppermute | solution.py:387
  10.5 12.8 %collective-permute-start = (f32[2,2,128,256]{3,2,1,0:T(8,128)}, f32[2,2,128,256]{3,2,1,0:T(8,128)}, u32[]{:S(2)}, u32[]{:S(2)}) collective-permute-start(f32[2,2,128,256]{3,2,1,0:T(8,128)} %get-tuple-element.91), channel_id=1, source_target_pairs={{0,16},{2,18},{4,20},{6,22},{8,24},{10,26},{12,28},{14,30},{16,0},... | collective-permute-start | bytes 1572872 | tf_op jit(solution)/shard_map/ppermute | solution.py:387
  12.8 14.9 %collective-permute-start.3 = (f32[2,2,256,128]{3,2,1,0:T(8,128)}, f32[2,2,256,128]{3,2,1,0:T(8,128)}, u32[]{:S(2)}, u32[]{:S(2)}) collective-permute-start(f32[2,2,256,128]{3,2,1,0:T(8,128)} %get-tuple-element.88), channel_id=1, source_target_pairs={{0,14},{2,4},{4,2},{6,8},{8,6},{10,12},{12,10},{14,0},{16,30},{18,... | collective-permute-start | bytes 1572872 | tf_op jit(solution)/shard_map/ppermute | solution.py:387
  14.9 12.9 %collective-permute-start.2 = (f32[2,2,256,128]{3,2,1,0:T(8,128)}, f32[2,2,256,128]{3,2,1,0:T(8,128)}, u32[]{:S(2)}, u32[]{:S(2)}) collective-permute-start(f32[2,2,256,128]{3,2,1,0:T(8,128)} %get-tuple-element.89), channel_id=1, source_target_pairs={{0,2},{2,0},{4,6},{6,4},{8,10},{10,8},{12,14},{14,12},{16,18},{18,... | collective-permute-start | bytes 1572872 | tf_op jit(solution)/shard_map/ppermute | solution.py:387
  15.8 1.0 copy-start.2
  16.9 1.0 copy-start.3
  17.9 1.0 copy-start.4
  18.9 0.9 copy-start.6
  19.9 0.9 copy-start.7
  23.0 12.5 %copy-start = (f32[1,2,2,256,256]{4,3,2,1,0:T(8,128)S(1)}, f32[1,2,2,256,256]{4,3,2,1,0:T(8,128)}, u32[]{:S(2)}) copy-start(f32[1,2,2,256,256]{4,3,2,1,0:T(8,128)} %param.10) | copy-start | bytes 3145732
  23.0 12.5 %copy-start.8 = (s32[1,2,2]{2,1,0:T(2,128)S(1)}, s32[1,2,2]{2,1,0:T(2,128)}, u32[]{:S(2)}) copy-start(s32[1,2,2]{2,1,0:T(2,128)} %param.13) | copy-start | bytes 52
  24.6 3.5 %collective-permute-start.4 = (f32[2,2,2,128,128]{4,3,2,1,0:T(8,128)S(1)}, f32[2,2,2,128,128]{4,3,2,1,0:T(8,128)S(1)}, u32[]{:S(2)}, u32[]{:S(2)}) collective-permute-start(f32[2,2,2,128,128]{4,3,2,1,0:T(8,128)S(1)} %get-tuple-element.46), channel_id=1, source_target_pairs={{0,2},{2,0},{4,6},{6,4},{8,10},{10,8},{12,14},{14,12},{16,18},{18,... | collective-permute-start | bytes 1572872 | tf_op jit(solution)/shard_map/ppermute | solution.py:387
  26.6 8.9 %collective-permute-start.5 = (f32[2,2,2,128,128]{4,3,2,1,0:T(8,128)S(1)}, f32[2,2,2,128,128]{4,3,2,1,0:T(8,128)S(1)}, u32[]{:S(2)}, u32[]{:S(2)}) collective-permute-start(f32[2,2,2,128,128]{4,3,2,1,0:T(8,128)S(1)} %get-tuple-element.47), channel_id=1, source_target_pairs={{0,14},{2,4},{4,2},{6,8},{8,6},{10,12},{12,10},{14,0},{16,30},{18,... | collective-permute-start | bytes 1572872 | tf_op jit(solution)/shard_map/ppermute | solution.py:387
  43.0 10.0 %collective-permute-start.6 = (f32[256,256]{1,0:T(8,128)S(1)}, f32[256,256]{1,0:T(8,128)S(1)}, u32[]{:S(2)}, u32[]{:S(2)}) collective-permute-start(f32[256,256]{1,0:T(8,128)S(1)} %get-tuple-element.52.refs_1_), channel_id=1, source_target_pairs={{0,1},{1,0},{2,3},{3,2},{4,5},{5,4},{6,7},{7,6},{8,9},{9,8},{10,11... | collective-permute-start | bytes 786440 | tf_op jit(solution)/shard_map/ppermute | solution.py:391
  51.9 8.1 %collective-permute-start.8 = (f32[256,256]{1,0:T(8,128)S(1)}, f32[256,256]{1,0:T(8,128)S(1)}, u32[]{:S(2)}, u32[]{:S(2)}) collective-permute-start(f32[256,256]{1,0:T(8,128)S(1)} %get-tuple-element.66.refs_4_), channel_id=1, source_target_pairs={{0,1},{1,0},{2,3},{3,2},{4,5},{5,4},{6,7},{7,6},{8,9},{9,8},{10,11... | collective-permute-start | bytes 786440 | tf_op jit(solution)/shard_map/ppermute | solution.py:391
  63.8 11.1 %collective-permute-start.10 = (f32[2,512,128]{2,1,0:T(8,128)S(1)}, f32[2,512,128]{2,1,0:T(8,128)S(1)}, u32[]{:S(2)}, u32[]{:S(2)}) collective-permute-start(f32[2,512,128]{2,1,0:T(8,128)S(1)} %get-tuple-element.75), channel_id=1, source_target_pairs={{0,2},{2,0},{4,6},{6,4},{8,10},{10,8},{12,14},{14,12},{16,18},{18,... | collective-permute-start | bytes 1572872 | tf_op jit(solution)/shard_map/ppermute | solution.py:387
  66.1 8.9 %collective-permute-start.11 = (f32[2,512,128]{2,1,0:T(8,128)S(1)}, f32[2,512,128]{2,1,0:T(8,128)S(1)}, u32[]{:S(2)}, u32[]{:S(2)}) collective-permute-start(f32[2,512,128]{2,1,0:T(8,128)S(1)} %get-tuple-element.76), channel_id=1, source_target_pairs={{0,14},{2,4},{4,2},{6,8},{8,6},{10,12},{12,10},{14,0},{16,30},{18,... | collective-permute-start | bytes 1572872 | tf_op jit(solution)/shard_map/ppermute | solution.py:387
  67.0 10.3 %collective-permute-start.7 = (f32[1,256,256]{2,1,0:T(8,128)S(1)}, f32[1,256,256]{2,1,0:T(8,128)S(1)}, u32[]{:S(2)}, u32[]{:S(2)}) collective-permute-start(f32[1,256,256]{2,1,0:T(8,128)S(1)} %get-tuple-element.63), channel_id=1, source_target_pairs={{0,1},{1,0},{2,3},{3,2},{4,5},{5,4},{6,7},{7,6},{8,9},{9,8},{10,11... | collective-permute-start | bytes 786440 | tf_op jit(solution)/shard_map/ppermute | solution.py:391
  72.3 7.4 %collective-permute-start.9 = (f32[1,256,256]{2,1,0:T(8,128)S(1)}, f32[1,256,256]{2,1,0:T(8,128)S(1)}, u32[]{:S(2)}, u32[]{:S(2)}) collective-permute-start(f32[1,256,256]{2,1,0:T(8,128)S(1)} %get-tuple-element.73), channel_id=1, source_target_pairs={{0,1},{1,0},{2,3},{3,2},{4,5},{5,4},{6,7},{7,6},{8,9},{9,8},{10,11... | collective-permute-start | bytes 786440 | tf_op jit(solution)/shard_map/ppermute | solution.py:391
  75.7 15.0 %collective-permute-start.17 = (f32[2,128,256]{2,1,0:T(8,128)S(1)}, f32[2,128,256]{2,1,0:T(8,128)S(1)}, u32[]{:S(2)}, u32[]{:S(2)}) collective-permute-start(f32[2,128,256]{2,1,0:T(8,128)S(1)} %get-tuple-element.84), channel_id=1, source_target_pairs={{0,240},{2,242},{4,244},{6,246},{8,248},{10,250},{12,252},{14,254}... | collective-permute-start | bytes 786440 | tf_op jit(solution)/shard_map/ppermute | solution.py:387
  77.3 13.4 %collective-permute-start.16 = (f32[2,128,256]{2,1,0:T(8,128)S(1)}, f32[2,128,256]{2,1,0:T(8,128)S(1)}, u32[]{:S(2)}, u32[]{:S(2)}) collective-permute-start(f32[2,128,256]{2,1,0:T(8,128)S(1)} %get-tuple-element.77.refs_6_), channel_id=1, source_target_pairs={{0,16},{2,18},{4,20},{6,22},{8,24},{10,26},{12,28},{14,30},{16,0},... | collective-permute-start | bytes 786440 | tf_op jit(solution)/shard_map/ppermute | solution.py:387
  80.8 14.3 %collective-permute-start.13 = (f32[1,512,128]{2,1,0:T(8,128)S(1)}, f32[1,512,128]{2,1,0:T(8,128)S(1)}, u32[]{:S(2)}, u32[]{:S(2)}) collective-permute-start(f32[1,512,128]{2,1,0:T(8,128)S(1)} %get-tuple-element.79), channel_id=1, source_target_pairs={{0,14},{2,4},{4,2},{6,8},{8,6},{10,12},{12,10},{14,0},{16,30},{18,... | collective-permute-start | bytes 786440 | tf_op jit(solution)/shard_map/ppermute | solution.py:387
  90.7 4.4 %collective-permute-start.12 = (f32[1,512,128]{2,1,0:T(8,128)S(1)}, f32[1,512,128]{2,1,0:T(8,128)S(1)}, u32[]{:S(2)}, u32[]{:S(2)}) collective-permute-start(f32[1,512,128]{2,1,0:T(8,128)S(1)} %get-tuple-element.78.refs_5_), channel_id=1, source_target_pairs={{0,2},{2,0},{4,6},{6,4},{8,10},{10,8},{12,14},{14,12},{16,18},{18,... | collective-permute-start | bytes 786440 | tf_op jit(solution)/shard_map/ppermute | solution.py:387
  91.3 10.5 %collective-permute-start.18 = (f32[1,256,256]{2,1,0:T(8,128)S(1)}, f32[1,256,256]{2,1,0:T(8,128)S(1)}, u32[]{:S(2)}, u32[]{:S(2)}) collective-permute-start(f32[1,256,256]{2,1,0:T(8,128)S(1)} %get-tuple-element.85.refs_3_), channel_id=1, source_target_pairs={{0,1},{1,0},{2,3},{3,2},{4,5},{5,4},{6,7},{7,6},{8,9},{9,8},{10,11... | collective-permute-start | bytes 786440 | tf_op jit(solution)/shard_map/ppermute | solution.py:391
  95.7 4.7 %collective-permute-start.14 = (f32[1,128,256]{2,1,0:T(8,128)S(1)}, f32[1,128,256]{2,1,0:T(8,128)S(1)}, u32[]{:S(2)}, u32[]{:S(2)}) collective-permute-start(f32[1,128,256]{2,1,0:T(8,128)S(1)} %get-tuple-element.81), channel_id=1, source_target_pairs={{0,16},{2,18},{4,20},{6,22},{8,24},{10,26},{12,28},{14,30},{16,0},... | collective-permute-start | bytes 393224 | tf_op jit(solution)/shard_map/ppermute | solution.py:387
  95.8 6.1 %collective-permute-start.15 = (f32[1,128,256]{2,1,0:T(8,128)S(1)}, f32[1,128,256]{2,1,0:T(8,128)S(1)}, u32[]{:S(2)}, u32[]{:S(2)}) collective-permute-start(f32[1,128,256]{2,1,0:T(8,128)S(1)} %get-tuple-element.82), channel_id=1, source_target_pairs={{0,240},{2,242},{4,244},{6,246},{8,248},{10,250},{12,252},{14,254}... | collective-permute-start | bytes 393224 | tf_op jit(solution)/shard_map/ppermute | solution.py:387
  97.7 11.6 %collective-permute-start.20 = (f32[1,256,256]{2,1,0:T(8,128)S(1)}, f32[1,256,256]{2,1,0:T(8,128)S(1)}, u32[]{:S(2)}, u32[]{:S(2)}) collective-permute-start(f32[1,256,256]{2,1,0:T(8,128)S(1)} %get-tuple-element.86.refs_5_), channel_id=1, source_target_pairs={{0,1},{1,0},{2,3},{3,2},{4,5},{5,4},{6,7},{7,6},{8,9},{9,8},{10,11... | collective-permute-start | bytes 786440 | tf_op jit(solution)/shard_map/ppermute | solution.py:391
  102.4 12.5 %collective-permute-start.19 = (f32[1,256,256]{2,1,0:T(8,128)S(1)}, f32[1,256,256]{2,1,0:T(8,128)S(1)}, u32[]{:S(2)}, u32[]{:S(2)}) collective-permute-start(f32[1,256,256]{2,1,0:T(8,128)S(1)} %rows_first.1.refs_1_), channel_id=1, source_target_pairs={{0,1},{1,0},{2,3},{3,2},{4,5},{5,4},{6,7},{7,6},{8,9},{9,8},{10,11... | collective-permute-start | bytes 786440 | tf_op jit(solution)/shard_map/ppermute | solution.py:391

commit v6 on v5

--- a/solution.py
+++ b/solution.py
@@ -41,17 +41,8 @@
 
 def dft_tables(extent):
     re, im = dft_pair(extent)
-    h = extent // 2
-
-    def tables(re, im, evens_first):
-        by_row = [(re[b::2, :h], im[b::2, :h]) for b in range(2)]
-        by_col = [(re[:h, b::2], im[:h, b::2]) for b in range(2)]
-        lefts, rights = (by_row, by_col) if evens_first else (by_col, by_row)
-        return np.stack(
-            [left_form(*pair, np) for pair in lefts] + [right_form(*pair, np) for pair in rights]
-        )
-
-    return tables(re, im, True), tables(re, -im, False)
+    lefts = [left_form(re[b::2, : extent // 2], im[b::2, : extent // 2], np) for b in range(2)]
+    return np.stack(lefts + [left.T for left in lefts])
 
 
 def mm(a, b):
@@ -104,12 +95,12 @@
 def conj_dft_sandwich(tabs, e, o):
     h = e.shape[0] // 2
     e, o = e.astype(BF16), o.astype(BF16)
-    even = mm(tabs[0], above(beside(e[:h, :h], o[:h, :h]), beside(e[:h, h:], o[:h, h:])))
-    odd = mm(tabs[1], above(beside(e[h:, :h], o[h:, :h]), beside(e[h:, h:], o[h:, h:])))
+    even = mm(tabs[2], above(beside(e[:h, :h], o[:h, :h]), beside(e[:h, h:], o[:h, h:])))
+    odd = mm(tabs[3], above(beside(e[h:, :h], o[h:, :h]), beside(e[h:, h:], o[h:, h:])))
     re = above(even[:h] + odd[:h], even[:h] - odd[:h]).astype(BF16)
     im = above(even[h:] + odd[h:], even[h:] - odd[h:]).astype(BF16)
-    e = mm(beside(re[:, :h], im[:, :h]), tabs[2])
-    o = mm(beside(re[:, h:], im[:, h:]), tabs[3])
+    e = mm(beside(re[:, :h], im[:, :h]), tabs[0])
+    o = mm(beside(re[:, h:], im[:, h:]), tabs[1])
     return (
         beside(e[:, :h] + o[:, :h], e[:, :h] - o[:, :h]),
         beside(e[:, h:] + o[:, h:], e[:, h:] - o[:, h:]),
@@ -135,20 +126,16 @@
     return jnp.where(good, value, 0.0)
 
 
-def build_canvas(info, own, rows_a, rows_b, cols_a, cols_b, corners_a, corners_b, canvas):
+def build_canvas(layer, info, own, rows_a, rows_b, cols_a, cols_b, canvas):
     n = own.shape[-1]
     h = n // 2
     ra, rb, row_ok = ends(info, 0, 0, h + n)
     ca, cb, col_ok = ends(info, 1, 0, h + n)
-    canvas[:, :, h : h + n, h : h + n] = own[...]
-    canvas[:, :, pl.ds(ra, h), h : h + n] = rows_a[...]
-    canvas[:, :, pl.ds(rb, h), h : h + n] = kept(row_ok, rows_b[...])
-    canvas[:, :, h : h + n, pl.ds(ca, h)] = cols_a[...]
-    canvas[:, :, h : h + n, pl.ds(cb, h)] = kept(col_ok, cols_b[...])
-    canvas[:, :, pl.ds(ra, h), pl.ds(ca, h)] = corners_a[0]
-    canvas[:, :, pl.ds(rb, h), pl.ds(ca, h)] = kept(row_ok, corners_a[1])
-    canvas[:, :, pl.ds(ra, h), pl.ds(cb, h)] = kept(col_ok, corners_b[0])
-    canvas[:, :, pl.ds(rb, h), pl.ds(cb, h)] = kept(row_ok & col_ok, corners_b[1])
+    canvas[:, h : h + n, h : h + n] = own[:, layer]
+    canvas[:, pl.ds(ra, h), h : h + n] = rows_a[...]
+    canvas[:, pl.ds(rb, h), h : h + n] = kept(row_ok, rows_b[...])
+    canvas[:, :, pl.ds(ca, h)] = cols_a[...]
+    canvas[:, :, pl.ds(cb, h)] = kept(col_ok, cols_b[...])
 
 
 def extract(off_ref, slot, canvas, patch):
@@ -158,10 +145,9 @@
     row_shift = jnp.where(row_rest == 0, 0, n + 8 - row_rest)
     col_shift = jnp.where(col_rest == 0, 0, n + h - col_rest)
     for part in range(2):
-        for layer in range(2):
-            window = canvas[part, layer, pl.ds(top, n + 8), pl.ds(block, n + h)]
-            window = pltpu.roll(window, col_shift, 1)[:, :n]
-            patch[part, layer] = pltpu.roll(window, row_shift, 0)[:n]
+        window = canvas[part, pl.ds(top, n + 8), pl.ds(block, n + h)]
+        window = pltpu.roll(window, col_shift, 1)[:, :n]
+        patch[part] = pltpu.roll(window, row_shift, 0)[:n]
 
 
 def lay(off_ref, grads, canvas):
@@ -182,40 +168,54 @@
         step(m)
 
 
-def forward(probe, patch, diag, corner, right, tabs, wave, far, inten):
-    n = inten.shape[0]
-    h = n // 2
+def times(a_re, a_im, b_re, b_im):
+    return a_re * b_re - a_im * b_im, a_re * b_im + a_im * b_re
+
+
+def waves(probe, patch, diag, corner, right, wave):
+    def step(m):
+        e_re, e_im = times(probe[0, m], probe[1, m], patch[0], patch[1])
+        wave[m, 0], wave[m, 1] = sandwich(diag, corner, e_re, e_im, right)
+
+    each_mode(probe.shape[1], step)
+
+
+def fars(wave, patch, tabs, far, inten):
+    h = inten.shape[0] // 2
     inten[...] = jnp.zeros_like(inten)
 
     def step(m):
-        p_re, p_im = probe[0, m], probe[1, m]
-        o_re, o_im = patch[0, 0], patch[1, 0]
-        w_re, w_im = sandwich(
-            diag, corner, p_re * o_re - p_im * o_im, p_re * o_im + p_im * o_re, right
-        )
-        wave[m, 0] = w_re
-        wave[m, 1] = w_im
-        o_re, o_im = patch[0, 1], patch[1, 1]
-        e, o = dft_sandwich(tabs, w_re * o_re - w_im * o_im, w_re * o_im + w_im * o_re)
+        e, o = dft_sandwich(tabs, *times(wave[m, 0], wave[m, 1], patch[0], patch[1]))
         far[m, 0] = e
         far[m, 1] = o
         e, o = e * e, o * o
         inten[...] += beside(e[:, :h] + e[:, h:], o[:, :h] + o[:, h:])
 
-    each_mode(probe.shape[1], step)
-
-
-def forward_first_kernel(off, info, own, rows_a, rows_b, cols_a, cols_b, corners_a, corners_b,
-                         probe, diag, corner, mat, tabs, canvas, patch, wave, far, inten):
-    build_canvas(info, own, rows_a, rows_b, cols_a, cols_b, corners_a, corners_b, canvas)
+    each_mode(wave.shape[0], step)
+
+
+def waves_first_kernel(off, info, own, rows_a, rows_b, cols_a, cols_b, probe, diag, corner,
+                       mat, canvas, patch, wave):
+    build_canvas(0, info, own, rows_a, rows_b, cols_a, cols_b, canvas)
     extract(off, 0, canvas, patch)
-    forward(probe, patch, diag, corner, mat, tabs, wave, far, inten)
-
-
-def forward_next_kernel(slot, off, canvas, probe, diag, corner, mat, tabs, patch, wave, far,
-                        inten):
-    extract(off, slot, canvas, patch)
-    forward(probe, patch, diag, corner, mat, tabs, wave, far, inten)
+    waves(probe, patch, diag, corner, mat, wave)
+
+
+def waves_next_kernel(off, canvas, probe, diag, corner, mat, patch, wave):
+    extract(off, 1, canvas, patch)
+    waves(probe, patch, diag, corner, mat, wave)
+
+
+def fars_first_kernel(off, info, own, rows_a, rows_b, cols_a, cols_b, wave, tabs, canvas, patch,
+                      far, inten):
+    build_canvas(1, info, own, rows_a, rows_b, cols_a, cols_b, canvas)
+    extract(off, 0, canvas, patch)
+    fars(wave, patch, tabs, far, inten)
+
+
+def fars_next_kernel(off, canvas, wave, tabs, patch, far, inten):
+    extract(off, 1, canvas, patch)
+    fars(wave, patch, tabs, far, inten)
 
 
 def back_last(slot, counts, mine, other, measured, far, wave, patch, tabs, grad, bar, resid):
@@ -232,7 +232,7 @@
         w_re, w_im = wave[m, 0], wave[m, 1]
         grad[0] += w_re * b_re + w_im * b_im
         grad[1] += w_re * b_im - w_im * b_re
-        o_re, o_im = patch[0, 1], patch[1, 1]
+        o_re, o_im = patch[0], patch[1]
         bar[m, 0] = (o_re * b_re + o_im * b_im).astype(BF16)
         bar[m, 1] = (o_re * b_im - o_im * b_re).astype(BF16)
 
@@ -249,7 +249,7 @@
     out_c[...] = canvas[:, :, h : h + n]
 
 
-def back_first(info, bar, probe, patch, diag, corner, mat, keep, send, grad, emit):
+def back_first_kernel(info, bar, probe, patch, diag, corner, mat, keep, send, part, grad):
     grad[...] = jnp.zeros_like(grad)
 
     def step(m):
@@ -257,30 +257,18 @@
         p_re, p_im = probe[0, m], probe[1, m]
         grad[0] += p_re * b_re + p_im * b_im
         grad[1] += p_re * b_im - p_im * b_re
-        o_re, o_im = patch[0, 0], patch[1, 0]
-        emit(m, o_re * b_re + o_im * b_im, o_re * b_im - o_im * b_re)
+        o_re, o_im = patch[0], patch[1]
+        part[0, m] = o_re * b_re + o_im * b_im
+        part[1, m] = o_re * b_im - o_im * b_re
 
     each_mode(probe.shape[1], step)
-    part = info[4]
-    keep[0] = grad[part]
-    send[0] = grad[1 - part]
-
-
-def back_first_kernel(info, bar, probe, patch, diag, corner, mat, keep, send, part, grad):
-    def emit(m, re, im):
-        part[0, m] = re
-        part[1, m] = im
-
-    back_first(info, bar, probe, patch, diag, corner, mat, keep, send, grad, emit)
-
-
-def back_first_add_kernel(info, bar, probe, patch, diag, corner, mat, part, keep, send, total,
-                          grad):
-    def emit(m, re, im):
-        total[0, 0, m] = part[0, m] + re
-        total[0, 1, m] = part[1, m] + im
-
-    back_first(info, bar, probe, patch, diag, corner, mat, keep, send, grad, emit)
+    mode = info[4]
+    keep[0] = grad[mode]
+    send[0] = grad[1 - mode]
+
+
+def probe_sum_kernel(part0, part1, total):
+    total[0] = part0[...] + part1[...]
 
 
 def sides(info, canvas, out_a, out_b):
@@ -339,22 +327,40 @@
     out[0, 1, 1] = mine_im[0] + other_im[0]
 
 
-def pick_corners_kernel(info, rows_a, rows_b, out_a, out_b):
-    h = out_a.shape[-1]
+def pick_rows_kernel(info, own, *refs):
+    *outs, sems = refs
+    h = outs[0].shape[1]
+    a, b, _ = ends(info, 0, 0, h)
+    copies = []
+    for layer in range(2):
+        for i, start in enumerate((a, b)):
+            k = 2 * layer + i
+            copies.append(pltpu.make_async_copy(
+                own.at[:, layer, pl.ds(start, h), :], outs[k], sems.at[k]))
+    for copy in copies:
+        copy.start()
+    for copy in copies:
+        copy.wait()
+
+
+def pick_cols_kernel(layer, info, own, rows_a, rows_b, out_a, out_b):
+    n = own.shape[-1]
+    h = n // 2
+    ra, rb, row_ok = ends(info, 0, 0, h + n)
     a, b, _ = ends(info, 1, 0, h)
-    for i, rows in enumerate((rows_a, rows_b)):
-        out_a[i] = rows[:, :, :, pl.ds(a, h)]
-        out_b[i] = rows[:, :, :, pl.ds(b, h)]
-
-
-def prepare_kernel(prop_in, probe_in, meas_in, order_in, order_t_in, dft_in, conj_in, diag, corner,
-                   right, back_diag, back_corner, back_right, probe_out, meas_out, dft_out,
-                   conj_out, prop, meas, order, order_t, sems):
-    moves = (
-        (prop_in, prop), (meas_in, meas), (order_in, order), (order_t_in, order_t),
-        (probe_in, probe_out), (dft_in, dft_out), (conj_in, conj_out),
-    )
-    copies = [pltpu.make_async_copy(a, b, sems.at[i]) for i, (a, b) in enumerate(moves)]
+    for start, out in ((a, out_a), (b, out_b)):
+        side = pl.ds(start, h)
+        out[:, h : h + n] = own[:, layer, :, side]
+        out[:, pl.ds(ra, h)] = rows_a[:, :, side]
+        out[:, pl.ds(rb, h)] = kept(row_ok, rows_b[:, :, side])
+
+
+def prepare_kernel(prop_in, probe_in, diag, corner, right, back_diag, back_corner, back_right,
+                   probe_out, prop, sems):
+    copies = [
+        pltpu.make_async_copy(prop_in, prop, sems.at[0]),
+        pltpu.make_async_copy(probe_in, probe_out, sems.at[1]),
+    ]
     for copy in copies:
         copy.start()
     copies[0].wait()
@@ -367,13 +373,24 @@
         edge[...] = corners.astype(BF16)
     right[...] = right_form(re_t, im_t, jnp).astype(BF16)
     back_right[...] = right_form(re, -im, jnp).astype(BF16)
-    for copy in copies[1:]:
-        copy.wait()
+    copies[1].wait()
+
+
+def reorder_kernel(measured, tabs, out, tabs_out):
+    n = out.shape[-1]
+    h = n // 2
+    tabs_out[...] = tabs[...]
     exact = functools.partial(
         jnp.dot, precision=lax.Precision.HIGHEST, preferred_element_type=F32
     )
-    for slot in range(meas.shape[0]):
-        meas_out[slot] = exact(exact(order[...], meas[slot]), order_t[...])
+
+    def order(to, of):
+        a = lax.broadcasted_iota(jnp.int32, (n, n), to)
+        b = lax.broadcasted_iota(jnp.int32, (n, n), of)
+        return jnp.where(jnp.where(a < h, 2 * a, 2 * a - n + 1) == b, 1.0, 0.0).astype(F32)
+
+    for slot in range(out.shape[0]):
+        out[slot] = exact(exact(order(0, 1), measured[slot]), order(1, 0))
 
 
 def swap(value, axis, second):
@@ -429,52 +446,61 @@
     paired = [(row > 0) & (row < n_rows - 1), (col > 0) & (col < GY - 1)]
     info = jnp.stack([odd_row, odd_col, *paired, lax.axis_index("mode") == 1]).astype(jnp.int32)
 
-    top, low = own[:, :, :h, :], own[:, :, h:, :]
-    rows_a = swap(jnp.where(odd_row, top, low), 0, False)
-    rows_b = swap(jnp.where(odd_row, low, top), 0, True)
-    left, right = own[:, :, :, :h], own[:, :, :, h:]
-    cols_a = swap(jnp.where(odd_col, left, right), 1, False)
-    cols_b = swap(jnp.where(odd_col, right, left), 1, True)
-    dft, conj_dft = dft_tables(n)
-    order = np.eye(n, dtype=np.float32)[np.r_[0:n:2, 1:n:2]]
-    plane, pair, mat = ((n, n), F32), ((2, n, n), F32), ((2 * n, 2 * n), BF16)
-    patch_out, field = ((2, 2, n, n), F32), ((modes, 2, n, n), F32)
-    probes, tables = ((2, modes, n, n), F32), (dft.shape, BF16)
+    one, pair, mat = ((1, n, n), F32), ((2, n, n), F32), ((2 * n, 2 * n), BF16)
+    plane, field, probes = ((n, n), F32), ((modes, 2, n, n), F32), ((2, modes, n, n), F32)
     band = (((2, n, n), BF16), ((4 * BAND, 4 * BAND), BF16), mat)
-    *made, probe, measured, dft, conj_dft = call(
+    strip, tall = ((2, h, n), F32), ((2, 2 * n, h), F32)
+
+    picked = call(pick_rows_kernel, "pick_rows", (strip,) * 4, (info, own), copies=4)
+    rows = [[swap(picked[2 * i + k], 0, k == 1) for k in range(2)] for i in range(2)]
+    *made, probe = call(
         prepare_kernel,
         "prepare",
-        band + band + (probes, ((slots, n, n), F32), tables, tables),
-        (propagator, probe_modes, measured[0], jnp.asarray(order), jnp.asarray(order.T.copy()),
-         jnp.asarray(dft), jnp.asarray(conj_dft)),
-        scratch=(((2, n, n), BF16), ((slots, n, n), F32), plane, plane),
+        band + band + (probes,),
+        (propagator, probe_modes),
+        scratch=(((2, n, n), BF16),),
         smem=0,
-        copies=7,
+        copies=2,
     )
     prop, back_prop = made[:3], made[3:]
-    quarter = ((2, 2, 2, h, h), F32)
-    corners_a, corners_b = call(
-        pick_corners_kernel,
-        "pick_corners",
-        (quarter, quarter),
-        (info, rows_a, rows_b),
-        after=(probe,),
-    )
-    corners_a, corners_b = swap(corners_a, 1, False), swap(corners_b, 1, True)
-
-    canvas, patch0, wave0, far0, inten0 = call(
-        forward_first_kernel,
-        "forward_0",
-        (((2, 2, 2 * n, 2 * n), F32), patch_out, field, field, plane),
-        (off, info, own, rows_a, rows_b, cols_a, cols_b, corners_a, corners_b, probe, *prop, dft),
+    tabs = jnp.asarray(dft_tables(n))
+    measured, tabs = call(
+        reorder_kernel,
+        "reorder",
+        (((slots, n, n), F32), (tabs.shape, BF16)),
+        (measured[0], tabs),
+        smem=0,
+    )
+
+    def beside_tiles(layer, after):
+        picked = call(functools.partial(pick_cols_kernel, layer), f"pick_cols_{layer}", (tall,) * 2,
+                      (info, own, *rows[layer]), after=after)
+        return (own, *rows[layer], *(swap(picked[k], 1, k == 1) for k in range(2)))
+
+    first = beside_tiles(0, (probe,))
+    last = beside_tiles(1, (measured,))
+    canvas, patch_first0, wave0 = call(
+        waves_first_kernel,
+        "waves_0",
+        (((2, 2 * n, 2 * n), F32), pair, field),
+        (off, info, *first, probe, *prop),
         smem=2,
+        after=(),
+    )
+    patch_first1, wave1 = call(
+        waves_next_kernel, "waves_1", (pair, field), (off, canvas, probe, *prop), after=()
+    )
+    canvas, patch_last0, far0, inten0 = call(
+        fars_first_kernel,
+        "fars_0",
+        (((2, 2 * n, 2 * n), F32), pair, field, plane),
+        (off, info, *last, wave0, tabs),
+        smem=2,
+        after=(patch_first1,),
     )
     other0 = swap_mode(inten0)
-    patch1, wave1, far1, inten1 = call(
-        functools.partial(forward_next_kernel, 1),
-        "forward_1",
-        (patch_out, field, field, plane),
-        (off, canvas, probe, *prop, dft),
+    patch_last1, far1, inten1 = call(
+        fars_next_kernel, "fars_1", (pair, field, plane), (off, canvas, wave1, tabs)
     )
     other1 = swap_mode(inten1)
 
@@ -485,15 +511,14 @@
         functools.partial(back_last, 0),
         "back_last_0",
         (pair, bar_out),
-        (counts, inten0, other0, measured, far0, wave0, patch0, conj_dft),
+        (counts, inten0, other0, measured, far0, wave0, patch_last0, tabs),
         scratch=(pair,),
     )
-    one = ((1, n, n), F32)
-    keep0, send0, part = call(
+    keep0, send0, part0 = call(
         back_first_kernel,
         "back_first_0",
         (one, one, probes),
-        (info, bar0, probe, patch0, *back_prop),
+        (info, bar0, probe, patch_first0, *back_prop),
         scratch=(pair,),
     )
     got0 = swap_mode(send0)
@@ -501,7 +526,7 @@
         functools.partial(back_last_place_kernel, 1),
         "back_last_1",
         (bar_out,) + strips,
-        (counts, off, info, grad_last0, inten1, other1, measured, far1, wave1, patch1, conj_dft),
+        (counts, off, info, grad_last0, inten1, other1, measured, far1, wave1, patch_last1, tabs),
         scratch=(pair, pair, wide),
         smem=3,
         after=(keep0,),
@@ -519,13 +544,12 @@
         return call(fold_rows_kernel, name, (one,) * mid.shape[0], (info, mid, got_a, got_b),
                     after=after)
 
-    keep1, send1, probe_grad = call(
-        back_first_add_kernel,
+    keep1, send1, part1 = call(
+        back_first_kernel,
         "back_first_1",
-        (one, one, ((1, 2, modes, n, n), F32)),
-        (info, bar1, probe, patch1, *back_prop, part),
+        (one, one, probes),
+        (info, bar1, probe, patch_first1, *back_prop),
         scratch=(pair,),
-        after=(),
     )
     got1 = swap_mode(send1)
     strips_last = fold_cols("cols_last", out_a, out_c, out_b, (keep1,))
@@ -554,6 +578,14 @@
     strips_first = fold_cols("cols_first", out_a, out_c, out_b, ())
     (mine_first,) = fold_rows("rows_first", *strips_first, (other_re,))
     other_first = swap_mode(mine_first)
+    (probe_grad,) = call(
+        probe_sum_kernel,
+        "probe_sum",
+        (((1, 2, modes, n, n), F32),),
+        (part0, part1),
+        smem=0,
+        after=(),
+    )
     (object_grad,) = call(
         finish_kernel,
         "finish",

time: 117 us -> 112 us (0.957)
  starting transfers between devices: 43.9 us -> 52.4 us
  waiting for transfers between devices: 24 us -> 16.1 us
  other arithmetic: 4.72 us -> 0.01 us
    ppermute x14 -> x16, starting transfers between devices: 30.2 us -> 36.8 us  [swap(): return lax.ppermute(value, 'tile', pairs)]
    ppermute x7, waiting for transfers between devices: 14.1 us -> 8.71 us  [swap_mode(): return lax.ppermute(value, 'mode', [(0, 1), (1, 0)])]
    select_n x2 -> x0, other arithmetic: 4.71 us -> none  [the longest x1 2.43 us: body(): rows_b = swap(jnp.where(odd_row, low, top), 0, True)]
    ppermute x14 -> x16, waiting for transfers between devices: 9.89 us -> 7.38 us  [swap(): return lax.ppermute(value, 'tile', pairs)]
    ppermute x7, starting transfers between devices: 13.8 us -> 15.6 us  [swap_mode(): return lax.ppermute(value, 'mode', [(0, 1), (1, 0)])]
    unnamed x18 -> x14, local copies, waits for them, and re-layouts: 5.04 us -> 4.08 us
    pallas_call x15 -> x21, Pallas kernels: 37.3 us -> 37.9 us  [call(): pl.pallas_call(run, out_shape=tuple((jax.ShapeDtypeStruct(shape, dtype) f...]
  transfers between devices with their start and end apart: 21 -> 23, of which waited for: 10 -> 9; matrix products, arithmetic and copies ran while one was open for 2% -> 0% of each run, Pallas kernels for 21% -> 26%
where the time goes in v6:
time: 112 us
  starting transfers between devices  52.4 us (47%)
  Pallas kernels  37.9 us (34%)
  waiting for transfers between devices  16.1 us (14%)
  local copies, waits for them, and re-layouts  4.19 us (4%)
  between operations  1.58 us (1%)
    pallas_call x21, Pallas kernels, call(): pl.pallas_call(run, out_shape=tuple((jax.ShapeDtypeStruct(shape, dtype) f...  37.9 us
    ppermute x16, starting transfers between devices, swap(): return lax.ppermute(value, 'tile', pairs)  36.8 us
    ppermute x7, starting transfers between devices, swap_mode(): return lax.ppermute(value, 'mode', [(0, 1), (1, 0)])  15.6 us
    ppermute x7, waiting for transfers between devices, swap_mode(): return lax.ppermute(value, 'mode', [(0, 1), (1, 0)])  8.71 us
    ppermute x16, waiting for transfers between devices, swap(): return lax.ppermute(value, 'tile', pairs)  7.38 us
    unnamed x14, local copies, waits for them, and re-layouts  4.08 us
  transfers between devices with their start and end apart: 23, of which 9 were waited for; matrix products, arithmetic and copies ran while one was open for 0% of the time, Pallas kernels for 26%

profile of v6, /device:TPU:1, one launch (start us, length us, event | category | flops | bytes accessed | tf_op | source)
XLA Modules:
  0.0 112.2 jit_solution(17521010092464026851)
XLA Ops:
  0.8 1.2 %copy-done = f32[1,2,2,256,256]{4,3,2,1,0:T(8,128)S(1)} copy-done((f32[1,2,2,256,256]{4,3,2,1,0:T(8,128)S(1)}, f32[1,2,2,256,256]{4,3,2,1,0:T(8,128)}, u32[]{:S(2)}) %copy-start) | copy-done | bytes 1048600
  2.7 2.6 %collective-permute-start.4 = (f32[2,128,256]{2,1,0:T(8,128)S(1)}, f32[2,128,256]{2,1,0:T(8,128)S(1)}, u32[]{:S(2)}, u32[]{:S(2)}) collective-permute-start(f32[2,128,256]{2,1,0:T(8,128)S(1)} %get-tuple-element.58), channel_id=1, source_target_pairs={{0,16},{2,18},{4,20},{6,22},{8,24},{10,26},{12,28},{14,30},{16,0},... | collective-permute-start | bytes 786440 | tf_op jit(solution)/shard_map/ppermute | solution.py:404
  5.3 5.7 %collective-permute-start.5 = (f32[2,128,256]{2,1,0:T(8,128)S(1)}, f32[2,128,256]{2,1,0:T(8,128)S(1)}, u32[]{:S(2)}, u32[]{:S(2)}) collective-permute-start(f32[2,128,256]{2,1,0:T(8,128)S(1)} %get-tuple-element.59), channel_id=1, source_target_pairs={{0,240},{2,242},{4,244},{6,246},{8,248},{10,250},{12,252},{14,254}... | collective-permute-start | bytes 786440 | tf_op jit(solution)/shard_map/ppermute | solution.py:404
  10.9 1.5 %collective-permute-start.1 = (f32[2,128,256]{2,1,0:T(8,128)S(1)}, f32[2,128,256]{2,1,0:T(8,128)S(1)}, u32[]{:S(2)}, u32[]{:S(2)}) collective-permute-start(f32[2,128,256]{2,1,0:T(8,128)S(1)} %get-tuple-element.54), channel_id=1, source_target_pairs={{0,240},{2,242},{4,244},{6,246},{8,248},{10,250},{12,252},{14,254}... | collective-permute-start | bytes 786440 | tf_op jit(solution)/shard_map/ppermute | solution.py:404
  12.4 1.9 %copy-done.2 = f32[2,6,256,256]{3,2,1,0:T(8,128)S(1)} copy-done((f32[2,6,256,256]{3,2,1,0:T(8,128)S(1)}, f32[2,6,256,256]{3,2,1,0:T(8,128)}, u32[]{:S(2)}) %copy-start.2) | copy-done | bytes 3145752
  17.3 2.8 %collective-permute-start.6 = (f32[2,512,128]{2,1,0:T(8,128)S(1)}, f32[2,512,128]{2,1,0:T(8,128)S(1)}, u32[]{:S(2)}, u32[]{:S(2)}) collective-permute-start(f32[2,512,128]{2,1,0:T(8,128)S(1)} %get-tuple-element.61), channel_id=1, source_target_pairs={{0,2},{2,0},{4,6},{6,4},{8,10},{10,8},{12,14},{14,12},{16,18},{18,... | collective-permute-start | bytes 1572872 | tf_op jit(solution)/shard_map/ppermute | solution.py:404
  21.3 1.5 %reorder.1 = (f32[2,256,256]{2,1,0:T(8,128)S(1)}, bf16[4,256,256]{2,1,0:T(8,128)(2,1)S(1)}) custom-call(f32[2,256,256]{2,1,0:T(8,128)S(1)} %bitcast.13, bf16[4,256,256]{2,1,0:T(8,128)(2,1)S(1)} %copy-done.4), custom_call_target="tpu_custom_call" | custom-call | tf_op jit(solution)/shard_map/reorder/pallas_call | solution.py:420
  23.4 1.8 %collective-permute-start.2 = (f32[2,512,128]{2,1,0:T(8,128)S(1)}, f32[2,512,128]{2,1,0:T(8,128)S(1)}, u32[]{:S(2)}, u32[]{:S(2)}) collective-permute-start(f32[2,512,128]{2,1,0:T(8,128)S(1)} %get-tuple-element.56), channel_id=1, source_target_pairs={{0,2},{2,0},{4,6},{6,4},{8,10},{10,8},{12,14},{14,12},{16,18},{18,... | collective-permute-start | bytes 1572872 | tf_op jit(solution)/shard_map/ppermute | solution.py:404
  25.9 3.1 %collective-permute-done.7.refs_6_ = f32[2,512,128]{2,1,0:T(8,128)S(1)} collective-permute-done((f32[2,512,128]{2,1,0:T(8,128)S(1)}, f32[2,512,128]{2,1,0:T(8,128)S(1)}, u32[]{:S(2)}, u32[]{:S(2)}) %collective-permute-start.7) | collective-permute-done | bytes 524320 | tf_op jit(solution)/shard_map/ppermute | solution.py:404
  29.0 3.8 %waves_0.1 = (f32[2,512,512]{2,1,0:T(8,128)S(1)}, f32[2,256,256]{2,1,0:T(8,128)S(1)}, f32[6,2,256,256]{3,2,1,0:T(8,128)S(1)}) custom-call(s32[2,2]{1,0:T(2,128)S(1)} %bitcast.14, s32[5]{0:T(128)S(1)} %convert_element_type.3.refs_0_.refs_1_.refs_2_, f32[2,2,256,256]{3,2,1,0:T(8,128)S(1)} %bitcast.11, ...), custom_call_target="tpu_custom_call" | custom-call | tf_op jit(solution)/shard_map/waves_0/pallas_call | solution.py:420
  32.7 3.5 %waves_1.1 = (f32[2,256,256]{2,1,0:T(8,128)S(1)}, f32[6,2,256,256]{3,2,1,0:T(8,128)S(1)}) custom-call(s32[2,2]{1,0:T(2,128)S(1)} %bitcast.15, f32[2,512,512]{2,1,0:T(8,128)S(1)} %get-tuple-element.68.refs_1_, f32[2,6,256,256]{3,2,1,0:T(8,128)S(1)} %get-tuple-element.60.refs_4_.refs_7_.refs_2_, bf16[2,256,256]{2,1,0:T(8,128)(2,1)S(1)} %get-tuple-element.63.refs_8_.refs_3_, ...), custom_call_target="tpu_custom_call" | custom-call | tf_op jit(solution)/shard_map/waves_1/pallas_call | solution.py:420
  36.2 3.2 %fars_0.1 = (f32[2,512,512]{2,1,0:T(8,128)S(1)}, f32[2,256,256]{2,1,0:T(8,128)S(1)}, f32[6,2,256,256]{3,2,1,0:T(8,128)S(1)}, f32[256,256]{1,0:T(8,128)S(1)}) custom-call(s32[2,2]{1,0:T(2,128)S(1)} %bitcast.16, s32[5]{0:T(128)S(1)} %convert_element_type.3.refs_0_.refs_1_.refs_2_, f32[2,2,256,256]{3,2,1,0:T(8,128)S(1)} %bitcast.12, ...), custom_call_target="tpu_custom_call" | custom-call | tf_op jit(solution)/shard_map/fars_0/pallas_call | solution.py:420
  39.5 2.7 %collective-permute-start.8 = (f32[256,256]{1,0:T(8,128)S(1)}, f32[256,256]{1,0:T(8,128)S(1)}, u32[]{:S(2)}, u32[]{:S(2)}) collective-permute-start(f32[256,256]{1,0:T(8,128)S(1)} %get-tuple-element.70.refs_1_), channel_id=1, source_target_pairs={{0,1},{1,0},{2,3},{3,2},{4,5},{5,4},{6,7},{7,6},{8,9},{9,8},{10,11... | collective-permute-start | bytes 786440 | tf_op jit(solution)/shard_map/ppermute | solution.py:408
  42.2 3.0 %fars_1.1 = (f32[2,256,256]{2,1,0:T(8,128)S(1)}, f32[6,2,256,256]{3,2,1,0:T(8,128)S(1)}, f32[256,256]{1,0:T(8,128)S(1)}) custom-call(s32[2,2]{1,0:T(2,128)S(1)} %bitcast.17, f32[2,512,512]{2,1,0:T(8,128)S(1)} %get-tuple-element.81.refs_1_, f32[6,2,256,256]{3,2,1,0:T(8,128)S(1)} %get-tuple-element.82.refs_2_.refs_8_, ...), custom_call_target="tpu_custom_call" | custom-call | tf_op jit(solution)/shard_map/fars_1/pallas_call | solution.py:420
  46.4 1.4 %collective-permute-done.8.refs_2_ = f32[256,256]{1,0:T(8,128)S(1)} collective-permute-done((f32[256,256]{1,0:T(8,128)S(1)}, f32[256,256]{1,0:T(8,128)S(1)}, u32[]{:S(2)}, u32[]{:S(2)}) %collective-permute-start.8) | collective-permute-done | bytes 262176 | tf_op jit(solution)/shard_map/ppermute | solution.py:408
  47.9 2.3 %back_last_0.1 = (f32[2,256,256]{2,1,0:T(8,128)S(1)}, bf16[6,2,256,256]{3,2,1,0:T(8,128)(2,1)S(1)}) custom-call(s32[1]{0:T(128)S(6)} %copy.9.refs_0_, f32[256,256]{1,0:T(8,128)S(1)} %get-tuple-element.70.refs_1_, f32[256,256]{1,0:T(8,128)S(1)} %collective-permute-done.8.refs_2_, f32[2,256,256]{2,1,0:T(8,128)S(1)} %get-tuple-element.55.refs_4_.refs_3_.refs_6_, ...), custom_call_target="tpu_custom_call" | custom-call | tf_op jit(solution)/shard_map/back_last_0/pallas_call | solution.py:420
  50.2 3.2 %back_first_0.1 = (f32[1,256,256]{2,1,0:T(8,128)S(1)}, f32[1,256,256]{2,1,0:T(8,128)S(1)}, f32[2,6,256,256]{3,2,1,0:T(8,128)S(1)}) custom-call(s32[5]{0:T(128)S(1)} %convert_element_type.3.refs_0_.refs_1_.refs_2_, bf16[6,2,256,256]{3,2,1,0:T(8,128)(2,1)S(1)} %get-tuple-element.73.refs_1_, f32[2,6,256,256]{3,2,1,0:T(8,128)S(1)} %get-tuple-element.60.refs_4_.refs_7_.refs_2_, ...), custom_call_target="tpu_custom_call" | custom-call | tf_op jit(solution)/shard_map/back_first_0/pallas_call | solution.py:420
  53.5 3.8 %back_last_1.1 = (bf16[6,2,256,256]{3,2,1,0:T(8,128)(2,1)S(1)}, f32[2,512,128]{2,1,0:T(8,128)S(1)}, f32[2,512,256]{2,1,0:T(8,128)S(1)}, f32[2,512,128]{2,1,0:T(8,128)S(1)}) custom-call(s32[1]{0:T(128)S(6)} %copy.9.refs_0_, s32[2,2]{1,0:T(2,128)S(1)} %bitcast.18, s32[5]{0:T(128)S(1)} %convert_element_type.3.refs_0_.refs_1_.refs_2_, ...), custom_call_target="tpu_custom_call" | custom-call | tf_op jit(solution)/shard_map/back_last_1/pallas_call | solution.py:420
  57.2 2.4 %collective-permute-start.12 = (f32[2,512,128]{2,1,0:T(8,128)S(1)}, f32[2,512,128]{2,1,0:T(8,128)S(1)}, u32[]{:S(2)}, u32[]{:S(2)}) collective-permute-start(f32[2,512,128]{2,1,0:T(8,128)S(1)} %get-tuple-element.90), channel_id=1, source_target_pairs={{0,2},{2,0},{4,6},{6,4},{8,10},{10,8},{12,14},{14,12},{16,18},{18,... | collective-permute-start | bytes 1572872 | tf_op jit(solution)/shard_map/ppermute | solution.py:404
  60.8 2.6 %collective-permute-start.9 = (f32[1,256,256]{2,1,0:T(8,128)S(1)}, f32[1,256,256]{2,1,0:T(8,128)S(1)}, u32[]{:S(2)}, u32[]{:S(2)}) collective-permute-start(f32[1,256,256]{2,1,0:T(8,128)S(1)} %get-tuple-element.79), channel_id=1, source_target_pairs={{0,1},{1,0},{2,3},{3,2},{4,5},{5,4},{6,7},{7,6},{8,9},{9,8},{10,11... | collective-permute-start | bytes 786440 | tf_op jit(solution)/shard_map/ppermute | solution.py:408
  63.3 3.2 %back_first_1.1 = (f32[1,256,256]{2,1,0:T(8,128)S(1)}, f32[1,256,256]{2,1,0:T(8,128)S(1)}, f32[2,6,256,256]{3,2,1,0:T(8,128)S(1)}) custom-call(s32[5]{0:T(128)S(1)} %convert_element_type.3.refs_0_.refs_1_.refs_2_, bf16[6,2,256,256]{3,2,1,0:T(8,128)(2,1)S(1)} %get-tuple-element.86.refs_1_, f32[2,6,256,256]{3,2,1,0:T(8,128)S(1)} %get-tuple-element.60.refs_4_.refs_7_.refs_2_, ...), custom_call_target="tpu_custom_call" | custom-call | tf_op jit(solution)/shard_map/back_first_1/pallas_call | solution.py:420
  67.0 1.5 %collective-permute-done.13.refs_3_ = f32[2,512,128]{2,1,0:T(8,128)S(1)} collective-permute-done((f32[2,512,128]{2,1,0:T(8,128)S(1)}, f32[2,512,128]{2,1,0:T(8,128)S(1)}, u32[]{:S(2)}, u32[]{:S(2)}) %collective-permute-start.13) | collective-permute-done | bytes 524320 | tf_op jit(solution)/shard_map/ppermute | solution.py:404
  69.2 3.8 %collective-permute-start.19 = (f32[2,128,256]{2,1,0:T(8,128)S(1)}, f32[2,128,256]{2,1,0:T(8,128)S(1)}, u32[]{:S(2)}, u32[]{:S(2)}) collective-permute-start(f32[2,128,256]{2,1,0:T(8,128)S(1)} %get-tuple-element.99), channel_id=1, source_target_pairs={{0,240},{2,242},{4,244},{6,246},{8,248},{10,250},{12,252},{14,254}... | collective-permute-start | bytes 786440 | tf_op jit(solution)/shard_map/ppermute | solution.py:404
  74.8 9.8 %collective-permute-start.15 = (f32[1,512,128]{2,1,0:T(8,128)S(1)}, f32[1,512,128]{2,1,0:T(8,128)S(1)}, u32[]{:S(2)}, u32[]{:S(2)}) collective-permute-start(f32[1,512,128]{2,1,0:T(8,128)S(1)} %get-tuple-element.94), channel_id=1, source_target_pairs={{0,14},{2,4},{4,2},{6,8},{8,6},{10,12},{12,10},{14,0},{16,30},{18,... | collective-permute-start | bytes 786440 | tf_op jit(solution)/shard_map/ppermute | solution.py:404
  85.5 3.7 %collective-permute-start.20 = (f32[1,256,256]{2,1,0:T(8,128)S(1)}, f32[1,256,256]{2,1,0:T(8,128)S(1)}, u32[]{:S(2)}, u32[]{:S(2)}) collective-permute-start(f32[1,256,256]{2,1,0:T(8,128)S(1)} %get-tuple-element.100.refs_3_), channel_id=1, source_target_pairs={{0,1},{1,0},{2,3},{3,2},{4,5},{5,4},{6,7},{7,6},{8,9},{9,8},{10,11... | collective-permute-start | bytes 786440 | tf_op jit(solution)/shard_map/ppermute | solution.py:408
  90.9 3.1 %collective-permute-start.17 = (f32[1,128,256]{2,1,0:T(8,128)S(1)}, f32[1,128,256]{2,1,0:T(8,128)S(1)}, u32[]{:S(2)}, u32[]{:S(2)}) collective-permute-start(f32[1,128,256]{2,1,0:T(8,128)S(1)} %get-tuple-element.97), channel_id=1, source_target_pairs={{0,240},{2,242},{4,244},{6,246},{8,248},{10,250},{12,252},{14,254}... | collective-permute-start | bytes 393224 | tf_op jit(solution)/shard_map/ppermute | solution.py:404
  94.1 1.9 %collective-permute-start.22 = (f32[1,256,256]{2,1,0:T(8,128)S(1)}, f32[1,256,256]{2,1,0:T(8,128)S(1)}, u32[]{:S(2)}, u32[]{:S(2)}) collective-permute-start(f32[1,256,256]{2,1,0:T(8,128)S(1)} %get-tuple-element.101.refs_5_), channel_id=1, source_target_pairs={{0,1},{1,0},{2,3},{3,2},{4,5},{5,4},{6,7},{7,6},{8,9},{9,8},{10,11... | collective-permute-start | bytes 786440 | tf_op jit(solution)/shard_map/ppermute | solution.py:408
  96.0 1.9 %collective-permute-done.17.refs_3_ = f32[1,128,256]{2,1,0:T(8,128)S(1)} collective-permute-done((f32[1,128,256]{2,1,0:T(8,128)S(1)}, f32[1,128,256]{2,1,0:T(8,128)S(1)}, u32[]{:S(2)}, u32[]{:S(2)}) %collective-permute-start.17) | collective-permute-done | bytes 131104 | tf_op jit(solution)/shard_map/ppermute | solution.py:404
  98.5 3.6 %collective-permute-start.21 = (f32[1,256,256]{2,1,0:T(8,128)S(1)}, f32[1,256,256]{2,1,0:T(8,128)S(1)}, u32[]{:S(2)}, u32[]{:S(2)}) collective-permute-start(f32[1,256,256]{2,1,0:T(8,128)S(1)} %rows_first.1.refs_1_), channel_id=1, source_target_pairs={{0,1},{1,0},{2,3},{3,2},{4,5},{5,4},{6,7},{7,6},{8,9},{9,8},{10,11... | collective-permute-start | bytes 786440 | tf_op jit(solution)/shard_map/ppermute | solution.py:408
  102.1 2.0 %probe_sum.1 = f32[1,2,6,256,256]{4,3,2,1,0:T(8,128)} custom-call(f32[2,6,256,256]{3,2,1,0:T(8,128)S(1)} %get-tuple-element.102.refs_0_, f32[2,6,256,256]{3,2,1,0:T(8,128)S(1)} %get-tuple-element.103.refs_1_), custom_call_target="tpu_custom_call" | custom-call | tf_op jit(solution)/shard_map/probe_sum/pallas_call | solution.py:420
  105.0 5.6 %collective-permute-done.21.refs_2_ = f32[1,256,256]{2,1,0:T(8,128)S(1)} collective-permute-done((f32[1,256,256]{2,1,0:T(8,128)S(1)}, f32[1,256,256]{2,1,0:T(8,128)S(1)}, u32[]{:S(2)}, u32[]{:S(2)}) %collective-permute-start.21) | collective-permute-done | bytes 262176 | tf_op jit(solution)/shard_map/ppermute | solution.py:408
  110.6 1.6 %finish.1 = f32[1,2,2,256,256]{4,3,2,1,0:T(8,128)} custom-call(s32[5]{0:T(128)S(1)} %convert_element_type.3.refs_0_.refs_1_.refs_2_, f32[1,256,256]{2,1,0:T(8,128)S(1)} %rows_first.1.refs_1_, f32[1,256,256]{2,1,0:T(8,128)S(1)} %collective-permute-done.21.refs_2_, f32[1,256,256]{2,1,0:T(8,128)S(1)} %get-tuple-element.100.refs_3_, ...), custom_call_target="tpu_custom_call" | custom-call | tf_op jit(solution)/shard_map/finish/pallas_call | solution.py:420
  (51 shorter events, 15.2 us)
Async XLA Ops:
  0.8 1.2 %copy-start = (f32[1,2,2,256,256]{4,3,2,1,0:T(8,128)S(1)}, f32[1,2,2,256,256]{4,3,2,1,0:T(8,128)}, u32[]{:S(2)}) copy-start(f32[1,2,2,256,256]{4,3,2,1,0:T(8,128)} %param.7) | copy-start | bytes 3145732
  2.0 14.6 %copy-start.1 = (f32[1,2,2,256,256]{4,3,2,1,0:T(8,128)S(1)}, f32[1,2,2,256,256]{4,3,2,1,0:T(8,128)}, u32[]{:S(2)}) copy-start(f32[1,2,2,256,256]{4,3,2,1,0:T(8,128)} %param.7) | copy-start | bytes 3145732
  2.7 13.1 %collective-permute-start.4 = (f32[2,128,256]{2,1,0:T(8,128)S(1)}, f32[2,128,256]{2,1,0:T(8,128)S(1)}, u32[]{:S(2)}, u32[]{:S(2)}) collective-permute-start(f32[2,128,256]{2,1,0:T(8,128)S(1)} %get-tuple-element.58), channel_id=1, source_target_pairs={{0,16},{2,18},{4,20},{6,22},{8,24},{10,26},{12,28},{14,30},{16,0},... | collective-permute-start | bytes 786440 | tf_op jit(solution)/shard_map/ppermute | solution.py:404
  5.3 11.4 %collective-permute-start.5 = (f32[2,128,256]{2,1,0:T(8,128)S(1)}, f32[2,128,256]{2,1,0:T(8,128)S(1)}, u32[]{:S(2)}, u32[]{:S(2)}) collective-permute-start(f32[2,128,256]{2,1,0:T(8,128)S(1)} %get-tuple-element.59), channel_id=1, source_target_pairs={{0,240},{2,242},{4,244},{6,246},{8,248},{10,250},{12,252},{14,254}... | collective-permute-start | bytes 786440 | tf_op jit(solution)/shard_map/ppermute | solution.py:404
  10.9 11.9 %collective-permute-start = (f32[2,128,256]{2,1,0:T(8,128)S(1)}, f32[2,128,256]{2,1,0:T(8,128)S(1)}, u32[]{:S(2)}, u32[]{:S(2)}) collective-permute-start(f32[2,128,256]{2,1,0:T(8,128)S(1)} %get-tuple-element.53), channel_id=1, source_target_pairs={{0,16},{2,18},{4,20},{6,22},{8,24},{10,26},{12,28},{14,30},{16,0},... | collective-permute-start | bytes 786440 | tf_op jit(solution)/shard_map/ppermute | solution.py:404
  10.9 11.9 %collective-permute-start.1 = (f32[2,128,256]{2,1,0:T(8,128)S(1)}, f32[2,128,256]{2,1,0:T(8,128)S(1)}, u32[]{:S(2)}, u32[]{:S(2)}) collective-permute-start(f32[2,128,256]{2,1,0:T(8,128)S(1)} %get-tuple-element.54), channel_id=1, source_target_pairs={{0,240},{2,242},{4,244},{6,246},{8,248},{10,250},{12,252},{14,254}... | collective-permute-start | bytes 786440 | tf_op jit(solution)/shard_map/ppermute | solution.py:404
  12.4 1.9 %copy-start.2 = (f32[2,6,256,256]{3,2,1,0:T(8,128)S(1)}, f32[2,6,256,256]{3,2,1,0:T(8,128)}, u32[]{:S(2)}) copy-start(f32[2,6,256,256]{3,2,1,0:T(8,128)} %refs_1_.2) | copy-start | bytes 9437188
  14.3 0.9 copy-start.5
  15.8 5.5 %copy-start.3 = (f32[1,2,256,256]{3,2,1,0:T(8,128)S(1)}, f32[1,2,256,256]{3,2,1,0:T(8,128)}, u32[]{:S(2)}) copy-start(f32[1,2,256,256]{3,2,1,0:T(8,128)} %param.12) | copy-start | bytes 1572868
  15.8 5.5 %copy-start.4 = (bf16[4,256,256]{2,1,0:T(8,128)(2,1)S(1)}, bf16[4,256,256]{2,1,0:T(8,128)(2,1)}, u32[]{:S(2)}) copy-start(bf16[4,256,256]{2,1,0:T(8,128)(2,1)} %constant.54.clone.refs_1_) | copy-start | bytes 1572868
  16.7 12.3 %copy-start.6 = (s32[1,2,2]{2,1,0:T(2,128)S(1)}, s32[1,2,2]{2,1,0:T(2,128)}, u32[]{:S(2)}) copy-start(s32[1,2,2]{2,1,0:T(2,128)} %param.10) | copy-start | bytes 52
  17.3 8.6 %collective-permute-start.6 = (f32[2,512,128]{2,1,0:T(8,128)S(1)}, f32[2,512,128]{2,1,0:T(8,128)S(1)}, u32[]{:S(2)}, u32[]{:S(2)}) collective-permute-start(f32[2,512,128]{2,1,0:T(8,128)S(1)} %get-tuple-element.61), channel_id=1, source_target_pairs={{0,2},{2,0},{4,6},{6,4},{8,10},{10,8},{12,14},{14,12},{16,18},{18,... | collective-permute-start | bytes 1572872 | tf_op jit(solution)/shard_map/ppermute | solution.py:404
  20.1 8.9 %collective-permute-start.7 = (f32[2,512,128]{2,1,0:T(8,128)S(1)}, f32[2,512,128]{2,1,0:T(8,128)S(1)}, u32[]{:S(2)}, u32[]{:S(2)}) collective-permute-start(f32[2,512,128]{2,1,0:T(8,128)S(1)} %get-tuple-element.62), channel_id=1, source_target_pairs={{0,14},{2,4},{4,2},{6,8},{8,6},{10,12},{12,10},{14,0},{16,30},{18,... | collective-permute-start | bytes 1572872 | tf_op jit(solution)/shard_map/ppermute | solution.py:404
  23.4 12.8 %collective-permute-start.2 = (f32[2,512,128]{2,1,0:T(8,128)S(1)}, f32[2,512,128]{2,1,0:T(8,128)S(1)}, u32[]{:S(2)}, u32[]{:S(2)}) collective-permute-start(f32[2,512,128]{2,1,0:T(8,128)S(1)} %get-tuple-element.56), channel_id=1, source_target_pairs={{0,2},{2,0},{4,6},{6,4},{8,10},{10,8},{12,14},{14,12},{16,18},{18,... | collective-permute-start | bytes 1572872 | tf_op jit(solution)/shard_map/ppermute | solution.py:404
  25.2 11.0 %collective-permute-start.3 = (f32[2,512,128]{2,1,0:T(8,128)S(1)}, f32[2,512,128]{2,1,0:T(8,128)S(1)}, u32[]{:S(2)}, u32[]{:S(2)}) collective-permute-start(f32[2,512,128]{2,1,0:T(8,128)S(1)} %get-tuple-element.57), channel_id=1, source_target_pairs={{0,14},{2,4},{4,2},{6,8},{8,6},{10,12},{12,10},{14,0},{16,30},{18,... | collective-permute-start | bytes 1572872 | tf_op jit(solution)/shard_map/ppermute | solution.py:404
  39.5 8.4 %collective-permute-start.8 = (f32[256,256]{1,0:T(8,128)S(1)}, f32[256,256]{1,0:T(8,128)S(1)}, u32[]{:S(2)}, u32[]{:S(2)}) collective-permute-start(f32[256,256]{1,0:T(8,128)S(1)} %get-tuple-element.70.refs_1_), channel_id=1, source_target_pairs={{0,1},{1,0},{2,3},{3,2},{4,5},{5,4},{6,7},{7,6},{8,9},{9,8},{10,11... | collective-permute-start | bytes 786440 | tf_op jit(solution)/shard_map/ppermute | solution.py:408
  45.1 8.3 %collective-permute-start.10 = (f32[256,256]{1,0:T(8,128)S(1)}, f32[256,256]{1,0:T(8,128)S(1)}, u32[]{:S(2)}, u32[]{:S(2)}) collective-permute-start(f32[256,256]{1,0:T(8,128)S(1)} %get-tuple-element.83.refs_4_), channel_id=1, source_target_pairs={{0,1},{1,0},{2,3},{3,2},{4,5},{5,4},{6,7},{7,6},{8,9},{9,8},{10,11... | collective-permute-start | bytes 786440 | tf_op jit(solution)/shard_map/ppermute | solution.py:408
  57.2 9.8 %collective-permute-start.12 = (f32[2,512,128]{2,1,0:T(8,128)S(1)}, f32[2,512,128]{2,1,0:T(8,128)S(1)}, u32[]{:S(2)}, u32[]{:S(2)}) collective-permute-start(f32[2,512,128]{2,1,0:T(8,128)S(1)} %get-tuple-element.90), channel_id=1, source_target_pairs={{0,2},{2,0},{4,6},{6,4},{8,10},{10,8},{12,14},{14,12},{16,18},{18,... | collective-permute-start | bytes 1572872 | tf_op jit(solution)/shard_map/ppermute | solution.py:404
  59.6 8.9 %collective-permute-start.13 = (f32[2,512,128]{2,1,0:T(8,128)S(1)}, f32[2,512,128]{2,1,0:T(8,128)S(1)}, u32[]{:S(2)}, u32[]{:S(2)}) collective-permute-start(f32[2,512,128]{2,1,0:T(8,128)S(1)} %get-tuple-element.91), channel_id=1, source_target_pairs={{0,14},{2,4},{4,2},{6,8},{8,6},{10,12},{12,10},{14,0},{16,30},{18,... | collective-permute-start | bytes 1572872 | tf_op jit(solution)/shard_map/ppermute | solution.py:404
  60.8 12.3 %collective-permute-start.9 = (f32[1,256,256]{2,1,0:T(8,128)S(1)}, f32[1,256,256]{2,1,0:T(8,128)S(1)}, u32[]{:S(2)}, u32[]{:S(2)}) collective-permute-start(f32[1,256,256]{2,1,0:T(8,128)S(1)} %get-tuple-element.79), channel_id=1, source_target_pairs={{0,1},{1,0},{2,3},{3,2},{4,5},{5,4},{6,7},{7,6},{8,9},{9,8},{10,11... | collective-permute-start | bytes 786440 | tf_op jit(solution)/shard_map/ppermute | solution.py:408
  66.5 7.2 %collective-permute-start.11 = (f32[1,256,256]{2,1,0:T(8,128)S(1)}, f32[1,256,256]{2,1,0:T(8,128)S(1)}, u32[]{:S(2)}, u32[]{:S(2)}) collective-permute-start(f32[1,256,256]{2,1,0:T(8,128)S(1)} %get-tuple-element.88), channel_id=1, source_target_pairs={{0,1},{1,0},{2,3},{3,2},{4,5},{5,4},{6,7},{7,6},{8,9},{9,8},{10,11... | collective-permute-start | bytes 786440 | tf_op jit(solution)/shard_map/ppermute | solution.py:408
  69.2 15.7 %collective-permute-start.19 = (f32[2,128,256]{2,1,0:T(8,128)S(1)}, f32[2,128,256]{2,1,0:T(8,128)S(1)}, u32[]{:S(2)}, u32[]{:S(2)}) collective-permute-start(f32[2,128,256]{2,1,0:T(8,128)S(1)} %get-tuple-element.99), channel_id=1, source_target_pairs={{0,240},{2,242},{4,244},{6,246},{8,248},{10,250},{12,252},{14,254}... | collective-permute-start | bytes 786440 | tf_op jit(solution)/shard_map/ppermute | solution.py:404
  73.1 11.8 %collective-permute-start.18 = (f32[2,128,256]{2,1,0:T(8,128)S(1)}, f32[2,128,256]{2,1,0:T(8,128)S(1)}, u32[]{:S(2)}, u32[]{:S(2)}) collective-permute-start(f32[2,128,256]{2,1,0:T(8,128)S(1)} %get-tuple-element.92.refs_6_), channel_id=1, source_target_pairs={{0,16},{2,18},{4,20},{6,22},{8,24},{10,26},{12,28},{14,30},{16,0},... | collective-permute-start | bytes 786440 | tf_op jit(solution)/shard_map/ppermute | solution.py:404
  74.8 15.4 %collective-permute-start.15 = (f32[1,512,128]{2,1,0:T(8,128)S(1)}, f32[1,512,128]{2,1,0:T(8,128)S(1)}, u32[]{:S(2)}, u32[]{:S(2)}) collective-permute-start(f32[1,512,128]{2,1,0:T(8,128)S(1)} %get-tuple-element.94), channel_id=1, source_target_pairs={{0,14},{2,4},{4,2},{6,8},{8,6},{10,12},{12,10},{14,0},{16,30},{18,... | collective-permute-start | bytes 786440 | tf_op jit(solution)/shard_map/ppermute | solution.py:404
  84.6 5.6 %collective-permute-start.14 = (f32[1,512,128]{2,1,0:T(8,128)S(1)}, f32[1,512,128]{2,1,0:T(8,128)S(1)}, u32[]{:S(2)}, u32[]{:S(2)}) collective-permute-start(f32[1,512,128]{2,1,0:T(8,128)S(1)} %get-tuple-element.93.refs_5_), channel_id=1, source_target_pairs={{0,2},{2,0},{4,6},{6,4},{8,10},{10,8},{12,14},{14,12},{16,18},{18,... | collective-permute-start | bytes 786440 | tf_op jit(solution)/shard_map/ppermute | solution.py:404
  85.5 12.4 %collective-permute-start.20 = (f32[1,256,256]{2,1,0:T(8,128)S(1)}, f32[1,256,256]{2,1,0:T(8,128)S(1)}, u32[]{:S(2)}, u32[]{:S(2)}) collective-permute-start(f32[1,256,256]{2,1,0:T(8,128)S(1)} %get-tuple-element.100.refs_3_), channel_id=1, source_target_pairs={{0,1},{1,0},{2,3},{3,2},{4,5},{5,4},{6,7},{7,6},{8,9},{9,8},{10,11... | collective-permute-start | bytes 786440 | tf_op jit(solution)/shard_map/ppermute | solution.py:408
  90.8 5.2 %collective-permute-start.16 = (f32[1,128,256]{2,1,0:T(8,128)S(1)}, f32[1,128,256]{2,1,0:T(8,128)S(1)}, u32[]{:S(2)}, u32[]{:S(2)}) collective-permute-start(f32[1,128,256]{2,1,0:T(8,128)S(1)} %get-tuple-element.96), channel_id=1, source_target_pairs={{0,16},{2,18},{4,20},{6,22},{8,24},{10,26},{12,28},{14,30},{16,0},... | collective-permute-start | bytes 393224 | tf_op jit(solution)/shard_map/ppermute | solution.py:404
  90.9 7.0 %collective-permute-start.17 = (f32[1,128,256]{2,1,0:T(8,128)S(1)}, f32[1,128,256]{2,1,0:T(8,128)S(1)}, u32[]{:S(2)}, u32[]{:S(2)}) collective-permute-start(f32[1,128,256]{2,1,0:T(8,128)S(1)} %get-tuple-element.97), channel_id=1, source_target_pairs={{0,240},{2,242},{4,244},{6,246},{8,248},{10,250},{12,252},{14,254}... | collective-permute-start | bytes 393224 | tf_op jit(solution)/shard_map/ppermute | solution.py:404
  94.1 10.9 %collective-permute-start.22 = (f32[1,256,256]{2,1,0:T(8,128)S(1)}, f32[1,256,256]{2,1,0:T(8,128)S(1)}, u32[]{:S(2)}, u32[]{:S(2)}) collective-permute-start(f32[1,256,256]{2,1,0:T(8,128)S(1)} %get-tuple-element.101.refs_5_), channel_id=1, source_target_pairs={{0,1},{1,0},{2,3},{3,2},{4,5},{5,4},{6,7},{7,6},{8,9},{9,8},{10,11... | collective-permute-start | bytes 786440 | tf_op jit(solution)/shard_map/ppermute | solution.py:408
  98.5 12.1 %collective-permute-start.21 = (f32[1,256,256]{2,1,0:T(8,128)S(1)}, f32[1,256,256]{2,1,0:T(8,128)S(1)}, u32[]{:S(2)}, u32[]{:S(2)}) collective-permute-start(f32[1,256,256]{2,1,0:T(8,128)S(1)} %rows_first.1.refs_1_), channel_id=1, source_target_pairs={{0,1},{1,0},{2,3},{3,2},{4,5},{5,4},{6,7},{7,6},{8,9},{9,8},{10,11... | collective-permute-start | bytes 786440 | tf_op jit(solution)/shard_map/ppermute | solution.py:408

commit v7 on v6

--- a/solution.py
+++ b/solution.py
@@ -67,7 +67,7 @@
     return diag, left_form(*corners, jnp)
 
 
-def sandwich(diag, corner, re, im, right):
+def prop_left(diag, corner, re, im):
     n = re.shape[0]
     h, a, b = n // 2, n // 2 - BAND, n // 2 + BAND
     re, im = re.astype(BF16), im.astype(BF16)
@@ -78,33 +78,27 @@
     mid, top, low = mid[2 * BAND :], top[h:], low[h:]
     im = [top[:a], top[a:h] + mid[:BAND], low[:BAND] + mid[BAND:], low[BAND:]]
     re, im = jnp.concatenate(re, axis=0), jnp.concatenate(im, axis=0)
-    both = mm(beside(re.astype(BF16), im.astype(BF16)), right[...])
-    return both[:, :n], both[:, n:]
-
-
-def dft_sandwich(tabs, re, im):
+    return beside(re.astype(BF16), im.astype(BF16))
+
+
+def dft_left(tabs, re, im):
     h = re.shape[0] // 2
     even = mm(tabs[0], above(re[:h] + re[h:], im[:h] + im[h:]).astype(BF16))
     odd = mm(tabs[1], above(re[:h] - re[h:], im[:h] - im[h:]).astype(BF16))
     re, im = above(even[:h], odd[:h]), above(even[h:], odd[h:])
-    e = mm(beside(re[:, :h] + re[:, h:], im[:, :h] + im[:, h:]).astype(BF16), tabs[2])
-    o = mm(beside(re[:, :h] - re[:, h:], im[:, :h] - im[:, h:]).astype(BF16), tabs[3])
-    return e, o
-
-
-def conj_dft_sandwich(tabs, e, o):
+    e = beside(re[:, :h] + re[:, h:], im[:, :h] + im[:, h:])
+    o = beside(re[:, :h] - re[:, h:], im[:, :h] - im[:, h:])
+    return beside(e.astype(BF16), o.astype(BF16))
+
+
+def conj_dft_left(tabs, e, o):
     h = e.shape[0] // 2
     e, o = e.astype(BF16), o.astype(BF16)
     even = mm(tabs[2], above(beside(e[:h, :h], o[:h, :h]), beside(e[:h, h:], o[:h, h:])))
     odd = mm(tabs[3], above(beside(e[h:, :h], o[h:, :h]), beside(e[h:, h:], o[h:, h:])))
     re = above(even[:h] + odd[:h], even[:h] - odd[:h]).astype(BF16)
     im = above(even[h:] + odd[h:], even[h:] - odd[h:]).astype(BF16)
-    e = mm(beside(re[:, :h], im[:, :h]), tabs[0])
-    o = mm(beside(re[:, h:], im[:, h:]), tabs[1])
-    return (
-        beside(e[:, :h] + o[:, :h], e[:, :h] - o[:, :h]),
-        beside(e[:, h:] + o[:, h:], e[:, h:] - o[:, h:]),
-    )
+    return beside(beside(re[:, :h], im[:, :h]), beside(re[:, h:], im[:, h:]))
 
 
 def place_of(off_ref, slot, h):
@@ -163,85 +157,107 @@
             canvas[part, pl.ds(top, n + 8), pl.ds(block, n + h)] += pltpu.roll(wide, col_rest, 1)
 
 
-def each_mode(modes, step):
-    for m in range(modes):
-        step(m)
-
-
 def times(a_re, a_im, b_re, b_im):
     return a_re * b_re - a_im * b_im, a_re * b_im + a_im * b_re
 
 
-def waves(probe, patch, diag, corner, right, wave):
-    def step(m):
-        e_re, e_im = times(probe[0, m], probe[1, m], patch[0], patch[1])
-        wave[m, 0], wave[m, 1] = sandwich(diag, corner, e_re, e_im, right)
-
-    each_mode(probe.shape[1], step)
-
-
-def fars(wave, patch, tabs, far, inten):
-    h = inten.shape[0] // 2
-    inten[...] = jnp.zeros_like(inten)
-
-    def step(m):
-        e, o = dft_sandwich(tabs, *times(wave[m, 0], wave[m, 1], patch[0], patch[1]))
+def by_mode(held, modes, left):
+    n = held.shape[0] // modes
+    rows = [slice(m * n, (m + 1) * n) for m in range(modes)]
+    for m in range(modes):
+        held[rows[m]] = left(m)
+    return rows
+
+
+def waves(probe, patch, diag, corner, right, wave, held):
+    n = patch.shape[-1]
+
+    def left(m):
+        return prop_left(diag, corner, *times(probe[0, m], probe[1, m], patch[0], patch[1]))
+
+    rows = by_mode(held, probe.shape[1], left)
+    both = mm(held[...], right[...])
+    for m, at in enumerate(rows):
+        wave[m, 0] = both[at, :n]
+        wave[m, 1] = both[at, n:]
+
+
+def fars(wave, patch, tabs, far, inten, held):
+    n = patch.shape[-1]
+    h = n // 2
+
+    def left(m):
+        return dft_left(tabs, *times(wave[m, 0], wave[m, 1], patch[0], patch[1]))
+
+    rows = by_mode(held, wave.shape[0], left)
+    evens, odds = mm(held[:, :n], tabs[2]), mm(held[:, n:], tabs[3])
+    total_e = total_o = 0.0
+    for m, at in enumerate(rows):
+        e, o = evens[at], odds[at]
         far[m, 0] = e
         far[m, 1] = o
-        e, o = e * e, o * o
-        inten[...] += beside(e[:, :h] + e[:, h:], o[:, :h] + o[:, h:])
-
-    each_mode(wave.shape[0], step)
+        total_e += e * e
+        total_o += o * o
+    inten[...] = beside(total_e[:, :h] + total_e[:, h:], total_o[:, :h] + total_o[:, h:])
 
 
 def waves_first_kernel(off, info, own, rows_a, rows_b, cols_a, cols_b, probe, diag, corner,
-                       mat, canvas, patch, wave):
+                       mat, canvas, patch, wave, held):
     build_canvas(0, info, own, rows_a, rows_b, cols_a, cols_b, canvas)
     extract(off, 0, canvas, patch)
-    waves(probe, patch, diag, corner, mat, wave)
-
-
-def waves_next_kernel(off, canvas, probe, diag, corner, mat, patch, wave):
+    waves(probe, patch, diag, corner, mat, wave, held)
+
+
+def waves_next_kernel(off, canvas, probe, diag, corner, mat, patch, wave, held):
     extract(off, 1, canvas, patch)
-    waves(probe, patch, diag, corner, mat, wave)
+    waves(probe, patch, diag, corner, mat, wave, held)
 
 
 def fars_first_kernel(off, info, own, rows_a, rows_b, cols_a, cols_b, wave, tabs, canvas, patch,
-                      far, inten):
+                      far, inten, held):
     build_canvas(1, info, own, rows_a, rows_b, cols_a, cols_b, canvas)
     extract(off, 0, canvas, patch)
-    fars(wave, patch, tabs, far, inten)
-
-
-def fars_next_kernel(off, canvas, wave, tabs, patch, far, inten):
+    fars(wave, patch, tabs, far, inten, held)
+
+
+def fars_next_kernel(off, canvas, wave, tabs, patch, far, inten, held):
     extract(off, 1, canvas, patch)
-    fars(wave, patch, tabs, far, inten)
-
-
-def back_last(slot, counts, mine, other, measured, far, wave, patch, tabs, grad, bar, resid):
+    fars(wave, patch, tabs, far, inten, held)
+
+
+def back_last(slot, counts, mine, other, measured, far, wave, patch, tabs, grad, bar, resid, held):
     n = mine.shape[0]
     h = n // 2
     live = jnp.where(slot < counts[0], 2.0, 0.0).astype(F32)
     r = (mine[...] + other[...] - measured[slot]) * live
     resid[0] = beside(r[:, :h], r[:, :h])
     resid[1] = beside(r[:, h:], r[:, h:])
-    grad[...] = jnp.zeros_like(grad)
-
-    def step(m):
-        b_re, b_im = conj_dft_sandwich(tabs, resid[0] * far[m, 0], resid[1] * far[m, 1])
+    rows = by_mode(
+        held,
+        far.shape[0],
+        lambda m: conj_dft_left(tabs, resid[0] * far[m, 0], resid[1] * far[m, 1]),
+    )
+    evens, odds = mm(held[:, :n], tabs[0]), mm(held[:, n:], tabs[1])
+    g_re = g_im = 0.0
+    o_re, o_im = patch[0], patch[1]
+    for m, at in enumerate(rows):
+        e, o = evens[at], odds[at]
+        b_re = beside(e[:, :h] + o[:, :h], e[:, :h] - o[:, :h])
+        b_im = beside(e[:, h:] + o[:, h:], e[:, h:] - o[:, h:])
         w_re, w_im = wave[m, 0], wave[m, 1]
-        grad[0] += w_re * b_re + w_im * b_im
-        grad[1] += w_re * b_im - w_im * b_re
-        o_re, o_im = patch[0], patch[1]
+        g_re += w_re * b_re + w_im * b_im
+        g_im += w_re * b_im - w_im * b_re
         bar[m, 0] = (o_re * b_re + o_im * b_im).astype(BF16)
         bar[m, 1] = (o_re * b_im - o_im * b_re).astype(BF16)
-
-    each_mode(far.shape[0], step)
+    grad[0] = g_re
+    grad[1] = g_im
 
 
 def back_last_place_kernel(slot, counts, off, info, before, mine, other, measured, far, wave, patch,
-                           tabs, bar, out_a, out_c, out_b, resid, grad, canvas):
-    back_last(slot, counts, mine, other, measured, far, wave, patch, tabs, grad, bar, resid)
+                           tabs, bar, out_a, out_c, out_b, resid, held, grad, canvas):
+    back_last(
+        slot, counts, mine, other, measured, far, wave, patch, tabs, grad, bar, resid, held
+    )
     lay(off, (before, grad), canvas)
     n = grad.shape[-1]
     h = n // 2
@@ -249,19 +265,23 @@
     out_c[...] = canvas[:, :, h : h + n]
 
 
-def back_first_kernel(info, bar, probe, patch, diag, corner, mat, keep, send, part, grad):
-    grad[...] = jnp.zeros_like(grad)
-
-    def step(m):
-        b_re, b_im = sandwich(diag, corner, bar[m, 0], bar[m, 1], mat)
+def back_first_kernel(info, bar, probe, patch, diag, corner, mat, keep, send, part, grad, held):
+    n = patch.shape[-1]
+    rows = by_mode(
+        held, probe.shape[1], lambda m: prop_left(diag, corner, bar[m, 0], bar[m, 1])
+    )
+    both = mm(held[...], mat[...])
+    g_re = g_im = 0.0
+    o_re, o_im = patch[0], patch[1]
+    for m, at in enumerate(rows):
+        b_re, b_im = both[at, :n], both[at, n:]
         p_re, p_im = probe[0, m], probe[1, m]
-        grad[0] += p_re * b_re + p_im * b_im
-        grad[1] += p_re * b_im - p_im * b_re
-        o_re, o_im = patch[0], patch[1]
+        g_re += p_re * b_re + p_im * b_im
+        g_im += p_re * b_im - p_im * b_re
         part[0, m] = o_re * b_re + o_im * b_im
         part[1, m] = o_re * b_im - o_im * b_re
-
-    each_mode(probe.shape[1], step)
+    grad[0] = g_re
+    grad[1] = g_im
     mode = info[4]
     keep[0] = grad[mode]
     send[0] = grad[1 - mode]
@@ -449,6 +469,7 @@
     one, pair, mat = ((1, n, n), F32), ((2, n, n), F32), ((2 * n, 2 * n), BF16)
     plane, field, probes = ((n, n), F32), ((modes, 2, n, n), F32), ((2, modes, n, n), F32)
     band = (((2, n, n), BF16), ((4 * BAND, 4 * BAND), BF16), mat)
+    held = ((modes * n, 2 * n), BF16)
     strip, tall = ((2, h, n), F32), ((2, 2 * n, h), F32)
 
     picked = call(pick_rows_kernel, "pick_rows", (strip,) * 4, (info, own), copies=4)
@@ -484,23 +505,26 @@
         "waves_0",
         (((2, 2 * n, 2 * n), F32), pair, field),
         (off, info, *first, probe, *prop),
+        scratch=(held,),
         smem=2,
         after=(),
     )
     patch_first1, wave1 = call(
-        waves_next_kernel, "waves_1", (pair, field), (off, canvas, probe, *prop), after=()
+        waves_next_kernel, "waves_1", (pair, field), (off, canvas, probe, *prop), scratch=(held,),
+        after=()
     )
     canvas, patch_last0, far0, inten0 = call(
         fars_first_kernel,
         "fars_0",
         (((2, 2 * n, 2 * n), F32), pair, field, plane),
         (off, info, *last, wave0, tabs),
+        scratch=(held,),
         smem=2,
         after=(patch_first1,),
     )
     other0 = swap_mode(inten0)
     patch_last1, far1, inten1 = call(
-        fars_next_kernel, "fars_1", (pair, field, plane), (off, canvas, wave1, tabs)
+        fars_next_kernel, "fars_1", (pair, field, plane), (off, canvas, wave1, tabs), scratch=(held,)
     )
     other1 = swap_mode(inten1)
 
@@ -512,14 +536,14 @@
         "back_last_0",
         (pair, bar_out),
         (counts, inten0, other0, measured, far0, wave0, patch_last0, tabs),
-        scratch=(pair,),
+        scratch=(pair, held),
     )
     keep0, send0, part0 = call(
         back_first_kernel,
         "back_first_0",
         (one, one, probes),
         (info, bar0, probe, patch_first0, *back_prop),
-        scratch=(pair,),
+        scratch=(pair, held),
     )
     got0 = swap_mode(send0)
     bar1, out_a, out_c, out_b = call(
@@ -527,7 +551,7 @@
         "back_last_1",
         (bar_out,) + strips,
         (counts, off, info, grad_last0, inten1, other1, measured, far1, wave1, patch_last1, tabs),
-        scratch=(pair, pair, wide),
+        scratch=(pair, held, pair, wide),
         smem=3,
         after=(keep0,),
     )
@@ -549,7 +573,7 @@
         "back_first_1",
         (one, one, probes),
         (info, bar1, probe, patch_first1, *back_prop),
-        scratch=(pair,),
+        scratch=(pair, held),
     )
     got1 = swap_mode(send1)
     strips_last = fold_cols("cols_last", out_a, out_c, out_b, (keep1,))

time: 112 us -> 110 us (0.982)
  waiting for transfers between devices: 16.1 us -> 20.8 us
  starting transfers between devices: 52.4 us -> 48.2 us
  Pallas kernels: 37.9 us -> 34.6 us
    ppermute x7, waiting for transfers between devices: 8.71 us -> 15 us  [swap_mode(): return lax.ppermute(value, 'mode', [(0, 1), (1, 0)])]
    ppermute x16, starting transfers between devices: 36.8 us -> 32.1 us  [swap(): return lax.ppermute(value, 'tile', pairs)]
    pallas_call x21, Pallas kernels: 37.9 us -> 34.6 us  [call(): pl.pallas_call(run, out_shape=tuple((jax.ShapeDtypeStruct(shape, dtype) f...]
    ppermute x16, waiting for transfers between devices: 7.38 us -> 5.8 us  [swap(): return lax.ppermute(value, 'tile', pairs)]
  transfers between devices with their start and end apart: 23 -> 23, of which waited for: 9 -> 8; matrix products, arithmetic and copies ran while one was open for 0% -> 0% of each run, Pallas kernels for 26% -> 24%
where the time goes in v7:
time: 110 us; the launch traced here: 109 us
  starting transfers between devices  48.2 us (44%)
  Pallas kernels  34.6 us (31%)
  waiting for transfers between devices  20.8 us (19%)
  local copies, waits for them, and re-layouts  4.19 us (4%)
  between operations  1.59 us (1%)
    pallas_call x21, Pallas kernels, call(): pl.pallas_call(run, out_shape=tuple((jax.ShapeDtypeStruct(shape, dtype) f...  34.6 us
    ppermute x16, starting transfers between devices, swap(): return lax.ppermute(value, 'tile', pairs)  32.1 us
    ppermute x7, starting transfers between devices, swap_mode(): return lax.ppermute(value, 'mode', [(0, 1), (1, 0)])  16.1 us
    ppermute x7, waiting for transfers between devices, swap_mode(): return lax.ppermute(value, 'mode', [(0, 1), (1, 0)])  15 us
    ppermute x16, waiting for transfers between devices, swap(): return lax.ppermute(value, 'tile', pairs)  5.8 us
    unnamed x14, local copies, waits for them, and re-layouts  4.08 us
  transfers between devices with their start and end apart: 23, of which 8 were waited for; matrix products, arithmetic and copies ran while one was open for 0% of the time, Pallas kernels for 24%

profile of v7, /device:TPU:1, one launch (start us, length us, event | category | flops | bytes accessed | tf_op | source)
XLA Modules:
  0.0 109.4 jit_solution(4004035955838020812)
XLA Ops:
  2.7 2.6 %collective-permute-start.4 = (f32[2,128,256]{2,1,0:T(8,128)S(1)}, f32[2,128,256]{2,1,0:T(8,128)S(1)}, u32[]{:S(2)}, u32[]{:S(2)}) collective-permute-start(f32[2,128,256]{2,1,0:T(8,128)S(1)} %get-tuple-element.58), channel_id=1, source_target_pairs={{0,16},{2,18},{4,20},{6,22},{8,24},{10,26},{12,28},{14,30},{16,0},... | collective-permute-start | bytes 786440 | tf_op jit(solution)/shard_map/ppermute | solution.py:424
  5.3 5.7 %collective-permute-start.5 = (f32[2,128,256]{2,1,0:T(8,128)S(1)}, f32[2,128,256]{2,1,0:T(8,128)S(1)}, u32[]{:S(2)}, u32[]{:S(2)}) collective-permute-start(f32[2,128,256]{2,1,0:T(8,128)S(1)} %get-tuple-element.59), channel_id=1, source_target_pairs={{0,240},{2,242},{4,244},{6,246},{8,248},{10,250},{12,252},{14,254}... | collective-permute-start | bytes 786440 | tf_op jit(solution)/shard_map/ppermute | solution.py:424
  10.9 1.5 %collective-permute-start.1 = (f32[2,128,256]{2,1,0:T(8,128)S(1)}, f32[2,128,256]{2,1,0:T(8,128)S(1)}, u32[]{:S(2)}, u32[]{:S(2)}) collective-permute-start(f32[2,128,256]{2,1,0:T(8,128)S(1)} %get-tuple-element.54), channel_id=1, source_target_pairs={{0,240},{2,242},{4,244},{6,246},{8,248},{10,250},{12,252},{14,254}... | collective-permute-start | bytes 786440 | tf_op jit(solution)/shard_map/ppermute | solution.py:424
  12.4 1.9 %copy-done.2 = f32[2,6,256,256]{3,2,1,0:T(8,128)S(1)} copy-done((f32[2,6,256,256]{3,2,1,0:T(8,128)S(1)}, f32[2,6,256,256]{3,2,1,0:T(8,128)}, u32[]{:S(2)}) %copy-start.2) | copy-done | bytes 3145752
  17.3 2.8 %collective-permute-start.6 = (f32[2,512,128]{2,1,0:T(8,128)S(1)}, f32[2,512,128]{2,1,0:T(8,128)S(1)}, u32[]{:S(2)}, u32[]{:S(2)}) collective-permute-start(f32[2,512,128]{2,1,0:T(8,128)S(1)} %get-tuple-element.61), channel_id=1, source_target_pairs={{0,2},{2,0},{4,6},{6,4},{8,10},{10,8},{12,14},{14,12},{16,18},{18,... | collective-permute-start | bytes 1572872 | tf_op jit(solution)/shard_map/ppermute | solution.py:424
  21.3 1.5 %reorder.1 = (f32[2,256,256]{2,1,0:T(8,128)S(1)}, bf16[4,256,256]{2,1,0:T(8,128)(2,1)S(1)}) custom-call(f32[2,256,256]{2,1,0:T(8,128)S(1)} %bitcast.13, bf16[4,256,256]{2,1,0:T(8,128)(2,1)S(1)} %copy-done.4), custom_call_target="tpu_custom_call" | custom-call | tf_op jit(solution)/shard_map/reorder/pallas_call | solution.py:440
  23.4 1.8 %collective-permute-start.2 = (f32[2,512,128]{2,1,0:T(8,128)S(1)}, f32[2,512,128]{2,1,0:T(8,128)S(1)}, u32[]{:S(2)}, u32[]{:S(2)}) collective-permute-start(f32[2,512,128]{2,1,0:T(8,128)S(1)} %get-tuple-element.56), channel_id=1, source_target_pairs={{0,2},{2,0},{4,6},{6,4},{8,10},{10,8},{12,14},{14,12},{16,18},{18,... | collective-permute-start | bytes 1572872 | tf_op jit(solution)/shard_map/ppermute | solution.py:424
  25.9 3.1 %collective-permute-done.7.refs_6_ = f32[2,512,128]{2,1,0:T(8,128)S(1)} collective-permute-done((f32[2,512,128]{2,1,0:T(8,128)S(1)}, f32[2,512,128]{2,1,0:T(8,128)S(1)}, u32[]{:S(2)}, u32[]{:S(2)}) %collective-permute-start.7) | collective-permute-done | bytes 524320 | tf_op jit(solution)/shard_map/ppermute | solution.py:424
  29.0 3.2 %waves_0.1 = (f32[2,512,512]{2,1,0:T(8,128)S(1)}, f32[2,256,256]{2,1,0:T(8,128)S(1)}, f32[6,2,256,256]{3,2,1,0:T(8,128)S(1)}) custom-call(s32[2,2]{1,0:T(2,128)S(1)} %bitcast.14, s32[5]{0:T(128)S(1)} %convert_element_type.3.refs_0_.refs_1_.refs_2_, f32[2,2,256,256]{3,2,1,0:T(8,128)S(1)} %bitcast.11, ...), custom_call_target="tpu_custom_call" | custom-call | tf_op jit(solution)/shard_map/waves_0/pallas_call | solution.py:440
  32.2 2.9 %waves_1.1 = (f32[2,256,256]{2,1,0:T(8,128)S(1)}, f32[6,2,256,256]{3,2,1,0:T(8,128)S(1)}) custom-call(s32[2,2]{1,0:T(2,128)S(1)} %bitcast.15, f32[2,512,512]{2,1,0:T(8,128)S(1)} %get-tuple-element.68.refs_1_, f32[2,6,256,256]{3,2,1,0:T(8,128)S(1)} %get-tuple-element.60.refs_4_.refs_7_.refs_2_, bf16[2,256,256]{2,1,0:T(8,128)(2,1)S(1)} %get-tuple-element.63.refs_8_.refs_3_, ...), custom_call_target="tpu_custom_call" | custom-call | tf_op jit(solution)/shard_map/waves_1/pallas_call | solution.py:440
  35.1 2.9 %fars_0.1 = (f32[2,512,512]{2,1,0:T(8,128)S(1)}, f32[2,256,256]{2,1,0:T(8,128)S(1)}, f32[6,2,256,256]{3,2,1,0:T(8,128)S(1)}, f32[256,256]{1,0:T(8,128)S(1)}) custom-call(s32[2,2]{1,0:T(2,128)S(1)} %bitcast.16, s32[5]{0:T(128)S(1)} %convert_element_type.3.refs_0_.refs_1_.refs_2_, f32[2,2,256,256]{3,2,1,0:T(8,128)S(1)} %bitcast.12, ...), custom_call_target="tpu_custom_call" | custom-call | tf_op jit(solution)/shard_map/fars_0/pallas_call | solution.py:440
  38.1 2.7 %collective-permute-start.8 = (f32[256,256]{1,0:T(8,128)S(1)}, f32[256,256]{1,0:T(8,128)S(1)}, u32[]{:S(2)}, u32[]{:S(2)}) collective-permute-start(f32[256,256]{1,0:T(8,128)S(1)} %get-tuple-element.70.refs_1_), channel_id=1, source_target_pairs={{0,1},{1,0},{2,3},{3,2},{4,5},{5,4},{6,7},{7,6},{8,9},{9,8},{10,11... | collective-permute-start | bytes 786440 | tf_op jit(solution)/shard_map/ppermute | solution.py:428
  40.8 2.7 %fars_1.1 = (f32[2,256,256]{2,1,0:T(8,128)S(1)}, f32[6,2,256,256]{3,2,1,0:T(8,128)S(1)}, f32[256,256]{1,0:T(8,128)S(1)}) custom-call(s32[2,2]{1,0:T(2,128)S(1)} %bitcast.17, f32[2,512,512]{2,1,0:T(8,128)S(1)} %get-tuple-element.81.refs_1_, f32[6,2,256,256]{3,2,1,0:T(8,128)S(1)} %get-tuple-element.82.refs_2_.refs_8_, ...), custom_call_target="tpu_custom_call" | custom-call | tf_op jit(solution)/shard_map/fars_1/pallas_call | solution.py:440
  44.7 1.7 %collective-permute-done.8.refs_2_ = f32[256,256]{1,0:T(8,128)S(1)} collective-permute-done((f32[256,256]{1,0:T(8,128)S(1)}, f32[256,256]{1,0:T(8,128)S(1)}, u32[]{:S(2)}, u32[]{:S(2)}) %collective-permute-start.8) | collective-permute-done | bytes 262176 | tf_op jit(solution)/shard_map/ppermute | solution.py:428
  46.4 1.8 %back_last_0.1 = (f32[2,256,256]{2,1,0:T(8,128)S(1)}, bf16[6,2,256,256]{3,2,1,0:T(8,128)(2,1)S(1)}) custom-call(s32[1]{0:T(128)S(6)} %copy.9.refs_0_, f32[256,256]{1,0:T(8,128)S(1)} %get-tuple-element.70.refs_1_, f32[256,256]{1,0:T(8,128)S(1)} %collective-permute-done.8.refs_2_, f32[2,256,256]{2,1,0:T(8,128)S(1)} %get-tuple-element.55.refs_4_.refs_3_.refs_6_, ...), custom_call_target="tpu_custom_call" | custom-call | tf_op jit(solution)/shard_map/back_last_0/pallas_call | solution.py:440
  48.3 2.8 %back_first_0.1 = (f32[1,256,256]{2,1,0:T(8,128)S(1)}, f32[1,256,256]{2,1,0:T(8,128)S(1)}, f32[2,6,256,256]{3,2,1,0:T(8,128)S(1)}) custom-call(s32[5]{0:T(128)S(1)} %convert_element_type.3.refs_0_.refs_1_.refs_2_, bf16[6,2,256,256]{3,2,1,0:T(8,128)(2,1)S(1)} %get-tuple-element.73.refs_1_, f32[2,6,256,256]{3,2,1,0:T(8,128)S(1)} %get-tuple-element.60.refs_4_.refs_7_.refs_2_, ...), custom_call_target="tpu_custom_call" | custom-call | tf_op jit(solution)/shard_map/back_first_0/pallas_call | solution.py:440
  51.8 3.4 %back_last_1.1 = (bf16[6,2,256,256]{3,2,1,0:T(8,128)(2,1)S(1)}, f32[2,512,128]{2,1,0:T(8,128)S(1)}, f32[2,512,256]{2,1,0:T(8,128)S(1)}, f32[2,512,128]{2,1,0:T(8,128)S(1)}) custom-call(s32[1]{0:T(128)S(6)} %copy.9.refs_0_, s32[2,2]{1,0:T(2,128)S(1)} %bitcast.18, s32[5]{0:T(128)S(1)} %convert_element_type.3.refs_0_.refs_1_.refs_2_, ...), custom_call_target="tpu_custom_call" | custom-call | tf_op jit(solution)/shard_map/back_last_1/pallas_call | solution.py:440
  55.3 2.3 %collective-permute-start.12 = (f32[2,512,128]{2,1,0:T(8,128)S(1)}, f32[2,512,128]{2,1,0:T(8,128)S(1)}, u32[]{:S(2)}, u32[]{:S(2)}) collective-permute-start(f32[2,512,128]{2,1,0:T(8,128)S(1)} %get-tuple-element.90), channel_id=1, source_target_pairs={{0,2},{2,0},{4,6},{6,4},{8,10},{10,8},{12,14},{14,12},{16,18},{18,... | collective-permute-start | bytes 1572872 | tf_op jit(solution)/shard_map/ppermute | solution.py:424
  58.7 2.6 %collective-permute-start.9 = (f32[1,256,256]{2,1,0:T(8,128)S(1)}, f32[1,256,256]{2,1,0:T(8,128)S(1)}, u32[]{:S(2)}, u32[]{:S(2)}) collective-permute-start(f32[1,256,256]{2,1,0:T(8,128)S(1)} %get-tuple-element.79), channel_id=1, source_target_pairs={{0,1},{1,0},{2,3},{3,2},{4,5},{5,4},{6,7},{7,6},{8,9},{9,8},{10,11... | collective-permute-start | bytes 786440 | tf_op jit(solution)/shard_map/ppermute | solution.py:428
  61.4 2.7 %back_first_1.1 = (f32[1,256,256]{2,1,0:T(8,128)S(1)}, f32[1,256,256]{2,1,0:T(8,128)S(1)}, f32[2,6,256,256]{3,2,1,0:T(8,128)S(1)}) custom-call(s32[5]{0:T(128)S(1)} %convert_element_type.3.refs_0_.refs_1_.refs_2_, bf16[6,2,256,256]{3,2,1,0:T(8,128)(2,1)S(1)} %get-tuple-element.86.refs_1_, f32[2,6,256,256]{3,2,1,0:T(8,128)S(1)} %get-tuple-element.60.refs_4_.refs_7_.refs_2_, ...), custom_call_target="tpu_custom_call" | custom-call | tf_op jit(solution)/shard_map/back_first_1/pallas_call | solution.py:440
  64.5 1.9 %collective-permute-done.13.refs_3_ = f32[2,512,128]{2,1,0:T(8,128)S(1)} collective-permute-done((f32[2,512,128]{2,1,0:T(8,128)S(1)}, f32[2,512,128]{2,1,0:T(8,128)S(1)}, u32[]{:S(2)}, u32[]{:S(2)}) %collective-permute-start.13) | collective-permute-done | bytes 524320 | tf_op jit(solution)/shard_map/ppermute | solution.py:424
  67.1 4.0 %collective-permute-start.19 = (f32[2,128,256]{2,1,0:T(8,128)S(1)}, f32[2,128,256]{2,1,0:T(8,128)S(1)}, u32[]{:S(2)}, u32[]{:S(2)}) collective-permute-start(f32[2,128,256]{2,1,0:T(8,128)S(1)} %get-tuple-element.99), channel_id=1, source_target_pairs={{0,240},{2,242},{4,244},{6,246},{8,248},{10,250},{12,252},{14,254}... | collective-permute-start | bytes 786440 | tf_op jit(solution)/shard_map/ppermute | solution.py:424
  71.1 5.6 %collective-permute-done.11.refs_5_.refs_4_ = f32[1,256,256]{2,1,0:T(8,128)S(1)} collective-permute-done((f32[1,256,256]{2,1,0:T(8,128)S(1)}, f32[1,256,256]{2,1,0:T(8,128)S(1)}, u32[]{:S(2)}, u32[]{:S(2)}) %collective-permute-start.11) | collective-permute-done | bytes 262176 | tf_op jit(solution)/shard_map/ppermute | solution.py:428
  77.7 4.8 %collective-permute-start.15 = (f32[1,512,128]{2,1,0:T(8,128)S(1)}, f32[1,512,128]{2,1,0:T(8,128)S(1)}, u32[]{:S(2)}, u32[]{:S(2)}) collective-permute-start(f32[1,512,128]{2,1,0:T(8,128)S(1)} %get-tuple-element.94), channel_id=1, source_target_pairs={{0,14},{2,4},{4,2},{6,8},{8,6},{10,12},{12,10},{14,0},{16,30},{18,... | collective-permute-start | bytes 786440 | tf_op jit(solution)/shard_map/ppermute | solution.py:424
  83.2 3.0 %collective-permute-start.20 = (f32[1,256,256]{2,1,0:T(8,128)S(1)}, f32[1,256,256]{2,1,0:T(8,128)S(1)}, u32[]{:S(2)}, u32[]{:S(2)}) collective-permute-start(f32[1,256,256]{2,1,0:T(8,128)S(1)} %get-tuple-element.100.refs_3_), channel_id=1, source_target_pairs={{0,1},{1,0},{2,3},{3,2},{4,5},{5,4},{6,7},{7,6},{8,9},{9,8},{10,11... | collective-permute-start | bytes 786440 | tf_op jit(solution)/shard_map/ppermute | solution.py:428
  88.0 3.6 %collective-permute-start.17 = (f32[1,128,256]{2,1,0:T(8,128)S(1)}, f32[1,128,256]{2,1,0:T(8,128)S(1)}, u32[]{:S(2)}, u32[]{:S(2)}) collective-permute-start(f32[1,128,256]{2,1,0:T(8,128)S(1)} %get-tuple-element.97), channel_id=1, source_target_pairs={{0,240},{2,242},{4,244},{6,246},{8,248},{10,250},{12,252},{14,254}... | collective-permute-start | bytes 393224 | tf_op jit(solution)/shard_map/ppermute | solution.py:424
  91.6 2.7 %collective-permute-start.22 = (f32[1,256,256]{2,1,0:T(8,128)S(1)}, f32[1,256,256]{2,1,0:T(8,128)S(1)}, u32[]{:S(2)}, u32[]{:S(2)}) collective-permute-start(f32[1,256,256]{2,1,0:T(8,128)S(1)} %get-tuple-element.101.refs_5_), channel_id=1, source_target_pairs={{0,1},{1,0},{2,3},{3,2},{4,5},{5,4},{6,7},{7,6},{8,9},{9,8},{10,11... | collective-permute-start | bytes 786440 | tf_op jit(solution)/shard_map/ppermute | solution.py:428
  94.9 3.9 %collective-permute-start.21 = (f32[1,256,256]{2,1,0:T(8,128)S(1)}, f32[1,256,256]{2,1,0:T(8,128)S(1)}, u32[]{:S(2)}, u32[]{:S(2)}) collective-permute-start(f32[1,256,256]{2,1,0:T(8,128)S(1)} %rows_first.1.refs_1_), channel_id=1, source_target_pairs={{0,1},{1,0},{2,3},{3,2},{4,5},{5,4},{6,7},{7,6},{8,9},{9,8},{10,11... | collective-permute-start | bytes 786440 | tf_op jit(solution)/shard_map/ppermute | solution.py:428
  98.9 2.0 %probe_sum.1 = f32[1,2,6,256,256]{4,3,2,1,0:T(8,128)} custom-call(f32[2,6,256,256]{3,2,1,0:T(8,128)S(1)} %get-tuple-element.102.refs_0_, f32[2,6,256,256]{3,2,1,0:T(8,128)S(1)} %get-tuple-element.103.refs_1_), custom_call_target="tpu_custom_call" | custom-call | tf_op jit(solution)/shard_map/probe_sum/pallas_call | solution.py:440
  100.9 1.3 %collective-permute-done.22.refs_6_ = f32[1,256,256]{2,1,0:T(8,128)S(1)} collective-permute-done((f32[1,256,256]{2,1,0:T(8,128)S(1)}, f32[1,256,256]{2,1,0:T(8,128)S(1)}, u32[]{:S(2)}, u32[]{:S(2)}) %collective-permute-start.22) | collective-permute-done | bytes 262176 | tf_op jit(solution)/shard_map/ppermute | solution.py:428
  102.2 5.6 %collective-permute-done.21.refs_2_ = f32[1,256,256]{2,1,0:T(8,128)S(1)} collective-permute-done((f32[1,256,256]{2,1,0:T(8,128)S(1)}, f32[1,256,256]{2,1,0:T(8,128)S(1)}, u32[]{:S(2)}, u32[]{:S(2)}) %collective-permute-start.21) | collective-permute-done | bytes 262176 | tf_op jit(solution)/shard_map/ppermute | solution.py:428
  107.8 1.6 %finish.1 = f32[1,2,2,256,256]{4,3,2,1,0:T(8,128)} custom-call(s32[5]{0:T(128)S(1)} %convert_element_type.3.refs_0_.refs_1_.refs_2_, f32[1,256,256]{2,1,0:T(8,128)S(1)} %rows_first.1.refs_1_, f32[1,256,256]{2,1,0:T(8,128)S(1)} %collective-permute-done.21.refs_2_, f32[1,256,256]{2,1,0:T(8,128)S(1)} %get-tuple-element.100.refs_3_, ...), custom_call_target="tpu_custom_call" | custom-call | tf_op jit(solution)/shard_map/finish/pallas_call | solution.py:440
  (51 shorter events, 15.3 us)
Async XLA Ops:
  0.8 1.2 %copy-start = (f32[1,2,2,256,256]{4,3,2,1,0:T(8,128)S(1)}, f32[1,2,2,256,256]{4,3,2,1,0:T(8,128)}, u32[]{:S(2)}) copy-start(f32[1,2,2,256,256]{4,3,2,1,0:T(8,128)} %param.7) | copy-start | bytes 3145732
  2.0 14.6 %copy-start.1 = (f32[1,2,2,256,256]{4,3,2,1,0:T(8,128)S(1)}, f32[1,2,2,256,256]{4,3,2,1,0:T(8,128)}, u32[]{:S(2)}) copy-start(f32[1,2,2,256,256]{4,3,2,1,0:T(8,128)} %param.7) | copy-start | bytes 3145732
  2.7 13.1 %collective-permute-start.4 = (f32[2,128,256]{2,1,0:T(8,128)S(1)}, f32[2,128,256]{2,1,0:T(8,128)S(1)}, u32[]{:S(2)}, u32[]{:S(2)}) collective-permute-start(f32[2,128,256]{2,1,0:T(8,128)S(1)} %get-tuple-element.58), channel_id=1, source_target_pairs={{0,16},{2,18},{4,20},{6,22},{8,24},{10,26},{12,28},{14,30},{16,0},... | collective-permute-start | bytes 786440 | tf_op jit(solution)/shard_map/ppermute | solution.py:424
  5.3 11.4 %collective-permute-start.5 = (f32[2,128,256]{2,1,0:T(8,128)S(1)}, f32[2,128,256]{2,1,0:T(8,128)S(1)}, u32[]{:S(2)}, u32[]{:S(2)}) collective-permute-start(f32[2,128,256]{2,1,0:T(8,128)S(1)} %get-tuple-element.59), channel_id=1, source_target_pairs={{0,240},{2,242},{4,244},{6,246},{8,248},{10,250},{12,252},{14,254}... | collective-permute-start | bytes 786440 | tf_op jit(solution)/shard_map/ppermute | solution.py:424
  10.9 11.9 %collective-permute-start = (f32[2,128,256]{2,1,0:T(8,128)S(1)}, f32[2,128,256]{2,1,0:T(8,128)S(1)}, u32[]{:S(2)}, u32[]{:S(2)}) collective-permute-start(f32[2,128,256]{2,1,0:T(8,128)S(1)} %get-tuple-element.53), channel_id=1, source_target_pairs={{0,16},{2,18},{4,20},{6,22},{8,24},{10,26},{12,28},{14,30},{16,0},... | collective-permute-start | bytes 786440 | tf_op jit(solution)/shard_map/ppermute | solution.py:424
  10.9 11.9 %collective-permute-start.1 = (f32[2,128,256]{2,1,0:T(8,128)S(1)}, f32[2,128,256]{2,1,0:T(8,128)S(1)}, u32[]{:S(2)}, u32[]{:S(2)}) collective-permute-start(f32[2,128,256]{2,1,0:T(8,128)S(1)} %get-tuple-element.54), channel_id=1, source_target_pairs={{0,240},{2,242},{4,244},{6,246},{8,248},{10,250},{12,252},{14,254}... | collective-permute-start | bytes 786440 | tf_op jit(solution)/shard_map/ppermute | solution.py:424
  12.4 1.9 %copy-start.2 = (f32[2,6,256,256]{3,2,1,0:T(8,128)S(1)}, f32[2,6,256,256]{3,2,1,0:T(8,128)}, u32[]{:S(2)}) copy-start(f32[2,6,256,256]{3,2,1,0:T(8,128)} %refs_1_.2) | copy-start | bytes 9437188
  14.3 0.9 copy-start.5
  15.8 5.5 %copy-start.3 = (f32[1,2,256,256]{3,2,1,0:T(8,128)S(1)}, f32[1,2,256,256]{3,2,1,0:T(8,128)}, u32[]{:S(2)}) copy-start(f32[1,2,256,256]{3,2,1,0:T(8,128)} %param.12) | copy-start | bytes 1572868
  15.8 5.5 %copy-start.4 = (bf16[4,256,256]{2,1,0:T(8,128)(2,1)S(1)}, bf16[4,256,256]{2,1,0:T(8,128)(2,1)}, u32[]{:S(2)}) copy-start(bf16[4,256,256]{2,1,0:T(8,128)(2,1)} %constant.54.clone.refs_1_) | copy-start | bytes 1572868
  16.7 12.3 %copy-start.6 = (s32[1,2,2]{2,1,0:T(2,128)S(1)}, s32[1,2,2]{2,1,0:T(2,128)}, u32[]{:S(2)}) copy-start(s32[1,2,2]{2,1,0:T(2,128)} %param.10) | copy-start | bytes 52
  17.3 8.6 %collective-permute-start.6 = (f32[2,512,128]{2,1,0:T(8,128)S(1)}, f32[2,512,128]{2,1,0:T(8,128)S(1)}, u32[]{:S(2)}, u32[]{:S(2)}) collective-permute-start(f32[2,512,128]{2,1,0:T(8,128)S(1)} %get-tuple-element.61), channel_id=1, source_target_pairs={{0,2},{2,0},{4,6},{6,4},{8,10},{10,8},{12,14},{14,12},{16,18},{18,... | collective-permute-start | bytes 1572872 | tf_op jit(solution)/shard_map/ppermute | solution.py:424
  20.1 8.9 %collective-permute-start.7 = (f32[2,512,128]{2,1,0:T(8,128)S(1)}, f32[2,512,128]{2,1,0:T(8,128)S(1)}, u32[]{:S(2)}, u32[]{:S(2)}) collective-permute-start(f32[2,512,128]{2,1,0:T(8,128)S(1)} %get-tuple-element.62), channel_id=1, source_target_pairs={{0,14},{2,4},{4,2},{6,8},{8,6},{10,12},{12,10},{14,0},{16,30},{18,... | collective-permute-start | bytes 1572872 | tf_op jit(solution)/shard_map/ppermute | solution.py:424
  23.4 11.7 %collective-permute-start.2 = (f32[2,512,128]{2,1,0:T(8,128)S(1)}, f32[2,512,128]{2,1,0:T(8,128)S(1)}, u32[]{:S(2)}, u32[]{:S(2)}) collective-permute-start(f32[2,512,128]{2,1,0:T(8,128)S(1)} %get-tuple-element.56), channel_id=1, source_target_pairs={{0,2},{2,0},{4,6},{6,4},{8,10},{10,8},{12,14},{14,12},{16,18},{18,... | collective-permute-start | bytes 1572872 | tf_op jit(solution)/shard_map/ppermute | solution.py:424
  25.2 9.9 %collective-permute-start.3 = (f32[2,512,128]{2,1,0:T(8,128)S(1)}, f32[2,512,128]{2,1,0:T(8,128)S(1)}, u32[]{:S(2)}, u32[]{:S(2)}) collective-permute-start(f32[2,512,128]{2,1,0:T(8,128)S(1)} %get-tuple-element.57), channel_id=1, source_target_pairs={{0,14},{2,4},{4,2},{6,8},{8,6},{10,12},{12,10},{14,0},{16,30},{18,... | collective-permute-start | bytes 1572872 | tf_op jit(solution)/shard_map/ppermute | solution.py:424
  38.1 8.4 %collective-permute-start.8 = (f32[256,256]{1,0:T(8,128)S(1)}, f32[256,256]{1,0:T(8,128)S(1)}, u32[]{:S(2)}, u32[]{:S(2)}) collective-permute-start(f32[256,256]{1,0:T(8,128)S(1)} %get-tuple-element.70.refs_1_), channel_id=1, source_target_pairs={{0,1},{1,0},{2,3},{3,2},{4,5},{5,4},{6,7},{7,6},{8,9},{9,8},{10,11... | collective-permute-start | bytes 786440 | tf_op jit(solution)/shard_map/ppermute | solution.py:428
  43.4 8.4 %collective-permute-start.10 = (f32[256,256]{1,0:T(8,128)S(1)}, f32[256,256]{1,0:T(8,128)S(1)}, u32[]{:S(2)}, u32[]{:S(2)}) collective-permute-start(f32[256,256]{1,0:T(8,128)S(1)} %get-tuple-element.83.refs_4_), channel_id=1, source_target_pairs={{0,1},{1,0},{2,3},{3,2},{4,5},{5,4},{6,7},{7,6},{8,9},{9,8},{10,11... | collective-permute-start | bytes 786440 | tf_op jit(solution)/shard_map/ppermute | solution.py:428
  55.3 9.3 %collective-permute-start.12 = (f32[2,512,128]{2,1,0:T(8,128)S(1)}, f32[2,512,128]{2,1,0:T(8,128)S(1)}, u32[]{:S(2)}, u32[]{:S(2)}) collective-permute-start(f32[2,512,128]{2,1,0:T(8,128)S(1)} %get-tuple-element.90), channel_id=1, source_target_pairs={{0,2},{2,0},{4,6},{6,4},{8,10},{10,8},{12,14},{14,12},{16,18},{18,... | collective-permute-start | bytes 1572872 | tf_op jit(solution)/shard_map/ppermute | solution.py:424
  57.5 8.9 %collective-permute-start.13 = (f32[2,512,128]{2,1,0:T(8,128)S(1)}, f32[2,512,128]{2,1,0:T(8,128)S(1)}, u32[]{:S(2)}, u32[]{:S(2)}) collective-permute-start(f32[2,512,128]{2,1,0:T(8,128)S(1)} %get-tuple-element.91), channel_id=1, source_target_pairs={{0,14},{2,4},{4,2},{6,8},{8,6},{10,12},{12,10},{14,0},{16,30},{18,... | collective-permute-start | bytes 1572872 | tf_op jit(solution)/shard_map/ppermute | solution.py:424
  58.7 12.4 %collective-permute-start.9 = (f32[1,256,256]{2,1,0:T(8,128)S(1)}, f32[1,256,256]{2,1,0:T(8,128)S(1)}, u32[]{:S(2)}, u32[]{:S(2)}) collective-permute-start(f32[1,256,256]{2,1,0:T(8,128)S(1)} %get-tuple-element.79), channel_id=1, source_target_pairs={{0,1},{1,0},{2,3},{3,2},{4,5},{5,4},{6,7},{7,6},{8,9},{9,8},{10,11... | collective-permute-start | bytes 786440 | tf_op jit(solution)/shard_map/ppermute | solution.py:428
  64.1 12.6 %collective-permute-start.11 = (f32[1,256,256]{2,1,0:T(8,128)S(1)}, f32[1,256,256]{2,1,0:T(8,128)S(1)}, u32[]{:S(2)}, u32[]{:S(2)}) collective-permute-start(f32[1,256,256]{2,1,0:T(8,128)S(1)} %get-tuple-element.88), channel_id=1, source_target_pairs={{0,1},{1,0},{2,3},{3,2},{4,5},{5,4},{6,7},{7,6},{8,9},{9,8},{10,11... | collective-permute-start | bytes 786440 | tf_op jit(solution)/shard_map/ppermute | solution.py:428
  67.1 15.5 %collective-permute-start.19 = (f32[2,128,256]{2,1,0:T(8,128)S(1)}, f32[2,128,256]{2,1,0:T(8,128)S(1)}, u32[]{:S(2)}, u32[]{:S(2)}) collective-permute-start(f32[2,128,256]{2,1,0:T(8,128)S(1)} %get-tuple-element.99), channel_id=1, source_target_pairs={{0,240},{2,242},{4,244},{6,246},{8,248},{10,250},{12,252},{14,254}... | collective-permute-start | bytes 786440 | tf_op jit(solution)/shard_map/ppermute | solution.py:424
  71.1 11.5 %collective-permute-start.18 = (f32[2,128,256]{2,1,0:T(8,128)S(1)}, f32[2,128,256]{2,1,0:T(8,128)S(1)}, u32[]{:S(2)}, u32[]{:S(2)}) collective-permute-start(f32[2,128,256]{2,1,0:T(8,128)S(1)} %get-tuple-element.92.refs_6_), channel_id=1, source_target_pairs={{0,16},{2,18},{4,20},{6,22},{8,24},{10,26},{12,28},{14,30},{16,0},... | collective-permute-start | bytes 786440 | tf_op jit(solution)/shard_map/ppermute | solution.py:424
  77.7 9.5 %collective-permute-start.15 = (f32[1,512,128]{2,1,0:T(8,128)S(1)}, f32[1,512,128]{2,1,0:T(8,128)S(1)}, u32[]{:S(2)}, u32[]{:S(2)}) collective-permute-start(f32[1,512,128]{2,1,0:T(8,128)S(1)} %get-tuple-element.94), channel_id=1, source_target_pairs={{0,14},{2,4},{4,2},{6,8},{8,6},{10,12},{12,10},{14,0},{16,30},{18,... | collective-permute-start | bytes 786440 | tf_op jit(solution)/shard_map/ppermute | solution.py:424
  82.6 4.7 %collective-permute-start.14 = (f32[1,512,128]{2,1,0:T(8,128)S(1)}, f32[1,512,128]{2,1,0:T(8,128)S(1)}, u32[]{:S(2)}, u32[]{:S(2)}) collective-permute-start(f32[1,512,128]{2,1,0:T(8,128)S(1)} %get-tuple-element.93.refs_5_), channel_id=1, source_target_pairs={{0,2},{2,0},{4,6},{6,4},{8,10},{10,8},{12,14},{14,12},{16,18},{18,... | collective-permute-start | bytes 786440 | tf_op jit(solution)/shard_map/ppermute | solution.py:424
  83.2 11.1 %collective-permute-start.20 = (f32[1,256,256]{2,1,0:T(8,128)S(1)}, f32[1,256,256]{2,1,0:T(8,128)S(1)}, u32[]{:S(2)}, u32[]{:S(2)}) collective-permute-start(f32[1,256,256]{2,1,0:T(8,128)S(1)} %get-tuple-element.100.refs_3_), channel_id=1, source_target_pairs={{0,1},{1,0},{2,3},{3,2},{4,5},{5,4},{6,7},{7,6},{8,9},{9,8},{10,11... | collective-permute-start | bytes 786440 | tf_op jit(solution)/shard_map/ppermute | solution.py:428
  87.9 6.4 %collective-permute-start.16 = (f32[1,128,256]{2,1,0:T(8,128)S(1)}, f32[1,128,256]{2,1,0:T(8,128)S(1)}, u32[]{:S(2)}, u32[]{:S(2)}) collective-permute-start(f32[1,128,256]{2,1,0:T(8,128)S(1)} %get-tuple-element.96), channel_id=1, source_target_pairs={{0,16},{2,18},{4,20},{6,22},{8,24},{10,26},{12,28},{14,30},{16,0},... | collective-permute-start | bytes 393224 | tf_op jit(solution)/shard_map/ppermute | solution.py:424
  88.0 6.3 %collective-permute-start.17 = (f32[1,128,256]{2,1,0:T(8,128)S(1)}, f32[1,128,256]{2,1,0:T(8,128)S(1)}, u32[]{:S(2)}, u32[]{:S(2)}) collective-permute-start(f32[1,128,256]{2,1,0:T(8,128)S(1)} %get-tuple-element.97), channel_id=1, source_target_pairs={{0,240},{2,242},{4,244},{6,246},{8,248},{10,250},{12,252},{14,254}... | collective-permute-start | bytes 393224 | tf_op jit(solution)/shard_map/ppermute | solution.py:424
  91.6 10.5 %collective-permute-start.22 = (f32[1,256,256]{2,1,0:T(8,128)S(1)}, f32[1,256,256]{2,1,0:T(8,128)S(1)}, u32[]{:S(2)}, u32[]{:S(2)}) collective-permute-start(f32[1,256,256]{2,1,0:T(8,128)S(1)} %get-tuple-element.101.refs_5_), channel_id=1, source_target_pairs={{0,1},{1,0},{2,3},{3,2},{4,5},{5,4},{6,7},{7,6},{8,9},{9,8},{10,11... | collective-permute-start | bytes 786440 | tf_op jit(solution)/shard_map/ppermute | solution.py:428
  94.9 12.8 %collective-permute-start.21 = (f32[1,256,256]{2,1,0:T(8,128)S(1)}, f32[1,256,256]{2,1,0:T(8,128)S(1)}, u32[]{:S(2)}, u32[]{:S(2)}) collective-permute-start(f32[1,256,256]{2,1,0:T(8,128)S(1)} %rows_first.1.refs_1_), channel_id=1, source_target_pairs={{0,1},{1,0},{2,3},{3,2},{4,5},{5,4},{6,7},{7,6},{8,9},{9,8},{10,11... | collective-permute-start | bytes 786440 | tf_op jit(solution)/shard_map/ppermute | solution.py:428

commit v8 on v7

--- a/solution.py
+++ b/solution.py
@@ -120,7 +120,7 @@
     return jnp.where(good, value, 0.0)
 
 
-def build_canvas(layer, info, own, rows_a, rows_b, cols_a, cols_b, canvas):
+def build_canvas(layer, info, own, rows_a, rows_b, cols_b, cols_a, corners_b, canvas):
     n = own.shape[-1]
     h = n // 2
     ra, rb, row_ok = ends(info, 0, 0, h + n)
@@ -129,7 +129,9 @@
     canvas[:, pl.ds(ra, h), h : h + n] = rows_a[...]
     canvas[:, pl.ds(rb, h), h : h + n] = kept(row_ok, rows_b[...])
     canvas[:, :, pl.ds(ca, h)] = cols_a[...]
-    canvas[:, :, pl.ds(cb, h)] = kept(col_ok, cols_b[...])
+    canvas[:, h : h + n, pl.ds(cb, h)] = kept(col_ok, cols_b[:, layer])
+    canvas[:, pl.ds(ra, h), pl.ds(cb, h)] = kept(col_ok, corners_b[0])
+    canvas[:, pl.ds(rb, h), pl.ds(cb, h)] = kept(row_ok & col_ok, corners_b[1])
 
 
 def extract(off_ref, slot, canvas, patch):
@@ -201,9 +203,9 @@
     inten[...] = beside(total_e[:, :h] + total_e[:, h:], total_o[:, :h] + total_o[:, h:])
 
 
-def waves_first_kernel(off, info, own, rows_a, rows_b, cols_a, cols_b, probe, diag, corner,
-                       mat, canvas, patch, wave, held):
-    build_canvas(0, info, own, rows_a, rows_b, cols_a, cols_b, canvas)
+def waves_first_kernel(off, info, own, rows_a, rows_b, cols_b, cols_a, corners_b, probe,
+                       diag, corner, mat, canvas, patch, wave, held):
+    build_canvas(0, info, own, rows_a, rows_b, cols_b, cols_a, corners_b, canvas)
     extract(off, 0, canvas, patch)
     waves(probe, patch, diag, corner, mat, wave, held)
 
@@ -213,9 +215,9 @@
     waves(probe, patch, diag, corner, mat, wave, held)
 
 
-def fars_first_kernel(off, info, own, rows_a, rows_b, cols_a, cols_b, wave, tabs, canvas, patch,
-                      far, inten, held):
-    build_canvas(1, info, own, rows_a, rows_b, cols_a, cols_b, canvas)
+def fars_first_kernel(off, info, own, rows_a, rows_b, cols_b, cols_a, corners_b, wave, tabs,
+                      canvas, patch, far, inten, held):
+    build_canvas(1, info, own, rows_a, rows_b, cols_b, cols_a, corners_b, canvas)
     extract(off, 0, canvas, patch)
     fars(wave, patch, tabs, far, inten, held)
 
@@ -339,12 +341,22 @@
         out[0, pl.ds(rb, h)] = mid[plane, pl.ds(rb, h)] + kept(row_ok, got_b[plane])
 
 
-def finish_kernel(info, mine_first, other_first, mine_re, other_re, mine_im, other_im, out):
-    part = info[4]
-    out[0, part, 0] = mine_first[0]
-    out[0, 1 - part, 0] = other_first[0]
-    out[0, 0, 1] = mine_re[0] + other_re[0]
-    out[0, 1, 1] = mine_im[0] + other_im[0]
+def finish_last_kernel(info, mine_first, mine_re, other_re, mine_im, other_im, out, sums, sems):
+    sums[0] = mine_re[0] + other_re[0]
+    sums[1] = mine_im[0] + other_im[0]
+    moves = ((sums.at[0], out.at[0, 0, 1]), (sums.at[1], out.at[0, 1, 1]),
+             (mine_first.at[0], out.at[0, info[4], 0]))
+    copies = [pltpu.make_async_copy(a, b, sems.at[i]) for i, (a, b) in enumerate(moves)]
+    for copy in copies:
+        copy.start()
+    for copy in copies:
+        copy.wait()
+
+
+def finish_kernel(info, other_first, partial, out, sems):
+    copy = pltpu.make_async_copy(other_first.at[0], out.at[0, 1 - info[4], 0], sems.at[0])
+    copy.start()
+    copy.wait()
 
 
 def pick_rows_kernel(info, own, *refs):
@@ -363,16 +375,23 @@
         copy.wait()
 
 
-def pick_cols_kernel(layer, info, own, rows_a, rows_b, out_a, out_b):
+def pick_cols_kernel(info, own, out_b):
+    h = out_b.shape[-1]
+    _, b, _ = ends(info, 1, 0, h)
+    out_b[...] = own[:, :, :, pl.ds(b, h)]
+
+
+def pick_rest_kernel(layer, info, own, rows_a, rows_b, out_a, corners_b):
     n = own.shape[-1]
     h = n // 2
     ra, rb, row_ok = ends(info, 0, 0, h + n)
     a, b, _ = ends(info, 1, 0, h)
-    for start, out in ((a, out_a), (b, out_b)):
-        side = pl.ds(start, h)
-        out[:, h : h + n] = own[:, layer, :, side]
-        out[:, pl.ds(ra, h)] = rows_a[:, :, side]
-        out[:, pl.ds(rb, h)] = kept(row_ok, rows_b[:, :, side])
+    a, b = pl.ds(a, h), pl.ds(b, h)
+    out_a[:, h : h + n] = own[:, layer, :, a]
+    out_a[:, pl.ds(ra, h)] = rows_a[:, :, a]
+    out_a[:, pl.ds(rb, h)] = kept(row_ok, rows_b[:, :, a])
+    corners_b[0] = rows_a[:, :, b]
+    corners_b[1] = rows_b[:, :, b]
 
 
 def prepare_kernel(prop_in, probe_in, diag, corner, right, back_diag, back_corner, back_right,
@@ -428,14 +447,16 @@
     return lax.ppermute(value, "mode", [(0, 1), (1, 0)])
 
 
-def call(kernel, name, outs, args, scratch=(), smem=1, after=(), copies=0):
+def call(kernel, name, outs, args, scratch=(), smem=1, after=(), copies=0, out=None, alias=None):
     vmem = pl.BlockSpec(memory_space=pltpu.VMEM)
-    held = pl.BlockSpec(memory_space=pltpu.HBM) if copies else vmem
+    held = pl.BlockSpec(memory_space=pltpu.HBM) if copies and out is None else vmem
+    out = vmem if out is None else pl.BlockSpec(memory_space=out)
     scalars = pl.BlockSpec(memory_space=pltpu.SMEM)
     n_args, n_after = len(args), len(after)
 
     def run(*refs):
-        kernel(*refs[:n_args], *refs[n_args + n_after :])
+        kept_args = n_args if alias is None else n_args + n_after
+        kernel(*refs[:kept_args], *refs[n_args + n_after :])
 
     return pl.pallas_call(
         run,
@@ -443,7 +464,8 @@
         in_specs=[scalars] * smem
         + [held] * (n_args - smem)
         + [pl.BlockSpec(memory_space=pl.ANY)] * n_after,
-        out_specs=tuple(vmem for _ in outs),
+        out_specs=tuple(out for _ in outs),
+        input_output_aliases={} if alias is None else {alias: 0},
         scratch_shapes=[pltpu.VMEM(shape, dtype) for shape, dtype in scratch]
         + [pltpu.SemaphoreType.DMA((copies,))] * (copies > 0),
         compiler_params=pltpu.CompilerParams(vmem_limit_bytes=VMEM_LIMIT),
@@ -471,6 +493,7 @@
     band = (((2, n, n), BF16), ((4 * BAND, 4 * BAND), BF16), mat)
     held = ((modes * n, 2 * n), BF16)
     strip, tall = ((2, h, n), F32), ((2, 2 * n, h), F32)
+    side_strip, quarter = ((2, 2, n, h), F32), ((2, 2, h, h), F32)
 
     picked = call(pick_rows_kernel, "pick_rows", (strip,) * 4, (info, own), copies=4)
     rows = [[swap(picked[2 * i + k], 0, k == 1) for k in range(2)] for i in range(2)]
@@ -493,13 +516,17 @@
         smem=0,
     )
 
+    (picked,) = call(pick_cols_kernel, "pick_cols", (side_strip,), (info, own), after=())
+    cols_b = swap(picked, 1, True)
+
     def beside_tiles(layer, after):
-        picked = call(functools.partial(pick_cols_kernel, layer), f"pick_cols_{layer}", (tall,) * 2,
-                      (info, own, *rows[layer]), after=after)
-        return (own, *rows[layer], *(swap(picked[k], 1, k == 1) for k in range(2)))
+        picked = call(functools.partial(pick_rest_kernel, layer), f"pick_rest_{layer}",
+                      (tall, quarter), (info, own, *rows[layer]), after=after)
+        rest = [swap(picked[k], 1, k == 1) for k in range(2)]
+        return (own, *rows[layer], cols_b, *rest)
 
     first = beside_tiles(0, (probe,))
-    last = beside_tiles(1, (measured,))
+    last = beside_tiles(1, (measured, first[3],first[5]))
     canvas, patch_first0, wave0 = call(
         waves_first_kernel,
         "waves_0",
@@ -610,11 +637,25 @@
         smem=0,
         after=(),
     )
+    shape = ((object_tiles.shape, F32),)
+    (partial,) = call(
+        finish_last_kernel,
+        "finish_last",
+        shape,
+        (info, mine_first, mine_re, other_re, mine_im, other_im),
+        scratch=(pair,),
+        copies=3,
+        out=pl.ANY,
+    )
     (object_grad,) = call(
         finish_kernel,
         "finish",
-        ((object_tiles.shape, F32),),
-        (info, mine_first, other_first, mine_re, other_re, mine_im, other_im),
+        shape,
+        (info, other_first),
+        after=(partial,),
+        copies=1,
+        out=pl.ANY,
+        alias=2,
     )
     return (object_grad, probe_grad)
 

time: 110 us -> 108 us (0.982)
  starting transfers between devices: 48.2 us -> 44.5 us
  Pallas kernels: 34.6 us -> 36.1 us
    ppermute x16 -> x17, starting transfers between devices: 32.1 us -> 28.3 us  [swap(): return lax.ppermute(value, 'tile', pairs)]
    pallas_call x21 -> x23, Pallas kernels: 34.6 us -> 36.1 us  [call(): pl.pallas_call(run, out_shape=tuple((jax.ShapeDtypeStruct(shape, dtype) f...]
    ppermute x16 -> x17, waiting for transfers between devices: 5.8 us -> 6.64 us  [swap(): return lax.ppermute(value, 'tile', pairs)]
  transfers between devices with their start and end apart: 23 -> 24, of which waited for: 8 -> 9; matrix products, arithmetic and copies ran while one was open for 0% -> 0% of each run, Pallas kernels for 24% -> 26%
where the time goes in v8:
time: 108 us
  starting transfers between devices  44.5 us (41%)
  Pallas kernels  36.1 us (33%)
  waiting for transfers between devices  21.3 us (20%)
  local copies, waits for them, and re-layouts  4.19 us (4%)
  between operations  1.82 us (2%)
    pallas_call x23, Pallas kernels, call(): pl.pallas_call(run, out_shape=tuple((jax.ShapeDtypeStruct(shape, dtype) f...  36.1 us
    ppermute x17, starting transfers between devices, swap(): return lax.ppermute(value, 'tile', pairs)  28.3 us
    ppermute x7, starting transfers between devices, swap_mode(): return lax.ppermute(value, 'mode', [(0, 1), (1, 0)])  16.1 us
    ppermute x7, waiting for transfers between devices, swap_mode(): return lax.ppermute(value, 'mode', [(0, 1), (1, 0)])  14.6 us
    ppermute x17, waiting for transfers between devices, swap(): return lax.ppermute(value, 'tile', pairs)  6.64 us
    unnamed x14, local copies, waits for them, and re-layouts  4.09 us
  transfers between devices with their start and end apart: 24, of which 9 were waited for; matrix products, arithmetic and copies ran while one was open for 0% of the time, Pallas kernels for 26%

profile of v8, /device:TPU:1, one launch (start us, length us, event | category | flops | bytes accessed | tf_op | source)
XLA Modules:
  0.0 107.9 jit_solution(5134947175639063686)
XLA Ops:
  2.7 2.6 %collective-permute-start.3 = (f32[2,128,256]{2,1,0:T(8,128)S(1)}, f32[2,128,256]{2,1,0:T(8,128)S(1)}, u32[]{:S(2)}, u32[]{:S(2)}) collective-permute-start(f32[2,128,256]{2,1,0:T(8,128)S(1)} %get-tuple-element.56), channel_id=1, source_target_pairs={{0,16},{2,18},{4,20},{6,22},{8,24},{10,26},{12,28},{14,30},{16,0},... | collective-permute-start | bytes 786440 | tf_op jit(solution)/shard_map/ppermute | solution.py:443
  5.3 5.7 %collective-permute-start.4 = (f32[2,128,256]{2,1,0:T(8,128)S(1)}, f32[2,128,256]{2,1,0:T(8,128)S(1)}, u32[]{:S(2)}, u32[]{:S(2)}) collective-permute-start(f32[2,128,256]{2,1,0:T(8,128)S(1)} %get-tuple-element.57), channel_id=1, source_target_pairs={{0,240},{2,242},{4,244},{6,246},{8,248},{10,250},{12,252},{14,254}... | collective-permute-start | bytes 786440 | tf_op jit(solution)/shard_map/ppermute | solution.py:443
  11.5 2.4 %collective-permute-start.2 = (f32[2,2,256,128]{3,2,1,0:T(8,128)S(1)}, f32[2,2,256,128]{3,2,1,0:T(8,128)S(1)}, u32[]{:S(2)}, u32[]{:S(2)}) collective-permute-start(f32[2,2,256,128]{3,2,1,0:T(8,128)S(1)} %pick_cols.1), channel_id=1, source_target_pairs={{0,14},{2,4},{4,2},{6,8},{8,6},{10,12},{12,10},{14,0},{16,30},{18,... | collective-permute-start | bytes 1572872 | tf_op jit(solution)/shard_map/ppermute | solution.py:443
  15.4 1.9 %copy-done.2 = f32[2,6,256,256]{3,2,1,0:T(8,128)S(1)} copy-done((f32[2,6,256,256]{3,2,1,0:T(8,128)S(1)}, f32[2,6,256,256]{3,2,1,0:T(8,128)}, u32[]{:S(2)}) %copy-start.2) | copy-done | bytes 3145752
  21.4 1.5 %reorder.1 = (f32[2,256,256]{2,1,0:T(8,128)S(1)}, bf16[4,256,256]{2,1,0:T(8,128)(2,1)S(1)}) custom-call(f32[2,256,256]{2,1,0:T(8,128)S(1)} %bitcast.14, bf16[4,256,256]{2,1,0:T(8,128)(2,1)S(1)} %copy-done.4), custom_call_target="tpu_custom_call" | custom-call | tf_op jit(solution)/shard_map/reorder/pallas_call | solution.py:461
  23.4 2.3 %collective-permute-done.5.refs_6_.refs_7_ = f32[2,2,128,128]{3,2,1,0:T(8,128)S(1)} collective-permute-done((f32[2,2,128,128]{3,2,1,0:T(8,128)S(1)}, f32[2,2,128,128]{3,2,1,0:T(8,128)S(1)}, u32[]{:S(2)}, u32[]{:S(2)}) %collective-permute-start.5) | collective-permute-done | bytes 262176 | tf_op jit(solution)/shard_map/ppermute | solution.py:443
  26.3 2.1 %collective-permute-start.6 = (f32[2,512,128]{2,1,0:T(8,128)S(1)}, f32[2,512,128]{2,1,0:T(8,128)S(1)}, u32[]{:S(2)}, u32[]{:S(2)}) collective-permute-start(f32[2,512,128]{2,1,0:T(8,128)S(1)} %get-tuple-element.60), channel_id=1, source_target_pairs={{0,2},{2,0},{4,6},{6,4},{8,10},{10,8},{12,14},{14,12},{16,18},{18,... | collective-permute-start | bytes 1572872 | tf_op jit(solution)/shard_map/ppermute | solution.py:443
  28.4 3.2 %waves_0.1 = (f32[2,512,512]{2,1,0:T(8,128)S(1)}, f32[2,256,256]{2,1,0:T(8,128)S(1)}, f32[6,2,256,256]{3,2,1,0:T(8,128)S(1)}) custom-call(s32[2,2]{1,0:T(2,128)S(1)} %bitcast.15, s32[5]{0:T(128)S(1)} %convert_element_type.3.refs_0_.refs_1_.refs_2_, f32[2,2,256,256]{3,2,1,0:T(8,128)S(1)} %bitcast.12, ...), custom_call_target="tpu_custom_call" | custom-call | tf_op jit(solution)/shard_map/waves_0/pallas_call | solution.py:461
  31.6 3.0 %waves_1.1 = (f32[2,256,256]{2,1,0:T(8,128)S(1)}, f32[6,2,256,256]{3,2,1,0:T(8,128)S(1)}) custom-call(s32[2,2]{1,0:T(2,128)S(1)} %bitcast.16, f32[2,512,512]{2,1,0:T(8,128)S(1)} %get-tuple-element.68.refs_1_, f32[2,6,256,256]{3,2,1,0:T(8,128)S(1)} %get-tuple-element.58.refs_4_.refs_8_.refs_2_, bf16[2,256,256]{2,1,0:T(8,128)(2,1)S(1)} %get-tuple-element.63.refs_9_.refs_3_, ...), custom_call_target="tpu_custom_call" | custom-call | tf_op jit(solution)/shard_map/waves_1/pallas_call | solution.py:461
  34.5 3.0 %fars_0.1 = (f32[2,512,512]{2,1,0:T(8,128)S(1)}, f32[2,256,256]{2,1,0:T(8,128)S(1)}, f32[6,2,256,256]{3,2,1,0:T(8,128)S(1)}, f32[256,256]{1,0:T(8,128)S(1)}) custom-call(s32[2,2]{1,0:T(2,128)S(1)} %bitcast.17, s32[5]{0:T(128)S(1)} %convert_element_type.3.refs_0_.refs_1_.refs_2_, f32[2,2,256,256]{3,2,1,0:T(8,128)S(1)} %bitcast.13, ...), custom_call_target="tpu_custom_call" | custom-call | tf_op jit(solution)/shard_map/fars_0/pallas_call | solution.py:461
  37.5 2.7 %collective-permute-start.9 = (f32[256,256]{1,0:T(8,128)S(1)}, f32[256,256]{1,0:T(8,128)S(1)}, u32[]{:S(2)}, u32[]{:S(2)}) collective-permute-start(f32[256,256]{1,0:T(8,128)S(1)} %get-tuple-element.70.refs_1_), channel_id=1, source_target_pairs={{0,1},{1,0},{2,3},{3,2},{4,5},{5,4},{6,7},{7,6},{8,9},{9,8},{10,11... | collective-permute-start | bytes 786440 | tf_op jit(solution)/shard_map/ppermute | solution.py:447
  40.2 2.5 %fars_1.1 = (f32[2,256,256]{2,1,0:T(8,128)S(1)}, f32[6,2,256,256]{3,2,1,0:T(8,128)S(1)}, f32[256,256]{1,0:T(8,128)S(1)}) custom-call(s32[2,2]{1,0:T(2,128)S(1)} %bitcast.18, f32[2,512,512]{2,1,0:T(8,128)S(1)} %get-tuple-element.81.refs_1_, f32[6,2,256,256]{3,2,1,0:T(8,128)S(1)} %get-tuple-element.82.refs_2_.refs_8_, ...), custom_call_target="tpu_custom_call" | custom-call | tf_op jit(solution)/shard_map/fars_1/pallas_call | solution.py:461
  44.0 1.8 %collective-permute-done.9.refs_2_ = f32[256,256]{1,0:T(8,128)S(1)} collective-permute-done((f32[256,256]{1,0:T(8,128)S(1)}, f32[256,256]{1,0:T(8,128)S(1)}, u32[]{:S(2)}, u32[]{:S(2)}) %collective-permute-start.9) | collective-permute-done | bytes 262176 | tf_op jit(solution)/shard_map/ppermute | solution.py:447
  45.8 1.8 %back_last_0.1 = (f32[2,256,256]{2,1,0:T(8,128)S(1)}, bf16[6,2,256,256]{3,2,1,0:T(8,128)(2,1)S(1)}) custom-call(s32[1]{0:T(128)S(6)} %copy.11.refs_0_, f32[256,256]{1,0:T(8,128)S(1)} %get-tuple-element.70.refs_1_, f32[256,256]{1,0:T(8,128)S(1)} %collective-permute-done.9.refs_2_, f32[2,256,256]{2,1,0:T(8,128)S(1)} %get-tuple-element.55.refs_4_.refs_3_.refs_6_, ...), custom_call_target="tpu_custom_call" | custom-call | tf_op jit(solution)/shard_map/back_last_0/pallas_call | solution.py:461
  47.6 2.7 %back_first_0.1 = (f32[1,256,256]{2,1,0:T(8,128)S(1)}, f32[1,256,256]{2,1,0:T(8,128)S(1)}, f32[2,6,256,256]{3,2,1,0:T(8,128)S(1)}) custom-call(s32[5]{0:T(128)S(1)} %convert_element_type.3.refs_0_.refs_1_.refs_2_, bf16[6,2,256,256]{3,2,1,0:T(8,128)(2,1)S(1)} %get-tuple-element.73.refs_1_, f32[2,6,256,256]{3,2,1,0:T(8,128)S(1)} %get-tuple-element.58.refs_4_.refs_8_.refs_2_, ...), custom_call_target="tpu_custom_call" | custom-call | tf_op jit(solution)/shard_map/back_first_0/pallas_call | solution.py:461
  51.3 3.4 %back_last_1.1 = (bf16[6,2,256,256]{3,2,1,0:T(8,128)(2,1)S(1)}, f32[2,512,128]{2,1,0:T(8,128)S(1)}, f32[2,512,256]{2,1,0:T(8,128)S(1)}, f32[2,512,128]{2,1,0:T(8,128)S(1)}) custom-call(s32[1]{0:T(128)S(6)} %copy.11.refs_0_, s32[2,2]{1,0:T(2,128)S(1)} %bitcast.19, s32[5]{0:T(128)S(1)} %convert_element_type.3.refs_0_.refs_1_.refs_2_, ...), custom_call_target="tpu_custom_call" | custom-call | tf_op jit(solution)/shard_map/back_last_1/pallas_call | solution.py:461
  54.7 2.2 %collective-permute-start.13 = (f32[2,512,128]{2,1,0:T(8,128)S(1)}, f32[2,512,128]{2,1,0:T(8,128)S(1)}, u32[]{:S(2)}, u32[]{:S(2)}) collective-permute-start(f32[2,512,128]{2,1,0:T(8,128)S(1)} %get-tuple-element.90), channel_id=1, source_target_pairs={{0,2},{2,0},{4,6},{6,4},{8,10},{10,8},{12,14},{14,12},{16,18},{18,... | collective-permute-start | bytes 1572872 | tf_op jit(solution)/shard_map/ppermute | solution.py:443
  57.2 3.7 %collective-permute-start.10 = (f32[1,256,256]{2,1,0:T(8,128)S(1)}, f32[1,256,256]{2,1,0:T(8,128)S(1)}, u32[]{:S(2)}, u32[]{:S(2)}) collective-permute-start(f32[1,256,256]{2,1,0:T(8,128)S(1)} %get-tuple-element.79), channel_id=1, source_target_pairs={{0,1},{1,0},{2,3},{3,2},{4,5},{5,4},{6,7},{7,6},{8,9},{9,8},{10,11... | collective-permute-start | bytes 786440 | tf_op jit(solution)/shard_map/ppermute | solution.py:447
  60.9 2.8 %back_first_1.1 = (f32[1,256,256]{2,1,0:T(8,128)S(1)}, f32[1,256,256]{2,1,0:T(8,128)S(1)}, f32[2,6,256,256]{3,2,1,0:T(8,128)S(1)}) custom-call(s32[5]{0:T(128)S(1)} %convert_element_type.3.refs_0_.refs_1_.refs_2_, bf16[6,2,256,256]{3,2,1,0:T(8,128)(2,1)S(1)} %get-tuple-element.86.refs_1_, f32[2,6,256,256]{3,2,1,0:T(8,128)S(1)} %get-tuple-element.58.refs_4_.refs_8_.refs_2_, ...), custom_call_target="tpu_custom_call" | custom-call | tf_op jit(solution)/shard_map/back_first_1/pallas_call | solution.py:461
  63.8 2.1 %collective-permute-done.14.refs_3_ = f32[2,512,128]{2,1,0:T(8,128)S(1)} collective-permute-done((f32[2,512,128]{2,1,0:T(8,128)S(1)}, f32[2,512,128]{2,1,0:T(8,128)S(1)}, u32[]{:S(2)}, u32[]{:S(2)}) %collective-permute-start.14) | collective-permute-done | bytes 524320 | tf_op jit(solution)/shard_map/ppermute | solution.py:443
  66.6 3.1 %collective-permute-start.20 = (f32[2,128,256]{2,1,0:T(8,128)S(1)}, f32[2,128,256]{2,1,0:T(8,128)S(1)}, u32[]{:S(2)}, u32[]{:S(2)}) collective-permute-start(f32[2,128,256]{2,1,0:T(8,128)S(1)} %get-tuple-element.99), channel_id=1, source_target_pairs={{0,240},{2,242},{4,244},{6,246},{8,248},{10,250},{12,252},{14,254}... | collective-permute-start | bytes 786440 | tf_op jit(solution)/shard_map/ppermute | solution.py:443
  69.7 7.5 %collective-permute-done.12.refs_5_.refs_4_ = f32[1,256,256]{2,1,0:T(8,128)S(1)} collective-permute-done((f32[1,256,256]{2,1,0:T(8,128)S(1)}, f32[1,256,256]{2,1,0:T(8,128)S(1)}, u32[]{:S(2)}, u32[]{:S(2)}) %collective-permute-start.12) | collective-permute-done | bytes 262176 | tf_op jit(solution)/shard_map/ppermute | solution.py:447
  78.3 1.7 %collective-permute-start.16 = (f32[1,512,128]{2,1,0:T(8,128)S(1)}, f32[1,512,128]{2,1,0:T(8,128)S(1)}, u32[]{:S(2)}, u32[]{:S(2)}) collective-permute-start(f32[1,512,128]{2,1,0:T(8,128)S(1)} %get-tuple-element.94), channel_id=1, source_target_pairs={{0,14},{2,4},{4,2},{6,8},{8,6},{10,12},{12,10},{14,0},{16,30},{18,... | collective-permute-start | bytes 786440 | tf_op jit(solution)/shard_map/ppermute | solution.py:443
  80.0 1.5 %collective-permute-start.15 = (f32[1,512,128]{2,1,0:T(8,128)S(1)}, f32[1,512,128]{2,1,0:T(8,128)S(1)}, u32[]{:S(2)}, u32[]{:S(2)}) collective-permute-start(f32[1,512,128]{2,1,0:T(8,128)S(1)} %get-tuple-element.93.refs_5_), channel_id=1, source_target_pairs={{0,2},{2,0},{4,6},{6,4},{8,10},{10,8},{12,14},{14,12},{16,18},{18,... | collective-permute-start | bytes 786440 | tf_op jit(solution)/shard_map/ppermute | solution.py:443
  82.1 3.5 %collective-permute-start.21 = (f32[1,256,256]{2,1,0:T(8,128)S(1)}, f32[1,256,256]{2,1,0:T(8,128)S(1)}, u32[]{:S(2)}, u32[]{:S(2)}) collective-permute-start(f32[1,256,256]{2,1,0:T(8,128)S(1)} %get-tuple-element.100.refs_2_), channel_id=1, source_target_pairs={{0,1},{1,0},{2,3},{3,2},{4,5},{5,4},{6,7},{7,6},{8,9},{9,8},{10,11... | collective-permute-start | bytes 786440 | tf_op jit(solution)/shard_map/ppermute | solution.py:447
  87.4 3.3 %collective-permute-start.18 = (f32[1,128,256]{2,1,0:T(8,128)S(1)}, f32[1,128,256]{2,1,0:T(8,128)S(1)}, u32[]{:S(2)}, u32[]{:S(2)}) collective-permute-start(f32[1,128,256]{2,1,0:T(8,128)S(1)} %get-tuple-element.97), channel_id=1, source_target_pairs={{0,240},{2,242},{4,244},{6,246},{8,248},{10,250},{12,252},{14,254}... | collective-permute-start | bytes 393224 | tf_op jit(solution)/shard_map/ppermute | solution.py:443
  90.6 1.7 %collective-permute-start.23 = (f32[1,256,256]{2,1,0:T(8,128)S(1)}, f32[1,256,256]{2,1,0:T(8,128)S(1)}, u32[]{:S(2)}, u32[]{:S(2)}) collective-permute-start(f32[1,256,256]{2,1,0:T(8,128)S(1)} %get-tuple-element.101.refs_4_), channel_id=1, source_target_pairs={{0,1},{1,0},{2,3},{3,2},{4,5},{5,4},{6,7},{7,6},{8,9},{9,8},{10,11... | collective-permute-start | bytes 786440 | tf_op jit(solution)/shard_map/ppermute | solution.py:447
  92.4 1.8 %collective-permute-done.18.refs_3_ = f32[1,128,256]{2,1,0:T(8,128)S(1)} collective-permute-done((f32[1,128,256]{2,1,0:T(8,128)S(1)}, f32[1,128,256]{2,1,0:T(8,128)S(1)}, u32[]{:S(2)}, u32[]{:S(2)}) %collective-permute-start.18) | collective-permute-done | bytes 131104 | tf_op jit(solution)/shard_map/ppermute | solution.py:443
  94.8 3.7 %collective-permute-start.22 = (f32[1,256,256]{2,1,0:T(8,128)S(1)}, f32[1,256,256]{2,1,0:T(8,128)S(1)}, u32[]{:S(2)}, u32[]{:S(2)}) collective-permute-start(f32[1,256,256]{2,1,0:T(8,128)S(1)} %rows_first.1.refs_1_), channel_id=1, source_target_pairs={{0,1},{1,0},{2,3},{3,2},{4,5},{5,4},{6,7},{7,6},{8,9},{9,8},{10,11... | collective-permute-start | bytes 786440 | tf_op jit(solution)/shard_map/ppermute | solution.py:447
  98.5 2.0 %probe_sum.1 = f32[1,2,6,256,256]{4,3,2,1,0:T(8,128)} custom-call(f32[2,6,256,256]{3,2,1,0:T(8,128)S(1)} %get-tuple-element.102.refs_0_, f32[2,6,256,256]{3,2,1,0:T(8,128)S(1)} %get-tuple-element.103.refs_1_), custom_call_target="tpu_custom_call" | custom-call | tf_op jit(solution)/shard_map/probe_sum/pallas_call | solution.py:461
  100.8 1.5 %finish_last.1.refs_2_ = f32[1,2,2,256,256]{4,3,2,1,0:T(8,128)} custom-call(s32[5]{0:T(128)S(1)} %convert_element_type.3.refs_0_.refs_1_.refs_2_, f32[1,256,256]{2,1,0:T(8,128)S(1)} %rows_first.1.refs_1_, f32[1,256,256]{2,1,0:T(8,128)S(1)} %get-tuple-element.100.refs_2_, f32[1,256,256]{2,1,0:T(8,128)S(1)} %collective-permute-done.21.refs_4_.refs_3_, ...), custom_call_target="tpu_custom_call" | custom-call | tf_op jit(solution)/shard_map/finish_last/pallas_call | solution.py:461
  102.3 4.1 %collective-permute-done.22.refs_1_ = f32[1,256,256]{2,1,0:T(8,128)S(1)} collective-permute-done((f32[1,256,256]{2,1,0:T(8,128)S(1)}, f32[1,256,256]{2,1,0:T(8,128)S(1)}, u32[]{:S(2)}, u32[]{:S(2)}) %collective-permute-start.22) | collective-permute-done | bytes 262176 | tf_op jit(solution)/shard_map/ppermute | solution.py:447
  (55 shorter events, 17.3 us)
Async XLA Ops:
  0.8 1.2 %copy-start = (f32[1,2,2,256,256]{4,3,2,1,0:T(8,128)S(1)}, f32[1,2,2,256,256]{4,3,2,1,0:T(8,128)}, u32[]{:S(2)}) copy-start(f32[1,2,2,256,256]{4,3,2,1,0:T(8,128)} %param.7) | copy-start | bytes 3145732
  2.0 16.8 %copy-start.1 = (f32[1,2,2,256,256]{4,3,2,1,0:T(8,128)S(1)}, f32[1,2,2,256,256]{4,3,2,1,0:T(8,128)}, u32[]{:S(2)}) copy-start(f32[1,2,2,256,256]{4,3,2,1,0:T(8,128)} %param.7) | copy-start | bytes 3145732
  2.7 16.1 %collective-permute-start.3 = (f32[2,128,256]{2,1,0:T(8,128)S(1)}, f32[2,128,256]{2,1,0:T(8,128)S(1)}, u32[]{:S(2)}, u32[]{:S(2)}) collective-permute-start(f32[2,128,256]{2,1,0:T(8,128)S(1)} %get-tuple-element.56), channel_id=1, source_target_pairs={{0,16},{2,18},{4,20},{6,22},{8,24},{10,26},{12,28},{14,30},{16,0},... | collective-permute-start | bytes 786440 | tf_op jit(solution)/shard_map/ppermute | solution.py:443
  5.3 13.6 %collective-permute-start.4 = (f32[2,128,256]{2,1,0:T(8,128)S(1)}, f32[2,128,256]{2,1,0:T(8,128)S(1)}, u32[]{:S(2)}, u32[]{:S(2)}) collective-permute-start(f32[2,128,256]{2,1,0:T(8,128)S(1)} %get-tuple-element.57), channel_id=1, source_target_pairs={{0,240},{2,242},{4,244},{6,246},{8,248},{10,250},{12,252},{14,254}... | collective-permute-start | bytes 786440 | tf_op jit(solution)/shard_map/ppermute | solution.py:443
  11.5 11.9 %collective-permute-start.2 = (f32[2,2,256,128]{3,2,1,0:T(8,128)S(1)}, f32[2,2,256,128]{3,2,1,0:T(8,128)S(1)}, u32[]{:S(2)}, u32[]{:S(2)}) collective-permute-start(f32[2,2,256,128]{3,2,1,0:T(8,128)S(1)} %pick_cols.1), channel_id=1, source_target_pairs={{0,14},{2,4},{4,2},{6,8},{8,6},{10,12},{12,10},{14,0},{16,30},{18,... | collective-permute-start | bytes 1572872 | tf_op jit(solution)/shard_map/ppermute | solution.py:443
  13.9 9.0 %collective-permute-start = (f32[2,128,256]{2,1,0:T(8,128)S(1)}, f32[2,128,256]{2,1,0:T(8,128)S(1)}, u32[]{:S(2)}, u32[]{:S(2)}) collective-permute-start(f32[2,128,256]{2,1,0:T(8,128)S(1)} %get-tuple-element.53), channel_id=1, source_target_pairs={{0,16},{2,18},{4,20},{6,22},{8,24},{10,26},{12,28},{14,30},{16,0},... | collective-permute-start | bytes 786440 | tf_op jit(solution)/shard_map/ppermute | solution.py:443
  13.9 9.4 %collective-permute-start.1 = (f32[2,128,256]{2,1,0:T(8,128)S(1)}, f32[2,128,256]{2,1,0:T(8,128)S(1)}, u32[]{:S(2)}, u32[]{:S(2)}) collective-permute-start(f32[2,128,256]{2,1,0:T(8,128)S(1)} %get-tuple-element.54), channel_id=1, source_target_pairs={{0,240},{2,242},{4,244},{6,246},{8,248},{10,250},{12,252},{14,254}... | collective-permute-start | bytes 786440 | tf_op jit(solution)/shard_map/ppermute | solution.py:443
  15.4 1.9 %copy-start.2 = (f32[2,6,256,256]{3,2,1,0:T(8,128)S(1)}, f32[2,6,256,256]{3,2,1,0:T(8,128)}, u32[]{:S(2)}) copy-start(f32[2,6,256,256]{3,2,1,0:T(8,128)} %refs_1_.2) | copy-start | bytes 9437188
  17.3 0.9 copy-start.5
  18.8 2.6 %copy-start.3 = (f32[1,2,256,256]{3,2,1,0:T(8,128)S(1)}, f32[1,2,256,256]{3,2,1,0:T(8,128)}, u32[]{:S(2)}) copy-start(f32[1,2,256,256]{3,2,1,0:T(8,128)} %param.12) | copy-start | bytes 1572868
  18.8 2.6 %copy-start.4 = (bf16[4,256,256]{2,1,0:T(8,128)(2,1)S(1)}, bf16[4,256,256]{2,1,0:T(8,128)(2,1)}, u32[]{:S(2)}) copy-start(bf16[4,256,256]{2,1,0:T(8,128)(2,1)} %constant.54.clone.refs_1_) | copy-start | bytes 1572868
  19.5 8.9 %copy-start.6 = (s32[1,2,2]{2,1,0:T(2,128)S(1)}, s32[1,2,2]{2,1,0:T(2,128)}, u32[]{:S(2)}) copy-start(s32[1,2,2]{2,1,0:T(2,128)} %param.10) | copy-start | bytes 52
  19.5 6.2 %collective-permute-start.5 = (f32[2,2,128,128]{3,2,1,0:T(8,128)S(1)}, f32[2,2,128,128]{3,2,1,0:T(8,128)S(1)}, u32[]{:S(2)}, u32[]{:S(2)}) collective-permute-start(f32[2,2,128,128]{3,2,1,0:T(8,128)S(1)} %get-tuple-element.59), channel_id=1, source_target_pairs={{0,14},{2,4},{4,2},{6,8},{8,6},{10,12},{12,10},{14,0},{16,30},{18,... | collective-permute-start | bytes 786440 | tf_op jit(solution)/shard_map/ppermute | solution.py:443
  20.4 8.0 %collective-permute-start.8 = (f32[2,512,128]{2,1,0:T(8,128)S(1)}, f32[2,512,128]{2,1,0:T(8,128)S(1)}, u32[]{:S(2)}, u32[]{:S(2)}) collective-permute-start(f32[2,512,128]{2,1,0:T(8,128)S(1)} %get-tuple-element.62), channel_id=1, source_target_pairs={{0,2},{2,0},{4,6},{6,4},{8,10},{10,8},{12,14},{14,12},{16,18},{18,... | collective-permute-start | bytes 1572872 | tf_op jit(solution)/shard_map/ppermute | solution.py:443
  26.3 8.3 %collective-permute-start.6 = (f32[2,512,128]{2,1,0:T(8,128)S(1)}, f32[2,512,128]{2,1,0:T(8,128)S(1)}, u32[]{:S(2)}, u32[]{:S(2)}) collective-permute-start(f32[2,512,128]{2,1,0:T(8,128)S(1)} %get-tuple-element.60), channel_id=1, source_target_pairs={{0,2},{2,0},{4,6},{6,4},{8,10},{10,8},{12,14},{14,12},{16,18},{18,... | collective-permute-start | bytes 1572872 | tf_op jit(solution)/shard_map/ppermute | solution.py:443
  28.4 6.2 %collective-permute-start.7 = (f32[2,2,128,128]{3,2,1,0:T(8,128)S(1)}, f32[2,2,128,128]{3,2,1,0:T(8,128)S(1)}, u32[]{:S(2)}, u32[]{:S(2)}) collective-permute-start(f32[2,2,128,128]{3,2,1,0:T(8,128)S(1)} %get-tuple-element.61), channel_id=1, source_target_pairs={{0,14},{2,4},{4,2},{6,8},{8,6},{10,12},{12,10},{14,0},{16,30},{18,... | collective-permute-start | bytes 786440 | tf_op jit(solution)/shard_map/ppermute | solution.py:443
  37.5 8.3 %collective-permute-start.9 = (f32[256,256]{1,0:T(8,128)S(1)}, f32[256,256]{1,0:T(8,128)S(1)}, u32[]{:S(2)}, u32[]{:S(2)}) collective-permute-start(f32[256,256]{1,0:T(8,128)S(1)} %get-tuple-element.70.refs_1_), channel_id=1, source_target_pairs={{0,1},{1,0},{2,3},{3,2},{4,5},{5,4},{6,7},{7,6},{8,9},{9,8},{10,11... | collective-permute-start | bytes 786440 | tf_op jit(solution)/shard_map/ppermute | solution.py:447
  42.7 8.6 %collective-permute-start.11 = (f32[256,256]{1,0:T(8,128)S(1)}, f32[256,256]{1,0:T(8,128)S(1)}, u32[]{:S(2)}, u32[]{:S(2)}) collective-permute-start(f32[256,256]{1,0:T(8,128)S(1)} %get-tuple-element.83.refs_4_), channel_id=1, source_target_pairs={{0,1},{1,0},{2,3},{3,2},{4,5},{5,4},{6,7},{7,6},{8,9},{9,8},{10,11... | collective-permute-start | bytes 786440 | tf_op jit(solution)/shard_map/ppermute | solution.py:447
  54.7 9.0 %collective-permute-start.13 = (f32[2,512,128]{2,1,0:T(8,128)S(1)}, f32[2,512,128]{2,1,0:T(8,128)S(1)}, u32[]{:S(2)}, u32[]{:S(2)}) collective-permute-start(f32[2,512,128]{2,1,0:T(8,128)S(1)} %get-tuple-element.90), channel_id=1, source_target_pairs={{0,2},{2,0},{4,6},{6,4},{8,10},{10,8},{12,14},{14,12},{16,18},{18,... | collective-permute-start | bytes 1572872 | tf_op jit(solution)/shard_map/ppermute | solution.py:443
  57.0 8.9 %collective-permute-start.14 = (f32[2,512,128]{2,1,0:T(8,128)S(1)}, f32[2,512,128]{2,1,0:T(8,128)S(1)}, u32[]{:S(2)}, u32[]{:S(2)}) collective-permute-start(f32[2,512,128]{2,1,0:T(8,128)S(1)} %get-tuple-element.91), channel_id=1, source_target_pairs={{0,14},{2,4},{4,2},{6,8},{8,6},{10,12},{12,10},{14,0},{16,30},{18,... | collective-permute-start | bytes 1572872 | tf_op jit(solution)/shard_map/ppermute | solution.py:443
  57.2 12.5 %collective-permute-start.10 = (f32[1,256,256]{2,1,0:T(8,128)S(1)}, f32[1,256,256]{2,1,0:T(8,128)S(1)}, u32[]{:S(2)}, u32[]{:S(2)}) collective-permute-start(f32[1,256,256]{2,1,0:T(8,128)S(1)} %get-tuple-element.79), channel_id=1, source_target_pairs={{0,1},{1,0},{2,3},{3,2},{4,5},{5,4},{6,7},{7,6},{8,9},{9,8},{10,11... | collective-permute-start | bytes 786440 | tf_op jit(solution)/shard_map/ppermute | solution.py:447
  63.7 13.5 %collective-permute-start.12 = (f32[1,256,256]{2,1,0:T(8,128)S(1)}, f32[1,256,256]{2,1,0:T(8,128)S(1)}, u32[]{:S(2)}, u32[]{:S(2)}) collective-permute-start(f32[1,256,256]{2,1,0:T(8,128)S(1)} %get-tuple-element.88), channel_id=1, source_target_pairs={{0,1},{1,0},{2,3},{3,2},{4,5},{5,4},{6,7},{7,6},{8,9},{9,8},{10,11... | collective-permute-start | bytes 786440 | tf_op jit(solution)/shard_map/ppermute | solution.py:447
  66.6 14.9 %collective-permute-start.20 = (f32[2,128,256]{2,1,0:T(8,128)S(1)}, f32[2,128,256]{2,1,0:T(8,128)S(1)}, u32[]{:S(2)}, u32[]{:S(2)}) collective-permute-start(f32[2,128,256]{2,1,0:T(8,128)S(1)} %get-tuple-element.99), channel_id=1, source_target_pairs={{0,240},{2,242},{4,244},{6,246},{8,248},{10,250},{12,252},{14,254}... | collective-permute-start | bytes 786440 | tf_op jit(solution)/shard_map/ppermute | solution.py:443
  69.7 11.8 %collective-permute-start.19 = (f32[2,128,256]{2,1,0:T(8,128)S(1)}, f32[2,128,256]{2,1,0:T(8,128)S(1)}, u32[]{:S(2)}, u32[]{:S(2)}) collective-permute-start(f32[2,128,256]{2,1,0:T(8,128)S(1)} %get-tuple-element.92.refs_6_), channel_id=1, source_target_pairs={{0,16},{2,18},{4,20},{6,22},{8,24},{10,26},{12,28},{14,30},{16,0},... | collective-permute-start | bytes 786440 | tf_op jit(solution)/shard_map/ppermute | solution.py:443
  78.3 8.4 %collective-permute-start.16 = (f32[1,512,128]{2,1,0:T(8,128)S(1)}, f32[1,512,128]{2,1,0:T(8,128)S(1)}, u32[]{:S(2)}, u32[]{:S(2)}) collective-permute-start(f32[1,512,128]{2,1,0:T(8,128)S(1)} %get-tuple-element.94), channel_id=1, source_target_pairs={{0,14},{2,4},{4,2},{6,8},{8,6},{10,12},{12,10},{14,0},{16,30},{18,... | collective-permute-start | bytes 786440 | tf_op jit(solution)/shard_map/ppermute | solution.py:443
  80.0 6.7 %collective-permute-start.15 = (f32[1,512,128]{2,1,0:T(8,128)S(1)}, f32[1,512,128]{2,1,0:T(8,128)S(1)}, u32[]{:S(2)}, u32[]{:S(2)}) collective-permute-start(f32[1,512,128]{2,1,0:T(8,128)S(1)} %get-tuple-element.93.refs_5_), channel_id=1, source_target_pairs={{0,2},{2,0},{4,6},{6,4},{8,10},{10,8},{12,14},{14,12},{16,18},{18,... | collective-permute-start | bytes 786440 | tf_op jit(solution)/shard_map/ppermute | solution.py:443
  82.1 12.1 %collective-permute-start.21 = (f32[1,256,256]{2,1,0:T(8,128)S(1)}, f32[1,256,256]{2,1,0:T(8,128)S(1)}, u32[]{:S(2)}, u32[]{:S(2)}) collective-permute-start(f32[1,256,256]{2,1,0:T(8,128)S(1)} %get-tuple-element.100.refs_2_), channel_id=1, source_target_pairs={{0,1},{1,0},{2,3},{3,2},{4,5},{5,4},{6,7},{7,6},{8,9},{9,8},{10,11... | collective-permute-start | bytes 786440 | tf_op jit(solution)/shard_map/ppermute | solution.py:447
  87.3 5.1 %collective-permute-start.17 = (f32[1,128,256]{2,1,0:T(8,128)S(1)}, f32[1,128,256]{2,1,0:T(8,128)S(1)}, u32[]{:S(2)}, u32[]{:S(2)}) collective-permute-start(f32[1,128,256]{2,1,0:T(8,128)S(1)} %get-tuple-element.96), channel_id=1, source_target_pairs={{0,16},{2,18},{4,20},{6,22},{8,24},{10,26},{12,28},{14,30},{16,0},... | collective-permute-start | bytes 393224 | tf_op jit(solution)/shard_map/ppermute | solution.py:443
  87.4 6.9 %collective-permute-start.18 = (f32[1,128,256]{2,1,0:T(8,128)S(1)}, f32[1,128,256]{2,1,0:T(8,128)S(1)}, u32[]{:S(2)}, u32[]{:S(2)}) collective-permute-start(f32[1,128,256]{2,1,0:T(8,128)S(1)} %get-tuple-element.97), channel_id=1, source_target_pairs={{0,240},{2,242},{4,244},{6,246},{8,248},{10,250},{12,252},{14,254}... | collective-permute-start | bytes 393224 | tf_op jit(solution)/shard_map/ppermute | solution.py:443
  90.6 10.1 %collective-permute-start.23 = (f32[1,256,256]{2,1,0:T(8,128)S(1)}, f32[1,256,256]{2,1,0:T(8,128)S(1)}, u32[]{:S(2)}, u32[]{:S(2)}) collective-permute-start(f32[1,256,256]{2,1,0:T(8,128)S(1)} %get-tuple-element.101.refs_4_), channel_id=1, source_target_pairs={{0,1},{1,0},{2,3},{3,2},{4,5},{5,4},{6,7},{7,6},{8,9},{9,8},{10,11... | collective-permute-start | bytes 786440 | tf_op jit(solution)/shard_map/ppermute | solution.py:447
  94.8 11.6 %collective-permute-start.22 = (f32[1,256,256]{2,1,0:T(8,128)S(1)}, f32[1,256,256]{2,1,0:T(8,128)S(1)}, u32[]{:S(2)}, u32[]{:S(2)}) collective-permute-start(f32[1,256,256]{2,1,0:T(8,128)S(1)} %rows_first.1.refs_1_), channel_id=1, source_target_pairs={{0,1},{1,0},{2,3},{3,2},{4,5},{5,4},{6,7},{7,6},{8,9},{9,8},{10,11... | collective-permute-start | bytes 786440 | tf_op jit(solution)/shard_map/ppermute | solution.py:447

commit v9 on v8

--- a/solution.py
+++ b/solution.py
@@ -359,16 +359,13 @@
     copy.wait()
 
 
-def pick_rows_kernel(info, own, *refs):
-    *outs, sems = refs
-    h = outs[0].shape[1]
+def pick_rows_kernel(info, own, out_a, out_b, sems):
+    h = out_a.shape[1]
     a, b, _ = ends(info, 0, 0, h)
-    copies = []
-    for layer in range(2):
-        for i, start in enumerate((a, b)):
-            k = 2 * layer + i
-            copies.append(pltpu.make_async_copy(
-                own.at[:, layer, pl.ds(start, h), :], outs[k], sems.at[k]))
+    copies = [
+        pltpu.make_async_copy(own.at[:, 1, pl.ds(start, h), :], out, sems.at[k])
+        for k, (start, out) in enumerate(((a, out_a), (b, out_b)))
+    ]
     for copy in copies:
         copy.start()
     for copy in copies:
@@ -495,7 +492,9 @@
     strip, tall = ((2, h, n), F32), ((2, 2 * n, h), F32)
     side_strip, quarter = ((2, 2, n, h), F32), ((2, 2, h, h), F32)
 
-    picked = call(pick_rows_kernel, "pick_rows", (strip,) * 4, (info, own), copies=4)
+    top, low = own[:, 0, :h, :], own[:, 0, h:, :]
+    picked = [jnp.where(odd_row, top, low), jnp.where(odd_row, low, top)]
+    picked += call(pick_rows_kernel, "pick_rows", (strip,) * 2, (info, own), copies=2)
     rows = [[swap(picked[2 * i + k], 0, k == 1) for k in range(2)] for i in range(2)]
     *made, probe = call(
         prepare_kernel,
@@ -627,7 +626,7 @@
         after=(out_a,),
     )
     strips_first = fold_cols("cols_first", out_a, out_c, out_b, ())
-    (mine_first,) = fold_rows("rows_first", *strips_first, (other_re,))
+    (mine_first,) = fold_rows("rows_first", *strips_first, (other_re, other_im))
     other_first = swap_mode(mine_first)
     (probe_grad,) = call(
         probe_sum_kernel,

time: 108 us -> 112 us (1.037)
  waiting for transfers between devices: 21.3 us -> 26.8 us
  starting transfers between devices: 44.5 us -> 42.2 us
  other arithmetic: 0.01 us -> 1.17 us
    ppermute x7, waiting for transfers between devices: 14.6 us -> 18.9 us  [swap_mode(): return lax.ppermute(value, 'mode', [(0, 1), (1, 0)])]
    ppermute x7, starting transfers between devices: 16.1 us -> 12.4 us  [swap_mode(): return lax.ppermute(value, 'mode', [(0, 1), (1, 0)])]
    ppermute x17, starting transfers between devices: 28.3 us -> 29.8 us  [swap(): return lax.ppermute(value, 'tile', pairs)]
    ppermute x17, waiting for transfers between devices: 6.64 us -> 7.93 us  [swap(): return lax.ppermute(value, 'tile', pairs)]
    select_n x0 -> x1, other arithmetic: none -> 1.16 us  [body(): picked = [jnp.where(odd_row, top, low), jnp.where(odd_row, low, top)]]
  transfers between devices with their start and end apart: 24 -> 24, of which waited for: 9 -> 10; matrix products, arithmetic and copies ran while one was open for 0% -> 0% of each run, Pallas kernels for 26% -> 25%
where the time goes in v9:
time: 112 us
  starting transfers between devices  42.2 us (38%)
  Pallas kernels  36 us (32%)
  waiting for transfers between devices  26.8 us (24%)
  local copies, waits for them, and re-layouts  4.19 us (4%)
  between operations  1.82 us (2%)
  other arithmetic  1.17 us (1%)
    pallas_call x23, Pallas kernels, call(): pl.pallas_call(run, out_shape=tuple((jax.ShapeDtypeStruct(shape, dtype) f...  36 us
    ppermute x17, starting transfers between devices, swap(): return lax.ppermute(value, 'tile', pairs)  29.8 us
    ppermute x7, waiting for transfers between devices, swap_mode(): return lax.ppermute(value, 'mode', [(0, 1), (1, 0)])  18.9 us
    ppermute x7, starting transfers between devices, swap_mode(): return lax.ppermute(value, 'mode', [(0, 1), (1, 0)])  12.4 us
    ppermute x17, waiting for transfers between devices, swap(): return lax.ppermute(value, 'tile', pairs)  7.93 us
    unnamed x14, local copies, waits for them, and re-layouts  4.09 us
  transfers between devices with their start and end apart: 24, of which 10 were waited for; matrix products, arithmetic and copies ran while one was open for 0% of the time, Pallas kernels for 25%

profile of v9, /device:TPU:1, one launch (start us, length us, event | category | flops | bytes accessed | tf_op | source)
XLA Modules:
  0.0 112.3 jit_solution(389851441739921693)
XLA Ops:
  1.8 7.5 %collective-permute-start.4 = (f32[2,128,256]{2,1,0:T(8,128)S(1)}, f32[2,128,256]{2,1,0:T(8,128)S(1)}, u32[]{:S(2)}, u32[]{:S(2)}) collective-permute-start(f32[2,128,256]{2,1,0:T(8,128)S(1)} %get-tuple-element.100), channel_id=1, source_target_pairs={{0,240},{2,242},{4,244},{6,246},{8,248},{10,250},{12,252},{14,254}... | collective-permute-start | bytes 786440 | tf_op jit(solution)/shard_map/ppermute | solution.py:440
  11.3 2.1 %collective-permute-start.2 = (f32[2,2,256,128]{3,2,1,0:T(8,128)S(1)}, f32[2,2,256,128]{3,2,1,0:T(8,128)S(1)}, u32[]{:S(2)}, u32[]{:S(2)}) collective-permute-start(f32[2,2,256,128]{3,2,1,0:T(8,128)S(1)} %pick_cols.1), channel_id=1, source_target_pairs={{0,14},{2,4},{4,2},{6,8},{8,6},{10,12},{12,10},{14,0},{16,30},{18,... | collective-permute-start | bytes 1572872 | tf_op jit(solution)/shard_map/ppermute | solution.py:440
  14.0 1.8 %collective-permute-start = (f32[2,128,256]{2,1,0:T(8,128)S(1)}, f32[2,128,256]{2,1,0:T(8,128)S(1)}, u32[]{:S(2)}, u32[]{:S(2)}) collective-permute-start(f32[2,128,256]{2,1,0:T(8,128)S(1)} %get-tuple-element.51), channel_id=1, source_target_pairs={{0,16},{2,18},{4,20},{6,22},{8,24},{10,26},{12,28},{14,30},{16,0},... | collective-permute-start | bytes 786440 | tf_op jit(solution)/shard_map/ppermute | solution.py:440
  16.0 1.9 %copy-done.2 = f32[2,6,256,256]{3,2,1,0:T(8,128)S(1)} copy-done((f32[2,6,256,256]{3,2,1,0:T(8,128)S(1)}, f32[2,6,256,256]{3,2,1,0:T(8,128)}, u32[]{:S(2)}) %copy-start.2) | copy-done | bytes 3145752
  20.4 1.6 %collective-permute-start.8 = (f32[2,512,128]{2,1,0:T(8,128)S(1)}, f32[2,512,128]{2,1,0:T(8,128)S(1)}, u32[]{:S(2)}, u32[]{:S(2)}) collective-permute-start(f32[2,512,128]{2,1,0:T(8,128)S(1)} %get-tuple-element.58), channel_id=1, source_target_pairs={{0,2},{2,0},{4,6},{6,4},{8,10},{10,8},{12,14},{14,12},{16,18},{18,... | collective-permute-start | bytes 1572872 | tf_op jit(solution)/shard_map/ppermute | solution.py:440
  22.0 1.5 %reorder.1 = (f32[2,256,256]{2,1,0:T(8,128)S(1)}, bf16[4,256,256]{2,1,0:T(8,128)(2,1)S(1)}) custom-call(f32[2,256,256]{2,1,0:T(8,128)S(1)} %bitcast.19, bf16[4,256,256]{2,1,0:T(8,128)(2,1)S(1)} %copy-done.4), custom_call_target="tpu_custom_call" | custom-call | tf_op jit(solution)/shard_map/reorder/pallas_call | solution.py:458
  26.8 2.1 %collective-permute-start.6 = (f32[2,512,128]{2,1,0:T(8,128)S(1)}, f32[2,512,128]{2,1,0:T(8,128)S(1)}, u32[]{:S(2)}, u32[]{:S(2)}) collective-permute-start(f32[2,512,128]{2,1,0:T(8,128)S(1)} %get-tuple-element.56), channel_id=1, source_target_pairs={{0,2},{2,0},{4,6},{6,4},{8,10},{10,8},{12,14},{14,12},{16,18},{18,... | collective-permute-start | bytes 1572872 | tf_op jit(solution)/shard_map/ppermute | solution.py:440
  28.9 3.2 %waves_0.1 = (f32[2,512,512]{2,1,0:T(8,128)S(1)}, f32[2,256,256]{2,1,0:T(8,128)S(1)}, f32[6,2,256,256]{3,2,1,0:T(8,128)S(1)}) custom-call(s32[2,2]{1,0:T(2,128)S(1)} %bitcast.20, s32[5]{0:T(128)S(1)} %convert_element_type.3.refs_0_.refs_1_.refs_2_, f32[2,2,256,256]{3,2,1,0:T(8,128)S(1)} %bitcast.17, ...), custom_call_target="tpu_custom_call" | custom-call | tf_op jit(solution)/shard_map/waves_0/pallas_call | solution.py:458
  32.1 2.9 %waves_1.1 = (f32[2,256,256]{2,1,0:T(8,128)S(1)}, f32[6,2,256,256]{3,2,1,0:T(8,128)S(1)}) custom-call(s32[2,2]{1,0:T(2,128)S(1)} %bitcast.21, f32[2,512,512]{2,1,0:T(8,128)S(1)} %get-tuple-element.64.refs_1_, f32[2,6,256,256]{3,2,1,0:T(8,128)S(1)} %get-tuple-element.54.refs_4_.refs_8_.refs_2_, bf16[2,256,256]{2,1,0:T(8,128)(2,1)S(1)} %get-tuple-element.59.refs_9_.refs_3_, ...), custom_call_target="tpu_custom_call" | custom-call | tf_op jit(solution)/shard_map/waves_1/pallas_call | solution.py:458
  35.1 3.0 %fars_0.1 = (f32[2,512,512]{2,1,0:T(8,128)S(1)}, f32[2,256,256]{2,1,0:T(8,128)S(1)}, f32[6,2,256,256]{3,2,1,0:T(8,128)S(1)}, f32[256,256]{1,0:T(8,128)S(1)}) custom-call(s32[2,2]{1,0:T(2,128)S(1)} %bitcast.22, s32[5]{0:T(128)S(1)} %convert_element_type.3.refs_0_.refs_1_.refs_2_, f32[2,2,256,256]{3,2,1,0:T(8,128)S(1)} %bitcast.18, ...), custom_call_target="tpu_custom_call" | custom-call | tf_op jit(solution)/shard_map/fars_0/pallas_call | solution.py:458
  38.1 2.7 %collective-permute-start.9 = (f32[256,256]{1,0:T(8,128)S(1)}, f32[256,256]{1,0:T(8,128)S(1)}, u32[]{:S(2)}, u32[]{:S(2)}) collective-permute-start(f32[256,256]{1,0:T(8,128)S(1)} %get-tuple-element.66.refs_1_), channel_id=1, source_target_pairs={{0,1},{1,0},{2,3},{3,2},{4,5},{5,4},{6,7},{7,6},{8,9},{9,8},{10,11... | collective-permute-start | bytes 786440 | tf_op jit(solution)/shard_map/ppermute | solution.py:444
  40.8 2.5 %fars_1.1 = (f32[2,256,256]{2,1,0:T(8,128)S(1)}, f32[6,2,256,256]{3,2,1,0:T(8,128)S(1)}, f32[256,256]{1,0:T(8,128)S(1)}) custom-call(s32[2,2]{1,0:T(2,128)S(1)} %bitcast.23, f32[2,512,512]{2,1,0:T(8,128)S(1)} %get-tuple-element.77.refs_1_, f32[6,2,256,256]{3,2,1,0:T(8,128)S(1)} %get-tuple-element.78.refs_2_.refs_8_, ...), custom_call_target="tpu_custom_call" | custom-call | tf_op jit(solution)/shard_map/fars_1/pallas_call | solution.py:458
  44.6 1.8 %collective-permute-done.9.refs_2_ = f32[256,256]{1,0:T(8,128)S(1)} collective-permute-done((f32[256,256]{1,0:T(8,128)S(1)}, f32[256,256]{1,0:T(8,128)S(1)}, u32[]{:S(2)}, u32[]{:S(2)}) %collective-permute-start.9) | collective-permute-done | bytes 262176 | tf_op jit(solution)/shard_map/ppermute | solution.py:444
  46.3 1.8 %back_last_0.1 = (f32[2,256,256]{2,1,0:T(8,128)S(1)}, bf16[6,2,256,256]{3,2,1,0:T(8,128)(2,1)S(1)}) custom-call(s32[1]{0:T(128)S(6)} %copy.11.refs_0_, f32[256,256]{1,0:T(8,128)S(1)} %get-tuple-element.66.refs_1_, f32[256,256]{1,0:T(8,128)S(1)} %collective-permute-done.9.refs_2_, f32[2,256,256]{2,1,0:T(8,128)S(1)} %get-tuple-element.53.refs_4_.refs_3_.refs_6_, ...), custom_call_target="tpu_custom_call" | custom-call | tf_op jit(solution)/shard_map/back_last_0/pallas_call | solution.py:458
  48.2 2.7 %back_first_0.1 = (f32[1,256,256]{2,1,0:T(8,128)S(1)}, f32[1,256,256]{2,1,0:T(8,128)S(1)}, f32[2,6,256,256]{3,2,1,0:T(8,128)S(1)}) custom-call(s32[5]{0:T(128)S(1)} %convert_element_type.3.refs_0_.refs_1_.refs_2_, bf16[6,2,256,256]{3,2,1,0:T(8,128)(2,1)S(1)} %get-tuple-element.69.refs_1_, f32[2,6,256,256]{3,2,1,0:T(8,128)S(1)} %get-tuple-element.54.refs_4_.refs_8_.refs_2_, ...), custom_call_target="tpu_custom_call" | custom-call | tf_op jit(solution)/shard_map/back_first_0/pallas_call | solution.py:458
  51.9 3.4 %back_last_1.1 = (bf16[6,2,256,256]{3,2,1,0:T(8,128)(2,1)S(1)}, f32[2,512,128]{2,1,0:T(8,128)S(1)}, f32[2,512,256]{2,1,0:T(8,128)S(1)}, f32[2,512,128]{2,1,0:T(8,128)S(1)}) custom-call(s32[1]{0:T(128)S(6)} %copy.11.refs_0_, s32[2,2]{1,0:T(2,128)S(1)} %bitcast.24, s32[5]{0:T(128)S(1)} %convert_element_type.3.refs_0_.refs_1_.refs_2_, ...), custom_call_target="tpu_custom_call" | custom-call | tf_op jit(solution)/shard_map/back_last_1/pallas_call | solution.py:458
  55.3 2.2 %collective-permute-start.13 = (f32[2,512,128]{2,1,0:T(8,128)S(1)}, f32[2,512,128]{2,1,0:T(8,128)S(1)}, u32[]{:S(2)}, u32[]{:S(2)}) collective-permute-start(f32[2,512,128]{2,1,0:T(8,128)S(1)} %get-tuple-element.86), channel_id=1, source_target_pairs={{0,2},{2,0},{4,6},{6,4},{8,10},{10,8},{12,14},{14,12},{16,18},{18,... | collective-permute-start | bytes 1572872 | tf_op jit(solution)/shard_map/ppermute | solution.py:440
  58.2 3.3 %collective-permute-start.10 = (f32[1,256,256]{2,1,0:T(8,128)S(1)}, f32[1,256,256]{2,1,0:T(8,128)S(1)}, u32[]{:S(2)}, u32[]{:S(2)}) collective-permute-start(f32[1,256,256]{2,1,0:T(8,128)S(1)} %get-tuple-element.75), channel_id=1, source_target_pairs={{0,1},{1,0},{2,3},{3,2},{4,5},{5,4},{6,7},{7,6},{8,9},{9,8},{10,11... | collective-permute-start | bytes 786440 | tf_op jit(solution)/shard_map/ppermute | solution.py:444
  61.5 2.8 %back_first_1.1 = (f32[1,256,256]{2,1,0:T(8,128)S(1)}, f32[1,256,256]{2,1,0:T(8,128)S(1)}, f32[2,6,256,256]{3,2,1,0:T(8,128)S(1)}) custom-call(s32[5]{0:T(128)S(1)} %convert_element_type.3.refs_0_.refs_1_.refs_2_, bf16[6,2,256,256]{3,2,1,0:T(8,128)(2,1)S(1)} %get-tuple-element.82.refs_1_, f32[2,6,256,256]{3,2,1,0:T(8,128)S(1)} %get-tuple-element.54.refs_4_.refs_8_.refs_2_, ...), custom_call_target="tpu_custom_call" | custom-call | tf_op jit(solution)/shard_map/back_first_1/pallas_call | solution.py:458
  64.4 2.0 %collective-permute-done.14.refs_3_ = f32[2,512,128]{2,1,0:T(8,128)S(1)} collective-permute-done((f32[2,512,128]{2,1,0:T(8,128)S(1)}, f32[2,512,128]{2,1,0:T(8,128)S(1)}, u32[]{:S(2)}, u32[]{:S(2)}) %collective-permute-start.14) | collective-permute-done | bytes 524320 | tf_op jit(solution)/shard_map/ppermute | solution.py:440
  67.1 3.6 %collective-permute-start.20 = (f32[2,128,256]{2,1,0:T(8,128)S(1)}, f32[2,128,256]{2,1,0:T(8,128)S(1)}, u32[]{:S(2)}, u32[]{:S(2)}) collective-permute-start(f32[2,128,256]{2,1,0:T(8,128)S(1)} %get-tuple-element.95), channel_id=1, source_target_pairs={{0,240},{2,242},{4,244},{6,246},{8,248},{10,250},{12,252},{14,254}... | collective-permute-start | bytes 786440 | tf_op jit(solution)/shard_map/ppermute | solution.py:440
  70.7 7.2 %collective-permute-done.12.refs_5_.refs_4_ = f32[1,256,256]{2,1,0:T(8,128)S(1)} collective-permute-done((f32[1,256,256]{2,1,0:T(8,128)S(1)}, f32[1,256,256]{2,1,0:T(8,128)S(1)}, u32[]{:S(2)}, u32[]{:S(2)}) %collective-permute-start.12) | collective-permute-done | bytes 262176 | tf_op jit(solution)/shard_map/ppermute | solution.py:444
  78.9 1.7 %collective-permute-start.16 = (f32[1,512,128]{2,1,0:T(8,128)S(1)}, f32[1,512,128]{2,1,0:T(8,128)S(1)}, u32[]{:S(2)}, u32[]{:S(2)}) collective-permute-start(f32[1,512,128]{2,1,0:T(8,128)S(1)} %get-tuple-element.90), channel_id=1, source_target_pairs={{0,14},{2,4},{4,2},{6,8},{8,6},{10,12},{12,10},{14,0},{16,30},{18,... | collective-permute-start | bytes 786440 | tf_op jit(solution)/shard_map/ppermute | solution.py:440
  80.6 2.5 %collective-permute-start.15 = (f32[1,512,128]{2,1,0:T(8,128)S(1)}, f32[1,512,128]{2,1,0:T(8,128)S(1)}, u32[]{:S(2)}, u32[]{:S(2)}) collective-permute-start(f32[1,512,128]{2,1,0:T(8,128)S(1)} %get-tuple-element.89.refs_5_), channel_id=1, source_target_pairs={{0,2},{2,0},{4,6},{6,4},{8,10},{10,8},{12,14},{14,12},{16,18},{18,... | collective-permute-start | bytes 786440 | tf_op jit(solution)/shard_map/ppermute | solution.py:440
  83.6 2.6 %collective-permute-start.21 = (f32[1,256,256]{2,1,0:T(8,128)S(1)}, f32[1,256,256]{2,1,0:T(8,128)S(1)}, u32[]{:S(2)}, u32[]{:S(2)}) collective-permute-start(f32[1,256,256]{2,1,0:T(8,128)S(1)} %get-tuple-element.96.refs_2_), channel_id=1, source_target_pairs={{0,1},{1,0},{2,3},{3,2},{4,5},{5,4},{6,7},{7,6},{8,9},{9,8},{10,11... | collective-permute-start | bytes 786440 | tf_op jit(solution)/shard_map/ppermute | solution.py:444
  88.4 3.5 %collective-permute-start.18 = (f32[1,128,256]{2,1,0:T(8,128)S(1)}, f32[1,128,256]{2,1,0:T(8,128)S(1)}, u32[]{:S(2)}, u32[]{:S(2)}) collective-permute-start(f32[1,128,256]{2,1,0:T(8,128)S(1)} %get-tuple-element.93), channel_id=1, source_target_pairs={{0,240},{2,242},{4,244},{6,246},{8,248},{10,250},{12,252},{14,254}... | collective-permute-start | bytes 393224 | tf_op jit(solution)/shard_map/ppermute | solution.py:440
  92.9 2.2 %collective-permute-done.18.refs_3_ = f32[1,128,256]{2,1,0:T(8,128)S(1)} collective-permute-done((f32[1,128,256]{2,1,0:T(8,128)S(1)}, f32[1,128,256]{2,1,0:T(8,128)S(1)}, u32[]{:S(2)}, u32[]{:S(2)}) %collective-permute-start.18) | collective-permute-done | bytes 131104 | tf_op jit(solution)/shard_map/ppermute | solution.py:440
  95.1 6.5 %collective-permute-done.22.refs_5_ = f32[1,256,256]{2,1,0:T(8,128)S(1)} collective-permute-done((f32[1,256,256]{2,1,0:T(8,128)S(1)}, f32[1,256,256]{2,1,0:T(8,128)S(1)}, u32[]{:S(2)}, u32[]{:S(2)}) %collective-permute-start.22) | collective-permute-done | bytes 262176 | tf_op jit(solution)/shard_map/ppermute | solution.py:444
  102.2 2.6 %collective-permute-start.23 = (f32[1,256,256]{2,1,0:T(8,128)S(1)}, f32[1,256,256]{2,1,0:T(8,128)S(1)}, u32[]{:S(2)}, u32[]{:S(2)}) collective-permute-start(f32[1,256,256]{2,1,0:T(8,128)S(1)} %rows_first.1.refs_1_), channel_id=1, source_target_pairs={{0,1},{1,0},{2,3},{3,2},{4,5},{5,4},{6,7},{7,6},{8,9},{9,8},{10,11... | collective-permute-start | bytes 786440 | tf_op jit(solution)/shard_map/ppermute | solution.py:444
  104.8 2.0 %probe_sum.1 = f32[1,2,6,256,256]{4,3,2,1,0:T(8,128)} custom-call(f32[2,6,256,256]{3,2,1,0:T(8,128)S(1)} %get-tuple-element.98.refs_0_, f32[2,6,256,256]{3,2,1,0:T(8,128)S(1)} %get-tuple-element.99.refs_1_), custom_call_target="tpu_custom_call" | custom-call | tf_op jit(solution)/shard_map/probe_sum/pallas_call | solution.py:458
  106.7 1.5 %finish_last.1.refs_2_ = f32[1,2,2,256,256]{4,3,2,1,0:T(8,128)} custom-call(s32[5]{0:T(128)S(1)} %convert_element_type.3.refs_0_.refs_1_.refs_2_, f32[1,256,256]{2,1,0:T(8,128)S(1)} %rows_first.1.refs_1_, f32[1,256,256]{2,1,0:T(8,128)S(1)} %get-tuple-element.96.refs_2_, f32[1,256,256]{2,1,0:T(8,128)S(1)} %collective-permute-done.21.refs_4_.refs_3_, ...), custom_call_target="tpu_custom_call" | custom-call | tf_op jit(solution)/shard_map/finish_last/pallas_call | solution.py:458
  108.2 2.6 %collective-permute-done.23.refs_1_ = f32[1,256,256]{2,1,0:T(8,128)S(1)} collective-permute-done((f32[1,256,256]{2,1,0:T(8,128)S(1)}, f32[1,256,256]{2,1,0:T(8,128)S(1)}, u32[]{:S(2)}, u32[]{:S(2)}) %collective-permute-start.23) | collective-permute-done | bytes 262176 | tf_op jit(solution)/shard_map/ppermute | solution.py:444
  (56 shorter events, 19.3 us)
Async XLA Ops:
  0.7 18.7 %copy-start.1 = (f32[1,2,2,256,256]{4,3,2,1,0:T(8,128)S(1)}, f32[1,2,2,256,256]{4,3,2,1,0:T(8,128)}, u32[]{:S(2)}) copy-start(f32[1,2,2,256,256]{4,3,2,1,0:T(8,128)} %param.7) | copy-start | bytes 3145732
  1.8 17.5 %collective-permute-start.4 = (f32[2,128,256]{2,1,0:T(8,128)S(1)}, f32[2,128,256]{2,1,0:T(8,128)S(1)}, u32[]{:S(2)}, u32[]{:S(2)}) collective-permute-start(f32[2,128,256]{2,1,0:T(8,128)S(1)} %get-tuple-element.100), channel_id=1, source_target_pairs={{0,240},{2,242},{4,244},{6,246},{8,248},{10,250},{12,252},{14,254}... | collective-permute-start | bytes 786440 | tf_op jit(solution)/shard_map/ppermute | solution.py:440
  9.4 10.0 %collective-permute-start.3 = (f32[2,128,256]{2,1,0:T(8,128)S(1)}, f32[2,128,256]{2,1,0:T(8,128)S(1)}, u32[]{:S(2)}, u32[]{:S(2)}) collective-permute-start(f32[2,128,256]{2,1,0:T(8,128)S(1)} %get-tuple-element.101), channel_id=1, source_target_pairs={{0,16},{2,18},{4,20},{6,22},{8,24},{10,26},{12,28},{14,30},{16,0},... | collective-permute-start | bytes 786440 | tf_op jit(solution)/shard_map/ppermute | solution.py:440
  9.5 1.2 %copy-start = (f32[1,2,2,256,256]{4,3,2,1,0:T(8,128)S(1)}, f32[1,2,2,256,256]{4,3,2,1,0:T(8,128)}, u32[]{:S(2)}) copy-start(f32[1,2,2,256,256]{4,3,2,1,0:T(8,128)} %param.7) | copy-start | bytes 3145732
  11.3 13.7 %collective-permute-start.2 = (f32[2,2,256,128]{3,2,1,0:T(8,128)S(1)}, f32[2,2,256,128]{3,2,1,0:T(8,128)S(1)}, u32[]{:S(2)}, u32[]{:S(2)}) collective-permute-start(f32[2,2,256,128]{3,2,1,0:T(8,128)S(1)} %pick_cols.1), channel_id=1, source_target_pairs={{0,14},{2,4},{4,2},{6,8},{8,6},{10,12},{12,10},{14,0},{16,30},{18,... | collective-permute-start | bytes 1572872 | tf_op jit(solution)/shard_map/ppermute | solution.py:440
  14.0 9.5 %collective-permute-start = (f32[2,128,256]{2,1,0:T(8,128)S(1)}, f32[2,128,256]{2,1,0:T(8,128)S(1)}, u32[]{:S(2)}, u32[]{:S(2)}) collective-permute-start(f32[2,128,256]{2,1,0:T(8,128)S(1)} %get-tuple-element.51), channel_id=1, source_target_pairs={{0,16},{2,18},{4,20},{6,22},{8,24},{10,26},{12,28},{14,30},{16,0},... | collective-permute-start | bytes 786440 | tf_op jit(solution)/shard_map/ppermute | solution.py:440
  15.9 9.1 %collective-permute-start.1 = (f32[2,128,256]{2,1,0:T(8,128)S(1)}, f32[2,128,256]{2,1,0:T(8,128)S(1)}, u32[]{:S(2)}, u32[]{:S(2)}) collective-permute-start(f32[2,128,256]{2,1,0:T(8,128)S(1)} %get-tuple-element.52), channel_id=1, source_target_pairs={{0,240},{2,242},{4,244},{6,246},{8,248},{10,250},{12,252},{14,254}... | collective-permute-start | bytes 786440 | tf_op jit(solution)/shard_map/ppermute | solution.py:440
  16.0 1.9 %copy-start.2 = (f32[2,6,256,256]{3,2,1,0:T(8,128)S(1)}, f32[2,6,256,256]{3,2,1,0:T(8,128)}, u32[]{:S(2)}) copy-start(f32[2,6,256,256]{3,2,1,0:T(8,128)} %refs_1_.2) | copy-start | bytes 9437188
  17.8 0.9 copy-start.5
  19.3 2.6 %copy-start.3 = (f32[1,2,256,256]{3,2,1,0:T(8,128)S(1)}, f32[1,2,256,256]{3,2,1,0:T(8,128)}, u32[]{:S(2)}) copy-start(f32[1,2,256,256]{3,2,1,0:T(8,128)} %param.12) | copy-start | bytes 1572868
  19.4 2.6 %copy-start.4 = (bf16[4,256,256]{2,1,0:T(8,128)(2,1)S(1)}, bf16[4,256,256]{2,1,0:T(8,128)(2,1)}, u32[]{:S(2)}) copy-start(bf16[4,256,256]{2,1,0:T(8,128)(2,1)} %constant.54.clone.refs_1_) | copy-start | bytes 1572868
  20.0 8.9 %copy-start.6 = (s32[1,2,2]{2,1,0:T(2,128)S(1)}, s32[1,2,2]{2,1,0:T(2,128)}, u32[]{:S(2)}) copy-start(s32[1,2,2]{2,1,0:T(2,128)} %param.10) | copy-start | bytes 52
  20.0 6.2 %collective-permute-start.5 = (f32[2,2,128,128]{3,2,1,0:T(8,128)S(1)}, f32[2,2,128,128]{3,2,1,0:T(8,128)S(1)}, u32[]{:S(2)}, u32[]{:S(2)}) collective-permute-start(f32[2,2,128,128]{3,2,1,0:T(8,128)S(1)} %get-tuple-element.55), channel_id=1, source_target_pairs={{0,14},{2,4},{4,2},{6,8},{8,6},{10,12},{12,10},{14,0},{16,30},{18,... | collective-permute-start | bytes 786440 | tf_op jit(solution)/shard_map/ppermute | solution.py:440
  20.4 8.5 %collective-permute-start.8 = (f32[2,512,128]{2,1,0:T(8,128)S(1)}, f32[2,512,128]{2,1,0:T(8,128)S(1)}, u32[]{:S(2)}, u32[]{:S(2)}) collective-permute-start(f32[2,512,128]{2,1,0:T(8,128)S(1)} %get-tuple-element.58), channel_id=1, source_target_pairs={{0,2},{2,0},{4,6},{6,4},{8,10},{10,8},{12,14},{14,12},{16,18},{18,... | collective-permute-start | bytes 1572872 | tf_op jit(solution)/shard_map/ppermute | solution.py:440
  26.8 8.3 %collective-permute-start.6 = (f32[2,512,128]{2,1,0:T(8,128)S(1)}, f32[2,512,128]{2,1,0:T(8,128)S(1)}, u32[]{:S(2)}, u32[]{:S(2)}) collective-permute-start(f32[2,512,128]{2,1,0:T(8,128)S(1)} %get-tuple-element.56), channel_id=1, source_target_pairs={{0,2},{2,0},{4,6},{6,4},{8,10},{10,8},{12,14},{14,12},{16,18},{18,... | collective-permute-start | bytes 1572872 | tf_op jit(solution)/shard_map/ppermute | solution.py:440
  28.9 6.1 %collective-permute-start.7 = (f32[2,2,128,128]{3,2,1,0:T(8,128)S(1)}, f32[2,2,128,128]{3,2,1,0:T(8,128)S(1)}, u32[]{:S(2)}, u32[]{:S(2)}) collective-permute-start(f32[2,2,128,128]{3,2,1,0:T(8,128)S(1)} %get-tuple-element.57), channel_id=1, source_target_pairs={{0,14},{2,4},{4,2},{6,8},{8,6},{10,12},{12,10},{14,0},{16,30},{18,... | collective-permute-start | bytes 786440 | tf_op jit(solution)/shard_map/ppermute | solution.py:440
  38.1 8.3 %collective-permute-start.9 = (f32[256,256]{1,0:T(8,128)S(1)}, f32[256,256]{1,0:T(8,128)S(1)}, u32[]{:S(2)}, u32[]{:S(2)}) collective-permute-start(f32[256,256]{1,0:T(8,128)S(1)} %get-tuple-element.66.refs_1_), channel_id=1, source_target_pairs={{0,1},{1,0},{2,3},{3,2},{4,5},{5,4},{6,7},{7,6},{8,9},{9,8},{10,11... | collective-permute-start | bytes 786440 | tf_op jit(solution)/shard_map/ppermute | solution.py:444
  43.3 8.6 %collective-permute-start.11 = (f32[256,256]{1,0:T(8,128)S(1)}, f32[256,256]{1,0:T(8,128)S(1)}, u32[]{:S(2)}, u32[]{:S(2)}) collective-permute-start(f32[256,256]{1,0:T(8,128)S(1)} %get-tuple-element.79.refs_4_), channel_id=1, source_target_pairs={{0,1},{1,0},{2,3},{3,2},{4,5},{5,4},{6,7},{7,6},{8,9},{9,8},{10,11... | collective-permute-start | bytes 786440 | tf_op jit(solution)/shard_map/ppermute | solution.py:444
  55.3 9.1 %collective-permute-start.13 = (f32[2,512,128]{2,1,0:T(8,128)S(1)}, f32[2,512,128]{2,1,0:T(8,128)S(1)}, u32[]{:S(2)}, u32[]{:S(2)}) collective-permute-start(f32[2,512,128]{2,1,0:T(8,128)S(1)} %get-tuple-element.86), channel_id=1, source_target_pairs={{0,2},{2,0},{4,6},{6,4},{8,10},{10,8},{12,14},{14,12},{16,18},{18,... | collective-permute-start | bytes 1572872 | tf_op jit(solution)/shard_map/ppermute | solution.py:440
  57.5 8.9 %collective-permute-start.14 = (f32[2,512,128]{2,1,0:T(8,128)S(1)}, f32[2,512,128]{2,1,0:T(8,128)S(1)}, u32[]{:S(2)}, u32[]{:S(2)}) collective-permute-start(f32[2,512,128]{2,1,0:T(8,128)S(1)} %get-tuple-element.87), channel_id=1, source_target_pairs={{0,14},{2,4},{4,2},{6,8},{8,6},{10,12},{12,10},{14,0},{16,30},{18,... | collective-permute-start | bytes 1572872 | tf_op jit(solution)/shard_map/ppermute | solution.py:440
  58.2 12.5 %collective-permute-start.10 = (f32[1,256,256]{2,1,0:T(8,128)S(1)}, f32[1,256,256]{2,1,0:T(8,128)S(1)}, u32[]{:S(2)}, u32[]{:S(2)}) collective-permute-start(f32[1,256,256]{2,1,0:T(8,128)S(1)} %get-tuple-element.75), channel_id=1, source_target_pairs={{0,1},{1,0},{2,3},{3,2},{4,5},{5,4},{6,7},{7,6},{8,9},{9,8},{10,11... | collective-permute-start | bytes 786440 | tf_op jit(solution)/shard_map/ppermute | solution.py:444
  64.3 13.6 %collective-permute-start.12 = (f32[1,256,256]{2,1,0:T(8,128)S(1)}, f32[1,256,256]{2,1,0:T(8,128)S(1)}, u32[]{:S(2)}, u32[]{:S(2)}) collective-permute-start(f32[1,256,256]{2,1,0:T(8,128)S(1)} %get-tuple-element.84), channel_id=1, source_target_pairs={{0,1},{1,0},{2,3},{3,2},{4,5},{5,4},{6,7},{7,6},{8,9},{9,8},{10,11... | collective-permute-start | bytes 786440 | tf_op jit(solution)/shard_map/ppermute | solution.py:444
  67.1 15.9 %collective-permute-start.20 = (f32[2,128,256]{2,1,0:T(8,128)S(1)}, f32[2,128,256]{2,1,0:T(8,128)S(1)}, u32[]{:S(2)}, u32[]{:S(2)}) collective-permute-start(f32[2,128,256]{2,1,0:T(8,128)S(1)} %get-tuple-element.95), channel_id=1, source_target_pairs={{0,240},{2,242},{4,244},{6,246},{8,248},{10,250},{12,252},{14,254}... | collective-permute-start | bytes 786440 | tf_op jit(solution)/shard_map/ppermute | solution.py:440
  70.7 12.3 %collective-permute-start.19 = (f32[2,128,256]{2,1,0:T(8,128)S(1)}, f32[2,128,256]{2,1,0:T(8,128)S(1)}, u32[]{:S(2)}, u32[]{:S(2)}) collective-permute-start(f32[2,128,256]{2,1,0:T(8,128)S(1)} %get-tuple-element.88.refs_6_), channel_id=1, source_target_pairs={{0,16},{2,18},{4,20},{6,22},{8,24},{10,26},{12,28},{14,30},{16,0},... | collective-permute-start | bytes 786440 | tf_op jit(solution)/shard_map/ppermute | solution.py:440
  78.9 8.8 %collective-permute-start.16 = (f32[1,512,128]{2,1,0:T(8,128)S(1)}, f32[1,512,128]{2,1,0:T(8,128)S(1)}, u32[]{:S(2)}, u32[]{:S(2)}) collective-permute-start(f32[1,512,128]{2,1,0:T(8,128)S(1)} %get-tuple-element.90), channel_id=1, source_target_pairs={{0,14},{2,4},{4,2},{6,8},{8,6},{10,12},{12,10},{14,0},{16,30},{18,... | collective-permute-start | bytes 786440 | tf_op jit(solution)/shard_map/ppermute | solution.py:440
  80.6 7.1 %collective-permute-start.15 = (f32[1,512,128]{2,1,0:T(8,128)S(1)}, f32[1,512,128]{2,1,0:T(8,128)S(1)}, u32[]{:S(2)}, u32[]{:S(2)}) collective-permute-start(f32[1,512,128]{2,1,0:T(8,128)S(1)} %get-tuple-element.89.refs_5_), channel_id=1, source_target_pairs={{0,2},{2,0},{4,6},{6,4},{8,10},{10,8},{12,14},{14,12},{16,18},{18,... | collective-permute-start | bytes 786440 | tf_op jit(solution)/shard_map/ppermute | solution.py:440
  83.6 11.5 %collective-permute-start.21 = (f32[1,256,256]{2,1,0:T(8,128)S(1)}, f32[1,256,256]{2,1,0:T(8,128)S(1)}, u32[]{:S(2)}, u32[]{:S(2)}) collective-permute-start(f32[1,256,256]{2,1,0:T(8,128)S(1)} %get-tuple-element.96.refs_2_), channel_id=1, source_target_pairs={{0,1},{1,0},{2,3},{3,2},{4,5},{5,4},{6,7},{7,6},{8,9},{9,8},{10,11... | collective-permute-start | bytes 786440 | tf_op jit(solution)/shard_map/ppermute | solution.py:444
  86.2 15.4 %collective-permute-start.22 = (f32[1,256,256]{2,1,0:T(8,128)S(1)}, f32[1,256,256]{2,1,0:T(8,128)S(1)}, u32[]{:S(2)}, u32[]{:S(2)}) collective-permute-start(f32[1,256,256]{2,1,0:T(8,128)S(1)} %get-tuple-element.97.refs_4_), channel_id=1, source_target_pairs={{0,1},{1,0},{2,3},{3,2},{4,5},{5,4},{6,7},{7,6},{8,9},{9,8},{10,11... | collective-permute-start | bytes 786440 | tf_op jit(solution)/shard_map/ppermute | solution.py:444
  88.3 4.6 %collective-permute-start.17 = (f32[1,128,256]{2,1,0:T(8,128)S(1)}, f32[1,128,256]{2,1,0:T(8,128)S(1)}, u32[]{:S(2)}, u32[]{:S(2)}) collective-permute-start(f32[1,128,256]{2,1,0:T(8,128)S(1)} %get-tuple-element.92), channel_id=1, source_target_pairs={{0,16},{2,18},{4,20},{6,22},{8,24},{10,26},{12,28},{14,30},{16,0},... | collective-permute-start | bytes 393224 | tf_op jit(solution)/shard_map/ppermute | solution.py:440
  88.4 6.7 %collective-permute-start.18 = (f32[1,128,256]{2,1,0:T(8,128)S(1)}, f32[1,128,256]{2,1,0:T(8,128)S(1)}, u32[]{:S(2)}, u32[]{:S(2)}) collective-permute-start(f32[1,128,256]{2,1,0:T(8,128)S(1)} %get-tuple-element.93), channel_id=1, source_target_pairs={{0,240},{2,242},{4,244},{6,246},{8,248},{10,250},{12,252},{14,254}... | collective-permute-start | bytes 393224 | tf_op jit(solution)/shard_map/ppermute | solution.py:440
  102.2 8.6 %collective-permute-start.23 = (f32[1,256,256]{2,1,0:T(8,128)S(1)}, f32[1,256,256]{2,1,0:T(8,128)S(1)}, u32[]{:S(2)}, u32[]{:S(2)}) collective-permute-start(f32[1,256,256]{2,1,0:T(8,128)S(1)} %rows_first.1.refs_1_), channel_id=1, source_target_pairs={{0,1},{1,0},{2,3},{3,2},{4,5},{5,4},{6,7},{7,6},{8,9},{9,8},{10,11... | collective-permute-start | bytes 786440 | tf_op jit(solution)/shard_map/ppermute | solution.py:444

commit v10 on v8

--- a/solution.py
+++ b/solution.py
@@ -394,11 +394,12 @@
     corners_b[1] = rows_b[:, :, b]
 
 
-def prepare_kernel(prop_in, probe_in, diag, corner, right, back_diag, back_corner, back_right,
-                   probe_out, prop, sems):
+def prepare_kernel(prop_in, probe_in, tabs_in, diag, corner, right, back_diag, back_corner,
+                   back_right, probe_out, tabs_out, prop, sems):
     copies = [
         pltpu.make_async_copy(prop_in, prop, sems.at[0]),
         pltpu.make_async_copy(probe_in, probe_out, sems.at[1]),
+        pltpu.make_async_copy(tabs_in, tabs_out, sems.at[2]),
     ]
     for copy in copies:
         copy.start()
@@ -413,12 +414,12 @@
     right[...] = right_form(re_t, im_t, jnp).astype(BF16)
     back_right[...] = right_form(re, -im, jnp).astype(BF16)
     copies[1].wait()
-
-
-def reorder_kernel(measured, tabs, out, tabs_out):
+    copies[2].wait()
+
+
+def reorder_kernel(measured, out):
     n = out.shape[-1]
     h = n // 2
-    tabs_out[...] = tabs[...]
     exact = functools.partial(
         jnp.dot, precision=lax.Precision.HIGHEST, preferred_element_type=F32
     )
@@ -497,25 +498,6 @@
 
     picked = call(pick_rows_kernel, "pick_rows", (strip,) * 4, (info, own), copies=4)
     rows = [[swap(picked[2 * i + k], 0, k == 1) for k in range(2)] for i in range(2)]
-    *made, probe = call(
-        prepare_kernel,
-        "prepare",
-        band + band + (probes,),
-        (propagator, probe_modes),
-        scratch=(((2, n, n), BF16),),
-        smem=0,
-        copies=2,
-    )
-    prop, back_prop = made[:3], made[3:]
-    tabs = jnp.asarray(dft_tables(n))
-    measured, tabs = call(
-        reorder_kernel,
-        "reorder",
-        (((slots, n, n), F32), (tabs.shape, BF16)),
-        (measured[0], tabs),
-        smem=0,
-    )
-
     (picked,) = call(pick_cols_kernel, "pick_cols", (side_strip,), (info, own), after=())
     cols_b = swap(picked, 1, True)
 
@@ -523,15 +505,27 @@
         picked = call(functools.partial(pick_rest_kernel, layer), f"pick_rest_{layer}",
                       (tall, quarter), (info, own, *rows[layer]), after=after)
         rest = [swap(picked[k], 1, k == 1) for k in range(2)]
-        return (own, *rows[layer], cols_b, *rest)
-
-    first = beside_tiles(0, (probe,))
-    last = beside_tiles(1, (measured, first[3],first[5]))
+        return (own, *rows[layer], cols_b, *rest, picked[0])
+
+    first = beside_tiles(0, ())
+    tabs = jnp.asarray(dft_tables(n))
+    *made, probe, tabs = call(
+        prepare_kernel,
+        "prepare",
+        band + band + (probes, (tabs.shape, BF16)),
+        (propagator, probe_modes, tabs),
+        scratch=(((2, n, n), BF16),),
+        smem=0,
+        copies=3,
+        after=(first[6],),
+    )
+    prop, back_prop = made[:3], made[3:]
+    last = beside_tiles(1, (probe, first[3], first[5]))
     canvas, patch_first0, wave0 = call(
         waves_first_kernel,
         "waves_0",
         (((2, 2 * n, 2 * n), F32), pair, field),
-        (off, info, *first, probe, *prop),
+        (off, info, *first[:6], probe, *prop),
         scratch=(held,),
         smem=2,
         after=(),
@@ -544,7 +538,7 @@
         fars_first_kernel,
         "fars_0",
         (((2, 2 * n, 2 * n), F32), pair, field, plane),
-        (off, info, *last, wave0, tabs),
+        (off, info, *last[:6], wave0, tabs),
         scratch=(held,),
         smem=2,
         after=(patch_first1,),
@@ -554,6 +548,14 @@
         fars_next_kernel, "fars_1", (pair, field, plane), (off, canvas, wave1, tabs), scratch=(held,)
     )
     other1 = swap_mode(inten1)
+    (measured,) = call(
+        reorder_kernel,
+        "reorder",
+        (((slots, n, n), F32),),
+        (measured[0],),
+        smem=0,
+        after=(),
+    )
 
     bar_out = ((modes, 2, n, n), BF16)
     strips = (((2, 2 * n, h), F32), ((2, 2 * n, n), F32), ((2, 2 * n, h), F32))

time: 108 us -> 108 us (level)
  starting transfers between devices: 44.5 us -> 51.1 us
  waiting for transfers between devices: 21.3 us -> 17.7 us
  local copies, waits for them, and re-layouts: 4.19 us -> 1.36 us
    ppermute x17, starting transfers between devices: 28.3 us -> 38.8 us  [swap(): return lax.ppermute(value, 'tile', pairs)]
    ppermute x7, waiting for transfers between devices: 14.6 us -> 8.87 us  [swap_mode(): return lax.ppermute(value, 'mode', [(0, 1), (1, 0)])]
    ppermute x7, starting transfers between devices: 16.1 us -> 12.2 us  [swap_mode(): return lax.ppermute(value, 'mode', [(0, 1), (1, 0)])]
    unnamed x14, local copies, waits for them, and re-layouts: 4.09 us -> 1.26 us
    ppermute x17, waiting for transfers between devices: 6.64 us -> 8.83 us  [swap(): return lax.ppermute(value, 'tile', pairs)]
  transfers between devices with their start and end apart: 24 -> 24, of which waited for: 9 -> 10; matrix products, arithmetic and copies ran while one was open for 0% -> 0% of each run, Pallas kernels for 26% -> 26%
where the time goes in v10:
time: 108 us
  starting transfers between devices  51.1 us (47%)
  Pallas kernels  36 us (33%)
  waiting for transfers between devices  17.7 us (16%)
  between operations  1.81 us (2%)
  local copies, waits for them, and re-layouts  1.36 us (1%)
    ppermute x17, starting transfers between devices, swap(): return lax.ppermute(value, 'tile', pairs)  38.8 us
    pallas_call x23, Pallas kernels, call(): pl.pallas_call(run, out_shape=tuple((jax.ShapeDtypeStruct(shape, dtype) f...  36 us
    ppermute x7, starting transfers between devices, swap_mode(): return lax.ppermute(value, 'mode', [(0, 1), (1, 0)])  12.2 us
    ppermute x7, waiting for transfers between devices, swap_mode(): return lax.ppermute(value, 'mode', [(0, 1), (1, 0)])  8.87 us
    ppermute x17, waiting for transfers between devices, swap(): return lax.ppermute(value, 'tile', pairs)  8.83 us
  transfers between devices with their start and end apart: 24, of which 10 were waited for; matrix products, arithmetic and copies ran while one was open for 0% of the time, Pallas kernels for 26%

profile of v10, /device:TPU:1, one launch (start us, length us, event | category | flops | bytes accessed | tf_op | source)
XLA Modules:
  0.0 107.9 jit_solution(5662994702039611195)
XLA Ops:
  2.7 2.6 %collective-permute-start.3 = (f32[2,128,256]{2,1,0:T(8,128)S(1)}, f32[2,128,256]{2,1,0:T(8,128)S(1)}, u32[]{:S(2)}, u32[]{:S(2)}) collective-permute-start(f32[2,128,256]{2,1,0:T(8,128)S(1)} %get-tuple-element.54), channel_id=1, source_target_pairs={{0,16},{2,18},{4,20},{6,22},{8,24},{10,26},{12,28},{14,30},{16,0},... | collective-permute-start | bytes 786440 | tf_op jit(solution)/shard_map/ppermute | solution.py:444
  5.3 5.7 %collective-permute-start.4 = (f32[2,128,256]{2,1,0:T(8,128)S(1)}, f32[2,128,256]{2,1,0:T(8,128)S(1)}, u32[]{:S(2)}, u32[]{:S(2)}) collective-permute-start(f32[2,128,256]{2,1,0:T(8,128)S(1)} %get-tuple-element.55), channel_id=1, source_target_pairs={{0,240},{2,242},{4,244},{6,246},{8,248},{10,250},{12,252},{14,254}... | collective-permute-start | bytes 786440 | tf_op jit(solution)/shard_map/ppermute | solution.py:444
  11.5 2.4 %collective-permute-start.2 = (f32[2,2,256,128]{3,2,1,0:T(8,128)S(1)}, f32[2,2,256,128]{3,2,1,0:T(8,128)S(1)}, u32[]{:S(2)}, u32[]{:S(2)}) collective-permute-start(f32[2,2,256,128]{3,2,1,0:T(8,128)S(1)} %pick_cols.1), channel_id=1, source_target_pairs={{0,14},{2,4},{4,2},{6,8},{8,6},{10,12},{12,10},{14,0},{16,30},{18,... | collective-permute-start | bytes 1572872 | tf_op jit(solution)/shard_map/ppermute | solution.py:444
  14.0 1.5 %collective-permute-start.1 = (f32[2,128,256]{2,1,0:T(8,128)S(1)}, f32[2,128,256]{2,1,0:T(8,128)S(1)}, u32[]{:S(2)}, u32[]{:S(2)}) collective-permute-start(f32[2,128,256]{2,1,0:T(8,128)S(1)} %get-tuple-element.53), channel_id=1, source_target_pairs={{0,240},{2,242},{4,244},{6,246},{8,248},{10,250},{12,252},{14,254}... | collective-permute-start | bytes 786440 | tf_op jit(solution)/shard_map/ppermute | solution.py:444
  17.3 3.1 %collective-permute-start.5 = (f32[2,2,128,128]{3,2,1,0:T(8,128)S(1)}, f32[2,2,128,128]{3,2,1,0:T(8,128)S(1)}, u32[]{:S(2)}, u32[]{:S(2)}) collective-permute-start(f32[2,2,128,128]{3,2,1,0:T(8,128)S(1)} %get-tuple-element.58), channel_id=1, source_target_pairs={{0,14},{2,4},{4,2},{6,8},{8,6},{10,12},{12,10},{14,0},{16,30},{18,... | collective-permute-start | bytes 786440 | tf_op jit(solution)/shard_map/ppermute | solution.py:444
  21.3 2.1 %collective-permute-done.1.refs_3_.refs_4_ = f32[2,128,256]{2,1,0:T(8,128)S(1)} collective-permute-done((f32[2,128,256]{2,1,0:T(8,128)S(1)}, f32[2,128,256]{2,1,0:T(8,128)S(1)}, u32[]{:S(2)}, u32[]{:S(2)}) %collective-permute-start.1) | collective-permute-done | bytes 262176 | tf_op jit(solution)/shard_map/ppermute | solution.py:444
  23.4 1.3 %collective-permute-done.5.refs_6_.refs_7_ = f32[2,2,128,128]{3,2,1,0:T(8,128)S(1)} collective-permute-done((f32[2,2,128,128]{3,2,1,0:T(8,128)S(1)}, f32[2,2,128,128]{3,2,1,0:T(8,128)S(1)}, u32[]{:S(2)}, u32[]{:S(2)}) %collective-permute-start.5) | collective-permute-done | bytes 262176 | tf_op jit(solution)/shard_map/ppermute | solution.py:444
  25.3 1.6 %collective-permute-start.6 = (f32[2,512,128]{2,1,0:T(8,128)S(1)}, f32[2,512,128]{2,1,0:T(8,128)S(1)}, u32[]{:S(2)}, u32[]{:S(2)}) collective-permute-start(f32[2,512,128]{2,1,0:T(8,128)S(1)} %get-tuple-element.59), channel_id=1, source_target_pairs={{0,2},{2,0},{4,6},{6,4},{8,10},{10,8},{12,14},{14,12},{16,18},{18,... | collective-permute-start | bytes 1572872 | tf_op jit(solution)/shard_map/ppermute | solution.py:444
  27.1 3.2 %waves_0.1 = (f32[2,512,512]{2,1,0:T(8,128)S(1)}, f32[2,256,256]{2,1,0:T(8,128)S(1)}, f32[6,2,256,256]{3,2,1,0:T(8,128)S(1)}) custom-call(s32[2,2]{1,0:T(2,128)S(1)} %bitcast.15, s32[5]{0:T(128)S(1)} %convert_element_type.3.refs_0_.refs_1_.refs_2_, f32[2,2,256,256]{3,2,1,0:T(8,128)S(1)} %bitcast.12, ...), custom_call_target="tpu_custom_call" | custom-call | tf_op jit(solution)/shard_map/waves_0/pallas_call | solution.py:462
  30.3 2.9 %waves_1.1 = (f32[2,256,256]{2,1,0:T(8,128)S(1)}, f32[6,2,256,256]{3,2,1,0:T(8,128)S(1)}) custom-call(s32[2,2]{1,0:T(2,128)S(1)} %bitcast.16, f32[2,512,512]{2,1,0:T(8,128)S(1)} %get-tuple-element.66.refs_1_, f32[2,6,256,256]{3,2,1,0:T(8,128)S(1)} %get-tuple-element.57.refs_4_.refs_8_.refs_2_, bf16[2,256,256]{2,1,0:T(8,128)(2,1)S(1)} %get-tuple-element.61.refs_9_.refs_3_, ...), custom_call_target="tpu_custom_call" | custom-call | tf_op jit(solution)/shard_map/waves_1/pallas_call | solution.py:462
  33.2 2.8 %fars_0.1 = (f32[2,512,512]{2,1,0:T(8,128)S(1)}, f32[2,256,256]{2,1,0:T(8,128)S(1)}, f32[6,2,256,256]{3,2,1,0:T(8,128)S(1)}, f32[256,256]{1,0:T(8,128)S(1)}) custom-call(s32[2,2]{1,0:T(2,128)S(1)} %bitcast.17, s32[5]{0:T(128)S(1)} %convert_element_type.3.refs_0_.refs_1_.refs_2_, f32[2,2,256,256]{3,2,1,0:T(8,128)S(1)} %bitcast.13, ...), custom_call_target="tpu_custom_call" | custom-call | tf_op jit(solution)/shard_map/fars_0/pallas_call | solution.py:462
  36.0 2.7 %collective-permute-start.9 = (f32[256,256]{1,0:T(8,128)S(1)}, f32[256,256]{1,0:T(8,128)S(1)}, u32[]{:S(2)}, u32[]{:S(2)}) collective-permute-start(f32[256,256]{1,0:T(8,128)S(1)} %get-tuple-element.68.refs_1_), channel_id=1, source_target_pairs={{0,1},{1,0},{2,3},{3,2},{4,5},{5,4},{6,7},{7,6},{8,9},{9,8},{10,11... | collective-permute-start | bytes 786440 | tf_op jit(solution)/shard_map/ppermute | solution.py:448
  38.7 2.5 %fars_1.1 = (f32[2,256,256]{2,1,0:T(8,128)S(1)}, f32[6,2,256,256]{3,2,1,0:T(8,128)S(1)}, f32[256,256]{1,0:T(8,128)S(1)}) custom-call(s32[2,2]{1,0:T(2,128)S(1)} %bitcast.18, f32[2,512,512]{2,1,0:T(8,128)S(1)} %get-tuple-element.79.refs_1_, f32[6,2,256,256]{3,2,1,0:T(8,128)S(1)} %get-tuple-element.80.refs_2_.refs_8_, ...), custom_call_target="tpu_custom_call" | custom-call | tf_op jit(solution)/shard_map/fars_1/pallas_call | solution.py:462
  42.5 1.5 %reorder.1.refs_3_.refs_6_ = f32[2,256,256]{2,1,0:T(8,128)S(1)} custom-call(f32[2,256,256]{2,1,0:T(8,128)S(1)} %bitcast.14), custom_call_target="tpu_custom_call" | custom-call | tf_op jit(solution)/shard_map/reorder/pallas_call | solution.py:462
  44.0 1.9 %back_last_0.1 = (f32[2,256,256]{2,1,0:T(8,128)S(1)}, bf16[6,2,256,256]{3,2,1,0:T(8,128)(2,1)S(1)}) custom-call(s32[1]{0:T(128)S(6)} %copy.11.refs_0_, f32[256,256]{1,0:T(8,128)S(1)} %get-tuple-element.68.refs_1_, f32[256,256]{1,0:T(8,128)S(1)} %collective-permute-done.9.refs_2_, f32[2,256,256]{2,1,0:T(8,128)S(1)} %reorder.1.refs_3_.refs_6_, ...), custom_call_target="tpu_custom_call" | custom-call | tf_op jit(solution)/shard_map/back_last_0/pallas_call | solution.py:462
  45.9 2.7 %back_first_0.1 = (f32[1,256,256]{2,1,0:T(8,128)S(1)}, f32[1,256,256]{2,1,0:T(8,128)S(1)}, f32[2,6,256,256]{3,2,1,0:T(8,128)S(1)}) custom-call(s32[5]{0:T(128)S(1)} %convert_element_type.3.refs_0_.refs_1_.refs_2_, bf16[6,2,256,256]{3,2,1,0:T(8,128)(2,1)S(1)} %get-tuple-element.71.refs_1_, f32[2,6,256,256]{3,2,1,0:T(8,128)S(1)} %get-tuple-element.57.refs_4_.refs_8_.refs_2_, ...), custom_call_target="tpu_custom_call" | custom-call | tf_op jit(solution)/shard_map/back_first_0/pallas_call | solution.py:462
  49.1 3.4 %back_last_1.1 = (bf16[6,2,256,256]{3,2,1,0:T(8,128)(2,1)S(1)}, f32[2,512,128]{2,1,0:T(8,128)S(1)}, f32[2,512,256]{2,1,0:T(8,128)S(1)}, f32[2,512,128]{2,1,0:T(8,128)S(1)}) custom-call(s32[1]{0:T(128)S(6)} %copy.11.refs_0_, s32[2,2]{1,0:T(2,128)S(1)} %bitcast.19, s32[5]{0:T(128)S(1)} %convert_element_type.3.refs_0_.refs_1_.refs_2_, ...), custom_call_target="tpu_custom_call" | custom-call | tf_op jit(solution)/shard_map/back_last_1/pallas_call | solution.py:462
  52.5 3.3 %collective-permute-start.13 = (f32[2,512,128]{2,1,0:T(8,128)S(1)}, f32[2,512,128]{2,1,0:T(8,128)S(1)}, u32[]{:S(2)}, u32[]{:S(2)}) collective-permute-start(f32[2,512,128]{2,1,0:T(8,128)S(1)} %get-tuple-element.88), channel_id=1, source_target_pairs={{0,2},{2,0},{4,6},{6,4},{8,10},{10,8},{12,14},{14,12},{16,18},{18,... | collective-permute-start | bytes 1572872 | tf_op jit(solution)/shard_map/ppermute | solution.py:444
  57.0 2.6 %collective-permute-start.10 = (f32[1,256,256]{2,1,0:T(8,128)S(1)}, f32[1,256,256]{2,1,0:T(8,128)S(1)}, u32[]{:S(2)}, u32[]{:S(2)}) collective-permute-start(f32[1,256,256]{2,1,0:T(8,128)S(1)} %get-tuple-element.77), channel_id=1, source_target_pairs={{0,1},{1,0},{2,3},{3,2},{4,5},{5,4},{6,7},{7,6},{8,9},{9,8},{10,11... | collective-permute-start | bytes 786440 | tf_op jit(solution)/shard_map/ppermute | solution.py:448
  59.6 2.7 %back_first_1.1 = (f32[1,256,256]{2,1,0:T(8,128)S(1)}, f32[1,256,256]{2,1,0:T(8,128)S(1)}, f32[2,6,256,256]{3,2,1,0:T(8,128)S(1)}) custom-call(s32[5]{0:T(128)S(1)} %convert_element_type.3.refs_0_.refs_1_.refs_2_, bf16[6,2,256,256]{3,2,1,0:T(8,128)(2,1)S(1)} %get-tuple-element.84.refs_1_, f32[2,6,256,256]{3,2,1,0:T(8,128)S(1)} %get-tuple-element.57.refs_4_.refs_8_.refs_2_, ...), custom_call_target="tpu_custom_call" | custom-call | tf_op jit(solution)/shard_map/back_first_1/pallas_call | solution.py:462
  62.8 2.0 %collective-permute-done.14.refs_3_ = f32[2,512,128]{2,1,0:T(8,128)S(1)} collective-permute-done((f32[2,512,128]{2,1,0:T(8,128)S(1)}, f32[2,512,128]{2,1,0:T(8,128)S(1)}, u32[]{:S(2)}, u32[]{:S(2)}) %collective-permute-start.14) | collective-permute-done | bytes 524320 | tf_op jit(solution)/shard_map/ppermute | solution.py:444
  65.4 4.3 %collective-permute-start.20 = (f32[2,128,256]{2,1,0:T(8,128)S(1)}, f32[2,128,256]{2,1,0:T(8,128)S(1)}, u32[]{:S(2)}, u32[]{:S(2)}) collective-permute-start(f32[2,128,256]{2,1,0:T(8,128)S(1)} %get-tuple-element.97), channel_id=1, source_target_pairs={{0,240},{2,242},{4,244},{6,246},{8,248},{10,250},{12,252},{14,254}... | collective-permute-start | bytes 786440 | tf_op jit(solution)/shard_map/ppermute | solution.py:444
  71.2 7.5 %collective-permute-start.16 = (f32[1,512,128]{2,1,0:T(8,128)S(1)}, f32[1,512,128]{2,1,0:T(8,128)S(1)}, u32[]{:S(2)}, u32[]{:S(2)}) collective-permute-start(f32[1,512,128]{2,1,0:T(8,128)S(1)} %get-tuple-element.92), channel_id=1, source_target_pairs={{0,14},{2,4},{4,2},{6,8},{8,6},{10,12},{12,10},{14,0},{16,30},{18,... | collective-permute-start | bytes 786440 | tf_op jit(solution)/shard_map/ppermute | solution.py:444
  78.8 1.5 %collective-permute-start.15 = (f32[1,512,128]{2,1,0:T(8,128)S(1)}, f32[1,512,128]{2,1,0:T(8,128)S(1)}, u32[]{:S(2)}, u32[]{:S(2)}) collective-permute-start(f32[1,512,128]{2,1,0:T(8,128)S(1)} %get-tuple-element.91.refs_5_), channel_id=1, source_target_pairs={{0,2},{2,0},{4,6},{6,4},{8,10},{10,8},{12,14},{14,12},{16,18},{18,... | collective-permute-start | bytes 786440 | tf_op jit(solution)/shard_map/ppermute | solution.py:444
  80.9 3.5 %collective-permute-start.21 = (f32[1,256,256]{2,1,0:T(8,128)S(1)}, f32[1,256,256]{2,1,0:T(8,128)S(1)}, u32[]{:S(2)}, u32[]{:S(2)}) collective-permute-start(f32[1,256,256]{2,1,0:T(8,128)S(1)} %get-tuple-element.98.refs_2_), channel_id=1, source_target_pairs={{0,1},{1,0},{2,3},{3,2},{4,5},{5,4},{6,7},{7,6},{8,9},{9,8},{10,11... | collective-permute-start | bytes 786440 | tf_op jit(solution)/shard_map/ppermute | solution.py:448
  86.2 4.0 %collective-permute-start.18 = (f32[1,128,256]{2,1,0:T(8,128)S(1)}, f32[1,128,256]{2,1,0:T(8,128)S(1)}, u32[]{:S(2)}, u32[]{:S(2)}) collective-permute-start(f32[1,128,256]{2,1,0:T(8,128)S(1)} %get-tuple-element.95), channel_id=1, source_target_pairs={{0,240},{2,242},{4,244},{6,246},{8,248},{10,250},{12,252},{14,254}... | collective-permute-start | bytes 393224 | tf_op jit(solution)/shard_map/ppermute | solution.py:444
  90.1 1.8 %collective-permute-start.23 = (f32[1,256,256]{2,1,0:T(8,128)S(1)}, f32[1,256,256]{2,1,0:T(8,128)S(1)}, u32[]{:S(2)}, u32[]{:S(2)}) collective-permute-start(f32[1,256,256]{2,1,0:T(8,128)S(1)} %get-tuple-element.99.refs_4_), channel_id=1, source_target_pairs={{0,1},{1,0},{2,3},{3,2},{4,5},{5,4},{6,7},{7,6},{8,9},{9,8},{10,11... | collective-permute-start | bytes 786440 | tf_op jit(solution)/shard_map/ppermute | solution.py:448
  91.9 1.9 %collective-permute-done.18.refs_3_ = f32[1,128,256]{2,1,0:T(8,128)S(1)} collective-permute-done((f32[1,128,256]{2,1,0:T(8,128)S(1)}, f32[1,128,256]{2,1,0:T(8,128)S(1)}, u32[]{:S(2)}, u32[]{:S(2)}) %collective-permute-start.18) | collective-permute-done | bytes 131104 | tf_op jit(solution)/shard_map/ppermute | solution.py:444
  95.0 2.0 %probe_sum.1 = f32[1,2,6,256,256]{4,3,2,1,0:T(8,128)} custom-call(f32[2,6,256,256]{3,2,1,0:T(8,128)S(1)} %get-tuple-element.100.refs_0_, f32[2,6,256,256]{3,2,1,0:T(8,128)S(1)} %get-tuple-element.101.refs_1_), custom_call_target="tpu_custom_call" | custom-call | tf_op jit(solution)/shard_map/probe_sum/pallas_call | solution.py:462
  96.9 3.9 %collective-permute-done.23.refs_5_ = f32[1,256,256]{2,1,0:T(8,128)S(1)} collective-permute-done((f32[1,256,256]{2,1,0:T(8,128)S(1)}, f32[1,256,256]{2,1,0:T(8,128)S(1)}, u32[]{:S(2)}, u32[]{:S(2)}) %collective-permute-start.23) | collective-permute-done | bytes 262176 | tf_op jit(solution)/shard_map/ppermute | solution.py:448
  100.8 1.5 %finish_last.1.refs_2_ = f32[1,2,2,256,256]{4,3,2,1,0:T(8,128)} custom-call(s32[5]{0:T(128)S(1)} %convert_element_type.3.refs_0_.refs_1_.refs_2_, f32[1,256,256]{2,1,0:T(8,128)S(1)} %rows_first.1.refs_1_, f32[1,256,256]{2,1,0:T(8,128)S(1)} %get-tuple-element.98.refs_2_, f32[1,256,256]{2,1,0:T(8,128)S(1)} %collective-permute-done.21.refs_4_.refs_3_, ...), custom_call_target="tpu_custom_call" | custom-call | tf_op jit(solution)/shard_map/finish_last/pallas_call | solution.py:462
  102.3 4.1 %collective-permute-done.22.refs_1_ = f32[1,256,256]{2,1,0:T(8,128)S(1)} collective-permute-done((f32[1,256,256]{2,1,0:T(8,128)S(1)}, f32[1,256,256]{2,1,0:T(8,128)S(1)}, u32[]{:S(2)}, u32[]{:S(2)}) %collective-permute-start.22) | collective-permute-done | bytes 262176 | tf_op jit(solution)/shard_map/ppermute | solution.py:448
  (55 shorter events, 15.7 us)
Async XLA Ops:
  0.8 1.2 %copy-start = (f32[1,2,2,256,256]{4,3,2,1,0:T(8,128)S(1)}, f32[1,2,2,256,256]{4,3,2,1,0:T(8,128)}, u32[]{:S(2)}) copy-start(f32[1,2,2,256,256]{4,3,2,1,0:T(8,128)} %param.7) | copy-start | bytes 3145732
  2.0 18.3 %copy-start.2 = (f32[2,6,256,256]{3,2,1,0:T(8,128)S(1)}, f32[2,6,256,256]{3,2,1,0:T(8,128)}, u32[]{:S(2)}) copy-start(f32[2,6,256,256]{3,2,1,0:T(8,128)} %refs_1_.1) | copy-start | bytes 9437188
  2.0 18.3 %copy-start.3 = (bf16[4,256,256]{2,1,0:T(8,128)(2,1)S(1)}, bf16[4,256,256]{2,1,0:T(8,128)(2,1)}, u32[]{:S(2)}) copy-start(bf16[4,256,256]{2,1,0:T(8,128)(2,1)} %constant.54.clone.refs_2_) | copy-start | bytes 1572868
  2.0 18.3 %copy-start.5 = (bf16[2,256,256]{2,1,0:T(8,128)(2,1)S(1)}, bf16[2,256,256]{2,1,0:T(8,128)(2,1)}, u32[]{:S(2)}) copy-start(bf16[2,256,256]{2,1,0:T(8,128)(2,1)} %refs_0_.3) | copy-start | bytes 786436
  2.7 12.7 %collective-permute-start.3 = (f32[2,128,256]{2,1,0:T(8,128)S(1)}, f32[2,128,256]{2,1,0:T(8,128)S(1)}, u32[]{:S(2)}, u32[]{:S(2)}) collective-permute-start(f32[2,128,256]{2,1,0:T(8,128)S(1)} %get-tuple-element.54), channel_id=1, source_target_pairs={{0,16},{2,18},{4,20},{6,22},{8,24},{10,26},{12,28},{14,30},{16,0},... | collective-permute-start | bytes 786440 | tf_op jit(solution)/shard_map/ppermute | solution.py:444
  5.3 11.4 %collective-permute-start.4 = (f32[2,128,256]{2,1,0:T(8,128)S(1)}, f32[2,128,256]{2,1,0:T(8,128)S(1)}, u32[]{:S(2)}, u32[]{:S(2)}) collective-permute-start(f32[2,128,256]{2,1,0:T(8,128)S(1)} %get-tuple-element.55), channel_id=1, source_target_pairs={{0,240},{2,242},{4,244},{6,246},{8,248},{10,250},{12,252},{14,254}... | collective-permute-start | bytes 786440 | tf_op jit(solution)/shard_map/ppermute | solution.py:444
  11.5 13.2 %copy-start.1 = (f32[1,2,2,256,256]{4,3,2,1,0:T(8,128)S(1)}, f32[1,2,2,256,256]{4,3,2,1,0:T(8,128)}, u32[]{:S(2)}) copy-start(f32[1,2,2,256,256]{4,3,2,1,0:T(8,128)} %param.7) | copy-start | bytes 3145732
  11.5 11.9 %collective-permute-start.2 = (f32[2,2,256,128]{3,2,1,0:T(8,128)S(1)}, f32[2,2,256,128]{3,2,1,0:T(8,128)S(1)}, u32[]{:S(2)}, u32[]{:S(2)}) collective-permute-start(f32[2,2,256,128]{3,2,1,0:T(8,128)S(1)} %pick_cols.1), channel_id=1, source_target_pairs={{0,14},{2,4},{4,2},{6,8},{8,6},{10,12},{12,10},{14,0},{16,30},{18,... | collective-permute-start | bytes 1572872 | tf_op jit(solution)/shard_map/ppermute | solution.py:444
  14.0 7.3 %collective-permute-start = (f32[2,128,256]{2,1,0:T(8,128)S(1)}, f32[2,128,256]{2,1,0:T(8,128)S(1)}, u32[]{:S(2)}, u32[]{:S(2)}) collective-permute-start(f32[2,128,256]{2,1,0:T(8,128)S(1)} %get-tuple-element.52), channel_id=1, source_target_pairs={{0,16},{2,18},{4,20},{6,22},{8,24},{10,26},{12,28},{14,30},{16,0},... | collective-permute-start | bytes 786440 | tf_op jit(solution)/shard_map/ppermute | solution.py:444
  14.0 9.4 %collective-permute-start.1 = (f32[2,128,256]{2,1,0:T(8,128)S(1)}, f32[2,128,256]{2,1,0:T(8,128)S(1)}, u32[]{:S(2)}, u32[]{:S(2)}) collective-permute-start(f32[2,128,256]{2,1,0:T(8,128)S(1)} %get-tuple-element.53), channel_id=1, source_target_pairs={{0,240},{2,242},{4,244},{6,246},{8,248},{10,250},{12,252},{14,254}... | collective-permute-start | bytes 786440 | tf_op jit(solution)/shard_map/ppermute | solution.py:444
  17.3 7.4 %collective-permute-start.5 = (f32[2,2,128,128]{3,2,1,0:T(8,128)S(1)}, f32[2,2,128,128]{3,2,1,0:T(8,128)S(1)}, u32[]{:S(2)}, u32[]{:S(2)}) collective-permute-start(f32[2,2,128,128]{3,2,1,0:T(8,128)S(1)} %get-tuple-element.58), channel_id=1, source_target_pairs={{0,14},{2,4},{4,2},{6,8},{8,6},{10,12},{12,10},{14,0},{16,30},{18,... | collective-permute-start | bytes 786440 | tf_op jit(solution)/shard_map/ppermute | solution.py:444
  20.3 6.8 %collective-permute-start.8 = (f32[2,512,128]{2,1,0:T(8,128)S(1)}, f32[2,512,128]{2,1,0:T(8,128)S(1)}, u32[]{:S(2)}, u32[]{:S(2)}) collective-permute-start(f32[2,512,128]{2,1,0:T(8,128)S(1)} %get-tuple-element.56.refs_3_), channel_id=1, source_target_pairs={{0,2},{2,0},{4,6},{6,4},{8,10},{10,8},{12,14},{14,12},{16,18},{18,... | collective-permute-start | bytes 1572872 | tf_op jit(solution)/shard_map/ppermute | solution.py:444
  21.0 6.2 %copy-start.6 = (s32[1,2,2]{2,1,0:T(2,128)S(1)}, s32[1,2,2]{2,1,0:T(2,128)}, u32[]{:S(2)}) copy-start(s32[1,2,2]{2,1,0:T(2,128)} %param.10) | copy-start | bytes 52
  25.3 7.9 %collective-permute-start.6 = (f32[2,512,128]{2,1,0:T(8,128)S(1)}, f32[2,512,128]{2,1,0:T(8,128)S(1)}, u32[]{:S(2)}, u32[]{:S(2)}) collective-permute-start(f32[2,512,128]{2,1,0:T(8,128)S(1)} %get-tuple-element.59), channel_id=1, source_target_pairs={{0,2},{2,0},{4,6},{6,4},{8,10},{10,8},{12,14},{14,12},{16,18},{18,... | collective-permute-start | bytes 1572872 | tf_op jit(solution)/shard_map/ppermute | solution.py:444
  26.9 6.3 %collective-permute-start.7 = (f32[2,2,128,128]{3,2,1,0:T(8,128)S(1)}, f32[2,2,128,128]{3,2,1,0:T(8,128)S(1)}, u32[]{:S(2)}, u32[]{:S(2)}) collective-permute-start(f32[2,2,128,128]{3,2,1,0:T(8,128)S(1)} %get-tuple-element.60), channel_id=1, source_target_pairs={{0,14},{2,4},{4,2},{6,8},{8,6},{10,12},{12,10},{14,0},{16,30},{18,... | collective-permute-start | bytes 786440 | tf_op jit(solution)/shard_map/ppermute | solution.py:444
  36.0 6.5 %copy-start.4 = (f32[1,2,256,256]{3,2,1,0:T(8,128)S(1)}, f32[1,2,256,256]{3,2,1,0:T(8,128)}, u32[]{:S(2)}) copy-start(f32[1,2,256,256]{3,2,1,0:T(8,128)} %param.12) | copy-start | bytes 1572868
  36.0 8.0 %collective-permute-start.9 = (f32[256,256]{1,0:T(8,128)S(1)}, f32[256,256]{1,0:T(8,128)S(1)}, u32[]{:S(2)}, u32[]{:S(2)}) collective-permute-start(f32[256,256]{1,0:T(8,128)S(1)} %get-tuple-element.68.refs_1_), channel_id=1, source_target_pairs={{0,1},{1,0},{2,3},{3,2},{4,5},{5,4},{6,7},{7,6},{8,9},{9,8},{10,11... | collective-permute-start | bytes 786440 | tf_op jit(solution)/shard_map/ppermute | solution.py:448
  41.2 7.8 %collective-permute-start.11 = (f32[256,256]{1,0:T(8,128)S(1)}, f32[256,256]{1,0:T(8,128)S(1)}, u32[]{:S(2)}, u32[]{:S(2)}) collective-permute-start(f32[256,256]{1,0:T(8,128)S(1)} %get-tuple-element.81.refs_4_), channel_id=1, source_target_pairs={{0,1},{1,0},{2,3},{3,2},{4,5},{5,4},{6,7},{7,6},{8,9},{9,8},{10,11... | collective-permute-start | bytes 786440 | tf_op jit(solution)/shard_map/ppermute | solution.py:448
  52.5 10.3 %collective-permute-start.13 = (f32[2,512,128]{2,1,0:T(8,128)S(1)}, f32[2,512,128]{2,1,0:T(8,128)S(1)}, u32[]{:S(2)}, u32[]{:S(2)}) collective-permute-start(f32[2,512,128]{2,1,0:T(8,128)S(1)} %get-tuple-element.88), channel_id=1, source_target_pairs={{0,2},{2,0},{4,6},{6,4},{8,10},{10,8},{12,14},{14,12},{16,18},{18,... | collective-permute-start | bytes 1572872 | tf_op jit(solution)/shard_map/ppermute | solution.py:444
  55.8 8.9 %collective-permute-start.14 = (f32[2,512,128]{2,1,0:T(8,128)S(1)}, f32[2,512,128]{2,1,0:T(8,128)S(1)}, u32[]{:S(2)}, u32[]{:S(2)}) collective-permute-start(f32[2,512,128]{2,1,0:T(8,128)S(1)} %get-tuple-element.89), channel_id=1, source_target_pairs={{0,14},{2,4},{4,2},{6,8},{8,6},{10,12},{12,10},{14,0},{16,30},{18,... | collective-permute-start | bytes 1572872 | tf_op jit(solution)/shard_map/ppermute | solution.py:444
  57.0 12.8 %collective-permute-start.10 = (f32[1,256,256]{2,1,0:T(8,128)S(1)}, f32[1,256,256]{2,1,0:T(8,128)S(1)}, u32[]{:S(2)}, u32[]{:S(2)}) collective-permute-start(f32[1,256,256]{2,1,0:T(8,128)S(1)} %get-tuple-element.77), channel_id=1, source_target_pairs={{0,1},{1,0},{2,3},{3,2},{4,5},{5,4},{6,7},{7,6},{8,9},{9,8},{10,11... | collective-permute-start | bytes 786440 | tf_op jit(solution)/shard_map/ppermute | solution.py:448
  62.3 7.9 %collective-permute-start.12 = (f32[1,256,256]{2,1,0:T(8,128)S(1)}, f32[1,256,256]{2,1,0:T(8,128)S(1)}, u32[]{:S(2)}, u32[]{:S(2)}) collective-permute-start(f32[1,256,256]{2,1,0:T(8,128)S(1)} %get-tuple-element.86), channel_id=1, source_target_pairs={{0,1},{1,0},{2,3},{3,2},{4,5},{5,4},{6,7},{7,6},{8,9},{9,8},{10,11... | collective-permute-start | bytes 786440 | tf_op jit(solution)/shard_map/ppermute | solution.py:448
  65.4 14.9 %collective-permute-start.20 = (f32[2,128,256]{2,1,0:T(8,128)S(1)}, f32[2,128,256]{2,1,0:T(8,128)S(1)}, u32[]{:S(2)}, u32[]{:S(2)}) collective-permute-start(f32[2,128,256]{2,1,0:T(8,128)S(1)} %get-tuple-element.97), channel_id=1, source_target_pairs={{0,240},{2,242},{4,244},{6,246},{8,248},{10,250},{12,252},{14,254}... | collective-permute-start | bytes 786440 | tf_op jit(solution)/shard_map/ppermute | solution.py:444
  69.7 10.6 %collective-permute-start.19 = (f32[2,128,256]{2,1,0:T(8,128)S(1)}, f32[2,128,256]{2,1,0:T(8,128)S(1)}, u32[]{:S(2)}, u32[]{:S(2)}) collective-permute-start(f32[2,128,256]{2,1,0:T(8,128)S(1)} %get-tuple-element.90.refs_6_), channel_id=1, source_target_pairs={{0,16},{2,18},{4,20},{6,22},{8,24},{10,26},{12,28},{14,30},{16,0},... | collective-permute-start | bytes 786440 | tf_op jit(solution)/shard_map/ppermute | solution.py:444
  71.2 14.2 %collective-permute-start.16 = (f32[1,512,128]{2,1,0:T(8,128)S(1)}, f32[1,512,128]{2,1,0:T(8,128)S(1)}, u32[]{:S(2)}, u32[]{:S(2)}) collective-permute-start(f32[1,512,128]{2,1,0:T(8,128)S(1)} %get-tuple-element.92), channel_id=1, source_target_pairs={{0,14},{2,4},{4,2},{6,8},{8,6},{10,12},{12,10},{14,0},{16,30},{18,... | collective-permute-start | bytes 786440 | tf_op jit(solution)/shard_map/ppermute | solution.py:444
  78.8 6.7 %collective-permute-start.15 = (f32[1,512,128]{2,1,0:T(8,128)S(1)}, f32[1,512,128]{2,1,0:T(8,128)S(1)}, u32[]{:S(2)}, u32[]{:S(2)}) collective-permute-start(f32[1,512,128]{2,1,0:T(8,128)S(1)} %get-tuple-element.91.refs_5_), channel_id=1, source_target_pairs={{0,2},{2,0},{4,6},{6,4},{8,10},{10,8},{12,14},{14,12},{16,18},{18,... | collective-permute-start | bytes 786440 | tf_op jit(solution)/shard_map/ppermute | solution.py:444
  80.9 12.9 %collective-permute-start.21 = (f32[1,256,256]{2,1,0:T(8,128)S(1)}, f32[1,256,256]{2,1,0:T(8,128)S(1)}, u32[]{:S(2)}, u32[]{:S(2)}) collective-permute-start(f32[1,256,256]{2,1,0:T(8,128)S(1)} %get-tuple-element.98.refs_2_), channel_id=1, source_target_pairs={{0,1},{1,0},{2,3},{3,2},{4,5},{5,4},{6,7},{7,6},{8,9},{9,8},{10,11... | collective-permute-start | bytes 786440 | tf_op jit(solution)/shard_map/ppermute | solution.py:448
  86.1 5.8 %collective-permute-start.17 = (f32[1,128,256]{2,1,0:T(8,128)S(1)}, f32[1,128,256]{2,1,0:T(8,128)S(1)}, u32[]{:S(2)}, u32[]{:S(2)}) collective-permute-start(f32[1,128,256]{2,1,0:T(8,128)S(1)} %get-tuple-element.94), channel_id=1, source_target_pairs={{0,16},{2,18},{4,20},{6,22},{8,24},{10,26},{12,28},{14,30},{16,0},... | collective-permute-start | bytes 393224 | tf_op jit(solution)/shard_map/ppermute | solution.py:444
  86.2 7.6 %collective-permute-start.18 = (f32[1,128,256]{2,1,0:T(8,128)S(1)}, f32[1,128,256]{2,1,0:T(8,128)S(1)}, u32[]{:S(2)}, u32[]{:S(2)}) collective-permute-start(f32[1,128,256]{2,1,0:T(8,128)S(1)} %get-tuple-element.95), channel_id=1, source_target_pairs={{0,240},{2,242},{4,244},{6,246},{8,248},{10,250},{12,252},{14,254}... | collective-permute-start | bytes 393224 | tf_op jit(solution)/shard_map/ppermute | solution.py:444
  90.1 10.7 %collective-permute-start.23 = (f32[1,256,256]{2,1,0:T(8,128)S(1)}, f32[1,256,256]{2,1,0:T(8,128)S(1)}, u32[]{:S(2)}, u32[]{:S(2)}) collective-permute-start(f32[1,256,256]{2,1,0:T(8,128)S(1)} %get-tuple-element.99.refs_4_), channel_id=1, source_target_pairs={{0,1},{1,0},{2,3},{3,2},{4,5},{5,4},{6,7},{7,6},{8,9},{9,8},{10,11... | collective-permute-start | bytes 786440 | tf_op jit(solution)/shard_map/ppermute | solution.py:448
  94.4 12.0 %collective-permute-start.22 = (f32[1,256,256]{2,1,0:T(8,128)S(1)}, f32[1,256,256]{2,1,0:T(8,128)S(1)}, u32[]{:S(2)}, u32[]{:S(2)}) collective-permute-start(f32[1,256,256]{2,1,0:T(8,128)S(1)} %rows_first.1.refs_1_), channel_id=1, source_target_pairs={{0,1},{1,0},{2,3},{3,2},{4,5},{5,4},{6,7},{7,6},{8,9},{9,8},{10,11... | collective-permute-start | bytes 786440 | tf_op jit(solution)/shard_map/ppermute | solution.py:448

commit v11 on v10

--- a/solution.py
+++ b/solution.py
@@ -351,12 +351,6 @@
         copy.start()
     for copy in copies:
         copy.wait()
-
-
-def finish_kernel(info, other_first, partial, out, sems):
-    copy = pltpu.make_async_copy(other_first.at[0], out.at[0, 1 - info[4], 0], sems.at[0])
-    copy.start()
-    copy.wait()
 
 
 def pick_rows_kernel(info, own, *refs):
@@ -649,15 +643,8 @@
         copies=3,
         out=pl.ANY,
     )
-    (object_grad,) = call(
-        finish_kernel,
-        "finish",
-        shape,
-        (info, other_first),
-        after=(partial,),
-        copies=1,
-        out=pl.ANY,
-        alias=2,
+    object_grad = lax.dynamic_update_slice(
+        partial, other_first[:, None, None], (0, 1 - lax.axis_index("mode"), 0, 0, 0)
     )
     return (object_grad, probe_grad)
 

time: 108 us -> 109 us (level)
  waiting for transfers between devices: 17.7 us -> 11 us
  local copies, waits for them, and re-layouts: 1.36 us -> 6.58 us
  starting transfers between devices: 51.1 us -> 52.6 us
    unnamed x14 -> x22, local copies, waits for them, and re-layouts: 1.26 us -> 4.81 us
    ppermute x17, waiting for transfers between devices: 8.83 us -> 5.46 us  [swap(): return lax.ppermute(value, 'tile', pairs)]
    ppermute x7, waiting for transfers between devices: 8.87 us -> 5.55 us  [swap_mode(): return lax.ppermute(value, 'mode', [(0, 1), (1, 0)])]
    dynamic_update_slice x0 -> x1, local copies, waits for them, and re-layouts: none -> 1.67 us  [body(): lax.dynamic_update_slice(partial, other_first[:, None, None], (0, 1 - lax...]
    ppermute x17, starting transfers between devices: 38.8 us -> 40.1 us  [swap(): return lax.ppermute(value, 'tile', pairs)]
    pallas_call x23 -> x22, Pallas kernels: 36 us -> 36.9 us  [call(): pl.pallas_call(run, out_shape=tuple((jax.ShapeDtypeStruct(shape, dtype) f...]
  transfers between devices with their start and end apart: 24 -> 24, of which waited for: 10 -> 11; matrix products, arithmetic and copies ran while one was open for 0% -> 0% of each run, Pallas kernels for 26% -> 27%
where the time goes in v11:
time: 109 us
  starting transfers between devices  52.6 us (48%)
  Pallas kernels  36.9 us (34%)
  waiting for transfers between devices  11 us (10%)
  local copies, waits for them, and re-layouts  6.58 us (6%)
  between operations  1.61 us (1%)
    ppermute x17, starting transfers between devices, swap(): return lax.ppermute(value, 'tile', pairs)  40.1 us
    pallas_call x22, Pallas kernels, call(): pl.pallas_call(run, out_shape=tuple((jax.ShapeDtypeStruct(shape, dtype) f...  36.9 us
    ppermute x7, starting transfers between devices, swap_mode(): return lax.ppermute(value, 'mode', [(0, 1), (1, 0)])  12.5 us
    ppermute x7, waiting for transfers between devices, swap_mode(): return lax.ppermute(value, 'mode', [(0, 1), (1, 0)])  5.55 us
    ppermute x17, waiting for transfers between devices, swap(): return lax.ppermute(value, 'tile', pairs)  5.46 us
    unnamed x22, local copies, waits for them, and re-layouts  4.81 us
  transfers between devices with their start and end apart: 24, of which 11 were waited for; matrix products, arithmetic and copies ran while one was open for 0% of the time, Pallas kernels for 27%

profile of v11, /device:TPU:1, one launch (start us, length us, event | category | flops | bytes accessed | tf_op | source)
XLA Modules:
  0.0 108.7 jit_solution(1139547385999831888)
XLA Ops:
  2.7 2.6 %collective-permute-start.3 = (f32[2,128,256]{2,1,0:T(8,128)S(1)}, f32[2,128,256]{2,1,0:T(8,128)S(1)}, u32[]{:S(2)}, u32[]{:S(2)}) collective-permute-start(f32[2,128,256]{2,1,0:T(8,128)S(1)} %get-tuple-element.54), channel_id=1, source_target_pairs={{0,16},{2,18},{4,20},{6,22},{8,24},{10,26},{12,28},{14,30},{16,0},... | collective-permute-start | bytes 786440 | tf_op jit(solution)/shard_map/ppermute | solution.py:438
  5.3 5.7 %collective-permute-start.4 = (f32[2,128,256]{2,1,0:T(8,128)S(1)}, f32[2,128,256]{2,1,0:T(8,128)S(1)}, u32[]{:S(2)}, u32[]{:S(2)}) collective-permute-start(f32[2,128,256]{2,1,0:T(8,128)S(1)} %get-tuple-element.55), channel_id=1, source_target_pairs={{0,240},{2,242},{4,244},{6,246},{8,248},{10,250},{12,252},{14,254}... | collective-permute-start | bytes 786440 | tf_op jit(solution)/shard_map/ppermute | solution.py:438
  11.5 2.4 %collective-permute-start.2 = (f32[2,2,256,128]{3,2,1,0:T(8,128)S(1)}, f32[2,2,256,128]{3,2,1,0:T(8,128)S(1)}, u32[]{:S(2)}, u32[]{:S(2)}) collective-permute-start(f32[2,2,256,128]{3,2,1,0:T(8,128)S(1)} %pick_cols.1), channel_id=1, source_target_pairs={{0,14},{2,4},{4,2},{6,8},{8,6},{10,12},{12,10},{14,0},{16,30},{18,... | collective-permute-start | bytes 1572872 | tf_op jit(solution)/shard_map/ppermute | solution.py:438
  14.0 1.5 %collective-permute-start.1 = (f32[2,128,256]{2,1,0:T(8,128)S(1)}, f32[2,128,256]{2,1,0:T(8,128)S(1)}, u32[]{:S(2)}, u32[]{:S(2)}) collective-permute-start(f32[2,128,256]{2,1,0:T(8,128)S(1)} %get-tuple-element.53), channel_id=1, source_target_pairs={{0,240},{2,242},{4,244},{6,246},{8,248},{10,250},{12,252},{14,254}... | collective-permute-start | bytes 786440 | tf_op jit(solution)/shard_map/ppermute | solution.py:438
  17.3 3.1 %collective-permute-start.5 = (f32[2,2,128,128]{3,2,1,0:T(8,128)S(1)}, f32[2,2,128,128]{3,2,1,0:T(8,128)S(1)}, u32[]{:S(2)}, u32[]{:S(2)}) collective-permute-start(f32[2,2,128,128]{3,2,1,0:T(8,128)S(1)} %get-tuple-element.58), channel_id=1, source_target_pairs={{0,14},{2,4},{4,2},{6,8},{8,6},{10,12},{12,10},{14,0},{16,30},{18,... | collective-permute-start | bytes 786440 | tf_op jit(solution)/shard_map/ppermute | solution.py:438
  21.3 2.1 %collective-permute-done.1.refs_3_.refs_4_ = f32[2,128,256]{2,1,0:T(8,128)S(1)} collective-permute-done((f32[2,128,256]{2,1,0:T(8,128)S(1)}, f32[2,128,256]{2,1,0:T(8,128)S(1)}, u32[]{:S(2)}, u32[]{:S(2)}) %collective-permute-start.1) | collective-permute-done | bytes 262176 | tf_op jit(solution)/shard_map/ppermute | solution.py:438
  25.3 1.6 %collective-permute-start.6 = (f32[2,512,128]{2,1,0:T(8,128)S(1)}, f32[2,512,128]{2,1,0:T(8,128)S(1)}, u32[]{:S(2)}, u32[]{:S(2)}) collective-permute-start(f32[2,512,128]{2,1,0:T(8,128)S(1)} %get-tuple-element.59), channel_id=1, source_target_pairs={{0,2},{2,0},{4,6},{6,4},{8,10},{10,8},{12,14},{14,12},{16,18},{18,... | collective-permute-start | bytes 1572872 | tf_op jit(solution)/shard_map/ppermute | solution.py:438
  27.1 3.2 %waves_0.1 = (f32[2,512,512]{2,1,0:T(8,128)S(1)}, f32[2,256,256]{2,1,0:T(8,128)S(1)}, f32[6,2,256,256]{3,2,1,0:T(8,128)S(1)}) custom-call(s32[2,2]{1,0:T(2,128)S(1)} %bitcast.17, s32[5]{0:T(128)S(1)} %convert_element_type.3.refs_0_.refs_1_.refs_2_, f32[2,2,256,256]{3,2,1,0:T(8,128)S(1)} %bitcast.14, ...), custom_call_target="tpu_custom_call" | custom-call | tf_op jit(solution)/shard_map/waves_0/pallas_call | solution.py:456
  30.3 2.9 %waves_1.1 = (f32[2,256,256]{2,1,0:T(8,128)S(1)}, f32[6,2,256,256]{3,2,1,0:T(8,128)S(1)}) custom-call(s32[2,2]{1,0:T(2,128)S(1)} %bitcast.18, f32[2,512,512]{2,1,0:T(8,128)S(1)} %get-tuple-element.66.refs_1_, f32[2,6,256,256]{3,2,1,0:T(8,128)S(1)} %get-tuple-element.57.refs_4_.refs_8_.refs_2_, bf16[2,256,256]{2,1,0:T(8,128)(2,1)S(1)} %get-tuple-element.61.refs_9_.refs_3_, ...), custom_call_target="tpu_custom_call" | custom-call | tf_op jit(solution)/shard_map/waves_1/pallas_call | solution.py:456
  33.2 2.9 %fars_0.1 = (f32[2,512,512]{2,1,0:T(8,128)S(1)}, f32[2,256,256]{2,1,0:T(8,128)S(1)}, f32[6,2,256,256]{3,2,1,0:T(8,128)S(1)}, f32[256,256]{1,0:T(8,128)S(1)}) custom-call(s32[2,2]{1,0:T(2,128)S(1)} %bitcast.19, s32[5]{0:T(128)S(1)} %convert_element_type.3.refs_0_.refs_1_.refs_2_, f32[2,2,256,256]{3,2,1,0:T(8,128)S(1)} %bitcast.15, ...), custom_call_target="tpu_custom_call" | custom-call | tf_op jit(solution)/shard_map/fars_0/pallas_call | solution.py:456
  36.2 2.7 %collective-permute-start.9 = (f32[256,256]{1,0:T(8,128)S(1)}, f32[256,256]{1,0:T(8,128)S(1)}, u32[]{:S(2)}, u32[]{:S(2)}) collective-permute-start(f32[256,256]{1,0:T(8,128)S(1)} %get-tuple-element.68.refs_1_), channel_id=1, source_target_pairs={{0,1},{1,0},{2,3},{3,2},{4,5},{5,4},{6,7},{7,6},{8,9},{9,8},{10,11... | collective-permute-start | bytes 786440 | tf_op jit(solution)/shard_map/ppermute | solution.py:442
  38.9 2.5 %fars_1.1 = (f32[2,256,256]{2,1,0:T(8,128)S(1)}, f32[6,2,256,256]{3,2,1,0:T(8,128)S(1)}, f32[256,256]{1,0:T(8,128)S(1)}) custom-call(s32[2,2]{1,0:T(2,128)S(1)} %bitcast.20, f32[2,512,512]{2,1,0:T(8,128)S(1)} %get-tuple-element.79.refs_1_, f32[6,2,256,256]{3,2,1,0:T(8,128)S(1)} %get-tuple-element.80.refs_2_.refs_8_, ...), custom_call_target="tpu_custom_call" | custom-call | tf_op jit(solution)/shard_map/fars_1/pallas_call | solution.py:456
  42.7 1.5 %reorder.1.refs_3_.refs_6_ = f32[2,256,256]{2,1,0:T(8,128)S(1)} custom-call(f32[2,256,256]{2,1,0:T(8,128)S(1)} %bitcast.16), custom_call_target="tpu_custom_call" | custom-call | tf_op jit(solution)/shard_map/reorder/pallas_call | solution.py:456
  44.2 1.9 %back_last_0.1 = (f32[2,256,256]{2,1,0:T(8,128)S(1)}, bf16[6,2,256,256]{3,2,1,0:T(8,128)(2,1)S(1)}) custom-call(s32[1]{0:T(128)S(6)} %copy.10.refs_0_, f32[256,256]{1,0:T(8,128)S(1)} %get-tuple-element.68.refs_1_, f32[256,256]{1,0:T(8,128)S(1)} %collective-permute-done.9.refs_2_, f32[2,256,256]{2,1,0:T(8,128)S(1)} %reorder.1.refs_3_.refs_6_, ...), custom_call_target="tpu_custom_call" | custom-call | tf_op jit(solution)/shard_map/back_last_0/pallas_call | solution.py:456
  46.1 2.7 %back_first_0.1 = (f32[1,256,256]{2,1,0:T(8,128)S(1)}, f32[1,256,256]{2,1,0:T(8,128)S(1)}, f32[2,6,256,256]{3,2,1,0:T(8,128)S(1)}) custom-call(s32[5]{0:T(128)S(1)} %convert_element_type.3.refs_0_.refs_1_.refs_2_, bf16[6,2,256,256]{3,2,1,0:T(8,128)(2,1)S(1)} %get-tuple-element.71.refs_1_, f32[2,6,256,256]{3,2,1,0:T(8,128)S(1)} %get-tuple-element.57.refs_4_.refs_8_.refs_2_, ...), custom_call_target="tpu_custom_call" | custom-call | tf_op jit(solution)/shard_map/back_first_0/pallas_call | solution.py:456
  49.2 3.4 %back_last_1.1 = (bf16[6,2,256,256]{3,2,1,0:T(8,128)(2,1)S(1)}, f32[2,512,128]{2,1,0:T(8,128)S(1)}, f32[2,512,256]{2,1,0:T(8,128)S(1)}, f32[2,512,128]{2,1,0:T(8,128)S(1)}) custom-call(s32[1]{0:T(128)S(6)} %copy.10.refs_0_, s32[2,2]{1,0:T(2,128)S(1)} %bitcast.21, s32[5]{0:T(128)S(1)} %convert_element_type.3.refs_0_.refs_1_.refs_2_, ...), custom_call_target="tpu_custom_call" | custom-call | tf_op jit(solution)/shard_map/back_last_1/pallas_call | solution.py:456
  52.7 3.4 %collective-permute-start.13 = (f32[2,512,128]{2,1,0:T(8,128)S(1)}, f32[2,512,128]{2,1,0:T(8,128)S(1)}, u32[]{:S(2)}, u32[]{:S(2)}) collective-permute-start(f32[2,512,128]{2,1,0:T(8,128)S(1)} %get-tuple-element.88), channel_id=1, source_target_pairs={{0,2},{2,0},{4,6},{6,4},{8,10},{10,8},{12,14},{14,12},{16,18},{18,... | collective-permute-start | bytes 1572872 | tf_op jit(solution)/shard_map/ppermute | solution.py:438
  57.1 2.6 %collective-permute-start.10 = (f32[1,256,256]{2,1,0:T(8,128)S(1)}, f32[1,256,256]{2,1,0:T(8,128)S(1)}, u32[]{:S(2)}, u32[]{:S(2)}) collective-permute-start(f32[1,256,256]{2,1,0:T(8,128)S(1)} %get-tuple-element.77), channel_id=1, source_target_pairs={{0,1},{1,0},{2,3},{3,2},{4,5},{5,4},{6,7},{7,6},{8,9},{9,8},{10,11... | collective-permute-start | bytes 786440 | tf_op jit(solution)/shard_map/ppermute | solution.py:442
  59.8 2.7 %back_first_1.1 = (f32[1,256,256]{2,1,0:T(8,128)S(1)}, f32[1,256,256]{2,1,0:T(8,128)S(1)}, f32[2,6,256,256]{3,2,1,0:T(8,128)S(1)}) custom-call(s32[5]{0:T(128)S(1)} %convert_element_type.3.refs_0_.refs_1_.refs_2_, bf16[6,2,256,256]{3,2,1,0:T(8,128)(2,1)S(1)} %get-tuple-element.84.refs_1_, f32[2,6,256,256]{3,2,1,0:T(8,128)S(1)} %get-tuple-element.57.refs_4_.refs_8_.refs_2_, ...), custom_call_target="tpu_custom_call" | custom-call | tf_op jit(solution)/shard_map/back_first_1/pallas_call | solution.py:456
  62.5 1.7 %copy-done.3 = f32[2,6,256,256]{3,2,1,0:T(8,128)} copy-done((f32[2,6,256,256]{3,2,1,0:T(8,128)}, f32[2,6,256,256]{3,2,1,0:T(8,128)S(1)}, u32[]{:S(2)}) %copy-start.3) | copy-done | bytes 3145752
  65.6 4.3 %collective-permute-start.20 = (f32[2,128,256]{2,1,0:T(8,128)S(1)}, f32[2,128,256]{2,1,0:T(8,128)S(1)}, u32[]{:S(2)}, u32[]{:S(2)}) collective-permute-start(f32[2,128,256]{2,1,0:T(8,128)S(1)} %get-tuple-element.97), channel_id=1, source_target_pairs={{0,240},{2,242},{4,244},{6,246},{8,248},{10,250},{12,252},{14,254}... | collective-permute-start | bytes 786440 | tf_op jit(solution)/shard_map/ppermute | solution.py:438
  69.9 1.7 %collective-permute-done.12.refs_5_.refs_4_ = f32[1,256,256]{2,1,0:T(8,128)S(1)} collective-permute-done((f32[1,256,256]{2,1,0:T(8,128)S(1)}, f32[1,256,256]{2,1,0:T(8,128)S(1)}, u32[]{:S(2)}, u32[]{:S(2)}) %collective-permute-start.12) | collective-permute-done | bytes 262176 | tf_op jit(solution)/shard_map/ppermute | solution.py:442
  72.7 6.2 %collective-permute-start.16 = (f32[1,512,128]{2,1,0:T(8,128)S(1)}, f32[1,512,128]{2,1,0:T(8,128)S(1)}, u32[]{:S(2)}, u32[]{:S(2)}) collective-permute-start(f32[1,512,128]{2,1,0:T(8,128)S(1)} %get-tuple-element.92), channel_id=1, source_target_pairs={{0,14},{2,4},{4,2},{6,8},{8,6},{10,12},{12,10},{14,0},{16,30},{18,... | collective-permute-start | bytes 786440 | tf_op jit(solution)/shard_map/ppermute | solution.py:438
  78.9 4.1 %collective-permute-start.15 = (f32[1,512,128]{2,1,0:T(8,128)S(1)}, f32[1,512,128]{2,1,0:T(8,128)S(1)}, u32[]{:S(2)}, u32[]{:S(2)}) collective-permute-start(f32[1,512,128]{2,1,0:T(8,128)S(1)} %get-tuple-element.91.refs_5_), channel_id=1, source_target_pairs={{0,2},{2,0},{4,6},{6,4},{8,10},{10,8},{12,14},{14,12},{16,18},{18,... | collective-permute-start | bytes 786440 | tf_op jit(solution)/shard_map/ppermute | solution.py:438
  87.0 3.9 %collective-permute-start.18 = (f32[1,128,256]{2,1,0:T(8,128)S(1)}, f32[1,128,256]{2,1,0:T(8,128)S(1)}, u32[]{:S(2)}, u32[]{:S(2)}) collective-permute-start(f32[1,128,256]{2,1,0:T(8,128)S(1)} %get-tuple-element.95), channel_id=1, source_target_pairs={{0,240},{2,242},{4,244},{6,246},{8,248},{10,250},{12,252},{14,254}... | collective-permute-start | bytes 393224 | tf_op jit(solution)/shard_map/ppermute | solution.py:438
  90.9 2.6 %collective-permute-start.22 = (f32[1,256,256]{2,1,0:T(8,128)}, f32[1,256,256]{2,1,0:T(8,128)}, u32[]{:S(2)}, u32[]{:S(2)}) collective-permute-start(f32[1,256,256]{2,1,0:T(8,128)} %get-tuple-element.99.refs_4_), channel_id=1, source_target_pairs={{0,1},{1,0},{2,3},{3,2},{4,5},{5,4},{6,7},{7,6},{8,9},{9,8},{10,11... | collective-permute-start | bytes 786440 | tf_op jit(solution)/shard_map/ppermute | solution.py:442
  95.0 2.7 %collective-permute-start.23 = (f32[1,256,256]{2,1,0:T(8,128)}, f32[1,256,256]{2,1,0:T(8,128)}, u32[]{:S(2)}, u32[]{:S(2)}) collective-permute-start(f32[1,256,256]{2,1,0:T(8,128)} %rows_first.1.refs_1_), channel_id=1, source_target_pairs={{0,1},{1,0},{2,3},{3,2},{4,5},{5,4},{6,7},{7,6},{8,9},{9,8},{10,11... | collective-permute-start | bytes 786440 | tf_op jit(solution)/shard_map/ppermute | solution.py:442
  97.7 1.9 %copy-done.4 = f32[2,6,256,256]{3,2,1,0:T(8,128)S(1)} copy-done((f32[2,6,256,256]{3,2,1,0:T(8,128)S(1)}, f32[2,6,256,256]{3,2,1,0:T(8,128)}, u32[]{:S(2)}) %copy-start.4) | copy-done | bytes 3145752
  99.6 2.0 %probe_sum.1 = f32[1,2,6,256,256]{4,3,2,1,0:T(8,128)} custom-call(f32[2,6,256,256]{3,2,1,0:T(8,128)S(1)} %get-tuple-element.100.refs_0_, f32[2,6,256,256]{3,2,1,0:T(8,128)S(1)} %copy-done.4), custom_call_target="tpu_custom_call" | custom-call | tf_op jit(solution)/shard_map/probe_sum/pallas_call | solution.py:456
  101.7 2.1 %finish_last.1 = f32[1,2,2,256,256]{4,3,2,1,0:T(8,128)} custom-call(s32[5]{0:T(128)S(1)} %convert_element_type.3.refs_0_.refs_1_.refs_2_, f32[1,256,256]{2,1,0:T(8,128)} %rows_first.1.refs_1_, f32[1,256,256]{2,1,0:T(8,128)S(1)} %copy-done.9, f32[1,256,256]{2,1,0:T(8,128)S(1)} %collective-permute-done.21.refs_4_.refs_3_, ...), custom_call_target="tpu_custom_call" | custom-call | tf_op jit(solution)/shard_map/finish_last/pallas_call | solution.py:456
  103.8 3.2 %collective-permute-done.23 = f32[1,256,256]{2,1,0:T(8,128)} collective-permute-done((f32[1,256,256]{2,1,0:T(8,128)}, f32[1,256,256]{2,1,0:T(8,128)}, u32[]{:S(2)}, u32[]{:S(2)}) %collective-permute-start.23) | collective-permute-done | bytes 262176 | tf_op jit(solution)/shard_map/ppermute | solution.py:442
  107.0 1.7 %bitcast_dynamic-update-slice_fusion = f32[1,2,2,256,256]{4,3,2,1,0:T(8,128)} fusion(f32[1,2,2,256,256]{4,3,2,1,0:T(8,128)} %finish_last.1, s32[]{:T(128)S(6)} %select_n.26, f32[1,256,256]{2,1,0:T(8,128)} %collective-permute-done.23), kind=kLoop, calls=%fused_computation | loop fusion | bytes 524292 | tf_op jit(solution)/shard_map/dynamic_update_slice | solution.py:646
  (63 shorter events, 17.8 us)
Async XLA Ops:
  2.0 18.3 %copy-start.2 = (f32[2,6,256,256]{3,2,1,0:T(8,128)S(1)}, f32[2,6,256,256]{3,2,1,0:T(8,128)}, u32[]{:S(2)}) copy-start(f32[2,6,256,256]{3,2,1,0:T(8,128)} %refs_1_.1) | copy-start | bytes 9437188
  2.0 18.3 %copy-start.5 = (bf16[4,256,256]{2,1,0:T(8,128)(2,1)S(1)}, bf16[4,256,256]{2,1,0:T(8,128)(2,1)}, u32[]{:S(2)}) copy-start(bf16[4,256,256]{2,1,0:T(8,128)(2,1)} %constant.55.clone.refs_2_) | copy-start | bytes 1572868
  2.0 18.3 %copy-start.7 = (bf16[2,256,256]{2,1,0:T(8,128)(2,1)S(1)}, bf16[2,256,256]{2,1,0:T(8,128)(2,1)}, u32[]{:S(2)}) copy-start(bf16[2,256,256]{2,1,0:T(8,128)(2,1)} %refs_0_.3) | copy-start | bytes 786436
  2.7 12.7 %collective-permute-start.3 = (f32[2,128,256]{2,1,0:T(8,128)S(1)}, f32[2,128,256]{2,1,0:T(8,128)S(1)}, u32[]{:S(2)}, u32[]{:S(2)}) collective-permute-start(f32[2,128,256]{2,1,0:T(8,128)S(1)} %get-tuple-element.54), channel_id=1, source_target_pairs={{0,16},{2,18},{4,20},{6,22},{8,24},{10,26},{12,28},{14,30},{16,0},... | collective-permute-start | bytes 786440 | tf_op jit(solution)/shard_map/ppermute | solution.py:438
  5.3 11.4 %collective-permute-start.4 = (f32[2,128,256]{2,1,0:T(8,128)S(1)}, f32[2,128,256]{2,1,0:T(8,128)S(1)}, u32[]{:S(2)}, u32[]{:S(2)}) collective-permute-start(f32[2,128,256]{2,1,0:T(8,128)S(1)} %get-tuple-element.55), channel_id=1, source_target_pairs={{0,240},{2,242},{4,244},{6,246},{8,248},{10,250},{12,252},{14,254}... | collective-permute-start | bytes 786440 | tf_op jit(solution)/shard_map/ppermute | solution.py:438
  11.5 13.2 %copy-start.1 = (f32[1,2,2,256,256]{4,3,2,1,0:T(8,128)S(1)}, f32[1,2,2,256,256]{4,3,2,1,0:T(8,128)}, u32[]{:S(2)}) copy-start(f32[1,2,2,256,256]{4,3,2,1,0:T(8,128)} %param.7) | copy-start | bytes 3145732
  11.5 11.9 %collective-permute-start.2 = (f32[2,2,256,128]{3,2,1,0:T(8,128)S(1)}, f32[2,2,256,128]{3,2,1,0:T(8,128)S(1)}, u32[]{:S(2)}, u32[]{:S(2)}) collective-permute-start(f32[2,2,256,128]{3,2,1,0:T(8,128)S(1)} %pick_cols.1), channel_id=1, source_target_pairs={{0,14},{2,4},{4,2},{6,8},{8,6},{10,12},{12,10},{14,0},{16,30},{18,... | collective-permute-start | bytes 1572872 | tf_op jit(solution)/shard_map/ppermute | solution.py:438
  14.0 7.3 %collective-permute-start = (f32[2,128,256]{2,1,0:T(8,128)S(1)}, f32[2,128,256]{2,1,0:T(8,128)S(1)}, u32[]{:S(2)}, u32[]{:S(2)}) collective-permute-start(f32[2,128,256]{2,1,0:T(8,128)S(1)} %get-tuple-element.52), channel_id=1, source_target_pairs={{0,16},{2,18},{4,20},{6,22},{8,24},{10,26},{12,28},{14,30},{16,0},... | collective-permute-start | bytes 786440 | tf_op jit(solution)/shard_map/ppermute | solution.py:438
  14.0 9.4 %collective-permute-start.1 = (f32[2,128,256]{2,1,0:T(8,128)S(1)}, f32[2,128,256]{2,1,0:T(8,128)S(1)}, u32[]{:S(2)}, u32[]{:S(2)}) collective-permute-start(f32[2,128,256]{2,1,0:T(8,128)S(1)} %get-tuple-element.53), channel_id=1, source_target_pairs={{0,240},{2,242},{4,244},{6,246},{8,248},{10,250},{12,252},{14,254}... | collective-permute-start | bytes 786440 | tf_op jit(solution)/shard_map/ppermute | solution.py:438
  17.3 7.4 %collective-permute-start.5 = (f32[2,2,128,128]{3,2,1,0:T(8,128)S(1)}, f32[2,2,128,128]{3,2,1,0:T(8,128)S(1)}, u32[]{:S(2)}, u32[]{:S(2)}) collective-permute-start(f32[2,2,128,128]{3,2,1,0:T(8,128)S(1)} %get-tuple-element.58), channel_id=1, source_target_pairs={{0,14},{2,4},{4,2},{6,8},{8,6},{10,12},{12,10},{14,0},{16,30},{18,... | collective-permute-start | bytes 786440 | tf_op jit(solution)/shard_map/ppermute | solution.py:438
  20.3 6.8 %collective-permute-start.8 = (f32[2,512,128]{2,1,0:T(8,128)S(1)}, f32[2,512,128]{2,1,0:T(8,128)S(1)}, u32[]{:S(2)}, u32[]{:S(2)}) collective-permute-start(f32[2,512,128]{2,1,0:T(8,128)S(1)} %get-tuple-element.56.refs_3_), channel_id=1, source_target_pairs={{0,2},{2,0},{4,6},{6,4},{8,10},{10,8},{12,14},{14,12},{16,18},{18,... | collective-permute-start | bytes 1572872 | tf_op jit(solution)/shard_map/ppermute | solution.py:438
  21.0 6.2 %copy-start.10 = (s32[1,2,2]{2,1,0:T(2,128)S(1)}, s32[1,2,2]{2,1,0:T(2,128)}, u32[]{:S(2)}) copy-start(s32[1,2,2]{2,1,0:T(2,128)} %param.10) | copy-start | bytes 52
  25.3 7.9 %collective-permute-start.6 = (f32[2,512,128]{2,1,0:T(8,128)S(1)}, f32[2,512,128]{2,1,0:T(8,128)S(1)}, u32[]{:S(2)}, u32[]{:S(2)}) collective-permute-start(f32[2,512,128]{2,1,0:T(8,128)S(1)} %get-tuple-element.59), channel_id=1, source_target_pairs={{0,2},{2,0},{4,6},{6,4},{8,10},{10,8},{12,14},{14,12},{16,18},{18,... | collective-permute-start | bytes 1572872 | tf_op jit(solution)/shard_map/ppermute | solution.py:438
  26.9 6.3 %collective-permute-start.7 = (f32[2,2,128,128]{3,2,1,0:T(8,128)S(1)}, f32[2,2,128,128]{3,2,1,0:T(8,128)S(1)}, u32[]{:S(2)}, u32[]{:S(2)}) collective-permute-start(f32[2,2,128,128]{3,2,1,0:T(8,128)S(1)} %get-tuple-element.60), channel_id=1, source_target_pairs={{0,14},{2,4},{4,2},{6,8},{8,6},{10,12},{12,10},{14,0},{16,30},{18,... | collective-permute-start | bytes 786440 | tf_op jit(solution)/shard_map/ppermute | solution.py:438
  36.2 6.5 %copy-start.6 = (f32[1,2,256,256]{3,2,1,0:T(8,128)S(1)}, f32[1,2,256,256]{3,2,1,0:T(8,128)}, u32[]{:S(2)}) copy-start(f32[1,2,256,256]{3,2,1,0:T(8,128)} %param.12) | copy-start | bytes 1572868
  36.2 8.0 %collective-permute-start.9 = (f32[256,256]{1,0:T(8,128)S(1)}, f32[256,256]{1,0:T(8,128)S(1)}, u32[]{:S(2)}, u32[]{:S(2)}) collective-permute-start(f32[256,256]{1,0:T(8,128)S(1)} %get-tuple-element.68.refs_1_), channel_id=1, source_target_pairs={{0,1},{1,0},{2,3},{3,2},{4,5},{5,4},{6,7},{7,6},{8,9},{9,8},{10,11... | collective-permute-start | bytes 786440 | tf_op jit(solution)/shard_map/ppermute | solution.py:442
  41.4 7.8 %collective-permute-start.11 = (f32[256,256]{1,0:T(8,128)S(1)}, f32[256,256]{1,0:T(8,128)S(1)}, u32[]{:S(2)}, u32[]{:S(2)}) collective-permute-start(f32[256,256]{1,0:T(8,128)S(1)} %get-tuple-element.81.refs_4_), channel_id=1, source_target_pairs={{0,1},{1,0},{2,3},{3,2},{4,5},{5,4},{6,7},{7,6},{8,9},{9,8},{10,11... | collective-permute-start | bytes 786440 | tf_op jit(solution)/shard_map/ppermute | solution.py:442
  52.7 11.9 %collective-permute-start.13 = (f32[2,512,128]{2,1,0:T(8,128)S(1)}, f32[2,512,128]{2,1,0:T(8,128)S(1)}, u32[]{:S(2)}, u32[]{:S(2)}) collective-permute-start(f32[2,512,128]{2,1,0:T(8,128)S(1)} %get-tuple-element.88), channel_id=1, source_target_pairs={{0,2},{2,0},{4,6},{6,4},{8,10},{10,8},{12,14},{14,12},{16,18},{18,... | collective-permute-start | bytes 1572872 | tf_op jit(solution)/shard_map/ppermute | solution.py:438
  56.0 8.9 %collective-permute-start.14 = (f32[2,512,128]{2,1,0:T(8,128)S(1)}, f32[2,512,128]{2,1,0:T(8,128)S(1)}, u32[]{:S(2)}, u32[]{:S(2)}) collective-permute-start(f32[2,512,128]{2,1,0:T(8,128)S(1)} %get-tuple-element.89), channel_id=1, source_target_pairs={{0,14},{2,4},{4,2},{6,8},{8,6},{10,12},{12,10},{14,0},{16,30},{18,... | collective-permute-start | bytes 1572872 | tf_op jit(solution)/shard_map/ppermute | solution.py:438
  57.1 12.8 %collective-permute-start.10 = (f32[1,256,256]{2,1,0:T(8,128)S(1)}, f32[1,256,256]{2,1,0:T(8,128)S(1)}, u32[]{:S(2)}, u32[]{:S(2)}) collective-permute-start(f32[1,256,256]{2,1,0:T(8,128)S(1)} %get-tuple-element.77), channel_id=1, source_target_pairs={{0,1},{1,0},{2,3},{3,2},{4,5},{5,4},{6,7},{7,6},{8,9},{9,8},{10,11... | collective-permute-start | bytes 786440 | tf_op jit(solution)/shard_map/ppermute | solution.py:442
  64.2 7.4 %collective-permute-start.12 = (f32[1,256,256]{2,1,0:T(8,128)S(1)}, f32[1,256,256]{2,1,0:T(8,128)S(1)}, u32[]{:S(2)}, u32[]{:S(2)}) collective-permute-start(f32[1,256,256]{2,1,0:T(8,128)S(1)} %get-tuple-element.86), channel_id=1, source_target_pairs={{0,1},{1,0},{2,3},{3,2},{4,5},{5,4},{6,7},{7,6},{8,9},{9,8},{10,11... | collective-permute-start | bytes 786440 | tf_op jit(solution)/shard_map/ppermute | solution.py:442
  65.6 17.3 %collective-permute-start.20 = (f32[2,128,256]{2,1,0:T(8,128)S(1)}, f32[2,128,256]{2,1,0:T(8,128)S(1)}, u32[]{:S(2)}, u32[]{:S(2)}) collective-permute-start(f32[2,128,256]{2,1,0:T(8,128)S(1)} %get-tuple-element.97), channel_id=1, source_target_pairs={{0,240},{2,242},{4,244},{6,246},{8,248},{10,250},{12,252},{14,254}... | collective-permute-start | bytes 786440 | tf_op jit(solution)/shard_map/ppermute | solution.py:438
  69.9 13.1 %collective-permute-start.19 = (f32[2,128,256]{2,1,0:T(8,128)S(1)}, f32[2,128,256]{2,1,0:T(8,128)S(1)}, u32[]{:S(2)}, u32[]{:S(2)}) collective-permute-start(f32[2,128,256]{2,1,0:T(8,128)S(1)} %get-tuple-element.90.refs_6_), channel_id=1, source_target_pairs={{0,16},{2,18},{4,20},{6,22},{8,24},{10,26},{12,28},{14,30},{16,0},... | collective-permute-start | bytes 786440 | tf_op jit(solution)/shard_map/ppermute | solution.py:438
  72.7 13.6 %collective-permute-start.16 = (f32[1,512,128]{2,1,0:T(8,128)S(1)}, f32[1,512,128]{2,1,0:T(8,128)S(1)}, u32[]{:S(2)}, u32[]{:S(2)}) collective-permute-start(f32[1,512,128]{2,1,0:T(8,128)S(1)} %get-tuple-element.92), channel_id=1, source_target_pairs={{0,14},{2,4},{4,2},{6,8},{8,6},{10,12},{12,10},{14,0},{16,30},{18,... | collective-permute-start | bytes 786440 | tf_op jit(solution)/shard_map/ppermute | solution.py:438
  78.9 7.4 %collective-permute-start.15 = (f32[1,512,128]{2,1,0:T(8,128)S(1)}, f32[1,512,128]{2,1,0:T(8,128)S(1)}, u32[]{:S(2)}, u32[]{:S(2)}) collective-permute-start(f32[1,512,128]{2,1,0:T(8,128)S(1)} %get-tuple-element.91.refs_5_), channel_id=1, source_target_pairs={{0,2},{2,0},{4,6},{6,4},{8,10},{10,8},{12,14},{14,12},{16,18},{18,... | collective-permute-start | bytes 786440 | tf_op jit(solution)/shard_map/ppermute | solution.py:438
  84.3 9.5 %copy-start.8 = (f32[1,256,256]{2,1,0:T(8,128)}, f32[1,256,256]{2,1,0:T(8,128)S(1)}, u32[]{:S(2)}) copy-start(f32[1,256,256]{2,1,0:T(8,128)S(1)} %get-tuple-element.98.refs_2_) | copy-start | bytes 786436
  84.3 9.5 %collective-permute-start.21 = (f32[1,256,256]{2,1,0:T(8,128)S(1)}, f32[1,256,256]{2,1,0:T(8,128)S(1)}, u32[]{:S(2)}, u32[]{:S(2)}) collective-permute-start(f32[1,256,256]{2,1,0:T(8,128)S(1)} %get-tuple-element.98.refs_2_), channel_id=1, source_target_pairs={{0,1},{1,0},{2,3},{3,2},{4,5},{5,4},{6,7},{7,6},{8,9},{9,8},{10,11... | collective-permute-start | bytes 786440 | tf_op jit(solution)/shard_map/ppermute | solution.py:442
  86.9 6.6 %collective-permute-start.17 = (f32[1,128,256]{2,1,0:T(8,128)S(1)}, f32[1,128,256]{2,1,0:T(8,128)S(1)}, u32[]{:S(2)}, u32[]{:S(2)}) collective-permute-start(f32[1,128,256]{2,1,0:T(8,128)S(1)} %get-tuple-element.94), channel_id=1, source_target_pairs={{0,16},{2,18},{4,20},{6,22},{8,24},{10,26},{12,28},{14,30},{16,0},... | collective-permute-start | bytes 393224 | tf_op jit(solution)/shard_map/ppermute | solution.py:438
  87.0 6.6 %collective-permute-start.18 = (f32[1,128,256]{2,1,0:T(8,128)S(1)}, f32[1,128,256]{2,1,0:T(8,128)S(1)}, u32[]{:S(2)}, u32[]{:S(2)}) collective-permute-start(f32[1,128,256]{2,1,0:T(8,128)S(1)} %get-tuple-element.95), channel_id=1, source_target_pairs={{0,240},{2,242},{4,244},{6,246},{8,248},{10,250},{12,252},{14,254}... | collective-permute-start | bytes 393224 | tf_op jit(solution)/shard_map/ppermute | solution.py:438
  90.9 10.8 %collective-permute-start.22 = (f32[1,256,256]{2,1,0:T(8,128)}, f32[1,256,256]{2,1,0:T(8,128)}, u32[]{:S(2)}, u32[]{:S(2)}) collective-permute-start(f32[1,256,256]{2,1,0:T(8,128)} %get-tuple-element.99.refs_4_), channel_id=1, source_target_pairs={{0,1},{1,0},{2,3},{3,2},{4,5},{5,4},{6,7},{7,6},{8,9},{9,8},{10,11... | collective-permute-start | bytes 786440 | tf_op jit(solution)/shard_map/ppermute | solution.py:442
  95.0 12.0 %collective-permute-start.23 = (f32[1,256,256]{2,1,0:T(8,128)}, f32[1,256,256]{2,1,0:T(8,128)}, u32[]{:S(2)}, u32[]{:S(2)}) collective-permute-start(f32[1,256,256]{2,1,0:T(8,128)} %rows_first.1.refs_1_), channel_id=1, source_target_pairs={{0,1},{1,0},{2,3},{3,2},{4,5},{5,4},{6,7},{7,6},{8,9},{9,8},{10,11... | collective-permute-start | bytes 786440 | tf_op jit(solution)/shard_map/ppermute | solution.py:442
  99.6 2.1 %copy-start.9 = (f32[1,256,256]{2,1,0:T(8,128)S(1)}, f32[1,256,256]{2,1,0:T(8,128)}, u32[]{:S(2)}) copy-start(f32[1,256,256]{2,1,0:T(8,128)} %copy-done.8) | copy-start | bytes 786436
  (3 other events, 4.8 us)

commit v12 on v10

--- a/solution.py
+++ b/solution.py
@@ -267,7 +267,7 @@
     out_c[...] = canvas[:, :, h : h + n]
 
 
-def back_first_kernel(info, bar, probe, patch, diag, corner, mat, keep, send, part, grad, held):
+def back_first_kernel(info, bar, probe, patch, diag, corner, mat, keep, send, part, held):
     n = patch.shape[-1]
     rows = by_mode(
         held, probe.shape[1], lambda m: prop_left(diag, corner, bar[m, 0], bar[m, 1])
@@ -282,11 +282,9 @@
         g_im += p_re * b_im - p_im * b_re
         part[0, m] = o_re * b_re + o_im * b_im
         part[1, m] = o_re * b_im - o_im * b_re
-    grad[0] = g_re
-    grad[1] = g_im
-    mode = info[4]
-    keep[0] = grad[mode]
-    send[0] = grad[1 - mode]
+    first = info[4] == 0
+    keep[0] = jnp.where(first, g_re, g_im)
+    send[0] = jnp.where(first, g_im, g_re)
 
 
 def probe_sum_kernel(part0, part1, total):
@@ -572,7 +570,7 @@
         "back_first_0",
         (one, one, probes),
         (info, bar0, probe, patch_first0, *back_prop),
-        scratch=(pair, held),
+        scratch=(held,),
     )
     got0 = swap_mode(send0)
     bar1, out_a, out_c, out_b = call(
@@ -602,7 +600,7 @@
         "back_first_1",
         (one, one, probes),
         (info, bar1, probe, patch_first1, *back_prop),
-        scratch=(pair, held),
+        scratch=(held,),
     )
     got1 = swap_mode(send1)
     strips_last = fold_cols("cols_last", out_a, out_c, out_b, (keep1,))

time: 108 us -> 108 us (level)
  no operation moved by 1% of the time
where the time goes in v12:
time: 108 us
  starting transfers between devices  51.1 us (47%)
  Pallas kernels  35.9 us (33%)
  waiting for transfers between devices  17.7 us (16%)
  between operations  1.81 us (2%)
  local copies, waits for them, and re-layouts  1.36 us (1%)
    ppermute x17, starting transfers between devices, swap(): return lax.ppermute(value, 'tile', pairs)  38.9 us
    pallas_call x23, Pallas kernels, call(): pl.pallas_call(run, out_shape=tuple((jax.ShapeDtypeStruct(shape, dtype) f...  35.9 us
    ppermute x7, starting transfers between devices, swap_mode(): return lax.ppermute(value, 'mode', [(0, 1), (1, 0)])  12.2 us
    ppermute x7, waiting for transfers between devices, swap_mode(): return lax.ppermute(value, 'mode', [(0, 1), (1, 0)])  8.9 us
    ppermute x17, waiting for transfers between devices, swap(): return lax.ppermute(value, 'tile', pairs)  8.82 us
  transfers between devices with their start and end apart: 24, of which 10 were waited for; matrix products, arithmetic and copies ran while one was open for 0% of the time, Pallas kernels for 26%

profile of v12, /device:TPU:1, one launch (start us, length us, event | category | flops | bytes accessed | tf_op | source)
XLA Modules:
  0.0 107.9 jit_solution(16876285545885209614)
XLA Ops:
  2.7 2.6 %collective-permute-start.3 = (f32[2,128,256]{2,1,0:T(8,128)S(1)}, f32[2,128,256]{2,1,0:T(8,128)S(1)}, u32[]{:S(2)}, u32[]{:S(2)}) collective-permute-start(f32[2,128,256]{2,1,0:T(8,128)S(1)} %get-tuple-element.54), channel_id=1, source_target_pairs={{0,16},{2,18},{4,20},{6,22},{8,24},{10,26},{12,28},{14,30},{16,0},... | collective-permute-start | bytes 786440 | tf_op jit(solution)/shard_map/ppermute | solution.py:442
  5.3 5.7 %collective-permute-start.4 = (f32[2,128,256]{2,1,0:T(8,128)S(1)}, f32[2,128,256]{2,1,0:T(8,128)S(1)}, u32[]{:S(2)}, u32[]{:S(2)}) collective-permute-start(f32[2,128,256]{2,1,0:T(8,128)S(1)} %get-tuple-element.55), channel_id=1, source_target_pairs={{0,240},{2,242},{4,244},{6,246},{8,248},{10,250},{12,252},{14,254}... | collective-permute-start | bytes 786440 | tf_op jit(solution)/shard_map/ppermute | solution.py:442
  11.5 2.4 %collective-permute-start.2 = (f32[2,2,256,128]{3,2,1,0:T(8,128)S(1)}, f32[2,2,256,128]{3,2,1,0:T(8,128)S(1)}, u32[]{:S(2)}, u32[]{:S(2)}) collective-permute-start(f32[2,2,256,128]{3,2,1,0:T(8,128)S(1)} %pick_cols.1), channel_id=1, source_target_pairs={{0,14},{2,4},{4,2},{6,8},{8,6},{10,12},{12,10},{14,0},{16,30},{18,... | collective-permute-start | bytes 1572872 | tf_op jit(solution)/shard_map/ppermute | solution.py:442
  14.0 1.5 %collective-permute-start.1 = (f32[2,128,256]{2,1,0:T(8,128)S(1)}, f32[2,128,256]{2,1,0:T(8,128)S(1)}, u32[]{:S(2)}, u32[]{:S(2)}) collective-permute-start(f32[2,128,256]{2,1,0:T(8,128)S(1)} %get-tuple-element.53), channel_id=1, source_target_pairs={{0,240},{2,242},{4,244},{6,246},{8,248},{10,250},{12,252},{14,254}... | collective-permute-start | bytes 786440 | tf_op jit(solution)/shard_map/ppermute | solution.py:442
  17.3 3.1 %collective-permute-start.5 = (f32[2,2,128,128]{3,2,1,0:T(8,128)S(1)}, f32[2,2,128,128]{3,2,1,0:T(8,128)S(1)}, u32[]{:S(2)}, u32[]{:S(2)}) collective-permute-start(f32[2,2,128,128]{3,2,1,0:T(8,128)S(1)} %get-tuple-element.58), channel_id=1, source_target_pairs={{0,14},{2,4},{4,2},{6,8},{8,6},{10,12},{12,10},{14,0},{16,30},{18,... | collective-permute-start | bytes 786440 | tf_op jit(solution)/shard_map/ppermute | solution.py:442
  21.3 2.1 %collective-permute-done.1.refs_3_.refs_4_ = f32[2,128,256]{2,1,0:T(8,128)S(1)} collective-permute-done((f32[2,128,256]{2,1,0:T(8,128)S(1)}, f32[2,128,256]{2,1,0:T(8,128)S(1)}, u32[]{:S(2)}, u32[]{:S(2)}) %collective-permute-start.1) | collective-permute-done | bytes 262176 | tf_op jit(solution)/shard_map/ppermute | solution.py:442
  23.4 1.3 %collective-permute-done.5.refs_6_.refs_7_ = f32[2,2,128,128]{3,2,1,0:T(8,128)S(1)} collective-permute-done((f32[2,2,128,128]{3,2,1,0:T(8,128)S(1)}, f32[2,2,128,128]{3,2,1,0:T(8,128)S(1)}, u32[]{:S(2)}, u32[]{:S(2)}) %collective-permute-start.5) | collective-permute-done | bytes 262176 | tf_op jit(solution)/shard_map/ppermute | solution.py:442
  25.3 1.6 %collective-permute-start.6 = (f32[2,512,128]{2,1,0:T(8,128)S(1)}, f32[2,512,128]{2,1,0:T(8,128)S(1)}, u32[]{:S(2)}, u32[]{:S(2)}) collective-permute-start(f32[2,512,128]{2,1,0:T(8,128)S(1)} %get-tuple-element.59), channel_id=1, source_target_pairs={{0,2},{2,0},{4,6},{6,4},{8,10},{10,8},{12,14},{14,12},{16,18},{18,... | collective-permute-start | bytes 1572872 | tf_op jit(solution)/shard_map/ppermute | solution.py:442
  27.1 3.2 %waves_0.1 = (f32[2,512,512]{2,1,0:T(8,128)S(1)}, f32[2,256,256]{2,1,0:T(8,128)S(1)}, f32[6,2,256,256]{3,2,1,0:T(8,128)S(1)}) custom-call(s32[2,2]{1,0:T(2,128)S(1)} %bitcast.15, s32[5]{0:T(128)S(1)} %convert_element_type.3.refs_0_.refs_1_.refs_2_, f32[2,2,256,256]{3,2,1,0:T(8,128)S(1)} %bitcast.12, ...), custom_call_target="tpu_custom_call" | custom-call | tf_op jit(solution)/shard_map/waves_0/pallas_call | solution.py:460
  30.3 2.9 %waves_1.1 = (f32[2,256,256]{2,1,0:T(8,128)S(1)}, f32[6,2,256,256]{3,2,1,0:T(8,128)S(1)}) custom-call(s32[2,2]{1,0:T(2,128)S(1)} %bitcast.16, f32[2,512,512]{2,1,0:T(8,128)S(1)} %get-tuple-element.66.refs_1_, f32[2,6,256,256]{3,2,1,0:T(8,128)S(1)} %get-tuple-element.57.refs_4_.refs_8_.refs_2_, bf16[2,256,256]{2,1,0:T(8,128)(2,1)S(1)} %get-tuple-element.61.refs_9_.refs_3_, ...), custom_call_target="tpu_custom_call" | custom-call | tf_op jit(solution)/shard_map/waves_1/pallas_call | solution.py:460
  33.2 2.8 %fars_0.1 = (f32[2,512,512]{2,1,0:T(8,128)S(1)}, f32[2,256,256]{2,1,0:T(8,128)S(1)}, f32[6,2,256,256]{3,2,1,0:T(8,128)S(1)}, f32[256,256]{1,0:T(8,128)S(1)}) custom-call(s32[2,2]{1,0:T(2,128)S(1)} %bitcast.17, s32[5]{0:T(128)S(1)} %convert_element_type.3.refs_0_.refs_1_.refs_2_, f32[2,2,256,256]{3,2,1,0:T(8,128)S(1)} %bitcast.13, ...), custom_call_target="tpu_custom_call" | custom-call | tf_op jit(solution)/shard_map/fars_0/pallas_call | solution.py:460
  36.0 2.7 %collective-permute-start.9 = (f32[256,256]{1,0:T(8,128)S(1)}, f32[256,256]{1,0:T(8,128)S(1)}, u32[]{:S(2)}, u32[]{:S(2)}) collective-permute-start(f32[256,256]{1,0:T(8,128)S(1)} %get-tuple-element.68.refs_1_), channel_id=1, source_target_pairs={{0,1},{1,0},{2,3},{3,2},{4,5},{5,4},{6,7},{7,6},{8,9},{9,8},{10,11... | collective-permute-start | bytes 786440 | tf_op jit(solution)/shard_map/ppermute | solution.py:446
  38.7 2.5 %fars_1.1 = (f32[2,256,256]{2,1,0:T(8,128)S(1)}, f32[6,2,256,256]{3,2,1,0:T(8,128)S(1)}, f32[256,256]{1,0:T(8,128)S(1)}) custom-call(s32[2,2]{1,0:T(2,128)S(1)} %bitcast.18, f32[2,512,512]{2,1,0:T(8,128)S(1)} %get-tuple-element.79.refs_1_, f32[6,2,256,256]{3,2,1,0:T(8,128)S(1)} %get-tuple-element.80.refs_2_.refs_8_, ...), custom_call_target="tpu_custom_call" | custom-call | tf_op jit(solution)/shard_map/fars_1/pallas_call | solution.py:460
  42.5 1.5 %reorder.1.refs_3_.refs_6_ = f32[2,256,256]{2,1,0:T(8,128)S(1)} custom-call(f32[2,256,256]{2,1,0:T(8,128)S(1)} %bitcast.14), custom_call_target="tpu_custom_call" | custom-call | tf_op jit(solution)/shard_map/reorder/pallas_call | solution.py:460
  44.0 1.9 %back_last_0.1 = (f32[2,256,256]{2,1,0:T(8,128)S(1)}, bf16[6,2,256,256]{3,2,1,0:T(8,128)(2,1)S(1)}) custom-call(s32[1]{0:T(128)S(6)} %copy.11.refs_0_, f32[256,256]{1,0:T(8,128)S(1)} %get-tuple-element.68.refs_1_, f32[256,256]{1,0:T(8,128)S(1)} %collective-permute-done.9.refs_2_, f32[2,256,256]{2,1,0:T(8,128)S(1)} %reorder.1.refs_3_.refs_6_, ...), custom_call_target="tpu_custom_call" | custom-call | tf_op jit(solution)/shard_map/back_last_0/pallas_call | solution.py:460
  45.9 2.7 %back_first_0.1 = (f32[1,256,256]{2,1,0:T(8,128)S(1)}, f32[1,256,256]{2,1,0:T(8,128)S(1)}, f32[2,6,256,256]{3,2,1,0:T(8,128)S(1)}) custom-call(s32[5]{0:T(128)S(1)} %convert_element_type.3.refs_0_.refs_1_.refs_2_, bf16[6,2,256,256]{3,2,1,0:T(8,128)(2,1)S(1)} %get-tuple-element.71.refs_1_, f32[2,6,256,256]{3,2,1,0:T(8,128)S(1)} %get-tuple-element.57.refs_4_.refs_8_.refs_2_, ...), custom_call_target="tpu_custom_call" | custom-call | tf_op jit(solution)/shard_map/back_first_0/pallas_call | solution.py:460
  49.0 3.4 %back_last_1.1 = (bf16[6,2,256,256]{3,2,1,0:T(8,128)(2,1)S(1)}, f32[2,512,128]{2,1,0:T(8,128)S(1)}, f32[2,512,256]{2,1,0:T(8,128)S(1)}, f32[2,512,128]{2,1,0:T(8,128)S(1)}) custom-call(s32[1]{0:T(128)S(6)} %copy.11.refs_0_, s32[2,2]{1,0:T(2,128)S(1)} %bitcast.19, s32[5]{0:T(128)S(1)} %convert_element_type.3.refs_0_.refs_1_.refs_2_, ...), custom_call_target="tpu_custom_call" | custom-call | tf_op jit(solution)/shard_map/back_last_1/pallas_call | solution.py:460
  52.5 3.3 %collective-permute-start.13 = (f32[2,512,128]{2,1,0:T(8,128)S(1)}, f32[2,512,128]{2,1,0:T(8,128)S(1)}, u32[]{:S(2)}, u32[]{:S(2)}) collective-permute-start(f32[2,512,128]{2,1,0:T(8,128)S(1)} %get-tuple-element.88), channel_id=1, source_target_pairs={{0,2},{2,0},{4,6},{6,4},{8,10},{10,8},{12,14},{14,12},{16,18},{18,... | collective-permute-start | bytes 1572872 | tf_op jit(solution)/shard_map/ppermute | solution.py:442
  57.0 2.6 %collective-permute-start.10 = (f32[1,256,256]{2,1,0:T(8,128)S(1)}, f32[1,256,256]{2,1,0:T(8,128)S(1)}, u32[]{:S(2)}, u32[]{:S(2)}) collective-permute-start(f32[1,256,256]{2,1,0:T(8,128)S(1)} %get-tuple-element.77), channel_id=1, source_target_pairs={{0,1},{1,0},{2,3},{3,2},{4,5},{5,4},{6,7},{7,6},{8,9},{9,8},{10,11... | collective-permute-start | bytes 786440 | tf_op jit(solution)/shard_map/ppermute | solution.py:446
  59.6 2.7 %back_first_1.1 = (f32[1,256,256]{2,1,0:T(8,128)S(1)}, f32[1,256,256]{2,1,0:T(8,128)S(1)}, f32[2,6,256,256]{3,2,1,0:T(8,128)S(1)}) custom-call(s32[5]{0:T(128)S(1)} %convert_element_type.3.refs_0_.refs_1_.refs_2_, bf16[6,2,256,256]{3,2,1,0:T(8,128)(2,1)S(1)} %get-tuple-element.84.refs_1_, f32[2,6,256,256]{3,2,1,0:T(8,128)S(1)} %get-tuple-element.57.refs_4_.refs_8_.refs_2_, ...), custom_call_target="tpu_custom_call" | custom-call | tf_op jit(solution)/shard_map/back_first_1/pallas_call | solution.py:460
  62.7 2.0 %collective-permute-done.14.refs_3_ = f32[2,512,128]{2,1,0:T(8,128)S(1)} collective-permute-done((f32[2,512,128]{2,1,0:T(8,128)S(1)}, f32[2,512,128]{2,1,0:T(8,128)S(1)}, u32[]{:S(2)}, u32[]{:S(2)}) %collective-permute-start.14) | collective-permute-done | bytes 524320 | tf_op jit(solution)/shard_map/ppermute | solution.py:442
  65.4 4.3 %collective-permute-start.20 = (f32[2,128,256]{2,1,0:T(8,128)S(1)}, f32[2,128,256]{2,1,0:T(8,128)S(1)}, u32[]{:S(2)}, u32[]{:S(2)}) collective-permute-start(f32[2,128,256]{2,1,0:T(8,128)S(1)} %get-tuple-element.97), channel_id=1, source_target_pairs={{0,240},{2,242},{4,244},{6,246},{8,248},{10,250},{12,252},{14,254}... | collective-permute-start | bytes 786440 | tf_op jit(solution)/shard_map/ppermute | solution.py:442
  71.3 7.5 %collective-permute-start.16 = (f32[1,512,128]{2,1,0:T(8,128)S(1)}, f32[1,512,128]{2,1,0:T(8,128)S(1)}, u32[]{:S(2)}, u32[]{:S(2)}) collective-permute-start(f32[1,512,128]{2,1,0:T(8,128)S(1)} %get-tuple-element.92), channel_id=1, source_target_pairs={{0,14},{2,4},{4,2},{6,8},{8,6},{10,12},{12,10},{14,0},{16,30},{18,... | collective-permute-start | bytes 786440 | tf_op jit(solution)/shard_map/ppermute | solution.py:442
  78.7 1.6 %collective-permute-start.15 = (f32[1,512,128]{2,1,0:T(8,128)S(1)}, f32[1,512,128]{2,1,0:T(8,128)S(1)}, u32[]{:S(2)}, u32[]{:S(2)}) collective-permute-start(f32[1,512,128]{2,1,0:T(8,128)S(1)} %get-tuple-element.91.refs_5_), channel_id=1, source_target_pairs={{0,2},{2,0},{4,6},{6,4},{8,10},{10,8},{12,14},{14,12},{16,18},{18,... | collective-permute-start | bytes 786440 | tf_op jit(solution)/shard_map/ppermute | solution.py:442
  81.0 3.5 %collective-permute-start.21 = (f32[1,256,256]{2,1,0:T(8,128)S(1)}, f32[1,256,256]{2,1,0:T(8,128)S(1)}, u32[]{:S(2)}, u32[]{:S(2)}) collective-permute-start(f32[1,256,256]{2,1,0:T(8,128)S(1)} %get-tuple-element.98.refs_2_), channel_id=1, source_target_pairs={{0,1},{1,0},{2,3},{3,2},{4,5},{5,4},{6,7},{7,6},{8,9},{9,8},{10,11... | collective-permute-start | bytes 786440 | tf_op jit(solution)/shard_map/ppermute | solution.py:446
  86.2 3.9 %collective-permute-start.18 = (f32[1,128,256]{2,1,0:T(8,128)S(1)}, f32[1,128,256]{2,1,0:T(8,128)S(1)}, u32[]{:S(2)}, u32[]{:S(2)}) collective-permute-start(f32[1,128,256]{2,1,0:T(8,128)S(1)} %get-tuple-element.95), channel_id=1, source_target_pairs={{0,240},{2,242},{4,244},{6,246},{8,248},{10,250},{12,252},{14,254}... | collective-permute-start | bytes 393224 | tf_op jit(solution)/shard_map/ppermute | solution.py:442
  90.1 1.8 %collective-permute-start.23 = (f32[1,256,256]{2,1,0:T(8,128)S(1)}, f32[1,256,256]{2,1,0:T(8,128)S(1)}, u32[]{:S(2)}, u32[]{:S(2)}) collective-permute-start(f32[1,256,256]{2,1,0:T(8,128)S(1)} %get-tuple-element.99.refs_4_), channel_id=1, source_target_pairs={{0,1},{1,0},{2,3},{3,2},{4,5},{5,4},{6,7},{7,6},{8,9},{9,8},{10,11... | collective-permute-start | bytes 786440 | tf_op jit(solution)/shard_map/ppermute | solution.py:446
  91.9 1.9 %collective-permute-done.18.refs_3_ = f32[1,128,256]{2,1,0:T(8,128)S(1)} collective-permute-done((f32[1,128,256]{2,1,0:T(8,128)S(1)}, f32[1,128,256]{2,1,0:T(8,128)S(1)}, u32[]{:S(2)}, u32[]{:S(2)}) %collective-permute-start.18) | collective-permute-done | bytes 131104 | tf_op jit(solution)/shard_map/ppermute | solution.py:442
  95.0 2.0 %probe_sum.1 = f32[1,2,6,256,256]{4,3,2,1,0:T(8,128)} custom-call(f32[2,6,256,256]{3,2,1,0:T(8,128)S(1)} %get-tuple-element.100.refs_0_, f32[2,6,256,256]{3,2,1,0:T(8,128)S(1)} %get-tuple-element.101.refs_1_), custom_call_target="tpu_custom_call" | custom-call | tf_op jit(solution)/shard_map/probe_sum/pallas_call | solution.py:460
  96.9 3.9 %collective-permute-done.23.refs_5_ = f32[1,256,256]{2,1,0:T(8,128)S(1)} collective-permute-done((f32[1,256,256]{2,1,0:T(8,128)S(1)}, f32[1,256,256]{2,1,0:T(8,128)S(1)}, u32[]{:S(2)}, u32[]{:S(2)}) %collective-permute-start.23) | collective-permute-done | bytes 262176 | tf_op jit(solution)/shard_map/ppermute | solution.py:446
  100.8 1.5 %finish_last.1.refs_2_ = f32[1,2,2,256,256]{4,3,2,1,0:T(8,128)} custom-call(s32[5]{0:T(128)S(1)} %convert_element_type.3.refs_0_.refs_1_.refs_2_, f32[1,256,256]{2,1,0:T(8,128)S(1)} %rows_first.1.refs_1_, f32[1,256,256]{2,1,0:T(8,128)S(1)} %get-tuple-element.98.refs_2_, f32[1,256,256]{2,1,0:T(8,128)S(1)} %collective-permute-done.21.refs_4_.refs_3_, ...), custom_call_target="tpu_custom_call" | custom-call | tf_op jit(solution)/shard_map/finish_last/pallas_call | solution.py:460
  102.3 4.1 %collective-permute-done.22.refs_1_ = f32[1,256,256]{2,1,0:T(8,128)S(1)} collective-permute-done((f32[1,256,256]{2,1,0:T(8,128)S(1)}, f32[1,256,256]{2,1,0:T(8,128)S(1)}, u32[]{:S(2)}, u32[]{:S(2)}) %collective-permute-start.22) | collective-permute-done | bytes 262176 | tf_op jit(solution)/shard_map/ppermute | solution.py:446
  (55 shorter events, 15.7 us)
Async XLA Ops:
  0.8 1.2 %copy-start = (f32[1,2,2,256,256]{4,3,2,1,0:T(8,128)S(1)}, f32[1,2,2,256,256]{4,3,2,1,0:T(8,128)}, u32[]{:S(2)}) copy-start(f32[1,2,2,256,256]{4,3,2,1,0:T(8,128)} %param.7) | copy-start | bytes 3145732
  2.0 18.3 %copy-start.2 = (f32[2,6,256,256]{3,2,1,0:T(8,128)S(1)}, f32[2,6,256,256]{3,2,1,0:T(8,128)}, u32[]{:S(2)}) copy-start(f32[2,6,256,256]{3,2,1,0:T(8,128)} %refs_1_.1) | copy-start | bytes 9437188
  2.0 18.3 %copy-start.3 = (bf16[4,256,256]{2,1,0:T(8,128)(2,1)S(1)}, bf16[4,256,256]{2,1,0:T(8,128)(2,1)}, u32[]{:S(2)}) copy-start(bf16[4,256,256]{2,1,0:T(8,128)(2,1)} %constant.54.clone.refs_2_) | copy-start | bytes 1572868
  2.0 18.3 %copy-start.5 = (bf16[2,256,256]{2,1,0:T(8,128)(2,1)S(1)}, bf16[2,256,256]{2,1,0:T(8,128)(2,1)}, u32[]{:S(2)}) copy-start(bf16[2,256,256]{2,1,0:T(8,128)(2,1)} %refs_0_.3) | copy-start | bytes 786436
  2.7 12.7 %collective-permute-start.3 = (f32[2,128,256]{2,1,0:T(8,128)S(1)}, f32[2,128,256]{2,1,0:T(8,128)S(1)}, u32[]{:S(2)}, u32[]{:S(2)}) collective-permute-start(f32[2,128,256]{2,1,0:T(8,128)S(1)} %get-tuple-element.54), channel_id=1, source_target_pairs={{0,16},{2,18},{4,20},{6,22},{8,24},{10,26},{12,28},{14,30},{16,0},... | collective-permute-start | bytes 786440 | tf_op jit(solution)/shard_map/ppermute | solution.py:442
  5.3 11.4 %collective-permute-start.4 = (f32[2,128,256]{2,1,0:T(8,128)S(1)}, f32[2,128,256]{2,1,0:T(8,128)S(1)}, u32[]{:S(2)}, u32[]{:S(2)}) collective-permute-start(f32[2,128,256]{2,1,0:T(8,128)S(1)} %get-tuple-element.55), channel_id=1, source_target_pairs={{0,240},{2,242},{4,244},{6,246},{8,248},{10,250},{12,252},{14,254}... | collective-permute-start | bytes 786440 | tf_op jit(solution)/shard_map/ppermute | solution.py:442
  11.5 13.2 %copy-start.1 = (f32[1,2,2,256,256]{4,3,2,1,0:T(8,128)S(1)}, f32[1,2,2,256,256]{4,3,2,1,0:T(8,128)}, u32[]{:S(2)}) copy-start(f32[1,2,2,256,256]{4,3,2,1,0:T(8,128)} %param.7) | copy-start | bytes 3145732
  11.5 11.9 %collective-permute-start.2 = (f32[2,2,256,128]{3,2,1,0:T(8,128)S(1)}, f32[2,2,256,128]{3,2,1,0:T(8,128)S(1)}, u32[]{:S(2)}, u32[]{:S(2)}) collective-permute-start(f32[2,2,256,128]{3,2,1,0:T(8,128)S(1)} %pick_cols.1), channel_id=1, source_target_pairs={{0,14},{2,4},{4,2},{6,8},{8,6},{10,12},{12,10},{14,0},{16,30},{18,... | collective-permute-start | bytes 1572872 | tf_op jit(solution)/shard_map/ppermute | solution.py:442
  14.0 7.3 %collective-permute-start = (f32[2,128,256]{2,1,0:T(8,128)S(1)}, f32[2,128,256]{2,1,0:T(8,128)S(1)}, u32[]{:S(2)}, u32[]{:S(2)}) collective-permute-start(f32[2,128,256]{2,1,0:T(8,128)S(1)} %get-tuple-element.52), channel_id=1, source_target_pairs={{0,16},{2,18},{4,20},{6,22},{8,24},{10,26},{12,28},{14,30},{16,0},... | collective-permute-start | bytes 786440 | tf_op jit(solution)/shard_map/ppermute | solution.py:442
  14.0 9.4 %collective-permute-start.1 = (f32[2,128,256]{2,1,0:T(8,128)S(1)}, f32[2,128,256]{2,1,0:T(8,128)S(1)}, u32[]{:S(2)}, u32[]{:S(2)}) collective-permute-start(f32[2,128,256]{2,1,0:T(8,128)S(1)} %get-tuple-element.53), channel_id=1, source_target_pairs={{0,240},{2,242},{4,244},{6,246},{8,248},{10,250},{12,252},{14,254}... | collective-permute-start | bytes 786440 | tf_op jit(solution)/shard_map/ppermute | solution.py:442
  17.3 7.4 %collective-permute-start.5 = (f32[2,2,128,128]{3,2,1,0:T(8,128)S(1)}, f32[2,2,128,128]{3,2,1,0:T(8,128)S(1)}, u32[]{:S(2)}, u32[]{:S(2)}) collective-permute-start(f32[2,2,128,128]{3,2,1,0:T(8,128)S(1)} %get-tuple-element.58), channel_id=1, source_target_pairs={{0,14},{2,4},{4,2},{6,8},{8,6},{10,12},{12,10},{14,0},{16,30},{18,... | collective-permute-start | bytes 786440 | tf_op jit(solution)/shard_map/ppermute | solution.py:442
  20.3 6.8 %collective-permute-start.8 = (f32[2,512,128]{2,1,0:T(8,128)S(1)}, f32[2,512,128]{2,1,0:T(8,128)S(1)}, u32[]{:S(2)}, u32[]{:S(2)}) collective-permute-start(f32[2,512,128]{2,1,0:T(8,128)S(1)} %get-tuple-element.56.refs_3_), channel_id=1, source_target_pairs={{0,2},{2,0},{4,6},{6,4},{8,10},{10,8},{12,14},{14,12},{16,18},{18,... | collective-permute-start | bytes 1572872 | tf_op jit(solution)/shard_map/ppermute | solution.py:442
  21.0 6.2 %copy-start.6 = (s32[1,2,2]{2,1,0:T(2,128)S(1)}, s32[1,2,2]{2,1,0:T(2,128)}, u32[]{:S(2)}) copy-start(s32[1,2,2]{2,1,0:T(2,128)} %param.10) | copy-start | bytes 52
  25.3 7.9 %collective-permute-start.6 = (f32[2,512,128]{2,1,0:T(8,128)S(1)}, f32[2,512,128]{2,1,0:T(8,128)S(1)}, u32[]{:S(2)}, u32[]{:S(2)}) collective-permute-start(f32[2,512,128]{2,1,0:T(8,128)S(1)} %get-tuple-element.59), channel_id=1, source_target_pairs={{0,2},{2,0},{4,6},{6,4},{8,10},{10,8},{12,14},{14,12},{16,18},{18,... | collective-permute-start | bytes 1572872 | tf_op jit(solution)/shard_map/ppermute | solution.py:442
  26.9 6.3 %collective-permute-start.7 = (f32[2,2,128,128]{3,2,1,0:T(8,128)S(1)}, f32[2,2,128,128]{3,2,1,0:T(8,128)S(1)}, u32[]{:S(2)}, u32[]{:S(2)}) collective-permute-start(f32[2,2,128,128]{3,2,1,0:T(8,128)S(1)} %get-tuple-element.60), channel_id=1, source_target_pairs={{0,14},{2,4},{4,2},{6,8},{8,6},{10,12},{12,10},{14,0},{16,30},{18,... | collective-permute-start | bytes 786440 | tf_op jit(solution)/shard_map/ppermute | solution.py:442
  36.0 6.5 %copy-start.4 = (f32[1,2,256,256]{3,2,1,0:T(8,128)S(1)}, f32[1,2,256,256]{3,2,1,0:T(8,128)}, u32[]{:S(2)}) copy-start(f32[1,2,256,256]{3,2,1,0:T(8,128)} %param.12) | copy-start | bytes 1572868
  36.0 8.0 %collective-permute-start.9 = (f32[256,256]{1,0:T(8,128)S(1)}, f32[256,256]{1,0:T(8,128)S(1)}, u32[]{:S(2)}, u32[]{:S(2)}) collective-permute-start(f32[256,256]{1,0:T(8,128)S(1)} %get-tuple-element.68.refs_1_), channel_id=1, source_target_pairs={{0,1},{1,0},{2,3},{3,2},{4,5},{5,4},{6,7},{7,6},{8,9},{9,8},{10,11... | collective-permute-start | bytes 786440 | tf_op jit(solution)/shard_map/ppermute | solution.py:446
  41.2 7.8 %collective-permute-start.11 = (f32[256,256]{1,0:T(8,128)S(1)}, f32[256,256]{1,0:T(8,128)S(1)}, u32[]{:S(2)}, u32[]{:S(2)}) collective-permute-start(f32[256,256]{1,0:T(8,128)S(1)} %get-tuple-element.81.refs_4_), channel_id=1, source_target_pairs={{0,1},{1,0},{2,3},{3,2},{4,5},{5,4},{6,7},{7,6},{8,9},{9,8},{10,11... | collective-permute-start | bytes 786440 | tf_op jit(solution)/shard_map/ppermute | solution.py:446
  52.5 10.3 %collective-permute-start.13 = (f32[2,512,128]{2,1,0:T(8,128)S(1)}, f32[2,512,128]{2,1,0:T(8,128)S(1)}, u32[]{:S(2)}, u32[]{:S(2)}) collective-permute-start(f32[2,512,128]{2,1,0:T(8,128)S(1)} %get-tuple-element.88), channel_id=1, source_target_pairs={{0,2},{2,0},{4,6},{6,4},{8,10},{10,8},{12,14},{14,12},{16,18},{18,... | collective-permute-start | bytes 1572872 | tf_op jit(solution)/shard_map/ppermute | solution.py:442
  55.8 8.9 %collective-permute-start.14 = (f32[2,512,128]{2,1,0:T(8,128)S(1)}, f32[2,512,128]{2,1,0:T(8,128)S(1)}, u32[]{:S(2)}, u32[]{:S(2)}) collective-permute-start(f32[2,512,128]{2,1,0:T(8,128)S(1)} %get-tuple-element.89), channel_id=1, source_target_pairs={{0,14},{2,4},{4,2},{6,8},{8,6},{10,12},{12,10},{14,0},{16,30},{18,... | collective-permute-start | bytes 1572872 | tf_op jit(solution)/shard_map/ppermute | solution.py:442
  57.0 12.8 %collective-permute-start.10 = (f32[1,256,256]{2,1,0:T(8,128)S(1)}, f32[1,256,256]{2,1,0:T(8,128)S(1)}, u32[]{:S(2)}, u32[]{:S(2)}) collective-permute-start(f32[1,256,256]{2,1,0:T(8,128)S(1)} %get-tuple-element.77), channel_id=1, source_target_pairs={{0,1},{1,0},{2,3},{3,2},{4,5},{5,4},{6,7},{7,6},{8,9},{9,8},{10,11... | collective-permute-start | bytes 786440 | tf_op jit(solution)/shard_map/ppermute | solution.py:446
  62.3 7.9 %collective-permute-start.12 = (f32[1,256,256]{2,1,0:T(8,128)S(1)}, f32[1,256,256]{2,1,0:T(8,128)S(1)}, u32[]{:S(2)}, u32[]{:S(2)}) collective-permute-start(f32[1,256,256]{2,1,0:T(8,128)S(1)} %get-tuple-element.86), channel_id=1, source_target_pairs={{0,1},{1,0},{2,3},{3,2},{4,5},{5,4},{6,7},{7,6},{8,9},{9,8},{10,11... | collective-permute-start | bytes 786440 | tf_op jit(solution)/shard_map/ppermute | solution.py:446
  65.4 14.9 %collective-permute-start.20 = (f32[2,128,256]{2,1,0:T(8,128)S(1)}, f32[2,128,256]{2,1,0:T(8,128)S(1)}, u32[]{:S(2)}, u32[]{:S(2)}) collective-permute-start(f32[2,128,256]{2,1,0:T(8,128)S(1)} %get-tuple-element.97), channel_id=1, source_target_pairs={{0,240},{2,242},{4,244},{6,246},{8,248},{10,250},{12,252},{14,254}... | collective-permute-start | bytes 786440 | tf_op jit(solution)/shard_map/ppermute | solution.py:442
  69.7 10.6 %collective-permute-start.19 = (f32[2,128,256]{2,1,0:T(8,128)S(1)}, f32[2,128,256]{2,1,0:T(8,128)S(1)}, u32[]{:S(2)}, u32[]{:S(2)}) collective-permute-start(f32[2,128,256]{2,1,0:T(8,128)S(1)} %get-tuple-element.90.refs_6_), channel_id=1, source_target_pairs={{0,16},{2,18},{4,20},{6,22},{8,24},{10,26},{12,28},{14,30},{16,0},... | collective-permute-start | bytes 786440 | tf_op jit(solution)/shard_map/ppermute | solution.py:442
  71.3 14.2 %collective-permute-start.16 = (f32[1,512,128]{2,1,0:T(8,128)S(1)}, f32[1,512,128]{2,1,0:T(8,128)S(1)}, u32[]{:S(2)}, u32[]{:S(2)}) collective-permute-start(f32[1,512,128]{2,1,0:T(8,128)S(1)} %get-tuple-element.92), channel_id=1, source_target_pairs={{0,14},{2,4},{4,2},{6,8},{8,6},{10,12},{12,10},{14,0},{16,30},{18,... | collective-permute-start | bytes 786440 | tf_op jit(solution)/shard_map/ppermute | solution.py:442
  78.7 6.7 %collective-permute-start.15 = (f32[1,512,128]{2,1,0:T(8,128)S(1)}, f32[1,512,128]{2,1,0:T(8,128)S(1)}, u32[]{:S(2)}, u32[]{:S(2)}) collective-permute-start(f32[1,512,128]{2,1,0:T(8,128)S(1)} %get-tuple-element.91.refs_5_), channel_id=1, source_target_pairs={{0,2},{2,0},{4,6},{6,4},{8,10},{10,8},{12,14},{14,12},{16,18},{18,... | collective-permute-start | bytes 786440 | tf_op jit(solution)/shard_map/ppermute | solution.py:442
  81.0 12.9 %collective-permute-start.21 = (f32[1,256,256]{2,1,0:T(8,128)S(1)}, f32[1,256,256]{2,1,0:T(8,128)S(1)}, u32[]{:S(2)}, u32[]{:S(2)}) collective-permute-start(f32[1,256,256]{2,1,0:T(8,128)S(1)} %get-tuple-element.98.refs_2_), channel_id=1, source_target_pairs={{0,1},{1,0},{2,3},{3,2},{4,5},{5,4},{6,7},{7,6},{8,9},{9,8},{10,11... | collective-permute-start | bytes 786440 | tf_op jit(solution)/shard_map/ppermute | solution.py:446
  86.1 5.8 %collective-permute-start.17 = (f32[1,128,256]{2,1,0:T(8,128)S(1)}, f32[1,128,256]{2,1,0:T(8,128)S(1)}, u32[]{:S(2)}, u32[]{:S(2)}) collective-permute-start(f32[1,128,256]{2,1,0:T(8,128)S(1)} %get-tuple-element.94), channel_id=1, source_target_pairs={{0,16},{2,18},{4,20},{6,22},{8,24},{10,26},{12,28},{14,30},{16,0},... | collective-permute-start | bytes 393224 | tf_op jit(solution)/shard_map/ppermute | solution.py:442
  86.2 7.6 %collective-permute-start.18 = (f32[1,128,256]{2,1,0:T(8,128)S(1)}, f32[1,128,256]{2,1,0:T(8,128)S(1)}, u32[]{:S(2)}, u32[]{:S(2)}) collective-permute-start(f32[1,128,256]{2,1,0:T(8,128)S(1)} %get-tuple-element.95), channel_id=1, source_target_pairs={{0,240},{2,242},{4,244},{6,246},{8,248},{10,250},{12,252},{14,254}... | collective-permute-start | bytes 393224 | tf_op jit(solution)/shard_map/ppermute | solution.py:442
  90.1 10.7 %collective-permute-start.23 = (f32[1,256,256]{2,1,0:T(8,128)S(1)}, f32[1,256,256]{2,1,0:T(8,128)S(1)}, u32[]{:S(2)}, u32[]{:S(2)}) collective-permute-start(f32[1,256,256]{2,1,0:T(8,128)S(1)} %get-tuple-element.99.refs_4_), channel_id=1, source_target_pairs={{0,1},{1,0},{2,3},{3,2},{4,5},{5,4},{6,7},{7,6},{8,9},{9,8},{10,11... | collective-permute-start | bytes 786440 | tf_op jit(solution)/shard_map/ppermute | solution.py:446
  94.4 12.1 %collective-permute-start.22 = (f32[1,256,256]{2,1,0:T(8,128)S(1)}, f32[1,256,256]{2,1,0:T(8,128)S(1)}, u32[]{:S(2)}, u32[]{:S(2)}) collective-permute-start(f32[1,256,256]{2,1,0:T(8,128)S(1)} %rows_first.1.refs_1_), channel_id=1, source_target_pairs={{0,1},{1,0},{2,3},{3,2},{4,5},{5,4},{6,7},{7,6},{8,9},{9,8},{10,11... | collective-permute-start | bytes 786440 | tf_op jit(solution)/shard_map/ppermute | solution.py:446
